TPU v7x, 32 devices: a whole 2x2x4 slice. The times are simulated.
32 devices in a mesh: inline: 8 (over z, x), col: 4 (over y, core).
Axes of the slice: x: 2, y: 2, z: 4, core: 2. Of those that a mesh axis runs over, the one named last changes fastest.
Arguments:
- seismic: bfloat16 [4, 16, 32, 1024], P(None, 'inline', 'col'), may hold values from -12 to 12
- validity: int32 [4, 16, 32], P(None, 'inline', 'col'), may hold values 0 or 1
- prior_weight: float32 [16, 32], P('inline', 'col'), may hold values from 0.2 to 5
- lateral_strength: float32 [3], replicated, may hold values from 0.5 to 2
- avo_coeffs: float32 [4, 3, 1024], replicated, may hold values from -4 to 4
- wavelets: float32 [4, 129], replicated, may hold values from -0.5 to 0.5
Outputs:
- solution_field: float32 [3, 16, 32, 1024], P(None, 'inline', 'col')
- residual: float32 [3, 16, 32, 1024], P(None, 'inline', 'col')
All inputs are finite; a program needn't handle non-finite values. No bound on the sum of `validity` on one device may be relied on, other than what follows from the above.
Results may differ from a plain program's by a relative error of at most 0.0005.
Values sent between devices are 32-bit elements; how exact they have to be, the bound alone decides.
No kernel may reach another device: no remote copies, remote signals or barrier semaphores. Data moves between devices by JAX's collectives and lax.ppermute only.
A program may use at most 64 MiB of HBM per device.

v0:
```python
import functools

import jax
import jax.numpy as jnp
from jax import lax
from jax.experimental import pallas as pl
from jax.experimental.pallas import tpu as pltpu
from jax.sharding import PartitionSpec as P

LANES = 128
F32 = jnp.float32
BF16 = jnp.bfloat16


def split(value):
    high = value.astype(BF16)
    return high, (value - high.astype(F32)).astype(BF16)


def circulant(taps_ref, padded_ref, angle):
    line = jnp.broadcast_to(padded_ref[angle : angle + 1, :], (2 * LANES, 2 * LANES))
    return pltpu.roll(line, LANES, 1, stride=1, stride_axis=0)


def fill_taps(taps_ref, padded_ref):
    padded_ref[...] = jnp.zeros_like(padded_ref)
    padded_ref[0 : taps_ref.shape[0], 0 : taps_ref.shape[1]] = taps_ref[...]


def forward_band(circ):
    return jnp.concatenate(split(circ[:, :LANES]), axis=1)


def backward_band(circ):
    return jnp.concatenate(split(circ[LANES:, :]), axis=0)


def column(row):
    n = row.shape[1]
    same = lax.broadcasted_iota(jnp.int32, (n, n), 0) == lax.broadcasted_iota(jnp.int32, (n, n), 1)
    return jnp.sum(jnp.where(same, jnp.broadcast_to(row, (n, n)), 0.0), axis=1, keepdims=True)


def trace_columns(ref, *lead):
    rows = ref[lead].astype(F32) if lead else ref[...].astype(F32)
    return jnp.concatenate([column(rows[r : r + 1, :]) for r in range(rows.shape[0])], axis=0)


def windows(tiles):
    pairs = [jnp.concatenate(pair, axis=1) for pair in zip(tiles[:-1], tiles[1:])]
    return jnp.concatenate(pairs, axis=0)


def halves_sum(wide):
    return wide[:, :LANES] + wide[:, LANES:]


def forward(tiles, band):
    zero = jnp.zeros_like(tiles[0]).astype(BF16)
    highs, lows = zip(*[split(t) for t in tiles])
    n, size = len(tiles) + 1, tiles[0].shape[0]
    rows = [windows([zero, *part, zero]) for part in (highs, lows)]
    out = jnp.dot(jnp.concatenate(rows, axis=0), band, preferred_element_type=F32)
    out = halves_sum(out)
    out = out[: n * size] + out[n * size :]
    return [out[k * size : (k + 1) * size] for k in range(n)]


def backward(parts, band):
    n, size = len(parts[0]) - 1, parts[0][0].shape[0]
    rows = jnp.concatenate([windows(part) for part in parts], axis=0)
    out = lax.dot_general(rows, band, (((1,), (1,)), ((), ())), preferred_element_type=F32)
    out = halves_sum(out)
    total = out[: n * size]
    for p in range(1, len(parts)):
        total = total + out[p * n * size : (p + 1) * n * size]
    return [total[k * size : (k + 1) * size] for k in range(n)]


def coeff(avo_ref, angle, contrast, k):
    return avo_ref[angle, contrast : contrast + 1, pl.ds(k * LANES, LANES)]


def stack_tile(ref, contrast, k):
    rows = [ref[contrast, r, :, pl.ds(k * LANES, LANES)] for r in range(ref.shape[1])]
    return jnp.concatenate(rows, axis=0)


def store_tiles(out_ref, tiles):
    for c in range(out_ref.shape[0]):
        for k, tile in enumerate(tiles[c]):
            for r in range(out_ref.shape[1]):
                size = out_ref.shape[2]
                out_ref[c, r, :, pl.ds(k * LANES, LANES)] = tile[r * size : (r + 1) * size]


def store_edges(field_ref, top_ref, bottom_ref, left_ref, right_ref):
    contrasts, rows, traces, _ = field_ref.shape
    for c in range(contrasts):
        top_ref[c] = field_ref[c, 0]
        bottom_ref[c] = field_ref[c, rows - 1]
        for r in range(rows):
            left_ref[c * rows + r : c * rows + r + 1, :] = field_ref[c, r, 0:1, :]
            right_ref[c * rows + r : c * rows + r + 1, :] = field_ref[c, r, traces - 1 : traces, :]


def start_kernel(seis_ref, valid_ref, avo_ref, taps_ref, b_ref, top, bottom, left, right, padded):
    angles, rows, traces, samples = seis_ref.shape
    contrasts, n = avo_ref.shape[1], samples // LANES
    fill_taps(taps_ref, padded)
    lane = lax.broadcasted_iota(jnp.int32, (rows * traces, LANES), 1)
    total = [[None] * n for _ in range(contrasts)]
    for a in range(angles):
        mask = trace_columns(valid_ref, a)
        data = jnp.concatenate([seis_ref[a, r].astype(F32) for r in range(rows)], axis=0) * mask
        turned = [
            pltpu.roll(data[:, k * LANES : (k + 1) * LANES], LANES // 2, 1) for k in range(n)
        ]
        zero = jnp.zeros_like(turned[0])
        shifted = [
            jnp.where(lane < LANES // 2, before, here).astype(BF16)
            for before, here in zip([zero, *turned], [*turned, zero])
        ]
        band = backward_band(circulant(taps_ref, padded, a))
        result = backward([shifted], band)
        for c in range(contrasts):
            for k in range(n):
                term = coeff(avo_ref, a, c, k) * result[k]
                total[c][k] = term if a == 0 else total[c][k] + term
    store_tiles(b_ref, total)
    store_edges(b_ref, top, bottom, left, right)


def normal_kernel(field_ref, valid_ref, avo_ref, taps_ref, out_ref, padded):
    contrasts, rows, traces, samples = field_ref.shape
    angles, n = avo_ref.shape[0], samples // LANES
    fill_taps(taps_ref, padded)
    lane = lax.broadcasted_iota(jnp.int32, (rows * traces, LANES), 1)
    total = [[None] * n for _ in range(contrasts)]
    for a in range(angles):
        mask = trace_columns(valid_ref, a)
        circ = circulant(taps_ref, padded, a)
        mixed = []
        for k in range(n):
            parts = [coeff(avo_ref, a, c, k) * stack_tile(field_ref, c, k) for c in range(contrasts)]
            mixed.append(functools.reduce(jnp.add, parts))
        synth = [tile * mask for tile in forward(mixed, forward_band(circ))]
        synth[0] = jnp.where(lane < LANES // 2, 0.0, synth[0])
        synth[n] = jnp.where(lane < LANES // 2, synth[n], 0.0)
        result = backward(list(zip(*[split(t) for t in synth])), backward_band(circ))
        for c in range(contrasts):
            for k in range(n):
                term = coeff(avo_ref, a, c, k) * result[k]
                total[c][k] = term if a == 0 else total[c][k] + term
    store_tiles(out_ref, total)


def add_prior(field_ref, data_ref, prior_ref, strength_ref, above, below, left, right, out_ref):
    contrasts, rows, traces, samples = field_ref.shape
    place = lax.broadcasted_iota(jnp.int32, (traces, samples), 0)
    weights = [column(prior_ref[r : r + 1, :]) + 4.0 for r in range(rows)]
    for c in range(contrasts):
        for r in range(rows):
            here = field_ref[c, r]
            edge = c * rows + r
            west = jnp.where(place == 0, left[edge : edge + 1, :], pltpu.roll(here, 1, 0))
            east = jnp.where(
                place == traces - 1, right[edge : edge + 1, :], pltpu.roll(here, traces - 1, 0)
            )
            north = above[c] if r == 0 else field_ref[c, r - 1]
            south = below[c] if r == rows - 1 else field_ref[c, r + 1]
            prior = weights[r] * here - ((south + north) + (east + west))
            out_ref[c, r] = data_ref[c, r] + strength_ref[c] * prior


def first_image_kernel(
    field, data, prior, strength, above, below, left, right, out, o_top, o_bottom, o_left, o_right
):
    add_prior(field, data, prior, strength, above, below, left, right, out)
    store_edges(out, o_top, o_bottom, o_left, o_right)


def second_image_kernel(
    field, data, prior, strength, above, below, left, right, b_ref, out, gram_ref
):
    add_prior(field, data, prior, strength, above, below, left, right, out)
    contrasts, rows, traces, samples = field.shape
    pairs = ((b_ref, b_ref), (b_ref, field), (field, field), (field, out))
    gram_ref[...] = jnp.zeros_like(gram_ref)
    for q, (one, two) in enumerate(pairs):
        total = jnp.zeros((traces, LANES), F32)
        for c in range(contrasts):
            for r in range(rows):
                product = one[c, r] * two[c, r]
                tiles = [product[:, k : k + LANES] for k in range(0, samples, LANES)]
                total = total + functools.reduce(jnp.add, tiles)
        total = jnp.sum(jnp.sum(total, axis=0, keepdims=True), axis=1, keepdims=True)
        gram_ref[q : q + 1, :] = jnp.broadcast_to(total, (1, LANES))


def finish_kernel(gram_ref, b_ref, one_ref, two_ref, solution_ref, residual_ref):
    g00, g01, g11, g12 = (gram_ref[q : q + 1, 0:1] for q in range(4))
    first = g00 / g01
    ratio = first * g11 / g01
    second = (ratio - 1.0) * g01 / (first * g12 - ratio * g11)
    near = first + second * ratio
    far = first * second
    for c in range(b_ref.shape[0]):
        for r in range(b_ref.shape[1]):
            b, one, two = b_ref[c, r], one_ref[c, r], two_ref[c, r]
            solution_ref[c, r] = near * b - far * one
            residual_ref[c, r] = b - near * one + far * two


VMEM = pl.BlockSpec(memory_space=pltpu.VMEM)
SMEM = pl.BlockSpec(memory_space=pltpu.SMEM)


def call(kernel, outs, ins, flops, scratch=(), scalars=()):
    moved = sum(x.size * x.dtype.itemsize for x in (*ins, *outs))
    return pl.pallas_call(
        kernel,
        out_shape=outs,
        in_specs=[SMEM if i in scalars else VMEM for i in range(len(ins))],
        out_specs=jax.tree.map(lambda _: VMEM, outs),
        scratch_shapes=list(scratch),
        compiler_params=pltpu.CompilerParams(vmem_limit_bytes=24 * 1024 * 1024),
        cost_estimate=pl.CostEstimate(flops=flops, bytes_accessed=moved, transcendentals=0),
        name=kernel.__name__,
    )(*ins)


def exchange(edges):
    top, bottom, left, right = edges
    moved = []
    for axis, first, last in (("inline", top, bottom), ("col", left, right)):
        size = lax.axis_size(axis)
        ahead = [(i, i + 1) for i in range(size - 1)]
        back = [(j, i) for i, j in ahead]
        moved.append(lax.ppermute(last, axis, ahead))
        moved.append(lax.ppermute(first, axis, back))
    return moved


def shards(seismic, validity, prior_weight, lateral_strength, avo_coeffs, wavelets):
    angles, rows, traces, samples = seismic.shape
    contrasts = avo_coeffs.shape[1]
    field = jax.ShapeDtypeStruct((contrasts, rows, traces, samples), F32)
    row = jax.ShapeDtypeStruct((contrasts, traces, samples), F32)
    side = jax.ShapeDtypeStruct((contrasts * rows, samples), F32)
    edges = (row, row, side, side)
    taps = [pltpu.VMEM((8, 2 * LANES), F32)]
    work = 2 * angles * rows * traces * samples * 256 * 4

    b, *sent = call(
        start_kernel,
        (field, *edges),
        (seismic, validity, avo_coeffs, wavelets),
        work,
        taps,
    )
    around = exchange(sent)
    (data,) = call(normal_kernel, (field,), (b, validity, avo_coeffs, wavelets), 2 * work, taps)
    one, *sent = call(
        first_image_kernel,
        (field, *edges),
        (b, data, prior_weight, lateral_strength, *around),
        20 * field.size,
        scalars=(3,),
    )
    around = exchange(sent)
    (data,) = call(normal_kernel, (field,), (one, validity, avo_coeffs, wavelets), 2 * work, taps)
    two, gram = call(
        second_image_kernel,
        (field, jax.ShapeDtypeStruct((8, LANES), F32)),
        (one, data, prior_weight, lateral_strength, *around, b),
        30 * field.size,
        scalars=(3,),
    )
    gram = lax.psum(gram, ("inline", "col"))
    return tuple(call(finish_kernel, (field, field), (gram, b, one, two), 8 * field.size))


def solution(mesh):
    placed = (
        P(None, "inline", "col", None),
        P(None, "inline", "col"),
        P("inline", "col"),
        P(),
        P(),
        P(),
    )
    return jax.shard_map(
        shards,
        mesh=mesh,
        in_specs=placed,
        out_specs=(P(None, "inline", "col", None), P(None, "inline", "col", None)),
        check_vma=False,
    )
```

profile of v0, /device:TPU:0, one launch (start us, length us, event | category | flops | bytes accessed | tf_op | source)
XLA Modules:
  0.0 73.9 jit_solution(1676981051147232013)
XLA Ops:
  0.7 0.8 %copy.8.avo_ref = f32[4,3,1024]{2,1,0:T(4,128)S(1)} copy(f32[4,3,1024]{2,0,1:T(4,128)} %param.10) | data formatting | bytes 98304 | tf_op args[4]
  1.5 0.0 copy-start.2
  1.5 0.9 %copy-done.2 = bf16[4,2,8,1024]{3,2,1,0:T(8,128)(2,1)S(1)} copy-done((bf16[4,2,8,1024]{3,2,1,0:T(8,128)(2,1)S(1)}, bf16[4,2,8,1024]{3,2,1,0:T(8,128)(2,1)}, u32[]{:S(2)}) %copy-start.2) | copy-done | bytes 131096
  2.4 0.6 start_kernel.1
  3.0 4.8 %collective-permute-start = (f32[3,8,1024]{2,1,0:T(8,128)S(1)}, f32[3,8,1024]{2,1,0:T(8,128)S(1)}, u32[]{:S(2)}, u32[]{:S(2)}) collective-permute-start(f32[3,8,1024]{2,1,0:T(8,128)S(1)} %get-tuple-element.15), channel_id=1, source_target_pairs={{0,4},{4,8},{8,12},{12,16},{16,20},{20,24},{24,28},{1,5},{5,9},{9,... | collective-permute-start | bytes 294920 | tf_op jit(solution)/shard_map/ppermute | solution.py:240
  7.9 1.3 %collective-permute-start.1 = (f32[3,8,1024]{2,1,0:T(8,128)S(1)}, f32[3,8,1024]{2,1,0:T(8,128)S(1)}, u32[]{:S(2)}, u32[]{:S(2)}) collective-permute-start(f32[3,8,1024]{2,1,0:T(8,128)S(1)} %get-tuple-element.16), channel_id=1, source_target_pairs={{4,0},{8,4},{12,8},{16,12},{20,16},{24,20},{28,24},{5,1},{9,5},{13... | collective-permute-start | bytes 294920 | tf_op jit(solution)/shard_map/ppermute | solution.py:241
  9.2 1.5 %collective-permute-start.2 = (f32[6,1024]{1,0:T(8,128)S(1)}, f32[6,1024]{1,0:T(8,128)S(1)}, u32[]{:S(2)}, u32[]{:S(2)}) collective-permute-start(f32[6,1024]{1,0:T(8,128)S(1)} %get-tuple-element.17), channel_id=1, source_target_pairs={{0,1},{1,2},{2,3},{4,5},{5,6},{6,7},{8,9},{9,10},{10,11},{12,13},{... | collective-permute-start | bytes 73736 | tf_op jit(solution)/shard_map/ppermute | solution.py:240
  10.6 1.3 %collective-permute-start.3 = (f32[6,1024]{1,0:T(8,128)S(1)}, f32[6,1024]{1,0:T(8,128)S(1)}, u32[]{:S(2)}, u32[]{:S(2)}) collective-permute-start(f32[6,1024]{1,0:T(8,128)S(1)} %get-tuple-element.18), channel_id=1, source_target_pairs={{1,0},{2,1},{3,2},{5,4},{6,5},{7,6},{9,8},{10,9},{11,10},{13,12},{... | collective-permute-start | bytes 73736 | tf_op jit(solution)/shard_map/ppermute | solution.py:241
  11.9 0.0 copy-start
  11.9 0.0 copy-start.1
  12.0 0.8 %normal_kernel.2.data = f32[3,2,8,1024]{3,2,1,0:T(8,128)S(1)} custom-call(f32[3,2,8,1024]{3,2,1,0:T(8,128)S(1)} %get-tuple-element.14.field_ref.field.b_ref, s32[4,2,8]{2,1,0:T(2,128)S(1)} %copy-done.3, f32[4,3,1024]{2,1,0:T(4,128)S(1)} %copy.8.avo_ref, f32[4,129]{1,0:T(4,128)S(1)} %copy-done.4), custom_call_target="tpu_custom_call" | custom-call | flops 268435456 | bytes 444688 | tf_op jit(solution)/shard_map/normal_kernel/pallas_call | solution.py:221
  12.8 0.0 collective-permute-done.2.left
  12.8 2.5 %collective-permute-done.3.right = f32[6,1024]{1,0:T(8,128)S(1)} collective-permute-done((f32[6,1024]{1,0:T(8,128)S(1)}, f32[6,1024]{1,0:T(8,128)S(1)}, u32[]{:S(2)}, u32[]{:S(2)}) %collective-permute-start.3) | collective-permute-done | bytes 24608 | tf_op jit(solution)/shard_map/ppermute | solution.py:241
  15.3 0.0 collective-permute-done.above
  15.3 0.7 first_image_kernel.1
  16.0 4.6 %collective-permute-start.4 = (f32[3,8,1024]{2,1,0:T(8,128)S(1)}, f32[3,8,1024]{2,1,0:T(8,128)S(1)}, u32[]{:S(2)}, u32[]{:S(2)}) collective-permute-start(f32[3,8,1024]{2,1,0:T(8,128)S(1)} %get-tuple-element.20), channel_id=1, source_target_pairs={{0,4},{4,8},{8,12},{12,16},{16,20},{20,24},{24,28},{1,5},{5,9},{9,... | collective-permute-start | bytes 294920 | tf_op jit(solution)/shard_map/ppermute | solution.py:240
  20.6 1.3 %collective-permute-start.5 = (f32[3,8,1024]{2,1,0:T(8,128)S(1)}, f32[3,8,1024]{2,1,0:T(8,128)S(1)}, u32[]{:S(2)}, u32[]{:S(2)}) collective-permute-start(f32[3,8,1024]{2,1,0:T(8,128)S(1)} %get-tuple-element.21), channel_id=1, source_target_pairs={{4,0},{8,4},{12,8},{16,12},{20,16},{24,20},{28,24},{5,1},{9,5},{13... | collective-permute-start | bytes 294920 | tf_op jit(solution)/shard_map/ppermute | solution.py:241
  21.9 4.3 %collective-permute-start.6 = (f32[6,1024]{1,0:T(8,128)S(1)}, f32[6,1024]{1,0:T(8,128)S(1)}, u32[]{:S(2)}, u32[]{:S(2)}) collective-permute-start(f32[6,1024]{1,0:T(8,128)S(1)} %get-tuple-element.22), channel_id=1, source_target_pairs={{0,1},{1,2},{2,3},{4,5},{5,6},{6,7},{8,9},{9,10},{10,11},{12,13},{... | collective-permute-start | bytes 73736 | tf_op jit(solution)/shard_map/ppermute | solution.py:240
  26.1 1.3 %collective-permute-start.7 = (f32[6,1024]{1,0:T(8,128)S(1)}, f32[6,1024]{1,0:T(8,128)S(1)}, u32[]{:S(2)}, u32[]{:S(2)}) collective-permute-start(f32[6,1024]{1,0:T(8,128)S(1)} %get-tuple-element.23), channel_id=1, source_target_pairs={{1,0},{2,1},{3,2},{5,4},{6,5},{7,6},{9,8},{10,9},{11,10},{13,12},{... | collective-permute-start | bytes 73736 | tf_op jit(solution)/shard_map/ppermute | solution.py:241
  27.4 0.8 %normal_kernel.3.data = f32[3,2,8,1024]{3,2,1,0:T(8,128)S(1)} custom-call(f32[3,2,8,1024]{3,2,1,0:T(8,128)S(1)} %get-tuple-element.19.field_ref.field.one_ref, s32[4,2,8]{2,1,0:T(2,128)S(1)} %copy-done.3, f32[4,3,1024]{2,1,0:T(4,128)S(1)} %copy.8.avo_ref, f32[4,129]{1,0:T(4,128)S(1)} %copy-done.4), custom_call_target="tpu_custom_call" | custom-call | flops 268435456 | bytes 444688 | tf_op jit(solution)/shard_map/normal_kernel/pallas_call | solution.py:221
  28.3 1.0 %collective-permute-done.7.right = f32[6,1024]{1,0:T(8,128)S(1)} collective-permute-done((f32[6,1024]{1,0:T(8,128)S(1)}, f32[6,1024]{1,0:T(8,128)S(1)}, u32[]{:S(2)}, u32[]{:S(2)}) %collective-permute-start.7) | collective-permute-done | bytes 24608 | tf_op jit(solution)/shard_map/ppermute | solution.py:241
  29.2 0.8 %second_image_kernel.1 = (f32[3,2,8,1024]{3,2,1,0:T(8,128)S(1)}, f32[8,128]{1,0:T(8,128)S(1)}) custom-call(f32[3,2,8,1024]{3,2,1,0:T(8,128)S(1)} %get-tuple-element.19.field_ref.field.one_ref, f32[3,2,8,1024]{3,2,1,0:T(8,128)S(1)} %normal_kernel.3.data, f32[2,8]{1,0:T(2,128)S(1)} %copy-done, f32[3]{0:T(128)S(1)} %copy-done.1, ...), custom_call_target="tpu_custom_call" | custom-call | flops 1474560 | bytes 1036364 | tf_op jit(solution)/shard_map/second_image_kernel/pallas_call | solution.py:221
  30.0 43.0 %psum.7.gram_ref = f32[8,128]{1,0:T(8,128)S(1)} all-reduce(f32[8,128]{1,0:T(8,128)S(1)} %get-tuple-element.24), channel_id=1, replica_groups=mesh['inline'=8,'col'=4] {'inline','col'}, use_global_device_ids=true, to_apply=%region_0.0 | all-reduce | flops 1024 | bytes 8192 | tf_op jit(solution)/shard_map/psum | solution.py:280
  73.0 0.8 %finish_kernel.1 = (f32[3,2,8,1024]{3,2,1,0:T(8,128)}, f32[3,2,8,1024]{3,2,1,0:T(8,128)}) custom-call(f32[8,128]{1,0:T(8,128)S(1)} %psum.7.gram_ref, f32[3,2,8,1024]{3,2,1,0:T(8,128)S(1)} %get-tuple-element.14.field_ref.field.b_ref, f32[3,2,8,1024]{3,2,1,0:T(8,128)S(1)} %get-tuple-element.19.field_ref.field.one_ref, ...), custom_call_target="tpu_custom_call" | custom-call | flops 393216 | bytes 987136 | tf_op jit(solution)/shard_map/finish_kernel/pallas_call | solution.py:221
  (10 shorter events, 0.0 us)
Async XLA Ops:
  0.6 0.9 %copy-start.4 = (f32[4,129]{1,0:T(4,128)S(1)}, f32[4,129]{1,0:T(4,128)}, u32[]{:S(2)}) copy-start(f32[4,129]{1,0:T(4,128)} %taps_ref.5) | copy-start | bytes 6196
  0.6 0.9 %copy-start.3 = (s32[4,2,8]{2,1,0:T(2,128)S(1)}, s32[4,2,8]{2,1,0:T(2,128)}, u32[]{:S(2)}) copy-start(s32[4,2,8]{2,1,0:T(2,128)} %valid_ref.5) | copy-start | bytes 772
  1.5 0.9 %copy-start.2 = (bf16[4,2,8,1024]{3,2,1,0:T(8,128)(2,1)S(1)}, bf16[4,2,8,1024]{3,2,1,0:T(8,128)(2,1)}, u32[]{:S(2)}) copy-start(bf16[4,2,8,1024]{3,2,1,0:T(8,128)(2,1)} %seis_ref.1) | copy-start | bytes 393220
  3.0 12.3 %collective-permute-start = (f32[3,8,1024]{2,1,0:T(8,128)S(1)}, f32[3,8,1024]{2,1,0:T(8,128)S(1)}, u32[]{:S(2)}, u32[]{:S(2)}) collective-permute-start(f32[3,8,1024]{2,1,0:T(8,128)S(1)} %get-tuple-element.15), channel_id=1, source_target_pairs={{0,4},{4,8},{8,12},{12,16},{16,20},{20,24},{24,28},{1,5},{5,9},{9,... | collective-permute-start | bytes 294920 | tf_op jit(solution)/shard_map/ppermute | solution.py:240
  7.9 7.5 %collective-permute-start.1 = (f32[3,8,1024]{2,1,0:T(8,128)S(1)}, f32[3,8,1024]{2,1,0:T(8,128)S(1)}, u32[]{:S(2)}, u32[]{:S(2)}) collective-permute-start(f32[3,8,1024]{2,1,0:T(8,128)S(1)} %get-tuple-element.16), channel_id=1, source_target_pairs={{4,0},{8,4},{12,8},{16,12},{20,16},{24,20},{28,24},{5,1},{9,5},{13... | collective-permute-start | bytes 294920 | tf_op jit(solution)/shard_map/ppermute | solution.py:241
  9.2 3.6 %collective-permute-start.2 = (f32[6,1024]{1,0:T(8,128)S(1)}, f32[6,1024]{1,0:T(8,128)S(1)}, u32[]{:S(2)}, u32[]{:S(2)}) collective-permute-start(f32[6,1024]{1,0:T(8,128)S(1)} %get-tuple-element.17), channel_id=1, source_target_pairs={{0,1},{1,2},{2,3},{4,5},{5,6},{6,7},{8,9},{9,10},{10,11},{12,13},{... | collective-permute-start | bytes 73736 | tf_op jit(solution)/shard_map/ppermute | solution.py:240
  10.6 4.7 %collective-permute-start.3 = (f32[6,1024]{1,0:T(8,128)S(1)}, f32[6,1024]{1,0:T(8,128)S(1)}, u32[]{:S(2)}, u32[]{:S(2)}) collective-permute-start(f32[6,1024]{1,0:T(8,128)S(1)} %get-tuple-element.18), channel_id=1, source_target_pairs={{1,0},{2,1},{3,2},{5,4},{6,5},{7,6},{9,8},{10,9},{11,10},{13,12},{... | collective-permute-start | bytes 73736 | tf_op jit(solution)/shard_map/ppermute | solution.py:241
  11.9 3.4 %copy-start = (f32[2,8]{1,0:T(2,128)S(1)}, f32[2,8]{1,0:T(2,128)}, u32[]{:S(2)}) copy-start(f32[2,8]{1,0:T(2,128)} %prior.3) | copy-start | bytes 196
  11.9 3.4 %copy-start.1 = (f32[3]{0:T(128)S(1)}, f32[3]{0:T(128)}, u32[]{:S(2)}) copy-start(f32[3]{0:T(128)} %strength.3) | copy-start | bytes 40
  16.0 13.2 %collective-permute-start.4 = (f32[3,8,1024]{2,1,0:T(8,128)S(1)}, f32[3,8,1024]{2,1,0:T(8,128)S(1)}, u32[]{:S(2)}, u32[]{:S(2)}) collective-permute-start(f32[3,8,1024]{2,1,0:T(8,128)S(1)} %get-tuple-element.20), channel_id=1, source_target_pairs={{0,4},{4,8},{8,12},{12,16},{16,20},{20,24},{24,28},{1,5},{5,9},{9,... | collective-permute-start | bytes 294920 | tf_op jit(solution)/shard_map/ppermute | solution.py:240
  20.6 8.7 %collective-permute-start.5 = (f32[3,8,1024]{2,1,0:T(8,128)S(1)}, f32[3,8,1024]{2,1,0:T(8,128)S(1)}, u32[]{:S(2)}, u32[]{:S(2)}) collective-permute-start(f32[3,8,1024]{2,1,0:T(8,128)S(1)} %get-tuple-element.21), channel_id=1, source_target_pairs={{4,0},{8,4},{12,8},{16,12},{20,16},{24,20},{28,24},{5,1},{9,5},{13... | collective-permute-start | bytes 294920 | tf_op jit(solution)/shard_map/ppermute | solution.py:241
  21.9 6.4 %collective-permute-start.6 = (f32[6,1024]{1,0:T(8,128)S(1)}, f32[6,1024]{1,0:T(8,128)S(1)}, u32[]{:S(2)}, u32[]{:S(2)}) collective-permute-start(f32[6,1024]{1,0:T(8,128)S(1)} %get-tuple-element.22), channel_id=1, source_target_pairs={{0,1},{1,2},{2,3},{4,5},{5,6},{6,7},{8,9},{9,10},{10,11},{12,13},{... | collective-permute-start | bytes 73736 | tf_op jit(solution)/shard_map/ppermute | solution.py:240
  26.1 3.1 %collective-permute-start.7 = (f32[6,1024]{1,0:T(8,128)S(1)}, f32[6,1024]{1,0:T(8,128)S(1)}, u32[]{:S(2)}, u32[]{:S(2)}) collective-permute-start(f32[6,1024]{1,0:T(8,128)S(1)} %get-tuple-element.23), channel_id=1, source_target_pairs={{1,0},{2,1},{3,2},{5,4},{6,5},{7,6},{9,8},{10,9},{11,10},{13,12},{... | collective-permute-start | bytes 73736 | tf_op jit(solution)/shard_map/ppermute | solution.py:241
where the time goes:
time: 74.3 us; the launch traced here: 73.9 us
  blocking collectives  43 us (58%)
  starting transfers between devices  20.3 us (27%)
  Pallas kernels  4.47 us (6%)
  waiting for transfers between devices  3.54 us (5%)
  local copies, waits for them, and re-layouts  1.77 us (2%)
  between operations  0.81 us (1%)
    psum x1, blocking collectives, shards(): gram = lax.psum(gram, ('inline', 'col'))  43 us
    ppermute x4, starting transfers between devices, exchange(): moved.append(lax.ppermute(last, axis, ahead))  15.1 us
    ppermute x4, starting transfers between devices, exchange(): moved.append(lax.ppermute(first, axis, back))  5.17 us
    pallas_call x6, Pallas kernels, call(): pl.pallas_call(kernel, out_shape=outs, in_specs=[SMEM if i in scalars els...  4.47 us
    ppermute x4, waiting for transfers between devices, exchange(): moved.append(lax.ppermute(first, axis, back))  3.53 us
    unnamed x11, local copies, waits for them, and re-layouts  1.77 us
  transfers between devices with their start and end apart: 8, of which 2 were waited for; matrix products, arithmetic and copies ran while one was open for 0% of the time, Pallas kernels for 2%

commit v1 on v0

--- a/solution.py
+++ b/solution.py
@@ -195,11 +195,12 @@
                 tiles = [product[:, k : k + LANES] for k in range(0, samples, LANES)]
                 total = total + functools.reduce(jnp.add, tiles)
         total = jnp.sum(jnp.sum(total, axis=0, keepdims=True), axis=1, keepdims=True)
-        gram_ref[q : q + 1, :] = jnp.broadcast_to(total, (1, LANES))
+        gram_ref[:, q, :] = jnp.broadcast_to(total, (gram_ref.shape[0], LANES))
 
 
 def finish_kernel(gram_ref, b_ref, one_ref, two_ref, solution_ref, residual_ref):
-    g00, g01, g11, g12 = (gram_ref[q : q + 1, 0:1] for q in range(4))
+    sums = jnp.sum(gram_ref[...], axis=0)
+    g00, g01, g11, g12 = (sums[q : q + 1, 0:1] for q in range(4))
     first = g00 / g01
     ratio = first * g11 / g01
     second = (ratio - 1.0) * g01 / (first * g12 - ratio * g11)
@@ -245,6 +246,7 @@
 def shards(seismic, validity, prior_weight, lateral_strength, avo_coeffs, wavelets):
     angles, rows, traces, samples = seismic.shape
     contrasts = avo_coeffs.shape[1]
+    axes = ("inline", "col")
     field = jax.ShapeDtypeStruct((contrasts, rows, traces, samples), F32)
     row = jax.ShapeDtypeStruct((contrasts, traces, samples), F32)
     side = jax.ShapeDtypeStruct((contrasts * rows, samples), F32)
@@ -272,12 +274,12 @@
     (data,) = call(normal_kernel, (field,), (one, validity, avo_coeffs, wavelets), 2 * work, taps)
     two, gram = call(
         second_image_kernel,
-        (field, jax.ShapeDtypeStruct((8, LANES), F32)),
+        (field, jax.ShapeDtypeStruct((lax.axis_size(axes), 8, LANES), F32)),
         (one, data, prior_weight, lateral_strength, *around, b),
         30 * field.size,
         scalars=(3,),
     )
-    gram = lax.psum(gram, ("inline", "col"))
+    gram = lax.all_to_all(gram, axes, 0, 0)
     return tuple(call(finish_kernel, (field, field), (gram, b, one, two), 8 * field.size))
 
 

time: 74.3 us -> 48.3 us (0.65)
  blocking collectives: 43 us -> 17 us
    psum x1 -> x0, blocking collectives: 43 us -> none  [shards(): gram = lax.psum(gram, ('inline', 'col'))]
    all_to_all x0 -> x1, blocking collectives: none -> 17 us  [shards(): gram = lax.all_to_all(gram, axes, 0, 0)]
  transfers between devices with their start and end apart: 8 -> 8, of which waited for: 2 -> 2; matrix products, arithmetic and copies ran while one was open for 0% -> 0% of each run, Pallas kernels for 2% -> 3%
where the time goes in v1:
time: 48.3 us; the launch traced here: 47.9 us
  starting transfers between devices  20.3 us (42%)
  blocking collectives  17 us (35%)
  Pallas kernels  4.51 us (9%)
  waiting for transfers between devices  3.55 us (7%)
  local copies, waits for them, and re-layouts  1.77 us (4%)
  between operations  0.81 us (2%)
    all_to_all x1, blocking collectives, shards(): gram = lax.all_to_all(gram, axes, 0, 0)  17 us
    ppermute x4, starting transfers between devices, exchange(): moved.append(lax.ppermute(last, axis, ahead))  15.1 us
    ppermute x4, starting transfers between devices, exchange(): moved.append(lax.ppermute(first, axis, back))  5.17 us
    pallas_call x6, Pallas kernels, call(): pl.pallas_call(kernel, out_shape=outs, in_specs=[SMEM if i in scalars els...  4.51 us
    ppermute x4, waiting for transfers between devices, exchange(): moved.append(lax.ppermute(first, axis, back))  3.54 us
    unnamed x11, local copies, waits for them, and re-layouts  1.77 us
  transfers between devices with their start and end apart: 8, of which 2 were waited for; matrix products, arithmetic and copies ran while one was open for 0% of the time, Pallas kernels for 3%

profile of v1, /device:TPU:0, one launch (start us, length us, event | category | flops | bytes accessed | tf_op | source)
XLA Modules:
  0.0 47.9 jit_solution(15816726643809238768)
XLA Ops:
  0.7 0.8 %copy.8.avo_ref = f32[4,3,1024]{2,1,0:T(4,128)S(1)} copy(f32[4,3,1024]{2,0,1:T(4,128)} %param.10) | data formatting | bytes 98304 | tf_op args[4]
  1.5 0.0 copy-start.2
  1.5 0.9 %copy-done.2 = bf16[4,2,8,1024]{3,2,1,0:T(8,128)(2,1)S(1)} copy-done((bf16[4,2,8,1024]{3,2,1,0:T(8,128)(2,1)S(1)}, bf16[4,2,8,1024]{3,2,1,0:T(8,128)(2,1)}, u32[]{:S(2)}) %copy-start.2) | copy-done | bytes 131096
  2.4 0.6 %start_kernel.1 = (f32[3,2,8,1024]{3,2,1,0:T(8,128)S(1)}, f32[3,8,1024]{2,1,0:T(8,128)S(1)}, f32[3,8,1024]{2,1,0:T(8,128)S(1)}, f32[6,1024]{1,0:T(8,128)S(1)}, f32[6,1024]{1,0:T(8,128)S(1)}) custom-call(bf16[4,2,8,1024]{3,2,1,0:T(8,128)(2,1)S(1)} %copy-done.2, s32[4,2,8]{2,1,0:T(2,128)S(1)} %copy-done.3, f32[4,3,1024]{2,1,0:T(4,128)S(1)} %copy.8.avo_ref, ...), custom_call_target="tpu_custom_call" | custom-call | flops 134217728 | bytes 624912 | tf_op jit(solution)/shard_map/start_kernel/pallas_call | solution.py:222
  3.0 4.8 %collective-permute-start = (f32[3,8,1024]{2,1,0:T(8,128)S(1)}, f32[3,8,1024]{2,1,0:T(8,128)S(1)}, u32[]{:S(2)}, u32[]{:S(2)}) collective-permute-start(f32[3,8,1024]{2,1,0:T(8,128)S(1)} %get-tuple-element.15), channel_id=1, source_target_pairs={{0,4},{4,8},{8,12},{12,16},{16,20},{20,24},{24,28},{1,5},{5,9},{9,... | collective-permute-start | bytes 294920 | tf_op jit(solution)/shard_map/ppermute | solution.py:241
  7.9 1.3 %collective-permute-start.1 = (f32[3,8,1024]{2,1,0:T(8,128)S(1)}, f32[3,8,1024]{2,1,0:T(8,128)S(1)}, u32[]{:S(2)}, u32[]{:S(2)}) collective-permute-start(f32[3,8,1024]{2,1,0:T(8,128)S(1)} %get-tuple-element.16), channel_id=1, source_target_pairs={{4,0},{8,4},{12,8},{16,12},{20,16},{24,20},{28,24},{5,1},{9,5},{13... | collective-permute-start | bytes 294920 | tf_op jit(solution)/shard_map/ppermute | solution.py:242
  9.2 1.5 %collective-permute-start.2 = (f32[6,1024]{1,0:T(8,128)S(1)}, f32[6,1024]{1,0:T(8,128)S(1)}, u32[]{:S(2)}, u32[]{:S(2)}) collective-permute-start(f32[6,1024]{1,0:T(8,128)S(1)} %get-tuple-element.17), channel_id=1, source_target_pairs={{0,1},{1,2},{2,3},{4,5},{5,6},{6,7},{8,9},{9,10},{10,11},{12,13},{... | collective-permute-start | bytes 73736 | tf_op jit(solution)/shard_map/ppermute | solution.py:241
  10.6 1.3 %collective-permute-start.3 = (f32[6,1024]{1,0:T(8,128)S(1)}, f32[6,1024]{1,0:T(8,128)S(1)}, u32[]{:S(2)}, u32[]{:S(2)}) collective-permute-start(f32[6,1024]{1,0:T(8,128)S(1)} %get-tuple-element.18), channel_id=1, source_target_pairs={{1,0},{2,1},{3,2},{5,4},{6,5},{7,6},{9,8},{10,9},{11,10},{13,12},{... | collective-permute-start | bytes 73736 | tf_op jit(solution)/shard_map/ppermute | solution.py:242
  11.9 0.0 copy-start
  11.9 0.0 copy-start.1
  12.0 0.8 %normal_kernel.2.data = f32[3,2,8,1024]{3,2,1,0:T(8,128)S(1)} custom-call(f32[3,2,8,1024]{3,2,1,0:T(8,128)S(1)} %get-tuple-element.14.field_ref.field.b_ref, s32[4,2,8]{2,1,0:T(2,128)S(1)} %copy-done.3, f32[4,3,1024]{2,1,0:T(4,128)S(1)} %copy.8.avo_ref, f32[4,129]{1,0:T(4,128)S(1)} %copy-done.4), custom_call_target="tpu_custom_call" | custom-call | flops 268435456 | bytes 444688 | tf_op jit(solution)/shard_map/normal_kernel/pallas_call | solution.py:222
  12.8 2.5 %collective-permute-done.3.right = f32[6,1024]{1,0:T(8,128)S(1)} collective-permute-done((f32[6,1024]{1,0:T(8,128)S(1)}, f32[6,1024]{1,0:T(8,128)S(1)}, u32[]{:S(2)}, u32[]{:S(2)}) %collective-permute-start.3) | collective-permute-done | bytes 24608 | tf_op jit(solution)/shard_map/ppermute | solution.py:242
  15.3 0.0 collective-permute-done.1.below
  15.3 0.7 %first_image_kernel.1 = (f32[3,2,8,1024]{3,2,1,0:T(8,128)S(1)}, f32[3,8,1024]{2,1,0:T(8,128)S(1)}, f32[3,8,1024]{2,1,0:T(8,128)S(1)}, f32[6,1024]{1,0:T(8,128)S(1)}, f32[6,1024]{1,0:T(8,128)S(1)}) custom-call(f32[3,2,8,1024]{3,2,1,0:T(8,128)S(1)} %get-tuple-element.14.field_ref.field.b_ref, f32[3,2,8,1024]{3,2,1,0:T(8,128)S(1)} %normal_kernel.2.data, ...), custom_call_target="tpu_custom_call" | custom-call | flops 983040 | bytes 1081420 | tf_op jit(solution)/shard_map/first_image_kernel/pallas_call | solution.py:222
  16.0 4.6 %collective-permute-start.4 = (f32[3,8,1024]{2,1,0:T(8,128)S(1)}, f32[3,8,1024]{2,1,0:T(8,128)S(1)}, u32[]{:S(2)}, u32[]{:S(2)}) collective-permute-start(f32[3,8,1024]{2,1,0:T(8,128)S(1)} %get-tuple-element.20), channel_id=1, source_target_pairs={{0,4},{4,8},{8,12},{12,16},{16,20},{20,24},{24,28},{1,5},{5,9},{9,... | collective-permute-start | bytes 294920 | tf_op jit(solution)/shard_map/ppermute | solution.py:241
  20.6 1.3 %collective-permute-start.5 = (f32[3,8,1024]{2,1,0:T(8,128)S(1)}, f32[3,8,1024]{2,1,0:T(8,128)S(1)}, u32[]{:S(2)}, u32[]{:S(2)}) collective-permute-start(f32[3,8,1024]{2,1,0:T(8,128)S(1)} %get-tuple-element.21), channel_id=1, source_target_pairs={{4,0},{8,4},{12,8},{16,12},{20,16},{24,20},{28,24},{5,1},{9,5},{13... | collective-permute-start | bytes 294920 | tf_op jit(solution)/shard_map/ppermute | solution.py:242
  21.9 4.3 %collective-permute-start.6 = (f32[6,1024]{1,0:T(8,128)S(1)}, f32[6,1024]{1,0:T(8,128)S(1)}, u32[]{:S(2)}, u32[]{:S(2)}) collective-permute-start(f32[6,1024]{1,0:T(8,128)S(1)} %get-tuple-element.22), channel_id=1, source_target_pairs={{0,1},{1,2},{2,3},{4,5},{5,6},{6,7},{8,9},{9,10},{10,11},{12,13},{... | collective-permute-start | bytes 73736 | tf_op jit(solution)/shard_map/ppermute | solution.py:241
  26.1 1.3 %collective-permute-start.7 = (f32[6,1024]{1,0:T(8,128)S(1)}, f32[6,1024]{1,0:T(8,128)S(1)}, u32[]{:S(2)}, u32[]{:S(2)}) collective-permute-start(f32[6,1024]{1,0:T(8,128)S(1)} %get-tuple-element.23), channel_id=1, source_target_pairs={{1,0},{2,1},{3,2},{5,4},{6,5},{7,6},{9,8},{10,9},{11,10},{13,12},{... | collective-permute-start | bytes 73736 | tf_op jit(solution)/shard_map/ppermute | solution.py:242
  27.4 0.8 %normal_kernel.3.data = f32[3,2,8,1024]{3,2,1,0:T(8,128)S(1)} custom-call(f32[3,2,8,1024]{3,2,1,0:T(8,128)S(1)} %get-tuple-element.19.field_ref.field.one_ref, s32[4,2,8]{2,1,0:T(2,128)S(1)} %copy-done.3, f32[4,3,1024]{2,1,0:T(4,128)S(1)} %copy.8.avo_ref, f32[4,129]{1,0:T(4,128)S(1)} %copy-done.4), custom_call_target="tpu_custom_call" | custom-call | flops 268435456 | bytes 444688 | tf_op jit(solution)/shard_map/normal_kernel/pallas_call | solution.py:222
  28.2 0.0 collective-permute-done.6.left
  28.3 1.0 %collective-permute-done.7.right = f32[6,1024]{1,0:T(8,128)S(1)} collective-permute-done((f32[6,1024]{1,0:T(8,128)S(1)}, f32[6,1024]{1,0:T(8,128)S(1)}, u32[]{:S(2)}, u32[]{:S(2)}) %collective-permute-start.7) | collective-permute-done | bytes 24608 | tf_op jit(solution)/shard_map/ppermute | solution.py:242
  29.3 0.8 %second_image_kernel.1 = (f32[3,2,8,1024]{3,2,1,0:T(8,128)S(1)}, f32[32,8,128]{2,1,0:T(8,128)S(1)}) custom-call(f32[3,2,8,1024]{3,2,1,0:T(8,128)S(1)} %get-tuple-element.19.field_ref.field.one_ref, f32[3,2,8,1024]{3,2,1,0:T(8,128)S(1)} %normal_kernel.3.data, f32[2,8]{1,0:T(2,128)S(1)} %copy-done, f32[3]{0:T(128)S(1)} %copy-done.1, ...), custom_call_target="tpu_custom_call" | custom-call | flops 1474560 | bytes 1163340 | tf_op jit(solution)/shard_map/second_image_kernel/pallas_call | solution.py:222
  30.0 17.0 %all_to_all.5.gram_ref = f32[32,8,128]{2,1,0:T(8,128)S(1)} all-to-all(f32[32,8,128]{2,1,0:T(8,128)S(1)} %get-tuple-element.24), channel_id=1, replica_groups=mesh['inline'=8,'col'=4] {'inline','col'}, dimensions={0} | all-to-all | bytes 262144 | tf_op jit(solution)/shard_map/all_to_all | solution.py:282
  47.0 0.9 %finish_kernel.1 = (f32[3,2,8,1024]{3,2,1,0:T(8,128)}, f32[3,2,8,1024]{3,2,1,0:T(8,128)}) custom-call(f32[32,8,128]{2,1,0:T(8,128)S(1)} %all_to_all.5.gram_ref, f32[3,2,8,1024]{3,2,1,0:T(8,128)S(1)} %get-tuple-element.14.field_ref.field.b_ref, f32[3,2,8,1024]{3,2,1,0:T(8,128)S(1)} %get-tuple-element.19.field_ref.field.one_ref, ...), custom_call_target="tpu_custom_call" | custom-call | flops 393216 | bytes 1114112 | tf_op jit(solution)/shard_map/finish_kernel/pallas_call | solution.py:222
  (10 shorter events, 0.0 us)
Async XLA Ops:
  0.6 0.9 %copy-start.4 = (f32[4,129]{1,0:T(4,128)S(1)}, f32[4,129]{1,0:T(4,128)}, u32[]{:S(2)}) copy-start(f32[4,129]{1,0:T(4,128)} %taps_ref.5) | copy-start | bytes 6196
  0.6 0.9 %copy-start.3 = (s32[4,2,8]{2,1,0:T(2,128)S(1)}, s32[4,2,8]{2,1,0:T(2,128)}, u32[]{:S(2)}) copy-start(s32[4,2,8]{2,1,0:T(2,128)} %valid_ref.5) | copy-start | bytes 772
  1.5 0.9 %copy-start.2 = (bf16[4,2,8,1024]{3,2,1,0:T(8,128)(2,1)S(1)}, bf16[4,2,8,1024]{3,2,1,0:T(8,128)(2,1)}, u32[]{:S(2)}) copy-start(bf16[4,2,8,1024]{3,2,1,0:T(8,128)(2,1)} %seis_ref.1) | copy-start | bytes 393220
  3.0 12.3 %collective-permute-start = (f32[3,8,1024]{2,1,0:T(8,128)S(1)}, f32[3,8,1024]{2,1,0:T(8,128)S(1)}, u32[]{:S(2)}, u32[]{:S(2)}) collective-permute-start(f32[3,8,1024]{2,1,0:T(8,128)S(1)} %get-tuple-element.15), channel_id=1, source_target_pairs={{0,4},{4,8},{8,12},{12,16},{16,20},{20,24},{24,28},{1,5},{5,9},{9,... | collective-permute-start | bytes 294920 | tf_op jit(solution)/shard_map/ppermute | solution.py:241
  7.9 7.5 %collective-permute-start.1 = (f32[3,8,1024]{2,1,0:T(8,128)S(1)}, f32[3,8,1024]{2,1,0:T(8,128)S(1)}, u32[]{:S(2)}, u32[]{:S(2)}) collective-permute-start(f32[3,8,1024]{2,1,0:T(8,128)S(1)} %get-tuple-element.16), channel_id=1, source_target_pairs={{4,0},{8,4},{12,8},{16,12},{20,16},{24,20},{28,24},{5,1},{9,5},{13... | collective-permute-start | bytes 294920 | tf_op jit(solution)/shard_map/ppermute | solution.py:242
  9.2 3.6 %collective-permute-start.2 = (f32[6,1024]{1,0:T(8,128)S(1)}, f32[6,1024]{1,0:T(8,128)S(1)}, u32[]{:S(2)}, u32[]{:S(2)}) collective-permute-start(f32[6,1024]{1,0:T(8,128)S(1)} %get-tuple-element.17), channel_id=1, source_target_pairs={{0,1},{1,2},{2,3},{4,5},{5,6},{6,7},{8,9},{9,10},{10,11},{12,13},{... | collective-permute-start | bytes 73736 | tf_op jit(solution)/shard_map/ppermute | solution.py:241
  10.6 4.7 %collective-permute-start.3 = (f32[6,1024]{1,0:T(8,128)S(1)}, f32[6,1024]{1,0:T(8,128)S(1)}, u32[]{:S(2)}, u32[]{:S(2)}) collective-permute-start(f32[6,1024]{1,0:T(8,128)S(1)} %get-tuple-element.18), channel_id=1, source_target_pairs={{1,0},{2,1},{3,2},{5,4},{6,5},{7,6},{9,8},{10,9},{11,10},{13,12},{... | collective-permute-start | bytes 73736 | tf_op jit(solution)/shard_map/ppermute | solution.py:242
  11.9 3.4 %copy-start = (f32[2,8]{1,0:T(2,128)S(1)}, f32[2,8]{1,0:T(2,128)}, u32[]{:S(2)}) copy-start(f32[2,8]{1,0:T(2,128)} %prior.3) | copy-start | bytes 196
  11.9 3.4 %copy-start.1 = (f32[3]{0:T(128)S(1)}, f32[3]{0:T(128)}, u32[]{:S(2)}) copy-start(f32[3]{0:T(128)} %strength.3) | copy-start | bytes 40
  16.0 13.2 %collective-permute-start.4 = (f32[3,8,1024]{2,1,0:T(8,128)S(1)}, f32[3,8,1024]{2,1,0:T(8,128)S(1)}, u32[]{:S(2)}, u32[]{:S(2)}) collective-permute-start(f32[3,8,1024]{2,1,0:T(8,128)S(1)} %get-tuple-element.20), channel_id=1, source_target_pairs={{0,4},{4,8},{8,12},{12,16},{16,20},{20,24},{24,28},{1,5},{5,9},{9,... | collective-permute-start | bytes 294920 | tf_op jit(solution)/shard_map/ppermute | solution.py:241
  20.6 8.7 %collective-permute-start.5 = (f32[3,8,1024]{2,1,0:T(8,128)S(1)}, f32[3,8,1024]{2,1,0:T(8,128)S(1)}, u32[]{:S(2)}, u32[]{:S(2)}) collective-permute-start(f32[3,8,1024]{2,1,0:T(8,128)S(1)} %get-tuple-element.21), channel_id=1, source_target_pairs={{4,0},{8,4},{12,8},{16,12},{20,16},{24,20},{28,24},{5,1},{9,5},{13... | collective-permute-start | bytes 294920 | tf_op jit(solution)/shard_map/ppermute | solution.py:242
  21.9 6.4 %collective-permute-start.6 = (f32[6,1024]{1,0:T(8,128)S(1)}, f32[6,1024]{1,0:T(8,128)S(1)}, u32[]{:S(2)}, u32[]{:S(2)}) collective-permute-start(f32[6,1024]{1,0:T(8,128)S(1)} %get-tuple-element.22), channel_id=1, source_target_pairs={{0,1},{1,2},{2,3},{4,5},{5,6},{6,7},{8,9},{9,10},{10,11},{12,13},{... | collective-permute-start | bytes 73736 | tf_op jit(solution)/shard_map/ppermute | solution.py:241
  26.1 3.1 %collective-permute-start.7 = (f32[6,1024]{1,0:T(8,128)S(1)}, f32[6,1024]{1,0:T(8,128)S(1)}, u32[]{:S(2)}, u32[]{:S(2)}) collective-permute-start(f32[6,1024]{1,0:T(8,128)S(1)} %get-tuple-element.23), channel_id=1, source_target_pairs={{1,0},{2,1},{3,2},{5,4},{6,5},{7,6},{9,8},{10,9},{11,10},{13,12},{... | collective-permute-start | bytes 73736 | tf_op jit(solution)/shard_map/ppermute | solution.py:242

commit v2 on v1

--- a/solution.py
+++ b/solution.py
@@ -78,7 +78,7 @@
 
 
 def coeff(avo_ref, angle, contrast, k):
-    return avo_ref[angle, contrast : contrast + 1, pl.ds(k * LANES, LANES)]
+    return avo_ref[contrast, angle : angle + 1, pl.ds(k * LANES, LANES)]
 
 
 def stack_tile(ref, contrast, k):
@@ -106,7 +106,7 @@
 
 def start_kernel(seis_ref, valid_ref, avo_ref, taps_ref, b_ref, top, bottom, left, right, padded):
     angles, rows, traces, samples = seis_ref.shape
-    contrasts, n = avo_ref.shape[1], samples // LANES
+    contrasts, n = avo_ref.shape[0], samples // LANES
     fill_taps(taps_ref, padded)
     lane = lax.broadcasted_iota(jnp.int32, (rows * traces, LANES), 1)
     total = [[None] * n for _ in range(contrasts)]
@@ -133,7 +133,7 @@
 
 def normal_kernel(field_ref, valid_ref, avo_ref, taps_ref, out_ref, padded):
     contrasts, rows, traces, samples = field_ref.shape
-    angles, n = avo_ref.shape[0], samples // LANES
+    angles, n = avo_ref.shape[1], samples // LANES
     fill_taps(taps_ref, padded)
     lane = lax.broadcasted_iota(jnp.int32, (rows * traces, LANES), 1)
     total = [[None] * n for _ in range(contrasts)]
@@ -198,6 +198,10 @@
         gram_ref[:, q, :] = jnp.broadcast_to(total, (gram_ref.shape[0], LANES))
 
 
+def spread_kernel(parts_ref, out_ref):
+    out_ref[...] = jnp.broadcast_to(jnp.sum(parts_ref[...], axis=0, keepdims=True), out_ref.shape)
+
+
 def finish_kernel(gram_ref, b_ref, one_ref, two_ref, solution_ref, residual_ref):
     sums = jnp.sum(gram_ref[...], axis=0)
     g00, g01, g11, g12 = (sums[q : q + 1, 0:1] for q in range(4))
@@ -246,7 +250,8 @@
 def shards(seismic, validity, prior_weight, lateral_strength, avo_coeffs, wavelets):
     angles, rows, traces, samples = seismic.shape
     contrasts = avo_coeffs.shape[1]
-    axes = ("inline", "col")
+    avo_coeffs = jnp.swapaxes(avo_coeffs, 0, 1)
+    inline, col = lax.axis_size("inline"), lax.axis_size("col")
     field = jax.ShapeDtypeStruct((contrasts, rows, traces, samples), F32)
     row = jax.ShapeDtypeStruct((contrasts, traces, samples), F32)
     side = jax.ShapeDtypeStruct((contrasts * rows, samples), F32)
@@ -274,12 +279,14 @@
     (data,) = call(normal_kernel, (field,), (one, validity, avo_coeffs, wavelets), 2 * work, taps)
     two, gram = call(
         second_image_kernel,
-        (field, jax.ShapeDtypeStruct((lax.axis_size(axes), 8, LANES), F32)),
+        (field, jax.ShapeDtypeStruct((col, 8, LANES), F32)),
         (one, data, prior_weight, lateral_strength, *around, b),
         30 * field.size,
         scalars=(3,),
     )
-    gram = lax.all_to_all(gram, axes, 0, 0)
+    gram = lax.all_to_all(gram, "col", 0, 0)
+    (gram,) = call(spread_kernel, (jax.ShapeDtypeStruct((inline, 8, LANES), F32),), (gram,), 8)
+    gram = lax.all_to_all(gram, "inline", 0, 0)
     return tuple(call(finish_kernel, (field, field), (gram, b, one, two), 8 * field.size))
 
 

time: 48.3 us -> 54.4 us (1.13)
  blocking collectives: 17 us -> 21.6 us
  local copies, waits for them, and re-layouts: 1.77 us -> 3.1 us
    all_to_all x1 -> x2, blocking collectives: 17 us -> 21.6 us  [the longest x1 14.3 us: shards(): gram = lax.all_to_all(gram, 'inline', 0, 0)]
    unnamed x11 -> x18, local copies, waits for them, and re-layouts: 1.77 us -> 3.1 us
    pallas_call x6 -> x7, Pallas kernels: 4.51 us -> 4.48 us  [call(): pl.pallas_call(kernel, out_shape=outs, in_specs=[SMEM if i in scalars els...]
where the time goes in v2:
time: 54.4 us; the launch traced here: 53.8 us
  blocking collectives  21.6 us (40%)
  starting transfers between devices  20.3 us (37%)
  Pallas kernels  4.48 us (8%)
  waiting for transfers between devices  3.52 us (6%)
  local copies, waits for them, and re-layouts  3.1 us (6%)
  between operations  0.82 us (2%)
    ppermute x4, starting transfers between devices, exchange(): moved.append(lax.ppermute(last, axis, ahead))  15.1 us
    all_to_all x1, blocking collectives, shards(): gram = lax.all_to_all(gram, 'inline', 0, 0)  14.3 us
    all_to_all x1, blocking collectives, shards(): gram = lax.all_to_all(gram, 'col', 0, 0)  7.33 us
    ppermute x4, starting transfers between devices, exchange(): moved.append(lax.ppermute(first, axis, back))  5.17 us
    pallas_call x7, Pallas kernels, call(): pl.pallas_call(kernel, out_shape=outs, in_specs=[SMEM if i in scalars els...  4.48 us
    ppermute x4, waiting for transfers between devices, exchange(): moved.append(lax.ppermute(first, axis, back))  3.51 us
    unnamed x18, local copies, waits for them, and re-layouts  3.1 us
  transfers between devices with their start and end apart: 8, of which 2 were waited for; matrix products, arithmetic and copies ran while one was open for 0% of the time, Pallas kernels for 3%

profile of v2, /device:TPU:0, one launch (start us, length us, event | category | flops | bytes accessed | tf_op | source)
XLA Modules:
  0.0 53.8 jit_solution(6132595302207158640)
XLA Ops:
  0.6 0.9 %copy-done.2 = bf16[4,2,8,1024]{3,2,1,0:T(8,128)(2,1)S(1)} copy-done((bf16[4,2,8,1024]{3,2,1,0:T(8,128)(2,1)S(1)}, bf16[4,2,8,1024]{3,2,1,0:T(8,128)(2,1)}, u32[]{:S(2)}) %copy-start.2) | copy-done | bytes 131096
  1.5 0.8 %copy-done.3 = f32[4,3,1024]{2,0,1:T(4,128)S(1)} copy-done((f32[4,3,1024]{2,0,1:T(4,128)S(1)}, f32[4,3,1024]{2,0,1:T(4,128)}, u32[]{:S(2)}) %copy-start.3) | copy-done | bytes 49176
  2.3 0.7 %copy-done.5 = s32[4,2,8]{2,1,0:T(2,128)S(1)} copy-done((s32[4,2,8]{2,1,0:T(2,128)S(1)}, s32[4,2,8]{2,1,0:T(2,128)}, u32[]{:S(2)}) %copy-start.5) | copy-done | bytes 280
  3.0 0.7 %copy-done.7 = f32[4,129]{1,0:T(4,128)S(1)} copy-done((f32[4,129]{1,0:T(4,128)S(1)}, f32[4,129]{1,0:T(4,128)}, u32[]{:S(2)}) %copy-start.7) | copy-done | bytes 2088
  3.7 0.6 %start_kernel.1 = (f32[3,2,8,1024]{3,2,1,0:T(8,128)S(1)}, f32[3,8,1024]{2,1,0:T(8,128)S(1)}, f32[3,8,1024]{2,1,0:T(8,128)S(1)}, f32[6,1024]{1,0:T(8,128)S(1)}, f32[6,1024]{1,0:T(8,128)S(1)}) custom-call(bf16[4,2,8,1024]{3,2,1,0:T(8,128)(2,1)S(1)} %copy-done.2, s32[4,2,8]{2,1,0:T(2,128)S(1)} %copy-done.5, f32[3,4,1024]{2,1,0:T(4,128)S(1)} %bitcast.1, ...), custom_call_target="tpu_custom_call" | custom-call | flops 134217728 | bytes 624912 | tf_op jit(solution)/shard_map/start_kernel/pallas_call | solution.py:226
  4.3 0.0 copy-start.6
  4.3 4.8 %collective-permute-start = (f32[3,8,1024]{2,1,0:T(8,128)S(1)}, f32[3,8,1024]{2,1,0:T(8,128)S(1)}, u32[]{:S(2)}, u32[]{:S(2)}) collective-permute-start(f32[3,8,1024]{2,1,0:T(8,128)S(1)} %get-tuple-element.15), channel_id=1, source_target_pairs={{0,4},{4,8},{8,12},{12,16},{16,20},{20,24},{24,28},{1,5},{5,9},{9,... | collective-permute-start | bytes 294920 | tf_op jit(solution)/shard_map/ppermute | solution.py:245
  9.2 1.3 %collective-permute-start.1 = (f32[3,8,1024]{2,1,0:T(8,128)S(1)}, f32[3,8,1024]{2,1,0:T(8,128)S(1)}, u32[]{:S(2)}, u32[]{:S(2)}) collective-permute-start(f32[3,8,1024]{2,1,0:T(8,128)S(1)} %get-tuple-element.16), channel_id=1, source_target_pairs={{4,0},{8,4},{12,8},{16,12},{20,16},{24,20},{28,24},{5,1},{9,5},{13... | collective-permute-start | bytes 294920 | tf_op jit(solution)/shard_map/ppermute | solution.py:246
  10.5 1.5 %collective-permute-start.2 = (f32[6,1024]{1,0:T(8,128)S(1)}, f32[6,1024]{1,0:T(8,128)S(1)}, u32[]{:S(2)}, u32[]{:S(2)}) collective-permute-start(f32[6,1024]{1,0:T(8,128)S(1)} %get-tuple-element.17), channel_id=1, source_target_pairs={{0,1},{1,2},{2,3},{4,5},{5,6},{6,7},{8,9},{9,10},{10,11},{12,13},{... | collective-permute-start | bytes 73736 | tf_op jit(solution)/shard_map/ppermute | solution.py:245
  11.9 1.3 %collective-permute-start.3 = (f32[6,1024]{1,0:T(8,128)S(1)}, f32[6,1024]{1,0:T(8,128)S(1)}, u32[]{:S(2)}, u32[]{:S(2)}) collective-permute-start(f32[6,1024]{1,0:T(8,128)S(1)} %get-tuple-element.18), channel_id=1, source_target_pairs={{1,0},{2,1},{3,2},{5,4},{6,5},{7,6},{9,8},{10,9},{11,10},{13,12},{... | collective-permute-start | bytes 73736 | tf_op jit(solution)/shard_map/ppermute | solution.py:246
  13.2 0.0 copy-start
  13.3 0.8 %normal_kernel.2.data = f32[3,2,8,1024]{3,2,1,0:T(8,128)S(1)} custom-call(f32[3,2,8,1024]{3,2,1,0:T(8,128)S(1)} %get-tuple-element.14.field_ref.field.b_ref, s32[4,2,8]{2,1,0:T(2,128)S(1)} %copy-done.6, f32[3,4,1024]{2,1,0:T(4,128)S(1)} %bitcast.2, f32[4,129]{1,0:T(4,128)S(1)} %copy-done.7), custom_call_target="tpu_custom_call" | custom-call | flops 268435456 | bytes 444688 | tf_op jit(solution)/shard_map/normal_kernel/pallas_call | solution.py:226
  14.1 2.5 %collective-permute-done.3.right = f32[6,1024]{1,0:T(8,128)S(1)} collective-permute-done((f32[6,1024]{1,0:T(8,128)S(1)}, f32[6,1024]{1,0:T(8,128)S(1)}, u32[]{:S(2)}, u32[]{:S(2)}) %collective-permute-start.3) | collective-permute-done | bytes 24608 | tf_op jit(solution)/shard_map/ppermute | solution.py:246
  16.6 0.7 %first_image_kernel.1 = (f32[3,2,8,1024]{3,2,1,0:T(8,128)S(1)}, f32[3,8,1024]{2,1,0:T(8,128)S(1)}, f32[3,8,1024]{2,1,0:T(8,128)S(1)}, f32[6,1024]{1,0:T(8,128)S(1)}, f32[6,1024]{1,0:T(8,128)S(1)}) custom-call(f32[3,2,8,1024]{3,2,1,0:T(8,128)S(1)} %get-tuple-element.14.field_ref.field.b_ref, f32[3,2,8,1024]{3,2,1,0:T(8,128)S(1)} %normal_kernel.2.data, ...), custom_call_target="tpu_custom_call" | custom-call | flops 983040 | bytes 1081420 | tf_op jit(solution)/shard_map/first_image_kernel/pallas_call | solution.py:226
  17.3 4.6 %collective-permute-start.4 = (f32[3,8,1024]{2,1,0:T(8,128)S(1)}, f32[3,8,1024]{2,1,0:T(8,128)S(1)}, u32[]{:S(2)}, u32[]{:S(2)}) collective-permute-start(f32[3,8,1024]{2,1,0:T(8,128)S(1)} %get-tuple-element.20), channel_id=1, source_target_pairs={{0,4},{4,8},{8,12},{12,16},{16,20},{20,24},{24,28},{1,5},{5,9},{9,... | collective-permute-start | bytes 294920 | tf_op jit(solution)/shard_map/ppermute | solution.py:245
  21.9 1.3 %collective-permute-start.5 = (f32[3,8,1024]{2,1,0:T(8,128)S(1)}, f32[3,8,1024]{2,1,0:T(8,128)S(1)}, u32[]{:S(2)}, u32[]{:S(2)}) collective-permute-start(f32[3,8,1024]{2,1,0:T(8,128)S(1)} %get-tuple-element.21), channel_id=1, source_target_pairs={{4,0},{8,4},{12,8},{16,12},{20,16},{24,20},{28,24},{5,1},{9,5},{13... | collective-permute-start | bytes 294920 | tf_op jit(solution)/shard_map/ppermute | solution.py:246
  23.2 4.3 %collective-permute-start.6 = (f32[6,1024]{1,0:T(8,128)S(1)}, f32[6,1024]{1,0:T(8,128)S(1)}, u32[]{:S(2)}, u32[]{:S(2)}) collective-permute-start(f32[6,1024]{1,0:T(8,128)S(1)} %get-tuple-element.22), channel_id=1, source_target_pairs={{0,1},{1,2},{2,3},{4,5},{5,6},{6,7},{8,9},{9,10},{10,11},{12,13},{... | collective-permute-start | bytes 73736 | tf_op jit(solution)/shard_map/ppermute | solution.py:245
  27.4 1.3 %collective-permute-start.7 = (f32[6,1024]{1,0:T(8,128)S(1)}, f32[6,1024]{1,0:T(8,128)S(1)}, u32[]{:S(2)}, u32[]{:S(2)}) collective-permute-start(f32[6,1024]{1,0:T(8,128)S(1)} %get-tuple-element.23), channel_id=1, source_target_pairs={{1,0},{2,1},{3,2},{5,4},{6,5},{7,6},{9,8},{10,9},{11,10},{13,12},{... | collective-permute-start | bytes 73736 | tf_op jit(solution)/shard_map/ppermute | solution.py:246
  28.8 0.8 %normal_kernel.3.data = f32[3,2,8,1024]{3,2,1,0:T(8,128)S(1)} custom-call(f32[3,2,8,1024]{3,2,1,0:T(8,128)S(1)} %get-tuple-element.19.field_ref.field.one_ref, s32[4,2,8]{2,1,0:T(2,128)S(1)} %copy-done.6, f32[3,4,1024]{2,1,0:T(4,128)S(1)} %bitcast.3, f32[4,129]{1,0:T(4,128)S(1)} %copy-done.8), custom_call_target="tpu_custom_call" | custom-call | flops 268435456 | bytes 444688 | tf_op jit(solution)/shard_map/normal_kernel/pallas_call | solution.py:226
  29.6 1.0 %collective-permute-done.7.right = f32[6,1024]{1,0:T(8,128)S(1)} collective-permute-done((f32[6,1024]{1,0:T(8,128)S(1)}, f32[6,1024]{1,0:T(8,128)S(1)}, u32[]{:S(2)}, u32[]{:S(2)}) %collective-permute-start.7) | collective-permute-done | bytes 24608 | tf_op jit(solution)/shard_map/ppermute | solution.py:246
  30.6 0.8 %second_image_kernel.1 = (f32[3,2,8,1024]{3,2,1,0:T(8,128)S(1)}, f32[4,8,128]{2,1,0:T(8,128)S(1)}) custom-call(f32[3,2,8,1024]{3,2,1,0:T(8,128)S(1)} %get-tuple-element.19.field_ref.field.one_ref, f32[3,2,8,1024]{3,2,1,0:T(8,128)S(1)} %normal_kernel.3.data, f32[2,8]{1,0:T(2,128)S(1)} %copy-done, f32[3]{0:T(128)S(1)} %copy-done.1, ...), custom_call_target="tpu_custom_call" | custom-call | flops 1474560 | bytes 1048652 | tf_op jit(solution)/shard_map/second_image_kernel/pallas_call | solution.py:226
  31.3 7.3 %all_to_all.10.parts_ref = f32[4,8,128]{2,1,0:T(8,128)S(1)} all-to-all(f32[4,8,128]{2,1,0:T(8,128)S(1)} %get-tuple-element.24), channel_id=1, replica_groups=mesh['inline'=8,'col'=4] {'col'}, dimensions={0} | all-to-all | bytes 32768 | tf_op jit(solution)/shard_map/all_to_all | solution.py:287
  38.7 14.3 %all_to_all.11.gram_ref = f32[8,8,128]{2,1,0:T(8,128)S(1)} all-to-all(f32[8,8,128]{2,1,0:T(8,128)S(1)} %spread_kernel.1), channel_id=1, replica_groups=mesh['inline'=8,'col'=4] {'inline'}, dimensions={0} | all-to-all | bytes 65536 | tf_op jit(solution)/shard_map/all_to_all | solution.py:289
  53.0 0.9 %finish_kernel.1 = (f32[3,2,8,1024]{3,2,1,0:T(8,128)}, f32[3,2,8,1024]{3,2,1,0:T(8,128)}) custom-call(f32[8,8,128]{2,1,0:T(8,128)S(1)} %all_to_all.11.gram_ref, f32[3,2,8,1024]{3,2,1,0:T(8,128)S(1)} %get-tuple-element.14.field_ref.field.b_ref, f32[3,2,8,1024]{3,2,1,0:T(8,128)S(1)} %get-tuple-element.19.field_ref.field.one_ref, ...), custom_call_target="tpu_custom_call" | custom-call | flops 393216 | bytes 1015808 | tf_op jit(solution)/shard_map/finish_kernel/pallas_call | solution.py:226
  (19 shorter events, 0.0 us)
Async XLA Ops:
  0.6 0.9 %copy-start.2 = (bf16[4,2,8,1024]{3,2,1,0:T(8,128)(2,1)S(1)}, bf16[4,2,8,1024]{3,2,1,0:T(8,128)(2,1)}, u32[]{:S(2)}) copy-start(bf16[4,2,8,1024]{3,2,1,0:T(8,128)(2,1)} %seis_ref.1) | copy-start | bytes 393220
  1.5 0.8 %copy-start.3 = (f32[4,3,1024]{2,0,1:T(4,128)S(1)}, f32[4,3,1024]{2,0,1:T(4,128)}, u32[]{:S(2)}) copy-start(f32[4,3,1024]{2,0,1:T(4,128)} %param.10) | copy-start | bytes 147460
  2.3 0.7 %copy-start.5 = (s32[4,2,8]{2,1,0:T(2,128)S(1)}, s32[4,2,8]{2,1,0:T(2,128)}, u32[]{:S(2)}) copy-start(s32[4,2,8]{2,1,0:T(2,128)} %valid_ref.5) | copy-start | bytes 772
  3.0 0.7 %copy-start.7 = (f32[4,129]{1,0:T(4,128)S(1)}, f32[4,129]{1,0:T(4,128)}, u32[]{:S(2)}) copy-start(f32[4,129]{1,0:T(4,128)} %taps_ref.5) | copy-start | bytes 6196
  3.7 9.5 %copy-start.4 = (f32[4,3,1024]{2,0,1:T(4,128)S(1)}, f32[4,3,1024]{2,0,1:T(4,128)}, u32[]{:S(2)}) copy-start(f32[4,3,1024]{2,0,1:T(4,128)} %param.10) | copy-start | bytes 147460
  4.3 8.9 %copy-start.6 = (s32[4,2,8]{2,1,0:T(2,128)S(1)}, s32[4,2,8]{2,1,0:T(2,128)}, u32[]{:S(2)}) copy-start(s32[4,2,8]{2,1,0:T(2,128)} %valid_ref.5) | copy-start | bytes 772
  4.3 12.3 %collective-permute-start = (f32[3,8,1024]{2,1,0:T(8,128)S(1)}, f32[3,8,1024]{2,1,0:T(8,128)S(1)}, u32[]{:S(2)}, u32[]{:S(2)}) collective-permute-start(f32[3,8,1024]{2,1,0:T(8,128)S(1)} %get-tuple-element.15), channel_id=1, source_target_pairs={{0,4},{4,8},{8,12},{12,16},{16,20},{20,24},{24,28},{1,5},{5,9},{9,... | collective-permute-start | bytes 294920 | tf_op jit(solution)/shard_map/ppermute | solution.py:245
  9.2 7.5 %collective-permute-start.1 = (f32[3,8,1024]{2,1,0:T(8,128)S(1)}, f32[3,8,1024]{2,1,0:T(8,128)S(1)}, u32[]{:S(2)}, u32[]{:S(2)}) collective-permute-start(f32[3,8,1024]{2,1,0:T(8,128)S(1)} %get-tuple-element.16), channel_id=1, source_target_pairs={{4,0},{8,4},{12,8},{16,12},{20,16},{24,20},{28,24},{5,1},{9,5},{13... | collective-permute-start | bytes 294920 | tf_op jit(solution)/shard_map/ppermute | solution.py:246
  10.5 3.6 %collective-permute-start.2 = (f32[6,1024]{1,0:T(8,128)S(1)}, f32[6,1024]{1,0:T(8,128)S(1)}, u32[]{:S(2)}, u32[]{:S(2)}) collective-permute-start(f32[6,1024]{1,0:T(8,128)S(1)} %get-tuple-element.17), channel_id=1, source_target_pairs={{0,1},{1,2},{2,3},{4,5},{5,6},{6,7},{8,9},{9,10},{10,11},{12,13},{... | collective-permute-start | bytes 73736 | tf_op jit(solution)/shard_map/ppermute | solution.py:245
  11.9 4.7 %collective-permute-start.3 = (f32[6,1024]{1,0:T(8,128)S(1)}, f32[6,1024]{1,0:T(8,128)S(1)}, u32[]{:S(2)}, u32[]{:S(2)}) collective-permute-start(f32[6,1024]{1,0:T(8,128)S(1)} %get-tuple-element.18), channel_id=1, source_target_pairs={{1,0},{2,1},{3,2},{5,4},{6,5},{7,6},{9,8},{10,9},{11,10},{13,12},{... | collective-permute-start | bytes 73736 | tf_op jit(solution)/shard_map/ppermute | solution.py:246
  13.2 3.4 %copy-start = (f32[2,8]{1,0:T(2,128)S(1)}, f32[2,8]{1,0:T(2,128)}, u32[]{:S(2)}) copy-start(f32[2,8]{1,0:T(2,128)} %prior.3) | copy-start | bytes 196
  13.3 3.4 %copy-start.1 = (f32[3]{0:T(128)S(1)}, f32[3]{0:T(128)}, u32[]{:S(2)}) copy-start(f32[3]{0:T(128)} %strength.3) | copy-start | bytes 40
  17.3 11.4 %copy-start.8 = (f32[4,129]{1,0:T(4,128)S(1)}, f32[4,129]{1,0:T(4,128)}, u32[]{:S(2)}) copy-start(f32[4,129]{1,0:T(4,128)} %taps_ref.5) | copy-start | bytes 6196
  17.3 13.2 %collective-permute-start.4 = (f32[3,8,1024]{2,1,0:T(8,128)S(1)}, f32[3,8,1024]{2,1,0:T(8,128)S(1)}, u32[]{:S(2)}, u32[]{:S(2)}) collective-permute-start(f32[3,8,1024]{2,1,0:T(8,128)S(1)} %get-tuple-element.20), channel_id=1, source_target_pairs={{0,4},{4,8},{8,12},{12,16},{16,20},{20,24},{24,28},{1,5},{5,9},{9,... | collective-permute-start | bytes 294920 | tf_op jit(solution)/shard_map/ppermute | solution.py:245
  21.9 8.7 %collective-permute-start.5 = (f32[3,8,1024]{2,1,0:T(8,128)S(1)}, f32[3,8,1024]{2,1,0:T(8,128)S(1)}, u32[]{:S(2)}, u32[]{:S(2)}) collective-permute-start(f32[3,8,1024]{2,1,0:T(8,128)S(1)} %get-tuple-element.21), channel_id=1, source_target_pairs={{4,0},{8,4},{12,8},{16,12},{20,16},{24,20},{28,24},{5,1},{9,5},{13... | collective-permute-start | bytes 294920 | tf_op jit(solution)/shard_map/ppermute | solution.py:246
  23.2 6.4 %collective-permute-start.6 = (f32[6,1024]{1,0:T(8,128)S(1)}, f32[6,1024]{1,0:T(8,128)S(1)}, u32[]{:S(2)}, u32[]{:S(2)}) collective-permute-start(f32[6,1024]{1,0:T(8,128)S(1)} %get-tuple-element.22), channel_id=1, source_target_pairs={{0,1},{1,2},{2,3},{4,5},{5,6},{6,7},{8,9},{9,10},{10,11},{12,13},{... | collective-permute-start | bytes 73736 | tf_op jit(solution)/shard_map/ppermute | solution.py:245
  27.4 3.1 %collective-permute-start.7 = (f32[6,1024]{1,0:T(8,128)S(1)}, f32[6,1024]{1,0:T(8,128)S(1)}, u32[]{:S(2)}, u32[]{:S(2)}) collective-permute-start(f32[6,1024]{1,0:T(8,128)S(1)} %get-tuple-element.23), channel_id=1, source_target_pairs={{1,0},{2,1},{3,2},{5,4},{6,5},{7,6},{9,8},{10,9},{11,10},{13,12},{... | collective-permute-start | bytes 73736 | tf_op jit(solution)/shard_map/ppermute | solution.py:246

commit v3 on v0

v3 whole, which is shorter than its diff:
```python
import functools

import jax
import jax.numpy as jnp
from jax import lax
from jax.experimental import pallas as pl
from jax.experimental.pallas import tpu as pltpu
from jax.sharding import PartitionSpec as P

LANES = 128
F32 = jnp.float32
BF16 = jnp.bfloat16


def split(value):
    high = value.astype(BF16)
    return high, (value - high.astype(F32)).astype(BF16)


def circulant(padded_ref, angle):
    line = jnp.broadcast_to(padded_ref[angle : angle + 1, :], (2 * LANES, 2 * LANES))
    return pltpu.roll(line, LANES, 1, stride=1, stride_axis=0)


def fill_taps(taps_ref, padded_ref):
    padded_ref[...] = jnp.zeros_like(padded_ref)
    padded_ref[0 : taps_ref.shape[0], 0 : taps_ref.shape[1]] = taps_ref[...]


def forward_band(circ):
    return jnp.concatenate(split(circ[:, :LANES]), axis=1)


def backward_band(circ):
    return jnp.concatenate(split(circ[LANES:, :]), axis=0)


def column(row):
    n = row.shape[1]
    same = lax.broadcasted_iota(jnp.int32, (n, n), 0) == lax.broadcasted_iota(jnp.int32, (n, n), 1)
    return jnp.sum(jnp.where(same, jnp.broadcast_to(row, (n, n)), 0.0), axis=1, keepdims=True)


def trace_columns(ref, *lead):
    rows = ref[lead].astype(F32)
    return jnp.concatenate([column(rows[r : r + 1, :]) for r in range(rows.shape[0])], axis=0)


def windows(tiles):
    pairs = [jnp.concatenate(pair, axis=1) for pair in zip(tiles[:-1], tiles[1:])]
    return jnp.concatenate(pairs, axis=0)


def halves_sum(wide):
    return wide[:, :LANES] + wide[:, LANES:]


def forward(tiles, band):
    zero = jnp.zeros_like(tiles[0]).astype(BF16)
    highs, lows = zip(*[split(t) for t in tiles])
    n, size = len(tiles) + 1, tiles[0].shape[0]
    rows = [windows([zero, *part, zero]) for part in (highs, lows)]
    out = jnp.dot(jnp.concatenate(rows, axis=0), band, preferred_element_type=F32)
    out = halves_sum(out)
    out = out[: n * size] + out[n * size :]
    return [out[k * size : (k + 1) * size] for k in range(n)]


def backward(parts, band):
    n, size = len(parts[0]) - 1, parts[0][0].shape[0]
    rows = jnp.concatenate([windows(part) for part in parts], axis=0)
    out = lax.dot_general(rows, band, (((1,), (1,)), ((), ())), preferred_element_type=F32)
    out = halves_sum(out)
    total = out[: n * size]
    for p in range(1, len(parts)):
        total = total + out[p * n * size : (p + 1) * n * size]
    return [total[k * size : (k + 1) * size] for k in range(n)]


def coeff(avo_ref, angle, contrast, k):
    return avo_ref[contrast, angle : angle + 1, pl.ds(k * LANES, LANES)]


def add_terms(total, avo_ref, angle, result):
    for c, line in enumerate(total):
        for k, tile in enumerate(result):
            term = coeff(avo_ref, angle, c, k) * tile
            line[k] = term if angle == 0 else line[k] + term


def store_tiles(out_ref, tiles):
    size = out_ref.shape[2]
    for c in range(out_ref.shape[0]):
        for k, tile in enumerate(tiles[c]):
            for r in range(out_ref.shape[1]):
                out_ref[c, r, :, pl.ds(k * LANES, LANES)] = tile[r * size : (r + 1) * size]


def right_side(seis_ref, masks, avo_ref, circs):
    angles, rows, _, samples = seis_ref.shape
    n = samples // LANES
    total = [[None] * n for _ in range(avo_ref.shape[0])]
    for a in range(angles):
        data = jnp.concatenate([seis_ref[a, r].astype(F32) for r in range(rows)], axis=0)
        data = data * masks[a]
        turned = [
            pltpu.roll(data[:, k * LANES : (k + 1) * LANES], LANES // 2, 1) for k in range(n)
        ]
        zero = jnp.zeros_like(turned[0])
        left_half = lax.broadcasted_iota(jnp.int32, zero.shape, 1) < LANES // 2
        shifted = [
            jnp.where(left_half, before, here).astype(BF16)
            for before, here in zip([zero, *turned], [*turned, zero])
        ]
        add_terms(total, avo_ref, a, backward([shifted], backward_band(circs[a])))
    return total


def normal(field, masks, avo_ref, circs):
    contrasts, n = len(field), len(field[0])
    total = [[None] * n for _ in range(contrasts)]
    for a, circ in enumerate(circs):
        mixed = []
        for k in range(n):
            parts = [coeff(avo_ref, a, c, k) * field[c][k] for c in range(contrasts)]
            mixed.append(functools.reduce(jnp.add, parts))
        synth = [tile * masks[a] for tile in forward(mixed, forward_band(circ))]
        left_half = lax.broadcasted_iota(jnp.int32, synth[0].shape, 1) < LANES // 2
        synth[0] = jnp.where(left_half, 0.0, synth[0])
        synth[n] = jnp.where(left_half, synth[n], 0.0)
        result = backward(list(zip(*[split(t) for t in synth])), backward_band(circ))
        add_terms(total, avo_ref, a, result)
    return total


def lateral(here, north, south, west, east):
    traces = here.shape[0]
    place = lax.broadcasted_iota(jnp.int32, here.shape, 0)
    from_west = jnp.where(place == 0, 0.0 if west is None else west, pltpu.roll(here, 1, 0))
    from_east = jnp.where(
        place == traces - 1, 0.0 if east is None else east, pltpu.roll(here, traces - 1, 0)
    )
    around = from_west + from_east
    for other in (north, south):
        around = around if other is None else around + other
    return around


def copy_in(pairs, sems):
    copies = [pltpu.make_async_copy(a, b, sems.at[i]) for i, (a, b) in enumerate(pairs)]
    for copy in copies:
        copy.start()
    return copies


def start_kernel(
    seis_hbm, valid_hbm, avo_hbm, taps_hbm, prior_hbm, strength_ref,
    b_ref, p_ref, top_ref, bottom_ref,
    seis_ref, valid_ref, avo_ref, taps_ref, prior_ref, padded, sems,
):
    copies = copy_in(
        (
            (taps_hbm, taps_ref),
            (valid_hbm, valid_ref),
            (prior_hbm, prior_ref),
            (avo_hbm, avo_ref),
            (seis_hbm, seis_ref),
        ),
        sems,
    )
    for copy in copies[:3]:
        copy.wait()
    fill_taps(taps_ref, padded)
    contrasts, angles, samples = avo_ref.shape
    rows = seis_ref.shape[1]
    circs = [circulant(padded, a) for a in range(angles)]
    masks = [trace_columns(valid_ref, a) for a in range(angles)]
    for copy in copies[3:]:
        copy.wait()
    b = right_side(seis_ref, masks, avo_ref, circs)
    store_tiles(b_ref, b)
    store_tiles(p_ref, normal(b, masks, avo_ref, circs))
    weights = [column(prior_ref[r : r + 1, :]) + 4.0 for r in range(rows)]
    for c in range(contrasts):
        for r in range(rows):
            here = b_ref[c, r]
            north = b_ref[c, r - 1] if r else None
            south = b_ref[c, r + 1] if r < rows - 1 else None
            around = lateral(here, north, south, None, None)
            p_ref[c, r] = p_ref[c, r] + strength_ref[c] * (weights[r] * here - around)
        for out_ref, r in ((top_ref, 0), (bottom_ref, rows - 1)):
            out_ref[0, c] = b_ref[c, r]
            out_ref[1, c] = p_ref[c, r]


def inside(axis):
    place = lax.axis_index(axis)
    last = lax.axis_size(axis) - 1
    return (place > 0).astype(F32), (place < last).astype(F32)


def rows_kernel(b_ref, p_ref, above_ref, below_ref, strength_ref, v_ref, left_ref, right_ref):
    contrasts, rows, traces, _ = b_ref.shape
    has_above, has_below = inside("inline")
    for c in range(contrasts):
        strength = strength_ref[c]
        own = [p_ref[c, r] for r in range(rows)]
        own[0] = own[0] - strength * above_ref[0, c]
        own[-1] = own[-1] - strength * below_ref[0, c]
        over = has_above * (above_ref[1, c] - strength * b_ref[c, 0])
        under = has_below * (below_ref[1, c] - strength * b_ref[c, rows - 1])
        for r, line in enumerate([over, *own, under]):
            v_ref[c, r] = line
        lines = [above_ref[0, c], *[b_ref[c, r] for r in range(rows)], below_ref[0, c], *own]
        base = c * len(lines)
        for e, line in enumerate(lines):
            left_ref[base + e : base + e + 1, :] = line[0:1, :]
            right_ref[base + e : base + e + 1, :] = line[traces - 1 : traces, :]


def image_kernel(
    b_ref, v_ref, left_ref, right_ref, valid_ref, avo_ref, taps_ref, prior_ref, strength_ref,
    one_ref, two_ref, gram_ref, padded,
):
    contrasts, rows, traces, samples = b_ref.shape
    angles, n = avo_ref.shape[1], samples // LANES
    has_left, has_right = inside("col")
    place = lax.broadcasted_iota(jnp.int32, (traces, samples), 0)
    first, last = place == 0, place == traces - 1
    ext = rows + 2
    whole = []
    for c in range(contrasts):
        base = c * (ext + rows)
        lines = []
        for r in range(ext):
            edge = base + r
            missing = jnp.where(
                first,
                left_ref[edge : edge + 1, :],
                jnp.where(last, right_ref[edge : edge + 1, :], 0.0),
            )
            lines.append(v_ref[c, r] - strength_ref[c] * missing)
        whole.append(lines)
        for r in range(rows):
            one_ref[c, r] = lines[r + 1]
    fill_taps(taps_ref, padded)
    circs = [circulant(padded, a) for a in range(angles)]
    masks = [trace_columns(valid_ref, a) for a in range(angles)]
    field = [
        [
            jnp.concatenate([one_ref[c, r, :, pl.ds(k * LANES, LANES)] for r in range(rows)], axis=0)
            for k in range(n)
        ]
        for c in range(contrasts)
    ]
    store_tiles(two_ref, normal(field, masks, avo_ref, circs))
    weights = [column(prior_ref[r : r + 1, :]) + 4.0 for r in range(rows)]
    sums = [jnp.zeros((traces, LANES), F32) for _ in range(4)]
    for c in range(contrasts):
        strength = strength_ref[c]
        for r in range(rows):
            here = whole[c][r + 1]
            edge = c * (ext + rows) + ext + r
            b = b_ref[c, r]
            west = has_left * (left_ref[edge : edge + 1, :] - strength * b[0:1, :])
            east = has_right * (
                right_ref[edge : edge + 1, :] - strength * b[traces - 1 : traces, :]
            )
            around = lateral(here, whole[c][r], whole[c][r + 2], west, east)
            two = two_ref[c, r] + strength * (weights[r] * here - around)
            two_ref[c, r] = two
            for q, product in enumerate((b * b, b * here, here * here, here * two)):
                tiles = [product[:, k : k + LANES] for k in range(0, samples, LANES)]
                sums[q] = sums[q] + functools.reduce(jnp.add, tiles)
    lane = lax.broadcasted_iota(jnp.int32, (1, LANES), 1)
    packed = jnp.zeros((1, LANES), F32)
    for q, total in enumerate(sums):
        total = jnp.sum(jnp.sum(total, axis=0, keepdims=True), axis=1, keepdims=True)
        packed = jnp.where(lane == q, total, packed)
    gram_ref[...] = jnp.broadcast_to(packed[None], gram_ref.shape)


def finish_kernel(gram_ref, b_ref, one_ref, two_ref, solution_ref, residual_ref):
    sums = jnp.sum(gram_ref[...], axis=0)
    g00, g01, g11, g12 = (sums[:, q : q + 1] for q in range(4))
    first = g00 / g01
    ratio = first * g11 / g01
    second = (ratio - 1.0) * g01 / (first * g12 - ratio * g11)
    near = first + second * ratio
    far = first * second
    for c in range(b_ref.shape[0]):
        for r in range(b_ref.shape[1]):
            b, one, two = b_ref[c, r], one_ref[c, r], two_ref[c, r]
            solution_ref[c, r] = near * b - far * one
            residual_ref[c, r] = b - near * one + far * two


VMEM = pl.BlockSpec(memory_space=pltpu.VMEM)
SMEM = pl.BlockSpec(memory_space=pltpu.SMEM)
HBM = pl.BlockSpec(memory_space=pltpu.HBM)


def call(kernel, outs, ins, flops, scratch=(), places=None):
    moved = sum(x.size * x.dtype.itemsize for x in (*ins, *outs))
    return pl.pallas_call(
        kernel,
        out_shape=outs,
        in_specs=[VMEM] * len(ins) if places is None else places,
        out_specs=jax.tree.map(lambda _: VMEM, outs),
        scratch_shapes=list(scratch),
        compiler_params=pltpu.CompilerParams(vmem_limit_bytes=24 * 1024 * 1024),
        cost_estimate=pl.CostEstimate(flops=flops, bytes_accessed=moved, transcendentals=0),
        name=kernel.__name__,
    )(*ins)


def exchange(axis, first, last):
    size = lax.axis_size(axis)
    ahead = [(i, i + 1) for i in range(size - 1)]
    back = [(j, i) for i, j in ahead]
    return lax.ppermute(last, axis, ahead), lax.ppermute(first, axis, back)


def shards(seismic, validity, prior_weight, lateral_strength, avo_coeffs, wavelets):
    angles, rows, traces, samples = seismic.shape
    contrasts = avo_coeffs.shape[1]
    avo_coeffs = jnp.swapaxes(avo_coeffs, 0, 1)
    shape = lambda *dims: jax.ShapeDtypeStruct(dims, F32)
    field = shape(contrasts, rows, traces, samples)
    row = shape(2, contrasts, traces, samples)
    side = shape(contrasts * (2 * rows + 2), samples)
    padded = pltpu.VMEM((8, 2 * LANES), F32)
    work = 2 * angles * rows * traces * samples * 256 * 4
    placed = (seismic, validity, avo_coeffs, wavelets, prior_weight)

    b, part, top, bottom = call(
        start_kernel,
        (field, field, row, row),
        (*placed, lateral_strength),
        3 * work,
        [*[pltpu.VMEM(x.shape, x.dtype) for x in placed], padded, pltpu.SemaphoreType.DMA((5,))],
        [HBM] * 5 + [SMEM],
    )
    above, below = exchange("inline", top, bottom)
    ext, left, right = call(
        rows_kernel,
        (shape(contrasts, rows + 2, traces, samples), side, side),
        (b, part, above, below, lateral_strength),
        4 * field.size,
        places=[VMEM] * 4 + [SMEM],
    )
    left, right = exchange("col", left, right)
    axes = ("inline", "col")
    one, two, gram = call(
        image_kernel,
        (field, field, shape(lax.axis_size(axes), 1, LANES)),
        (b, ext, left, right, validity, avo_coeffs, wavelets, prior_weight, lateral_strength),
        2 * work,
        [padded],
        [VMEM] * 8 + [SMEM],
    )
    gram = lax.all_to_all(gram, axes, 0, 0)
    return tuple(call(finish_kernel, (field, field), (gram, b, one, two), 8 * field.size))


def solution(mesh):
    placed = (
        P(None, "inline", "col", None),
        P(None, "inline", "col"),
        P("inline", "col"),
        P(),
        P(),
        P(),
    )
    return jax.shard_map(
        shards,
        mesh=mesh,
        in_specs=placed,
        out_specs=(P(None, "inline", "col", None), P(None, "inline", "col", None)),
        check_vma=False,
    )
```

time: 74.3 us -> 45.2 us (0.61)
  blocking collectives: 43 us -> 15.7 us
  starting transfers between devices: 20.3 us -> 8.73 us
  waiting for transfers between devices: 3.54 us -> 10.6 us
  local copies, waits for them, and re-layouts: 1.77 us -> 3.77 us
  Pallas kernels: 4.47 us -> 5.26 us
    psum x1 -> x0, blocking collectives: 43 us -> none  [shards(): gram = lax.psum(gram, ('inline', 'col'))]
    all_to_all x0 -> x1, blocking collectives: none -> 15.7 us  [shards(): gram = lax.all_to_all(gram, axes, 0, 0)]
    ppermute x8 -> x4, starting transfers between devices: 20.3 us -> 8.73 us  [exchange(): return (lax.ppermute(last, axis, ahead), lax.ppermute(first, axis, back))]
    ppermute x8 -> x4, waiting for transfers between devices: 3.54 us -> 10.6 us  [exchange(): return (lax.ppermute(last, axis, ahead), lax.ppermute(first, axis, back))]
    unnamed x11 -> x18, local copies, waits for them, and re-layouts: 1.77 us -> 3.77 us
    pallas_call x6 -> x4, Pallas kernels: 4.47 us -> 5.26 us  [call(): pl.pallas_call(kernel, out_shape=outs, in_specs=[VMEM] * len(ins) if plac...]
  transfers between devices with their start and end apart: 8 -> 4, of which waited for: 2 -> 3; matrix products, arithmetic and copies ran while one was open for 0% -> 0% of each run, Pallas kernels for 2% -> 0%
where the time goes in v3:
time: 45.2 us; the launch traced here: 44.8 us
  blocking collectives  15.7 us (35%)
  waiting for transfers between devices  10.6 us (23%)
  starting transfers between devices  8.73 us (19%)
  Pallas kernels  5.26 us (12%)
  local copies, waits for them, and re-layouts  3.77 us (8%)
  between operations  0.72 us (2%)
    all_to_all x1, blocking collectives, shards(): gram = lax.all_to_all(gram, axes, 0, 0)  15.7 us
    ppermute x4, waiting for transfers between devices, exchange(): return (lax.ppermute(last, axis, ahead), lax.ppermute(first, axis, back))  10.6 us
    ppermute x4, starting transfers between devices, exchange(): return (lax.ppermute(last, axis, ahead), lax.ppermute(first, axis, back))  8.73 us
    pallas_call x4, Pallas kernels, call(): pl.pallas_call(kernel, out_shape=outs, in_specs=[VMEM] * len(ins) if plac...  5.26 us
    unnamed x18, local copies, waits for them, and re-layouts  3.77 us
  transfers between devices with their start and end apart: 4, of which 3 were waited for; matrix products, arithmetic and copies ran while one was open for 0% of the time, Pallas kernels for 0%

profile of v3, /device:TPU:0, one launch (start us, length us, event | category | flops | bytes accessed | tf_op | source)
XLA Modules:
  0.0 44.8 jit_solution(4141303379576076472)
XLA Ops:
  0.6 0.0 copy-start
  0.6 0.0 copy-start.8
  0.6 0.6 %copy-done = f32[3]{0:T(128)S(1)} copy-done((f32[3]{0:T(128)S(1)}, f32[3]{0:T(128)}, u32[]{:S(2)}) %copy-start) | copy-done | bytes 36
  1.3 0.0 copy-done.8
  1.3 0.9 %copy-done.1 = bf16[4,2,8,1024]{3,2,1,0:T(8,128)(2,1)S(1)} copy-done((bf16[4,2,8,1024]{3,2,1,0:T(8,128)(2,1)S(1)}, bf16[4,2,8,1024]{3,2,1,0:T(8,128)(2,1)}, u32[]{:S(2)}) %copy-start.1) | copy-done | bytes 131096
  2.2 0.8 %copy-done.2 = f32[4,3,1024]{2,0,1:T(4,128)S(1)} copy-done((f32[4,3,1024]{2,0,1:T(4,128)S(1)}, f32[4,3,1024]{2,0,1:T(4,128)}, u32[]{:S(2)}) %copy-start.2) | copy-done | bytes 49176
  3.0 0.7 %copy-done.4 = s32[4,2,8]{2,1,0:T(2,128)S(1)} copy-done((s32[4,2,8]{2,1,0:T(2,128)S(1)}, s32[4,2,8]{2,1,0:T(2,128)}, u32[]{:S(2)}) %copy-start.4) | copy-done | bytes 280
  3.7 0.7 %copy-done.6 = f32[4,129]{1,0:T(4,128)S(1)} copy-done((f32[4,129]{1,0:T(4,128)S(1)}, f32[4,129]{1,0:T(4,128)}, u32[]{:S(2)}) %copy-start.6) | copy-done | bytes 2088
  4.4 2.1 %start_kernel.1 = (f32[3,2,8,1024]{3,2,1,0:T(8,128)S(1)}, f32[3,2,8,1024]{3,2,1,0:T(8,128)S(1)}, f32[2,3,8,1024]{3,2,1,0:T(8,128)S(1)}, f32[2,3,8,1024]{3,2,1,0:T(8,128)S(1)}) custom-call(bf16[4,2,8,1024]{3,2,1,0:T(8,128)(2,1)S(1)} %copy-done.1, s32[4,2,8]{2,1,0:T(2,128)S(1)} %copy-done.4, f32[3,4,1024]{2,1,0:T(4,128)S(1)} %bitcast.1, ...), custom_call_target="tpu_custom_call" | custom-call | flops 402653184 | bytes 969052 | tf_op jit(solution)/shard_map/start_kernel/pallas_call | solution.py:305
  6.5 4.9 %collective-permute-start = (f32[2,3,8,1024]{3,2,1,0:T(8,128)S(1)}, f32[2,3,8,1024]{3,2,1,0:T(8,128)S(1)}, u32[]{:S(2)}, u32[]{:S(2)}) collective-permute-start(f32[2,3,8,1024]{3,2,1,0:T(8,128)S(1)} %get-tuple-element.14), channel_id=1, source_target_pairs={{0,4},{4,8},{8,12},{12,16},{16,20},{20,24},{24,28},{1,5},{5,9},{9,... | collective-permute-start | bytes 589832 | tf_op jit(solution)/shard_map/ppermute | solution.py:321
  11.3 1.3 %collective-permute-start.1 = (f32[2,3,8,1024]{3,2,1,0:T(8,128)S(1)}, f32[2,3,8,1024]{3,2,1,0:T(8,128)S(1)}, u32[]{:S(2)}, u32[]{:S(2)}) collective-permute-start(f32[2,3,8,1024]{3,2,1,0:T(8,128)S(1)} %get-tuple-element.15), channel_id=1, source_target_pairs={{4,0},{8,4},{12,8},{16,12},{20,16},{24,20},{28,24},{5,1},{9,5},{13... | collective-permute-start | bytes 589832 | tf_op jit(solution)/shard_map/ppermute | solution.py:321
  12.6 2.9 %collective-permute-done.above_ref = f32[2,3,8,1024]{3,2,1,0:T(8,128)S(1)} collective-permute-done((f32[2,3,8,1024]{3,2,1,0:T(8,128)S(1)}, f32[2,3,8,1024]{3,2,1,0:T(8,128)S(1)}, u32[]{:S(2)}, u32[]{:S(2)}) %collective-permute-start) | collective-permute-done | bytes 196640 | tf_op jit(solution)/shard_map/ppermute | solution.py:321
  15.6 4.0 %collective-permute-done.1.below_ref = f32[2,3,8,1024]{3,2,1,0:T(8,128)S(1)} collective-permute-done((f32[2,3,8,1024]{3,2,1,0:T(8,128)S(1)}, f32[2,3,8,1024]{3,2,1,0:T(8,128)S(1)}, u32[]{:S(2)}, u32[]{:S(2)}) %collective-permute-start.1) | collective-permute-done | bytes 196640 | tf_op jit(solution)/shard_map/ppermute | solution.py:321
  19.6 0.7 %rows_kernel.1 = (f32[3,4,8,1024]{3,2,1,0:T(8,128)S(1)}, f32[18,1024]{1,0:T(8,128)S(1)}, f32[18,1024]{1,0:T(8,128)S(1)}) custom-call(f32[3,2,8,1024]{3,2,1,0:T(8,128)S(1)} %get-tuple-element.12.b_ref, f32[3,2,8,1024]{3,2,1,0:T(8,128)S(1)} %get-tuple-element.13.p_ref, f32[2,3,8,1024]{3,2,1,0:T(8,128)S(1)} %collective-permute-done.above_ref, ...), custom_call_target="tpu_custom_call" | custom-call | flops 196608 | bytes 1327116 | tf_op jit(solution)/shard_map/rows_kernel/pallas_call | solution.py:305
  20.3 0.0 copy-start.5
  20.3 1.3 %collective-permute-start.2 = (f32[18,1024]{1,0:T(8,128)S(1)}, f32[18,1024]{1,0:T(8,128)S(1)}, u32[]{:S(2)}, u32[]{:S(2)}) collective-permute-start(f32[18,1024]{1,0:T(8,128)S(1)} %get-tuple-element.17), channel_id=1, source_target_pairs={{0,1},{1,2},{2,3},{4,5},{5,6},{6,7},{8,9},{9,10},{10,11},{12,13},{... | collective-permute-start | bytes 221192 | tf_op jit(solution)/shard_map/ppermute | solution.py:321
  21.6 1.3 %collective-permute-start.3 = (f32[18,1024]{1,0:T(8,128)S(1)}, f32[18,1024]{1,0:T(8,128)S(1)}, u32[]{:S(2)}, u32[]{:S(2)}) collective-permute-start(f32[18,1024]{1,0:T(8,128)S(1)} %get-tuple-element.18), channel_id=1, source_target_pairs={{1,0},{2,1},{3,2},{5,4},{6,5},{7,6},{9,8},{10,9},{11,10},{13,12},{... | collective-permute-start | bytes 221192 | tf_op jit(solution)/shard_map/ppermute | solution.py:321
  22.9 0.0 collective-permute-done.2.left_ref
  22.9 3.6 %collective-permute-done.3.right_ref = f32[18,1024]{1,0:T(8,128)S(1)} collective-permute-done((f32[18,1024]{1,0:T(8,128)S(1)}, f32[18,1024]{1,0:T(8,128)S(1)}, u32[]{:S(2)}, u32[]{:S(2)}) %collective-permute-start.3) | collective-permute-done | bytes 73760 | tf_op jit(solution)/shard_map/ppermute | solution.py:321
  26.5 0.0 copy-done.3
  26.5 0.0 copy-done.7
  26.5 1.6 %image_kernel.1 = (f32[3,2,8,1024]{3,2,1,0:T(8,128)S(1)}, f32[3,2,8,1024]{3,2,1,0:T(8,128)S(1)}, f32[32,1,128]{2,1,0:T(1,128)S(1)}) custom-call(f32[3,2,8,1024]{3,2,1,0:T(8,128)S(1)} %get-tuple-element.12.b_ref, f32[3,4,8,1024]{3,2,1,0:T(8,128)S(1)} %get-tuple-element.16.v_ref, f32[18,1024]{1,0:T(8,128)S(1)} %collective-permute-done.2.left_ref, ...), custom_call_target="tpu_custom_call" | custom-call | flops 268435456 | bytes 1198428 | tf_op jit(solution)/shard_map/image_kernel/pallas_call | solution.py:305
  28.1 15.7 %all_to_all.5.gram_ref = f32[32,1,128]{2,1,0:T(1,128)S(1)} all-to-all(f32[32,1,128]{2,1,0:T(1,128)S(1)} %get-tuple-element.19), channel_id=1, replica_groups=mesh['inline'=8,'col'=4] {'inline','col'}, dimensions={0} | all-to-all | bytes 32768 | tf_op jit(solution)/shard_map/all_to_all | solution.py:362
  43.9 0.9 %finish_kernel.1 = (f32[3,2,8,1024]{3,2,1,0:T(8,128)}, f32[3,2,8,1024]{3,2,1,0:T(8,128)}) custom-call(f32[32,1,128]{2,1,0:T(1,128)S(1)} %all_to_all.5.gram_ref, f32[3,2,8,1024]{3,2,1,0:T(8,128)S(1)} %get-tuple-element.12.b_ref, f32[3,2,8,1024]{3,2,1,0:T(8,128)S(1)} %get-tuple-element.20.one_ref, f32[3,2,8,1024]{3,2,1,0:T(8,128)S(1)} %get-tuple-element.21.two_ref), custom_call_target="tpu_custom_call" | custom-call | flops 393216 | bytes 999424 | tf_op jit(solution)/shard_map/finish_kernel/pallas_call | solution.py:305
  (7 shorter events, 0.0 us)
Async XLA Ops:
  0.6 0.7 %copy-start = (f32[3]{0:T(128)S(1)}, f32[3]{0:T(128)}, u32[]{:S(2)}) copy-start(f32[3]{0:T(128)} %strength_ref.5) | copy-start | bytes 40
  0.6 0.7 %copy-start.8 = (f32[2,8]{1,0:T(2,128)S(1)}, f32[2,8]{1,0:T(2,128)}, u32[]{:S(2)}) copy-start(f32[2,8]{1,0:T(2,128)} %prior_ref.1) | copy-start | bytes 196
  1.3 0.9 %copy-start.1 = (bf16[4,2,8,1024]{3,2,1,0:T(8,128)(2,1)S(1)}, bf16[4,2,8,1024]{3,2,1,0:T(8,128)(2,1)}, u32[]{:S(2)}) copy-start(bf16[4,2,8,1024]{3,2,1,0:T(8,128)(2,1)} %seis_hbm.1) | copy-start | bytes 393220
  2.2 0.8 %copy-start.2 = (f32[4,3,1024]{2,0,1:T(4,128)S(1)}, f32[4,3,1024]{2,0,1:T(4,128)}, u32[]{:S(2)}) copy-start(f32[4,3,1024]{2,0,1:T(4,128)} %param.10) | copy-start | bytes 147460
  3.0 0.7 %copy-start.4 = (s32[4,2,8]{2,1,0:T(2,128)S(1)}, s32[4,2,8]{2,1,0:T(2,128)}, u32[]{:S(2)}) copy-start(s32[4,2,8]{2,1,0:T(2,128)} %valid_ref.1) | copy-start | bytes 772
  3.7 0.7 %copy-start.6 = (f32[4,129]{1,0:T(4,128)S(1)}, f32[4,129]{1,0:T(4,128)}, u32[]{:S(2)}) copy-start(f32[4,129]{1,0:T(4,128)} %taps_ref.1) | copy-start | bytes 6196
  6.5 9.1 %collective-permute-start = (f32[2,3,8,1024]{3,2,1,0:T(8,128)S(1)}, f32[2,3,8,1024]{3,2,1,0:T(8,128)S(1)}, u32[]{:S(2)}, u32[]{:S(2)}) collective-permute-start(f32[2,3,8,1024]{3,2,1,0:T(8,128)S(1)} %get-tuple-element.14), channel_id=1, source_target_pairs={{0,4},{4,8},{8,12},{12,16},{16,20},{20,24},{24,28},{1,5},{5,9},{9,... | collective-permute-start | bytes 589832 | tf_op jit(solution)/shard_map/ppermute | solution.py:321
  11.3 8.3 %collective-permute-start.1 = (f32[2,3,8,1024]{3,2,1,0:T(8,128)S(1)}, f32[2,3,8,1024]{3,2,1,0:T(8,128)S(1)}, u32[]{:S(2)}, u32[]{:S(2)}) collective-permute-start(f32[2,3,8,1024]{3,2,1,0:T(8,128)S(1)} %get-tuple-element.15), channel_id=1, source_target_pairs={{4,0},{8,4},{12,8},{16,12},{20,16},{24,20},{28,24},{5,1},{9,5},{13... | collective-permute-start | bytes 589832 | tf_op jit(solution)/shard_map/ppermute | solution.py:321
  19.6 6.9 %copy-start.3 = (f32[4,3,1024]{2,0,1:T(4,128)S(1)}, f32[4,3,1024]{2,0,1:T(4,128)}, u32[]{:S(2)}) copy-start(f32[4,3,1024]{2,0,1:T(4,128)} %param.10) | copy-start | bytes 147460
  19.6 6.9 %copy-start.7 = (f32[4,129]{1,0:T(4,128)S(1)}, f32[4,129]{1,0:T(4,128)}, u32[]{:S(2)}) copy-start(f32[4,129]{1,0:T(4,128)} %taps_ref.1) | copy-start | bytes 6196
  20.3 6.3 %copy-start.5 = (s32[4,2,8]{2,1,0:T(2,128)S(1)}, s32[4,2,8]{2,1,0:T(2,128)}, u32[]{:S(2)}) copy-start(s32[4,2,8]{2,1,0:T(2,128)} %valid_ref.1) | copy-start | bytes 772
  20.3 2.6 %collective-permute-start.2 = (f32[18,1024]{1,0:T(8,128)S(1)}, f32[18,1024]{1,0:T(8,128)S(1)}, u32[]{:S(2)}, u32[]{:S(2)}) collective-permute-start(f32[18,1024]{1,0:T(8,128)S(1)} %get-tuple-element.17), channel_id=1, source_target_pairs={{0,1},{1,2},{2,3},{4,5},{5,6},{6,7},{8,9},{9,10},{10,11},{12,13},{... | collective-permute-start | bytes 221192 | tf_op jit(solution)/shard_map/ppermute | solution.py:321
  21.6 4.9 %collective-permute-start.3 = (f32[18,1024]{1,0:T(8,128)S(1)}, f32[18,1024]{1,0:T(8,128)S(1)}, u32[]{:S(2)}, u32[]{:S(2)}) collective-permute-start(f32[18,1024]{1,0:T(8,128)S(1)} %get-tuple-element.18), channel_id=1, source_target_pairs={{1,0},{2,1},{3,2},{5,4},{6,5},{7,6},{9,8},{10,9},{11,10},{13,12},{... | collective-permute-start | bytes 221192 | tf_op jit(solution)/shard_map/ppermute | solution.py:321

commit v4 on v3

--- a/solution.py
+++ b/solution.py
@@ -154,8 +154,8 @@
 
 
 def start_kernel(
-    seis_hbm, valid_hbm, avo_hbm, taps_hbm, prior_hbm, strength_ref,
-    b_ref, p_ref, top_ref, bottom_ref,
+    seis_hbm, valid_hbm, avo_hbm, taps_hbm, prior_hbm, strength_hbm,
+    b_ref, p_ref, top_b_ref, top_p_ref, bottom_ref, strength_ref,
     seis_ref, valid_ref, avo_ref, taps_ref, prior_ref, padded, sems,
 ):
     copies = copy_in(
@@ -163,34 +163,37 @@
             (taps_hbm, taps_ref),
             (valid_hbm, valid_ref),
             (prior_hbm, prior_ref),
+            (strength_hbm, strength_ref),
             (avo_hbm, avo_ref),
             (seis_hbm, seis_ref),
         ),
         sems,
     )
-    for copy in copies[:3]:
+    for copy in copies[:4]:
         copy.wait()
     fill_taps(taps_ref, padded)
     contrasts, angles, samples = avo_ref.shape
     rows = seis_ref.shape[1]
     circs = [circulant(padded, a) for a in range(angles)]
     masks = [trace_columns(valid_ref, a) for a in range(angles)]
-    for copy in copies[3:]:
+    for copy in copies[4:]:
         copy.wait()
     b = right_side(seis_ref, masks, avo_ref, circs)
     store_tiles(b_ref, b)
     store_tiles(p_ref, normal(b, masks, avo_ref, circs))
     weights = [column(prior_ref[r : r + 1, :]) + 4.0 for r in range(rows)]
     for c in range(contrasts):
+        strength = strength_ref[:, c : c + 1]
         for r in range(rows):
             here = b_ref[c, r]
             north = b_ref[c, r - 1] if r else None
             south = b_ref[c, r + 1] if r < rows - 1 else None
             around = lateral(here, north, south, None, None)
-            p_ref[c, r] = p_ref[c, r] + strength_ref[c] * (weights[r] * here - around)
-        for out_ref, r in ((top_ref, 0), (bottom_ref, rows - 1)):
-            out_ref[0, c] = b_ref[c, r]
-            out_ref[1, c] = p_ref[c, r]
+            p_ref[c, r] = p_ref[c, r] + strength * (weights[r] * here - around)
+        top_b_ref[c] = b_ref[c, 0]
+        top_p_ref[c] = p_ref[c, 0]
+        bottom_ref[0, c] = b_ref[c, rows - 1]
+        bottom_ref[1, c] = p_ref[c, rows - 1]
 
 
 def inside(axis):
@@ -199,32 +202,42 @@
     return (place > 0).astype(F32), (place < last).astype(F32)
 
 
-def rows_kernel(b_ref, p_ref, above_ref, below_ref, strength_ref, v_ref, left_ref, right_ref):
+def starts_pair():
+    return lax.axis_index("col") % 2 == 0
+
+
+def rows_kernel(b_ref, p_ref, above_ref, below_ref, strength_ref, v_ref, pair_ref, other_ref):
     contrasts, rows, traces, _ = b_ref.shape
-    has_above, has_below = inside("inline")
+    has_above, _ = inside("inline")
+    first_of_pair = starts_pair()
     for c in range(contrasts):
-        strength = strength_ref[c]
+        strength = strength_ref[:, c : c + 1]
         own = [p_ref[c, r] for r in range(rows)]
         own[0] = own[0] - strength * above_ref[0, c]
-        own[-1] = own[-1] - strength * below_ref[0, c]
+        own[-1] = own[-1] - strength * below_ref[c]
         over = has_above * (above_ref[1, c] - strength * b_ref[c, 0])
-        under = has_below * (below_ref[1, c] - strength * b_ref[c, rows - 1])
-        for r, line in enumerate([over, *own, under]):
+        for r, line in enumerate([over, *own]):
             v_ref[c, r] = line
-        lines = [above_ref[0, c], *[b_ref[c, r] for r in range(rows)], below_ref[0, c], *own]
+        lines = [above_ref[0, c], *[b_ref[c, r] for r in range(rows)], below_ref[c], *own]
         base = c * len(lines)
         for e, line in enumerate(lines):
-            left_ref[base + e : base + e + 1, :] = line[0:1, :]
-            right_ref[base + e : base + e + 1, :] = line[traces - 1 : traces, :]
+            left, right = line[0:1, :], line[traces - 1 : traces, :]
+            pair_ref[base + e : base + e + 1, :] = jnp.where(first_of_pair, right, left)
+            other_ref[base + e : base + e + 1, :] = jnp.where(first_of_pair, left, right)
 
 
 def image_kernel(
-    b_ref, v_ref, left_ref, right_ref, valid_ref, avo_ref, taps_ref, prior_ref, strength_ref,
+    b_ref, v_ref, under_ref, other_ref, pair_ref,
+    valid_ref, avo_ref, taps_ref, prior_ref, strength_ref,
     one_ref, two_ref, gram_ref, padded,
 ):
     contrasts, rows, traces, samples = b_ref.shape
     angles, n = avo_ref.shape[1], samples // LANES
     has_left, has_right = inside("col")
+    _, has_below = inside("inline")
+    first_of_pair = starts_pair()
+    left = jnp.where(first_of_pair, other_ref[...], pair_ref[...])
+    right = jnp.where(first_of_pair, pair_ref[...], other_ref[...])
     place = lax.broadcasted_iota(jnp.int32, (traces, samples), 0)
     first, last = place == 0, place == traces - 1
     ext = rows + 2
@@ -236,10 +249,14 @@
             edge = base + r
             missing = jnp.where(
                 first,
-                left_ref[edge : edge + 1, :],
-                jnp.where(last, right_ref[edge : edge + 1, :], 0.0),
+                left[edge : edge + 1, :],
+                jnp.where(last, right[edge : edge + 1, :], 0.0),
             )
-            lines.append(v_ref[c, r] - strength_ref[c] * missing)
+            if r < ext - 1:
+                line = v_ref[c, r]
+            else:
+                line = has_below * (under_ref[c] - strength_ref[:, c : c + 1] * b_ref[c, rows - 1])
+            lines.append(line - strength_ref[:, c : c + 1] * missing)
         whole.append(lines)
         for r in range(rows):
             one_ref[c, r] = lines[r + 1]
@@ -257,14 +274,14 @@
     weights = [column(prior_ref[r : r + 1, :]) + 4.0 for r in range(rows)]
     sums = [jnp.zeros((traces, LANES), F32) for _ in range(4)]
     for c in range(contrasts):
-        strength = strength_ref[c]
+        strength = strength_ref[:, c : c + 1]
         for r in range(rows):
             here = whole[c][r + 1]
             edge = c * (ext + rows) + ext + r
             b = b_ref[c, r]
-            west = has_left * (left_ref[edge : edge + 1, :] - strength * b[0:1, :])
+            west = has_left * (left[edge : edge + 1, :] - strength * b[0:1, :])
             east = has_right * (
-                right_ref[edge : edge + 1, :] - strength * b[traces - 1 : traces, :]
+                right[edge : edge + 1, :] - strength * b[traces - 1 : traces, :]
             )
             around = lateral(here, whole[c][r], whole[c][r + 2], west, east)
             two = two_ref[c, r] + strength * (weights[r] * here - around)
@@ -296,7 +313,6 @@
 
 
 VMEM = pl.BlockSpec(memory_space=pltpu.VMEM)
-SMEM = pl.BlockSpec(memory_space=pltpu.SMEM)
 HBM = pl.BlockSpec(memory_space=pltpu.HBM)
 
 
@@ -314,11 +330,14 @@
     )(*ins)
 
 
-def exchange(axis, first, last):
+def shift(axis, value, step):
     size = lax.axis_size(axis)
-    ahead = [(i, i + 1) for i in range(size - 1)]
-    back = [(j, i) for i, j in ahead]
-    return lax.ppermute(last, axis, ahead), lax.ppermute(first, axis, back)
+    return lax.ppermute(value, axis, [(i, i + step) for i in range(size) if 0 <= i + step < size])
+
+
+def swap(axis, value, first):
+    starts = range(first, lax.axis_size(axis) - 1, 2)
+    return lax.ppermute(value, axis, [(i + d, i + 1 - d) for i in starts for d in (0, 1)])
 
 
 def shards(seismic, validity, prior_weight, lateral_strength, avo_coeffs, wavelets):
@@ -327,37 +346,43 @@
     avo_coeffs = jnp.swapaxes(avo_coeffs, 0, 1)
     shape = lambda *dims: jax.ShapeDtypeStruct(dims, F32)
     field = shape(contrasts, rows, traces, samples)
-    row = shape(2, contrasts, traces, samples)
+    row = shape(contrasts, traces, samples)
     side = shape(contrasts * (2 * rows + 2), samples)
     padded = pltpu.VMEM((8, 2 * LANES), F32)
     work = 2 * angles * rows * traces * samples * 256 * 4
-    placed = (seismic, validity, avo_coeffs, wavelets, prior_weight)
-
-    b, part, top, bottom = call(
+
+    placed = (
+        seismic, validity, avo_coeffs, wavelets, prior_weight, lateral_strength.reshape(1, -1)
+    )
+    b, part, top_b, top_p, bottom, strength = call(
         start_kernel,
-        (field, field, row, row),
-        (*placed, lateral_strength),
+        (field, field, row, row, shape(2, *row.shape), shape(1, contrasts)),
+        [pltpu.with_memory_space_constraint(x, pltpu.HBM) for x in placed],
         3 * work,
-        [*[pltpu.VMEM(x.shape, x.dtype) for x in placed], padded, pltpu.SemaphoreType.DMA((5,))],
-        [HBM] * 5 + [SMEM],
-    )
-    above, below = exchange("inline", top, bottom)
-    ext, left, right = call(
+        [*[pltpu.VMEM(x.shape, x.dtype) for x in placed[:-1]], padded, pltpu.SemaphoreType.DMA((6,))],
+        [HBM] * 6,
+    )
+    above = shift("inline", bottom, 1)
+    below = shift("inline", top_b, -1)
+    under = shift("inline", top_p, -1)
+    ext, pair, other = call(
         rows_kernel,
-        (shape(contrasts, rows + 2, traces, samples), side, side),
-        (b, part, above, below, lateral_strength),
+        (shape(contrasts, rows + 1, traces, samples), side, side),
+        (b, part, above, below, strength),
         4 * field.size,
-        places=[VMEM] * 4 + [SMEM],
-    )
-    left, right = exchange("col", left, right)
+    )
+    other = swap("col", other, 1)
+    pair = swap("col", pair, 0)
     axes = ("inline", "col")
     one, two, gram = call(
         image_kernel,
         (field, field, shape(lax.axis_size(axes), 1, LANES)),
-        (b, ext, left, right, validity, avo_coeffs, wavelets, prior_weight, lateral_strength),
+        (
+            b, ext, under, other, pair,
+            validity, avo_coeffs, wavelets, prior_weight, strength,
+        ),
         2 * work,
         [padded],
-        [VMEM] * 8 + [SMEM],
     )
     gram = lax.all_to_all(gram, axes, 0, 0)
     return tuple(call(finish_kernel, (field, field), (gram, b, one, two), 8 * field.size))

time: 45.2 us -> 36.1 us (0.80)
  waiting for transfers between devices: 10.6 us -> 5.47 us
  local copies, waits for them, and re-layouts: 3.77 us -> 0.02 us
  starting transfers between devices: 8.73 us -> 11 us
  blocking collectives: 15.7 us -> 14.4 us
  Pallas kernels: 5.26 us -> 4.22 us
    ppermute x4 -> x5, waiting for transfers between devices: 10.6 us -> 5.47 us  [the longest x3 4.52 us: shift(): lax.ppermute(value, axis, [(i, i + step) for i in range(size) if 0 <= i +...]
    unnamed x18 -> x8, local copies, waits for them, and re-layouts: 3.77 us -> 0.02 us
    ppermute x4 -> x5, starting transfers between devices: 8.73 us -> 11 us  [the longest x3 7.44 us: shift(): lax.ppermute(value, axis, [(i, i + step) for i in range(size) if 0 <= i +...]
    all_to_all x1, blocking collectives: 15.7 us -> 14.4 us  [shards(): gram = lax.all_to_all(gram, axes, 0, 0)]
    pallas_call x4, Pallas kernels: 5.26 us -> 4.22 us  [call(): pl.pallas_call(kernel, out_shape=outs, in_specs=[VMEM] * len(ins) if plac...]
  transfers between devices with their start and end apart: 4 -> 5, of which waited for: 3 -> 2; matrix products, arithmetic and copies ran while one was open for 0% -> 0% of each run, Pallas kernels for 0% -> 1%
where the time goes in v4:
time: 36.1 us; the launch traced here: 35.8 us
  blocking collectives  14.4 us (40%)
  starting transfers between devices  11 us (30%)
  waiting for transfers between devices  5.47 us (15%)
  Pallas kernels  4.22 us (12%)
  between operations  0.7 us (2%)
    all_to_all x1, blocking collectives, shards(): gram = lax.all_to_all(gram, axes, 0, 0)  14.4 us
    ppermute x3, starting transfers between devices, shift(): lax.ppermute(value, axis, [(i, i + step) for i in range(size) if 0 <= i +...  7.44 us
    ppermute x3, waiting for transfers between devices, shift(): lax.ppermute(value, axis, [(i, i + step) for i in range(size) if 0 <= i +...  4.52 us
    pallas_call x4, Pallas kernels, call(): pl.pallas_call(kernel, out_shape=outs, in_specs=[VMEM] * len(ins) if plac...  4.22 us
    ppermute x2, starting transfers between devices, swap(): lax.ppermute(value, axis, [(i + d, i + 1 - d) for i in starts for d in (0...  3.61 us
    ppermute x2, waiting for transfers between devices, swap(): lax.ppermute(value, axis, [(i + d, i + 1 - d) for i in starts for d in (0...  0.94 us
  transfers between devices with their start and end apart: 5, of which 2 were waited for; matrix products, arithmetic and copies ran while one was open for 0% of the time, Pallas kernels for 1%

profile of v4, /device:TPU:0, one launch (start us, length us, event | category | flops | bytes accessed | tf_op | source)
XLA Modules:
  0.0 35.8 jit_solution(4250985878189567170)
XLA Ops:
  0.6 2.1 %start_kernel.1 = (f32[3,2,8,1024]{3,2,1,0:T(8,128)S(1)}, f32[3,2,8,1024]{3,2,1,0:T(8,128)S(1)}, f32[3,8,1024]{2,1,0:T(8,128)S(1)}, f32[3,8,1024]{2,1,0:T(8,128)...) custom-call(bf16[4,2,8,1024]{3,2,1,0:T(8,128)(2,1)} %seis_hbm.1, s32[4,2,8]{2,1,0:T(2,128)} %valid_ref.1, ...), custom_call_target="tpu_custom_call" | custom-call | flops 402653184 | bytes 969064 | tf_op jit(solution)/shard_map/start_kernel/pallas_call | solution.py:321
  2.7 4.9 %collective-permute-start = (f32[2,3,8,1024]{3,2,1,0:T(8,128)S(1)}, f32[2,3,8,1024]{3,2,1,0:T(8,128)S(1)}, u32[]{:S(2)}, u32[]{:S(2)}) collective-permute-start(f32[2,3,8,1024]{3,2,1,0:T(8,128)S(1)} %get-tuple-element.16), channel_id=1, source_target_pairs={{0,4},{4,8},{8,12},{12,16},{16,20},{20,24},{24,28},{1,5},{5,9},{9,... | collective-permute-start | bytes 589832 | tf_op jit(solution)/shard_map/ppermute | solution.py:335
  7.6 1.3 %collective-permute-start.1 = (f32[3,8,1024]{2,1,0:T(8,128)S(1)}, f32[3,8,1024]{2,1,0:T(8,128)S(1)}, u32[]{:S(2)}, u32[]{:S(2)}) collective-permute-start(f32[3,8,1024]{2,1,0:T(8,128)S(1)} %get-tuple-element.17), channel_id=1, source_target_pairs={{4,0},{8,4},{12,8},{16,12},{20,16},{24,20},{28,24},{5,1},{9,5},{13... | collective-permute-start | bytes 294920 | tf_op jit(solution)/shard_map/ppermute | solution.py:335
  8.9 1.3 %collective-permute-start.2 = (f32[3,8,1024]{2,1,0:T(8,128)S(1)}, f32[3,8,1024]{2,1,0:T(8,128)S(1)}, u32[]{:S(2)}, u32[]{:S(2)}) collective-permute-start(f32[3,8,1024]{2,1,0:T(8,128)S(1)} %get-tuple-element.20), channel_id=1, source_target_pairs={{4,0},{8,4},{12,8},{16,12},{20,16},{24,20},{28,24},{5,1},{9,5},{13... | collective-permute-start | bytes 294920 | tf_op jit(solution)/shard_map/ppermute | solution.py:335
  10.2 4.5 %collective-permute-done.1.below_ref = f32[3,8,1024]{2,1,0:T(8,128)S(1)} collective-permute-done((f32[3,8,1024]{2,1,0:T(8,128)S(1)}, f32[3,8,1024]{2,1,0:T(8,128)S(1)}, u32[]{:S(2)}, u32[]{:S(2)}) %collective-permute-start.1) | collective-permute-done | bytes 98336 | tf_op jit(solution)/shard_map/ppermute | solution.py:335
  14.7 0.0 collective-permute-done.above_ref
  14.7 0.0 copy-start
  14.7 0.0 copy-start.2
  14.7 0.2 rows_kernel.1
  14.9 0.0 copy-start.1
  14.9 0.7 %collective-permute-start.3 = (f32[18,1024]{1,0:T(8,128)S(1)}, f32[18,1024]{1,0:T(8,128)S(1)}, u32[]{:S(2)}, u32[]{:S(2)}) collective-permute-start(f32[18,1024]{1,0:T(8,128)S(1)} %get-tuple-element.21), channel_id=1, source_target_pairs={{1,2},{2,1},{5,6},{6,5},{9,10},{10,9},{13,14},{14,13},{17,18},{18,... | collective-permute-start | bytes 221192 | tf_op jit(solution)/shard_map/ppermute | solution.py:340
  15.6 0.0 copy-start.3
  15.6 2.9 %collective-permute-start.4 = (f32[18,1024]{1,0:T(8,128)S(1)}, f32[18,1024]{1,0:T(8,128)S(1)}, u32[]{:S(2)}, u32[]{:S(2)}) collective-permute-start(f32[18,1024]{1,0:T(8,128)S(1)} %get-tuple-element.22), channel_id=1, source_target_pairs={{0,1},{1,0},{2,3},{3,2},{4,5},{5,4},{6,7},{7,6},{8,9},{9,8},{10,11... | collective-permute-start | bytes 221192 | tf_op jit(solution)/shard_map/ppermute | solution.py:340
  18.5 0.0 collective-permute-done.2.under_ref
  18.5 0.0 collective-permute-done.3.other_ref
  18.5 0.9 %collective-permute-done.4.pair_ref = f32[18,1024]{1,0:T(8,128)S(1)} collective-permute-done((f32[18,1024]{1,0:T(8,128)S(1)}, f32[18,1024]{1,0:T(8,128)S(1)}, u32[]{:S(2)}, u32[]{:S(2)}) %collective-permute-start.4) | collective-permute-done | bytes 73760 | tf_op jit(solution)/shard_map/ppermute | solution.py:340
  19.5 0.0 copy-done
  19.5 0.0 copy-done.2
  19.5 0.0 copy-done.1
  19.5 0.0 copy-done.3
  19.5 1.0 %image_kernel.1 = (f32[3,2,8,1024]{3,2,1,0:T(8,128)S(1)}, f32[3,2,8,1024]{3,2,1,0:T(8,128)S(1)}, f32[32,1,128]{2,1,0:T(1,128)S(1)}) custom-call(f32[3,2,8,1024]{3,2,1,0:T(8,128)S(1)} %get-tuple-element.14.b_ref, f32[3,3,8,1024]{3,2,1,0:T(8,128)S(1)} %get-tuple-element.19.v_ref, f32[3,8,1024]{2,1,0:T(8,128)S(1)} %collective-permute-done.2.under_ref, ...), custom_call_target="tpu_custom_call" | custom-call | flops 268435456 | bytes 1198428 | tf_op jit(solution)/shard_map/image_kernel/pallas_call | solution.py:321
  20.5 14.4 %all_to_all.5.gram_ref = f32[32,1,128]{2,1,0:T(1,128)S(1)} all-to-all(f32[32,1,128]{2,1,0:T(1,128)S(1)} %get-tuple-element.23), channel_id=1, replica_groups=mesh['inline'=8,'col'=4] {'inline','col'}, dimensions={0} | all-to-all | bytes 32768 | tf_op jit(solution)/shard_map/all_to_all | solution.py:387
  34.9 0.9 %finish_kernel.1 = (f32[3,2,8,1024]{3,2,1,0:T(8,128)}, f32[3,2,8,1024]{3,2,1,0:T(8,128)}) custom-call(f32[32,1,128]{2,1,0:T(1,128)S(1)} %all_to_all.5.gram_ref, f32[3,2,8,1024]{3,2,1,0:T(8,128)S(1)} %get-tuple-element.14.b_ref, f32[3,2,8,1024]{3,2,1,0:T(8,128)S(1)} %get-tuple-element.24.one_ref, f32[3,2,8,1024]{3,2,1,0:T(8,128)S(1)} %get-tuple-element.25.two_ref), custom_call_target="tpu_custom_call" | custom-call | flops 393216 | bytes 999424 | tf_op jit(solution)/shard_map/finish_kernel/pallas_call | solution.py:321
Async XLA Ops:
  2.7 12.0 %collective-permute-start = (f32[2,3,8,1024]{3,2,1,0:T(8,128)S(1)}, f32[2,3,8,1024]{3,2,1,0:T(8,128)S(1)}, u32[]{:S(2)}, u32[]{:S(2)}) collective-permute-start(f32[2,3,8,1024]{3,2,1,0:T(8,128)S(1)} %get-tuple-element.16), channel_id=1, source_target_pairs={{0,4},{4,8},{8,12},{12,16},{16,20},{20,24},{24,28},{1,5},{5,9},{9,... | collective-permute-start | bytes 589832 | tf_op jit(solution)/shard_map/ppermute | solution.py:335
  7.6 7.1 %collective-permute-start.1 = (f32[3,8,1024]{2,1,0:T(8,128)S(1)}, f32[3,8,1024]{2,1,0:T(8,128)S(1)}, u32[]{:S(2)}, u32[]{:S(2)}) collective-permute-start(f32[3,8,1024]{2,1,0:T(8,128)S(1)} %get-tuple-element.17), channel_id=1, source_target_pairs={{4,0},{8,4},{12,8},{16,12},{20,16},{24,20},{28,24},{5,1},{9,5},{13... | collective-permute-start | bytes 294920 | tf_op jit(solution)/shard_map/ppermute | solution.py:335
  8.9 9.7 %collective-permute-start.2 = (f32[3,8,1024]{2,1,0:T(8,128)S(1)}, f32[3,8,1024]{2,1,0:T(8,128)S(1)}, u32[]{:S(2)}, u32[]{:S(2)}) collective-permute-start(f32[3,8,1024]{2,1,0:T(8,128)S(1)} %get-tuple-element.20), channel_id=1, source_target_pairs={{4,0},{8,4},{12,8},{16,12},{20,16},{24,20},{28,24},{5,1},{9,5},{13... | collective-permute-start | bytes 294920 | tf_op jit(solution)/shard_map/ppermute | solution.py:335
  14.7 4.8 %copy-start = (f32[4,3,1024]{2,0,1:T(4,128)S(1)}, f32[4,3,1024]{2,0,1:T(4,128)}, u32[]{:S(2)}) copy-start(f32[4,3,1024]{2,0,1:T(4,128)} %param.10) | copy-start | bytes 147460
  14.7 4.8 %copy-start.2 = (f32[4,129]{1,0:T(4,128)S(1)}, f32[4,129]{1,0:T(4,128)}, u32[]{:S(2)}) copy-start(f32[4,129]{1,0:T(4,128)} %taps_ref.1) | copy-start | bytes 6196
  14.9 4.6 %copy-start.1 = (s32[4,2,8]{2,1,0:T(2,128)S(1)}, s32[4,2,8]{2,1,0:T(2,128)}, u32[]{:S(2)}) copy-start(s32[4,2,8]{2,1,0:T(2,128)} %valid_ref.1) | copy-start | bytes 772
  14.9 3.6 %collective-permute-start.3 = (f32[18,1024]{1,0:T(8,128)S(1)}, f32[18,1024]{1,0:T(8,128)S(1)}, u32[]{:S(2)}, u32[]{:S(2)}) collective-permute-start(f32[18,1024]{1,0:T(8,128)S(1)} %get-tuple-element.21), channel_id=1, source_target_pairs={{1,2},{2,1},{5,6},{6,5},{9,10},{10,9},{13,14},{14,13},{17,18},{18,... | collective-permute-start | bytes 221192 | tf_op jit(solution)/shard_map/ppermute | solution.py:340
  15.6 3.9 %copy-start.3 = (f32[2,8]{1,0:T(2,128)S(1)}, f32[2,8]{1,0:T(2,128)}, u32[]{:S(2)}) copy-start(f32[2,8]{1,0:T(2,128)} %prior_ref.1) | copy-start | bytes 196
  15.6 3.9 %collective-permute-start.4 = (f32[18,1024]{1,0:T(8,128)S(1)}, f32[18,1024]{1,0:T(8,128)S(1)}, u32[]{:S(2)}, u32[]{:S(2)}) collective-permute-start(f32[18,1024]{1,0:T(8,128)S(1)} %get-tuple-element.22), channel_id=1, source_target_pairs={{0,1},{1,0},{2,3},{3,2},{4,5},{5,4},{6,7},{7,6},{8,9},{9,8},{10,11... | collective-permute-start | bytes 221192 | tf_op jit(solution)/shard_map/ppermute | solution.py:340

commit v5 on v4

--- a/solution.py
+++ b/solution.py
@@ -294,7 +294,7 @@
     for q, total in enumerate(sums):
         total = jnp.sum(jnp.sum(total, axis=0, keepdims=True), axis=1, keepdims=True)
         packed = jnp.where(lane == q, total, packed)
-    gram_ref[...] = jnp.broadcast_to(packed[None], gram_ref.shape)
+    gram_ref[...] = packed
 
 
 def finish_kernel(gram_ref, b_ref, one_ref, two_ref, solution_ref, residual_ref):
@@ -376,7 +376,7 @@
     axes = ("inline", "col")
     one, two, gram = call(
         image_kernel,
-        (field, field, shape(lax.axis_size(axes), 1, LANES)),
+        (field, field, shape(1, LANES)),
         (
             b, ext, under, other, pair,
             validity, avo_coeffs, wavelets, prior_weight, strength,
@@ -384,7 +384,7 @@
         2 * work,
         [padded],
     )
-    gram = lax.all_to_all(gram, axes, 0, 0)
+    gram = lax.all_gather(gram, axes)
     return tuple(call(finish_kernel, (field, field), (gram, b, one, two), 8 * field.size))
 
 

time: 36.1 us -> 63.8 us (1.77)
  blocking collectives: 14.4 us -> 42.1 us
    all_gather x0 -> x1, blocking collectives: none -> 42.1 us  [shards(): gram = lax.all_gather(gram, axes)]
    all_to_all x1 -> x0, blocking collectives: 14.4 us -> none  [shards(): gram = lax.all_to_all(gram, axes, 0, 0)]
  transfers between devices with their start and end apart: 5 -> 5, of which waited for: 2 -> 2; matrix products, arithmetic and copies ran while one was open for 0% -> 0% of each run, Pallas kernels for 1% -> 0%
where the time goes in v5:
time: 63.8 us; the launch traced here: 63.5 us
  blocking collectives  42.1 us (66%)
  starting transfers between devices  11 us (17%)
  waiting for transfers between devices  5.47 us (9%)
  Pallas kernels  4.21 us (7%)
  between operations  0.7 us (1%)
    all_gather x1, blocking collectives, shards(): gram = lax.all_gather(gram, axes)  42.1 us
    ppermute x3, starting transfers between devices, shift(): lax.ppermute(value, axis, [(i, i + step) for i in range(size) if 0 <= i +...  7.44 us
    ppermute x3, waiting for transfers between devices, shift(): lax.ppermute(value, axis, [(i, i + step) for i in range(size) if 0 <= i +...  4.52 us
    pallas_call x4, Pallas kernels, call(): pl.pallas_call(kernel, out_shape=outs, in_specs=[VMEM] * len(ins) if plac...  4.21 us
    ppermute x2, starting transfers between devices, swap(): lax.ppermute(value, axis, [(i + d, i + 1 - d) for i in starts for d in (0...  3.61 us
  transfers between devices with their start and end apart: 5, of which 2 were waited for; matrix products, arithmetic and copies ran while one was open for 0% of the time, Pallas kernels for 0%

profile of v5, /device:TPU:0, one launch (start us, length us, event | category | flops | bytes accessed | tf_op | source)
XLA Modules:
  0.0 63.5 jit_solution(2344732339622162735)
XLA Ops:
  0.6 2.1 %start_kernel.1 = (f32[3,2,8,1024]{3,2,1,0:T(8,128)S(1)}, f32[3,2,8,1024]{3,2,1,0:T(8,128)S(1)}, f32[3,8,1024]{2,1,0:T(8,128)S(1)}, f32[3,8,1024]{2,1,0:T(8,128)...) custom-call(bf16[4,2,8,1024]{3,2,1,0:T(8,128)(2,1)} %seis_hbm.1, s32[4,2,8]{2,1,0:T(2,128)} %valid_ref.1, ...), custom_call_target="tpu_custom_call" | custom-call | flops 402653184 | bytes 969064 | tf_op jit(solution)/shard_map/start_kernel/pallas_call | solution.py:321
  2.7 4.9 %collective-permute-start = (f32[2,3,8,1024]{3,2,1,0:T(8,128)S(1)}, f32[2,3,8,1024]{3,2,1,0:T(8,128)S(1)}, u32[]{:S(2)}, u32[]{:S(2)}) collective-permute-start(f32[2,3,8,1024]{3,2,1,0:T(8,128)S(1)} %get-tuple-element.16), channel_id=1, source_target_pairs={{0,4},{4,8},{8,12},{12,16},{16,20},{20,24},{24,28},{1,5},{5,9},{9,... | collective-permute-start | bytes 589832 | tf_op jit(solution)/shard_map/ppermute | solution.py:335
  7.6 1.3 %collective-permute-start.1 = (f32[3,8,1024]{2,1,0:T(8,128)S(1)}, f32[3,8,1024]{2,1,0:T(8,128)S(1)}, u32[]{:S(2)}, u32[]{:S(2)}) collective-permute-start(f32[3,8,1024]{2,1,0:T(8,128)S(1)} %get-tuple-element.17), channel_id=1, source_target_pairs={{4,0},{8,4},{12,8},{16,12},{20,16},{24,20},{28,24},{5,1},{9,5},{13... | collective-permute-start | bytes 294920 | tf_op jit(solution)/shard_map/ppermute | solution.py:335
  8.9 1.3 %collective-permute-start.2 = (f32[3,8,1024]{2,1,0:T(8,128)S(1)}, f32[3,8,1024]{2,1,0:T(8,128)S(1)}, u32[]{:S(2)}, u32[]{:S(2)}) collective-permute-start(f32[3,8,1024]{2,1,0:T(8,128)S(1)} %get-tuple-element.20), channel_id=1, source_target_pairs={{4,0},{8,4},{12,8},{16,12},{20,16},{24,20},{28,24},{5,1},{9,5},{13... | collective-permute-start | bytes 294920 | tf_op jit(solution)/shard_map/ppermute | solution.py:335
  10.2 4.5 %collective-permute-done.1.below_ref = f32[3,8,1024]{2,1,0:T(8,128)S(1)} collective-permute-done((f32[3,8,1024]{2,1,0:T(8,128)S(1)}, f32[3,8,1024]{2,1,0:T(8,128)S(1)}, u32[]{:S(2)}, u32[]{:S(2)}) %collective-permute-start.1) | collective-permute-done | bytes 98336 | tf_op jit(solution)/shard_map/ppermute | solution.py:335
  14.7 0.0 collective-permute-done.above_ref
  14.7 0.0 copy-start
  14.7 0.0 copy-start.2
  14.7 0.2 rows_kernel.1
  14.9 0.0 copy-start.1
  14.9 0.7 %collective-permute-start.3 = (f32[18,1024]{1,0:T(8,128)S(1)}, f32[18,1024]{1,0:T(8,128)S(1)}, u32[]{:S(2)}, u32[]{:S(2)}) collective-permute-start(f32[18,1024]{1,0:T(8,128)S(1)} %get-tuple-element.21), channel_id=1, source_target_pairs={{1,2},{2,1},{5,6},{6,5},{9,10},{10,9},{13,14},{14,13},{17,18},{18,... | collective-permute-start | bytes 221192 | tf_op jit(solution)/shard_map/ppermute | solution.py:340
  15.6 0.0 copy-start.3
  15.6 2.9 %collective-permute-start.4 = (f32[18,1024]{1,0:T(8,128)S(1)}, f32[18,1024]{1,0:T(8,128)S(1)}, u32[]{:S(2)}, u32[]{:S(2)}) collective-permute-start(f32[18,1024]{1,0:T(8,128)S(1)} %get-tuple-element.22), channel_id=1, source_target_pairs={{0,1},{1,0},{2,3},{3,2},{4,5},{5,4},{6,7},{7,6},{8,9},{9,8},{10,11... | collective-permute-start | bytes 221192 | tf_op jit(solution)/shard_map/ppermute | solution.py:340
  18.5 0.0 collective-permute-done.2.under_ref
  18.5 0.0 collective-permute-done.3.other_ref
  18.5 0.9 %collective-permute-done.4.pair_ref = f32[18,1024]{1,0:T(8,128)S(1)} collective-permute-done((f32[18,1024]{1,0:T(8,128)S(1)}, f32[18,1024]{1,0:T(8,128)S(1)}, u32[]{:S(2)}, u32[]{:S(2)}) %collective-permute-start.4) | collective-permute-done | bytes 73760 | tf_op jit(solution)/shard_map/ppermute | solution.py:340
  19.5 0.0 copy-done
  19.5 0.0 copy-done.2
  19.5 0.0 copy-done.1
  19.5 0.0 copy-done.3
  19.5 1.0 %image_kernel.1 = (f32[3,2,8,1024]{3,2,1,0:T(8,128)S(1)}, f32[3,2,8,1024]{3,2,1,0:T(8,128)S(1)}, f32[1,128]{1,0:T(1,128)S(1)}) custom-call(f32[3,2,8,1024]{3,2,1,0:T(8,128)S(1)} %get-tuple-element.14.b_ref, f32[3,3,8,1024]{3,2,1,0:T(8,128)S(1)} %get-tuple-element.19.v_ref, f32[3,8,1024]{2,1,0:T(8,128)S(1)} %collective-permute-done.2.under_ref, ...), custom_call_target="tpu_custom_call" | custom-call | flops 268435456 | bytes 1182556 | tf_op jit(solution)/shard_map/image_kernel/pallas_call | solution.py:321
  20.5 42.1 %all-gather.1.gram_ref = f32[32,1,128]{2,1,0:T(1,128)S(1)} all-gather(f32[1,1,128]{2,1,0:T(1,128)S(1)} %bitcast.3), channel_id=2, replica_groups=mesh['inline'=8,'col'=4] {'inline','col'}, dimensions={0}, use_global_device_ids=true | all-gather | bytes 16896 | tf_op jit(solution)/shard_map/all_gather | solution.py:387
  62.6 0.9 %finish_kernel.1 = (f32[3,2,8,1024]{3,2,1,0:T(8,128)}, f32[3,2,8,1024]{3,2,1,0:T(8,128)}) custom-call(f32[32,1,128]{2,1,0:T(1,128)S(1)} %all-gather.1.gram_ref, f32[3,2,8,1024]{3,2,1,0:T(8,128)S(1)} %get-tuple-element.14.b_ref, f32[3,2,8,1024]{3,2,1,0:T(8,128)S(1)} %get-tuple-element.24.one_ref, f32[3,2,8,1024]{3,2,1,0:T(8,128)S(1)} %get-tuple-element.25.two_ref), custom_call_target="tpu_custom_call" | custom-call | flops 393216 | bytes 999424 | tf_op jit(solution)/shard_map/finish_kernel/pallas_call | solution.py:321
Async XLA Ops:
  2.7 12.0 %collective-permute-start = (f32[2,3,8,1024]{3,2,1,0:T(8,128)S(1)}, f32[2,3,8,1024]{3,2,1,0:T(8,128)S(1)}, u32[]{:S(2)}, u32[]{:S(2)}) collective-permute-start(f32[2,3,8,1024]{3,2,1,0:T(8,128)S(1)} %get-tuple-element.16), channel_id=1, source_target_pairs={{0,4},{4,8},{8,12},{12,16},{16,20},{20,24},{24,28},{1,5},{5,9},{9,... | collective-permute-start | bytes 589832 | tf_op jit(solution)/shard_map/ppermute | solution.py:335
  7.6 7.1 %collective-permute-start.1 = (f32[3,8,1024]{2,1,0:T(8,128)S(1)}, f32[3,8,1024]{2,1,0:T(8,128)S(1)}, u32[]{:S(2)}, u32[]{:S(2)}) collective-permute-start(f32[3,8,1024]{2,1,0:T(8,128)S(1)} %get-tuple-element.17), channel_id=1, source_target_pairs={{4,0},{8,4},{12,8},{16,12},{20,16},{24,20},{28,24},{5,1},{9,5},{13... | collective-permute-start | bytes 294920 | tf_op jit(solution)/shard_map/ppermute | solution.py:335
  8.9 9.7 %collective-permute-start.2 = (f32[3,8,1024]{2,1,0:T(8,128)S(1)}, f32[3,8,1024]{2,1,0:T(8,128)S(1)}, u32[]{:S(2)}, u32[]{:S(2)}) collective-permute-start(f32[3,8,1024]{2,1,0:T(8,128)S(1)} %get-tuple-element.20), channel_id=1, source_target_pairs={{4,0},{8,4},{12,8},{16,12},{20,16},{24,20},{28,24},{5,1},{9,5},{13... | collective-permute-start | bytes 294920 | tf_op jit(solution)/shard_map/ppermute | solution.py:335
  14.7 4.8 %copy-start = (f32[4,3,1024]{2,0,1:T(4,128)S(1)}, f32[4,3,1024]{2,0,1:T(4,128)}, u32[]{:S(2)}) copy-start(f32[4,3,1024]{2,0,1:T(4,128)} %param.10) | copy-start | bytes 147460
  14.7 4.8 %copy-start.2 = (f32[4,129]{1,0:T(4,128)S(1)}, f32[4,129]{1,0:T(4,128)}, u32[]{:S(2)}) copy-start(f32[4,129]{1,0:T(4,128)} %taps_ref.1) | copy-start | bytes 6196
  14.9 4.6 %copy-start.1 = (s32[4,2,8]{2,1,0:T(2,128)S(1)}, s32[4,2,8]{2,1,0:T(2,128)}, u32[]{:S(2)}) copy-start(s32[4,2,8]{2,1,0:T(2,128)} %valid_ref.1) | copy-start | bytes 772
  14.9 3.6 %collective-permute-start.3 = (f32[18,1024]{1,0:T(8,128)S(1)}, f32[18,1024]{1,0:T(8,128)S(1)}, u32[]{:S(2)}, u32[]{:S(2)}) collective-permute-start(f32[18,1024]{1,0:T(8,128)S(1)} %get-tuple-element.21), channel_id=1, source_target_pairs={{1,2},{2,1},{5,6},{6,5},{9,10},{10,9},{13,14},{14,13},{17,18},{18,... | collective-permute-start | bytes 221192 | tf_op jit(solution)/shard_map/ppermute | solution.py:340
  15.6 3.9 %copy-start.3 = (f32[2,8]{1,0:T(2,128)S(1)}, f32[2,8]{1,0:T(2,128)}, u32[]{:S(2)}) copy-start(f32[2,8]{1,0:T(2,128)} %prior_ref.1) | copy-start | bytes 196
  15.6 3.9 %collective-permute-start.4 = (f32[18,1024]{1,0:T(8,128)S(1)}, f32[18,1024]{1,0:T(8,128)S(1)}, u32[]{:S(2)}, u32[]{:S(2)}) collective-permute-start(f32[18,1024]{1,0:T(8,128)S(1)} %get-tuple-element.22), channel_id=1, source_target_pairs={{0,1},{1,0},{2,3},{3,2},{4,5},{5,4},{6,7},{7,6},{8,9},{9,8},{10,11... | collective-permute-start | bytes 221192 | tf_op jit(solution)/shard_map/ppermute | solution.py:340

commit v6 on v4

--- a/solution.py
+++ b/solution.py
@@ -154,33 +154,45 @@
 
 
 def start_kernel(
-    seis_hbm, valid_hbm, avo_hbm, taps_hbm, prior_hbm, strength_hbm,
-    b_ref, p_ref, top_b_ref, top_p_ref, bottom_ref, strength_ref,
-    seis_ref, valid_ref, avo_ref, taps_ref, prior_ref, padded, sems,
+    seis_hbm, valid_hbm, avo_hbm, taps_hbm,
+    b_ref, pair_ref, other_ref,
+    seis_ref, valid_ref, avo_ref, taps_ref, padded, sems,
 ):
     copies = copy_in(
         (
             (taps_hbm, taps_ref),
             (valid_hbm, valid_ref),
-            (prior_hbm, prior_ref),
-            (strength_hbm, strength_ref),
             (avo_hbm, avo_ref),
             (seis_hbm, seis_ref),
         ),
         sems,
     )
-    for copy in copies[:4]:
+    for copy in copies[:2]:
         copy.wait()
     fill_taps(taps_ref, padded)
-    contrasts, angles, samples = avo_ref.shape
+    contrasts, angles, _ = avo_ref.shape
     rows = seis_ref.shape[1]
     circs = [circulant(padded, a) for a in range(angles)]
     masks = [trace_columns(valid_ref, a) for a in range(angles)]
-    for copy in copies[4:]:
+    for copy in copies[2:]:
         copy.wait()
-    b = right_side(seis_ref, masks, avo_ref, circs)
-    store_tiles(b_ref, b)
-    store_tiles(p_ref, normal(b, masks, avo_ref, circs))
+    store_tiles(b_ref, right_side(seis_ref, masks, avo_ref, circs))
+    first = starts_pair("inline")
+    for c in range(contrasts):
+        top, bottom = b_ref[c, 0], b_ref[c, rows - 1]
+        pair_ref[c] = jnp.where(first, bottom, top)
+        other_ref[c] = jnp.where(first, top, bottom)
+
+
+def part_kernel(
+    b_ref, valid_ref, avo_ref, taps_ref, prior_ref, strength_ref, p_ref, top_ref, bottom_ref, padded
+):
+    contrasts, rows = b_ref.shape[:2]
+    fill_taps(taps_ref, padded)
+    angles = avo_ref.shape[1]
+    circs = [circulant(padded, a) for a in range(angles)]
+    masks = [trace_columns(valid_ref, a) for a in range(angles)]
+    store_tiles(p_ref, normal(stack_tiles(b_ref), masks, avo_ref, circs))
     weights = [column(prior_ref[r : r + 1, :]) + 4.0 for r in range(rows)]
     for c in range(contrasts):
         strength = strength_ref[:, c : c + 1]
@@ -190,10 +202,19 @@
             south = b_ref[c, r + 1] if r < rows - 1 else None
             around = lateral(here, north, south, None, None)
             p_ref[c, r] = p_ref[c, r] + strength * (weights[r] * here - around)
-        top_b_ref[c] = b_ref[c, 0]
-        top_p_ref[c] = p_ref[c, 0]
-        bottom_ref[0, c] = b_ref[c, rows - 1]
-        bottom_ref[1, c] = p_ref[c, rows - 1]
+        top_ref[c] = p_ref[c, 0]
+        bottom_ref[c] = p_ref[c, rows - 1]
+
+
+def stack_tiles(ref):
+    contrasts, rows, _, samples = ref.shape
+    return [
+        [
+            jnp.concatenate([ref[c, r, :, pl.ds(k, LANES)] for r in range(rows)], axis=0)
+            for k in range(0, samples, LANES)
+        ]
+        for c in range(contrasts)
+    ]
 
 
 def inside(axis):
@@ -202,91 +223,79 @@
     return (place > 0).astype(F32), (place < last).astype(F32)
 
 
-def starts_pair():
-    return lax.axis_index("col") % 2 == 0
-
-
-def rows_kernel(b_ref, p_ref, above_ref, below_ref, strength_ref, v_ref, pair_ref, other_ref):
+def starts_pair(axis):
+    return lax.axis_index(axis) % 2 == 0
+
+
+def rows_kernel(b_ref, p_ref, next_ref, mate_ref, strength_ref, v_ref, pair_ref, other_ref):
     contrasts, rows, traces, _ = b_ref.shape
-    has_above, _ = inside("inline")
-    first_of_pair = starts_pair()
+    first_row, first_col = starts_pair("inline"), starts_pair("col")
     for c in range(contrasts):
         strength = strength_ref[:, c : c + 1]
+        above = jnp.where(first_row, next_ref[c], mate_ref[c])
+        below = jnp.where(first_row, mate_ref[c], next_ref[c])
         own = [p_ref[c, r] for r in range(rows)]
-        own[0] = own[0] - strength * above_ref[0, c]
-        own[-1] = own[-1] - strength * below_ref[c]
-        over = has_above * (above_ref[1, c] - strength * b_ref[c, 0])
-        for r, line in enumerate([over, *own]):
+        own[0] = own[0] - strength * above
+        own[-1] = own[-1] - strength * below
+        for r, line in enumerate(own):
             v_ref[c, r] = line
-        lines = [above_ref[0, c], *[b_ref[c, r] for r in range(rows)], below_ref[c], *own]
+        lines = [above, *[b_ref[c, r] for r in range(rows)], below, *own]
         base = c * len(lines)
         for e, line in enumerate(lines):
             left, right = line[0:1, :], line[traces - 1 : traces, :]
-            pair_ref[base + e : base + e + 1, :] = jnp.where(first_of_pair, right, left)
-            other_ref[base + e : base + e + 1, :] = jnp.where(first_of_pair, left, right)
+            pair_ref[base + e : base + e + 1, :] = jnp.where(first_col, right, left)
+            other_ref[base + e : base + e + 1, :] = jnp.where(first_col, left, right)
 
 
 def image_kernel(
-    b_ref, v_ref, under_ref, other_ref, pair_ref,
+    b_ref, v_ref, over_ref, other_ref, pair_ref,
     valid_ref, avo_ref, taps_ref, prior_ref, strength_ref,
     one_ref, two_ref, gram_ref, padded,
 ):
     contrasts, rows, traces, samples = b_ref.shape
-    angles, n = avo_ref.shape[1], samples // LANES
+    angles = avo_ref.shape[1]
     has_left, has_right = inside("col")
-    _, has_below = inside("inline")
-    first_of_pair = starts_pair()
-    left = jnp.where(first_of_pair, other_ref[...], pair_ref[...])
-    right = jnp.where(first_of_pair, pair_ref[...], other_ref[...])
+    has_above, has_below = inside("inline")
+    first_col = starts_pair("col")
+    left = jnp.where(first_col, other_ref[...], pair_ref[...])
+    right = jnp.where(first_col, pair_ref[...], other_ref[...])
     place = lax.broadcasted_iota(jnp.int32, (traces, samples), 0)
-    first, last = place == 0, place == traces - 1
     ext = rows + 2
-    whole = []
+    stride = ext + rows
+
+    def beside(c, r):
+        edge = c * stride + r
+        west, east = left[edge : edge + 1, :], right[edge : edge + 1, :]
+        return jnp.where(place == 0, west, jnp.where(place == traces - 1, east, 0.0))
+
     for c in range(contrasts):
-        base = c * (ext + rows)
-        lines = []
-        for r in range(ext):
-            edge = base + r
-            missing = jnp.where(
-                first,
-                left[edge : edge + 1, :],
-                jnp.where(last, right[edge : edge + 1, :], 0.0),
-            )
-            if r < ext - 1:
-                line = v_ref[c, r]
-            else:
-                line = has_below * (under_ref[c] - strength_ref[:, c : c + 1] * b_ref[c, rows - 1])
-            lines.append(line - strength_ref[:, c : c + 1] * missing)
-        whole.append(lines)
+        strength = strength_ref[:, c : c + 1]
         for r in range(rows):
-            one_ref[c, r] = lines[r + 1]
+            one_ref[c, r] = v_ref[c, r] - strength * beside(c, r + 1)
     fill_taps(taps_ref, padded)
     circs = [circulant(padded, a) for a in range(angles)]
     masks = [trace_columns(valid_ref, a) for a in range(angles)]
-    field = [
-        [
-            jnp.concatenate([one_ref[c, r, :, pl.ds(k * LANES, LANES)] for r in range(rows)], axis=0)
-            for k in range(n)
-        ]
-        for c in range(contrasts)
-    ]
-    store_tiles(two_ref, normal(field, masks, avo_ref, circs))
+    store_tiles(two_ref, normal(stack_tiles(one_ref), masks, avo_ref, circs))
     weights = [column(prior_ref[r : r + 1, :]) + 4.0 for r in range(rows)]
     sums = [jnp.zeros((traces, LANES), F32) for _ in range(4)]
     for c in range(contrasts):
         strength = strength_ref[:, c : c + 1]
+        over = over_ref[c] - strength * (has_above * b_ref[c, 0] + beside(c, 0))
+        under = -strength * (has_below * b_ref[c, rows - 1] + beside(c, ext - 1))
         for r in range(rows):
-            here = whole[c][r + 1]
-            edge = c * (ext + rows) + ext + r
-            b = b_ref[c, r]
+            here, b = one_ref[c, r], b_ref[c, r]
+            edge = c * stride + ext + r
             west = has_left * (left[edge : edge + 1, :] - strength * b[0:1, :])
             east = has_right * (
                 right[edge : edge + 1, :] - strength * b[traces - 1 : traces, :]
             )
-            around = lateral(here, whole[c][r], whole[c][r + 2], west, east)
+            north = one_ref[c, r - 1] if r else over
+            south = one_ref[c, r + 1] if r < rows - 1 else None
+            around = lateral(here, north, south, west, east)
             two = two_ref[c, r] + strength * (weights[r] * here - around)
-            two_ref[c, r] = two
-            for q, product in enumerate((b * b, b * here, here * here, here * two)):
+            twice = two if r else two - strength * over
+            two_ref[c, r] = two if r < rows - 1 else two - strength * under
+            for q, product in enumerate((b * b, b * here, here * here, here * twice)):
                 tiles = [product[:, k : k + LANES] for k in range(0, samples, LANES)]
                 sums[q] = sums[q] + functools.reduce(jnp.add, tiles)
     lane = lax.broadcasted_iota(jnp.int32, (1, LANES), 1)
@@ -297,7 +306,9 @@
     gram_ref[...] = jnp.broadcast_to(packed[None], gram_ref.shape)
 
 
-def finish_kernel(gram_ref, b_ref, one_ref, two_ref, solution_ref, residual_ref):
+def finish_kernel(
+    gram_ref, b_ref, one_ref, two_ref, under_ref, strength_ref, solution_ref, residual_ref
+):
     sums = jnp.sum(gram_ref[...], axis=0)
     g00, g01, g11, g12 = (sums[:, q : q + 1] for q in range(4))
     first = g00 / g01
@@ -305,9 +316,12 @@
     second = (ratio - 1.0) * g01 / (first * g12 - ratio * g11)
     near = first + second * ratio
     far = first * second
+    rows = b_ref.shape[1]
     for c in range(b_ref.shape[0]):
-        for r in range(b_ref.shape[1]):
+        for r in range(rows):
             b, one, two = b_ref[c, r], one_ref[c, r], two_ref[c, r]
+            if r == rows - 1:
+                two = two - strength_ref[:, c : c + 1] * under_ref[c]
             solution_ref[c, r] = near * b - far * one
             residual_ref[c, r] = b - near * one + far * two
 
@@ -344,6 +358,7 @@
     angles, rows, traces, samples = seismic.shape
     contrasts = avo_coeffs.shape[1]
     avo_coeffs = jnp.swapaxes(avo_coeffs, 0, 1)
+    strength = lateral_strength.reshape(1, -1)
     shape = lambda *dims: jax.ShapeDtypeStruct(dims, F32)
     field = shape(contrasts, rows, traces, samples)
     row = shape(contrasts, traces, samples)
@@ -351,41 +366,49 @@
     padded = pltpu.VMEM((8, 2 * LANES), F32)
     work = 2 * angles * rows * traces * samples * 256 * 4
 
-    placed = (
-        seismic, validity, avo_coeffs, wavelets, prior_weight, lateral_strength.reshape(1, -1)
-    )
-    b, part, top_b, top_p, bottom, strength = call(
+    placed = (seismic, validity, avo_coeffs, wavelets)
+    b, pair, other = call(
         start_kernel,
-        (field, field, row, row, shape(2, *row.shape), shape(1, contrasts)),
+        (field, row, row),
         [pltpu.with_memory_space_constraint(x, pltpu.HBM) for x in placed],
-        3 * work,
-        [*[pltpu.VMEM(x.shape, x.dtype) for x in placed[:-1]], padded, pltpu.SemaphoreType.DMA((6,))],
-        [HBM] * 6,
-    )
-    above = shift("inline", bottom, 1)
-    below = shift("inline", top_b, -1)
-    under = shift("inline", top_p, -1)
-    ext, pair, other = call(
+        work,
+        [*[pltpu.VMEM(x.shape, x.dtype) for x in placed], padded, pltpu.SemaphoreType.DMA((4,))],
+        [HBM] * 4,
+    )
+    other = swap("inline", other, 1)
+    pair = swap("inline", pair, 0)
+    part, top, bottom = call(
+        part_kernel,
+        (field, row, row),
+        (b, validity, avo_coeffs, wavelets, prior_weight, strength),
+        2 * work,
+        [padded],
+    )
+    over = shift("inline", bottom, 1)
+    image, pair, other = call(
         rows_kernel,
-        (shape(contrasts, rows + 1, traces, samples), side, side),
-        (b, part, above, below, strength),
+        (field, side, side),
+        (b, part, other, pair, strength),
         4 * field.size,
     )
     other = swap("col", other, 1)
     pair = swap("col", pair, 0)
+    top, image = lax.optimization_barrier((top, image))
+    under = shift("inline", top, -1)
     axes = ("inline", "col")
     one, two, gram = call(
         image_kernel,
         (field, field, shape(lax.axis_size(axes), 1, LANES)),
         (
-            b, ext, under, other, pair,
+            b, image, over, other, pair,
             validity, avo_coeffs, wavelets, prior_weight, strength,
         ),
         2 * work,
         [padded],
     )
     gram = lax.all_to_all(gram, axes, 0, 0)
-    return tuple(call(finish_kernel, (field, field), (gram, b, one, two), 8 * field.size))
+    last = (gram, b, one, two, under, strength)
+    return tuple(call(finish_kernel, (field, field), last, 8 * field.size))
 
 
 def solution(mesh):

time: 36.1 us -> 34.1 us (0.945)
  blocking collectives: 14.4 us -> 0 us
  starting transfers between devices: 11 us -> 20.2 us
  waiting for transfers between devices: 5.47 us -> 7.19 us
  Pallas kernels: 4.22 us -> 5.01 us
  local copies, waits for them, and re-layouts: 0.02 us -> 0.69 us
    all_to_all x1 -> x0, blocking collectives: 14.4 us -> none  [shards(): gram = lax.all_to_all(gram, axes, 0, 0)]
    all_to_all x0 -> x1, waiting for transfers between devices: none -> 7.06 us  [shards(): gram = lax.all_to_all(gram, axes, 0, 0)]
    all_to_all x0 -> x1, starting transfers between devices: none -> 6.95 us  [shards(): gram = lax.all_to_all(gram, axes, 0, 0)]
    ppermute x2 -> x4, starting transfers between devices: 3.61 us -> 10.1 us  [swap(): lax.ppermute(value, axis, [(i + d, i + 1 - d) for i in starts for d in (0...]
    ppermute x3 -> x2, waiting for transfers between devices: 4.52 us -> 0.01 us  [shift(): lax.ppermute(value, axis, [(i, i + step) for i in range(size) if 0 <= i +...]
    ppermute x3 -> x2, starting transfers between devices: 7.44 us -> 3.2 us  [shift(): lax.ppermute(value, axis, [(i, i + step) for i in range(size) if 0 <= i +...]
    ppermute x2 -> x4, waiting for transfers between devices: 0.94 us -> 0.12 us  [swap(): lax.ppermute(value, axis, [(i + d, i + 1 - d) for i in starts for d in (0...]
    pallas_call x4 -> x5, Pallas kernels: 4.22 us -> 5.01 us  [call(): pl.pallas_call(kernel, out_shape=outs, in_specs=[VMEM] * len(ins) if plac...]
  transfers between devices with their start and end apart: 5 -> 7, of which waited for: 2 -> 2; matrix products, arithmetic and copies ran while one was open for 0% -> 0% of each run, Pallas kernels for 1% -> 8%
where the time goes in v6:
time: 34.1 us; the launch traced here: 33.9 us
  starting transfers between devices  20.2 us (59%)
  waiting for transfers between devices  7.19 us (21%)
  Pallas kernels  5.01 us (15%)
  between operations  0.77 us (2%)
  local copies, waits for them, and re-layouts  0.69 us (2%)
    ppermute x4, starting transfers between devices, swap(): lax.ppermute(value, axis, [(i + d, i + 1 - d) for i in starts for d in (0...  10.1 us
    all_to_all x1, waiting for transfers between devices, shards(): gram = lax.all_to_all(gram, axes, 0, 0)  7.06 us
    all_to_all x1, starting transfers between devices, shards(): gram = lax.all_to_all(gram, axes, 0, 0)  6.95 us
    pallas_call x5, Pallas kernels, call(): pl.pallas_call(kernel, out_shape=outs, in_specs=[VMEM] * len(ins) if plac...  5.01 us
    ppermute x2, starting transfers between devices, shift(): lax.ppermute(value, axis, [(i, i + step) for i in range(size) if 0 <= i +...  3.2 us
    unnamed x10, local copies, waits for them, and re-layouts  0.69 us
  transfers between devices with their start and end apart: 7, of which 2 were waited for; matrix products, arithmetic and copies ran while one was open for 0% of the time, Pallas kernels for 8%

profile of v6, /device:TPU:0, one launch (start us, length us, event | category | flops | bytes accessed | tf_op | source)
XLA Modules:
  0.0 33.9 jit_solution(6399928541289946282)
XLA Ops:
  0.6 0.0 copy-start.1
  0.6 0.0 copy-start.3
  0.6 1.4 %start_kernel.1 = (f32[3,2,8,1024]{3,2,1,0:T(8,128)S(1)}, f32[3,8,1024]{2,1,0:T(8,128)S(1)}, f32[3,8,1024]{2,1,0:T(8,128)S(1)}) custom-call(bf16[4,2,8,1024]{3,2,1,0:T(8,128)(2,1)} %seis_hbm.1, s32[4,2,8]{2,1,0:T(2,128)} %valid_ref.3, f32[3,4,1024]{2,1,0:T(4,128)} %bitcast.6, f32[4,129]{1,0:T(4,128)} %taps_ref.3), custom_call_target="tpu_custom_call" | custom-call | flops 134217728 | bytes 575760 | tf_op jit(solution)/shard_map/start_kernel/pallas_call | solution.py:335
  2.1 0.0 copy-start.2
  2.1 0.7 %collective-permute-start = (f32[3,8,1024]{2,1,0:T(8,128)S(1)}, f32[3,8,1024]{2,1,0:T(8,128)S(1)}, u32[]{:S(2)}, u32[]{:S(2)}) collective-permute-start(f32[3,8,1024]{2,1,0:T(8,128)S(1)} %get-tuple-element.19), channel_id=1, source_target_pairs={{4,8},{8,4},{12,16},{16,12},{20,24},{24,20},{5,9},{9,5},{13,17},{1... | collective-permute-start | bytes 294920 | tf_op jit(solution)/shard_map/ppermute | solution.py:354
  2.8 5.8 %collective-permute-start.1 = (f32[3,8,1024]{2,1,0:T(8,128)S(1)}, f32[3,8,1024]{2,1,0:T(8,128)S(1)}, u32[]{:S(2)}, u32[]{:S(2)}) collective-permute-start(f32[3,8,1024]{2,1,0:T(8,128)S(1)} %get-tuple-element.20), channel_id=1, source_target_pairs={{0,4},{4,0},{8,12},{12,8},{16,20},{20,16},{24,28},{28,24},{1,5},{5... | collective-permute-start | bytes 294920 | tf_op jit(solution)/shard_map/ppermute | solution.py:354
  8.6 0.6 %copy-done = f32[3]{0:T(128)S(1)} copy-done((f32[3]{0:T(128)S(1)}, f32[3]{0:T(128)}, u32[]{:S(2)}) %copy-start) | copy-done | bytes 36
  9.2 0.0 copy-done.4
  9.3 0.8 %part_kernel.1 = (f32[3,2,8,1024]{3,2,1,0:T(8,128)S(1)}, f32[3,8,1024]{2,1,0:T(8,128)S(1)}, f32[3,8,1024]{2,1,0:T(8,128)S(1)}) custom-call(f32[3,2,8,1024]{3,2,1,0:T(8,128)S(1)} %get-tuple-element.16.b_ref, s32[4,2,8]{2,1,0:T(2,128)S(1)} %copy-done.2, f32[3,4,1024]{2,1,0:T(4,128)S(1)} %bitcast.7, f32[4,129]{1,0:T(4,128)S(1)} %copy-done.3, ...), custom_call_target="tpu_custom_call" | custom-call | flops 268435456 | bytes 641372 | tf_op jit(solution)/shard_map/part_kernel/pallas_call | solution.py:335
  10.1 1.9 %collective-permute-start.2 = (f32[3,8,1024]{2,1,0:T(8,128)S(1)}, f32[3,8,1024]{2,1,0:T(8,128)S(1)}, u32[]{:S(2)}, u32[]{:S(2)}) collective-permute-start(f32[3,8,1024]{2,1,0:T(8,128)S(1)} %get-tuple-element.23), channel_id=1, source_target_pairs={{0,4},{4,8},{8,12},{12,16},{16,20},{20,24},{24,28},{1,5},{5,9},{9,... | collective-permute-start | bytes 294920 | tf_op jit(solution)/shard_map/ppermute | solution.py:349
  12.0 0.0 collective-permute-done.next_ref
  12.0 0.1 collective-permute-done.1.mate_ref
  12.1 0.2 rows_kernel.1
  12.3 0.7 %collective-permute-start.3 = (f32[18,1024]{1,0:T(8,128)S(1)}, f32[18,1024]{1,0:T(8,128)S(1)}, u32[]{:S(2)}, u32[]{:S(2)}) collective-permute-start(f32[18,1024]{1,0:T(8,128)S(1)} %get-tuple-element.24), channel_id=1, source_target_pairs={{1,2},{2,1},{5,6},{6,5},{9,10},{10,9},{13,14},{14,13},{17,18},{18,... | collective-permute-start | bytes 221192 | tf_op jit(solution)/shard_map/ppermute | solution.py:354
  13.0 2.9 %collective-permute-start.4 = (f32[18,1024]{1,0:T(8,128)S(1)}, f32[18,1024]{1,0:T(8,128)S(1)}, u32[]{:S(2)}, u32[]{:S(2)}) collective-permute-start(f32[18,1024]{1,0:T(8,128)S(1)} %get-tuple-element.25), channel_id=1, source_target_pairs={{0,1},{1,0},{2,3},{3,2},{4,5},{5,4},{6,7},{7,6},{8,9},{9,8},{10,11... | collective-permute-start | bytes 221192 | tf_op jit(solution)/shard_map/ppermute | solution.py:354
  15.9 1.3 %collective-permute-start.5 = (f32[3,8,1024]{2,1,0:T(8,128)S(1)}, f32[3,8,1024]{2,1,0:T(8,128)S(1)}, u32[]{:S(2)}, u32[]{:S(2)}) collective-permute-start(f32[3,8,1024]{2,1,0:T(8,128)S(1)} %get-tuple-element.29), channel_id=1, source_target_pairs={{4,0},{8,4},{12,8},{16,12},{20,16},{24,20},{28,24},{5,1},{9,5},{13... | collective-permute-start | bytes 294920 | tf_op jit(solution)/shard_map/ppermute | solution.py:349
  17.2 0.0 collective-permute-done.2.over_ref
  17.2 0.0 collective-permute-done.3.other_ref
  17.2 0.0 collective-permute-done.4.pair_ref
  17.2 1.6 %image_kernel.1 = (f32[3,2,8,1024]{3,2,1,0:T(8,128)S(1)}, f32[3,2,8,1024]{3,2,1,0:T(8,128)S(1)}, f32[32,1,128]{2,1,0:T(1,128)}) custom-call(f32[3,2,8,1024]{3,2,1,0:T(8,128)S(1)} %get-tuple-element.16.b_ref, f32[3,2,8,1024]{3,2,1,0:T(8,128)S(1)} %get-tuple-element.22.v_ref, f32[3,8,1024]{2,1,0:T(8,128)S(1)} %collective-permute-done.2.over_ref, ...), custom_call_target="tpu_custom_call" | custom-call | flops 268435456 | bytes 1100124 | tf_op jit(solution)/shard_map/image_kernel/pallas_call | solution.py:335
  18.9 6.9 %all-to-all-start = ((f32[32,1,128]{2,1,0:T(1,128)}), f32[32,1,128]{2,1,0:T(1,128)S(1)}, u32[]{:S(2)}, u32[]{:S(2)}) async-start(f32[32,1,128]{2,1,0:T(1,128)} %get-tuple-element.26), calls=%async_computation | async-start | bytes 32768 | tf_op jit(solution)/shard_map/all_to_all | solution.py:409
  25.8 0.0 collective-permute-done.5.under_ref
  25.9 7.1 %all-to-all-done.gram_ref = f32[32,1,128]{2,1,0:T(1,128)S(1)} async-done(((f32[32,1,128]{2,1,0:T(1,128)}), f32[32,1,128]{2,1,0:T(1,128)S(1)}, u32[]{:S(2)}, u32[]{:S(2)}) %all-to-all-start) | async-done | bytes 16416 | tf_op jit(solution)/shard_map/all_to_all | solution.py:409
  32.9 1.0 %finish_kernel.1 = (f32[3,2,8,1024]{3,2,1,0:T(8,128)}, f32[3,2,8,1024]{3,2,1,0:T(8,128)}) custom-call(f32[32,1,128]{2,1,0:T(1,128)S(1)} %all-to-all-done.gram_ref, f32[3,2,8,1024]{3,2,1,0:T(8,128)S(1)} %get-tuple-element.16.b_ref, f32[3,2,8,1024]{3,2,1,0:T(8,128)S(1)} %get-tuple-element.27.one_ref, f32[3,2,8,1024]{3,2,1,0:T(8,128)S(1)} %get-tuple-element.28.two_ref, ...), custom_call_target="tpu_custom_call" | custom-call | flops 393216 | bytes 1097740 | tf_op jit(solution)/shard_map/finish_kernel/pallas_call | solution.py:335
  (5 shorter events, 0.0 us)
Async XLA Ops:
  0.6 7.9 %copy-start.1 = (f32[4,3,1024]{2,0,1:T(4,128)S(1)}, f32[4,3,1024]{2,0,1:T(4,128)}, u32[]{:S(2)}) copy-start(f32[4,3,1024]{2,0,1:T(4,128)} %param.10) | copy-start | bytes 147460
  0.6 7.9 %copy-start.3 = (f32[4,129]{1,0:T(4,128)S(1)}, f32[4,129]{1,0:T(4,128)}, u32[]{:S(2)}) copy-start(f32[4,129]{1,0:T(4,128)} %taps_ref.3) | copy-start | bytes 6196
  2.1 6.5 %copy-start.2 = (s32[4,2,8]{2,1,0:T(2,128)S(1)}, s32[4,2,8]{2,1,0:T(2,128)}, u32[]{:S(2)}) copy-start(s32[4,2,8]{2,1,0:T(2,128)} %valid_ref.3) | copy-start | bytes 772
  2.1 9.9 %collective-permute-start = (f32[3,8,1024]{2,1,0:T(8,128)S(1)}, f32[3,8,1024]{2,1,0:T(8,128)S(1)}, u32[]{:S(2)}, u32[]{:S(2)}) collective-permute-start(f32[3,8,1024]{2,1,0:T(8,128)S(1)} %get-tuple-element.19), channel_id=1, source_target_pairs={{4,8},{8,4},{12,16},{16,12},{20,24},{24,20},{5,9},{9,5},{13,17},{1... | collective-permute-start | bytes 294920 | tf_op jit(solution)/shard_map/ppermute | solution.py:354
  2.8 9.3 %collective-permute-start.1 = (f32[3,8,1024]{2,1,0:T(8,128)S(1)}, f32[3,8,1024]{2,1,0:T(8,128)S(1)}, u32[]{:S(2)}, u32[]{:S(2)}) collective-permute-start(f32[3,8,1024]{2,1,0:T(8,128)S(1)} %get-tuple-element.20), channel_id=1, source_target_pairs={{0,4},{4,0},{8,12},{12,8},{16,20},{20,16},{24,28},{28,24},{1,5},{5... | collective-permute-start | bytes 294920 | tf_op jit(solution)/shard_map/ppermute | solution.py:354
  8.6 0.7 %copy-start = (f32[3]{0:T(128)S(1)}, f32[3]{0:T(128)}, u32[]{:S(2)}) copy-start(f32[3]{0:T(128)} %param.9) | copy-start | bytes 40
  8.6 0.7 %copy-start.4 = (f32[2,8]{1,0:T(2,128)S(1)}, f32[2,8]{1,0:T(2,128)}, u32[]{:S(2)}) copy-start(f32[2,8]{1,0:T(2,128)} %prior_ref.3) | copy-start | bytes 196
  10.1 7.1 %collective-permute-start.2 = (f32[3,8,1024]{2,1,0:T(8,128)S(1)}, f32[3,8,1024]{2,1,0:T(8,128)S(1)}, u32[]{:S(2)}, u32[]{:S(2)}) collective-permute-start(f32[3,8,1024]{2,1,0:T(8,128)S(1)} %get-tuple-element.23), channel_id=1, source_target_pairs={{0,4},{4,8},{8,12},{12,16},{16,20},{20,24},{24,28},{1,5},{5,9},{9,... | collective-permute-start | bytes 294920 | tf_op jit(solution)/shard_map/ppermute | solution.py:349
  12.3 4.9 %collective-permute-start.3 = (f32[18,1024]{1,0:T(8,128)S(1)}, f32[18,1024]{1,0:T(8,128)S(1)}, u32[]{:S(2)}, u32[]{:S(2)}) collective-permute-start(f32[18,1024]{1,0:T(8,128)S(1)} %get-tuple-element.24), channel_id=1, source_target_pairs={{1,2},{2,1},{5,6},{6,5},{9,10},{10,9},{13,14},{14,13},{17,18},{18,... | collective-permute-start | bytes 221192 | tf_op jit(solution)/shard_map/ppermute | solution.py:354
  13.0 4.3 %collective-permute-start.4 = (f32[18,1024]{1,0:T(8,128)S(1)}, f32[18,1024]{1,0:T(8,128)S(1)}, u32[]{:S(2)}, u32[]{:S(2)}) collective-permute-start(f32[18,1024]{1,0:T(8,128)S(1)} %get-tuple-element.25), channel_id=1, source_target_pairs={{0,1},{1,0},{2,3},{3,2},{4,5},{5,4},{6,7},{7,6},{8,9},{9,8},{10,11... | collective-permute-start | bytes 221192 | tf_op jit(solution)/shard_map/ppermute | solution.py:354
  15.9 9.9 %collective-permute-start.5 = (f32[3,8,1024]{2,1,0:T(8,128)S(1)}, f32[3,8,1024]{2,1,0:T(8,128)S(1)}, u32[]{:S(2)}, u32[]{:S(2)}) collective-permute-start(f32[3,8,1024]{2,1,0:T(8,128)S(1)} %get-tuple-element.29), channel_id=1, source_target_pairs={{4,0},{8,4},{12,8},{16,12},{20,16},{24,20},{28,24},{5,1},{9,5},{13... | collective-permute-start | bytes 294920 | tf_op jit(solution)/shard_map/ppermute | solution.py:349
  18.9 14.0 %all-to-all-start = ((f32[32,1,128]{2,1,0:T(1,128)}), f32[32,1,128]{2,1,0:T(1,128)S(1)}, u32[]{:S(2)}, u32[]{:S(2)}) async-start(f32[32,1,128]{2,1,0:T(1,128)} %get-tuple-element.26), calls=%async_computation | async-start | bytes 32768 | tf_op jit(solution)/shard_map/all_to_all | solution.py:409

commit v7 on v6

--- a/solution.py
+++ b/solution.py
@@ -154,9 +154,9 @@
 
 
 def start_kernel(
-    seis_hbm, valid_hbm, avo_hbm, taps_hbm,
-    b_ref, pair_ref, other_ref,
-    seis_ref, valid_ref, avo_ref, taps_ref, padded, sems,
+    seis_hbm, valid_hbm, avo_hbm, taps_hbm, prior_hbm, strength_hbm,
+    b_ref, pair_ref, other_ref, valid_ref, avo_ref, taps_ref, prior_ref, strength_ref,
+    seis_ref, padded, sems,
 ):
     copies = copy_in(
         (
@@ -164,6 +164,8 @@
             (valid_hbm, valid_ref),
             (avo_hbm, avo_ref),
             (seis_hbm, seis_ref),
+            (prior_hbm, prior_ref),
+            (strength_hbm, strength_ref),
         ),
         sems,
     )
@@ -307,7 +309,9 @@
 
 
 def finish_kernel(
-    gram_ref, b_ref, one_ref, two_ref, under_ref, strength_ref, solution_ref, residual_ref
+    gram_ref, b_ref, one_ref, two_ref, under_ref, strength_ref,
+    solution_hbm, residual_hbm,
+    solution_ref, residual_ref, sems,
 ):
     sums = jnp.sum(gram_ref[...], axis=0)
     g00, g01, g11, g12 = (sums[:, q : q + 1] for q in range(4))
@@ -317,6 +321,7 @@
     near = first + second * ratio
     far = first * second
     rows = b_ref.shape[1]
+    copies = []
     for c in range(b_ref.shape[0]):
         for r in range(rows):
             b, one, two = b_ref[c, r], one_ref[c, r], two_ref[c, r]
@@ -324,19 +329,24 @@
                 two = two - strength_ref[:, c : c + 1] * under_ref[c]
             solution_ref[c, r] = near * b - far * one
             residual_ref[c, r] = b - near * one + far * two
+        for here, there in ((solution_ref, solution_hbm), (residual_ref, residual_hbm)):
+            copies.append(pltpu.make_async_copy(here.at[c], there.at[c], sems.at[len(copies)]))
+            copies[-1].start()
+    for copy in copies:
+        copy.wait()
 
 
 VMEM = pl.BlockSpec(memory_space=pltpu.VMEM)
 HBM = pl.BlockSpec(memory_space=pltpu.HBM)
 
 
-def call(kernel, outs, ins, flops, scratch=(), places=None):
+def call(kernel, outs, ins, flops, scratch=(), places=None, to=VMEM):
     moved = sum(x.size * x.dtype.itemsize for x in (*ins, *outs))
     return pl.pallas_call(
         kernel,
         out_shape=outs,
         in_specs=[VMEM] * len(ins) if places is None else places,
-        out_specs=jax.tree.map(lambda _: VMEM, outs),
+        out_specs=jax.tree.map(lambda _: to, outs),
         scratch_shapes=list(scratch),
         compiler_params=pltpu.CompilerParams(vmem_limit_bytes=24 * 1024 * 1024),
         cost_estimate=pl.CostEstimate(flops=flops, bytes_accessed=moved, transcendentals=0),
@@ -358,7 +368,6 @@
     angles, rows, traces, samples = seismic.shape
     contrasts = avo_coeffs.shape[1]
     avo_coeffs = jnp.swapaxes(avo_coeffs, 0, 1)
-    strength = lateral_strength.reshape(1, -1)
     shape = lambda *dims: jax.ShapeDtypeStruct(dims, F32)
     field = shape(contrasts, rows, traces, samples)
     row = shape(contrasts, traces, samples)
@@ -366,21 +375,22 @@
     padded = pltpu.VMEM((8, 2 * LANES), F32)
     work = 2 * angles * rows * traces * samples * 256 * 4
 
-    placed = (seismic, validity, avo_coeffs, wavelets)
-    b, pair, other = call(
+    given = (seismic, validity, avo_coeffs, wavelets, prior_weight, lateral_strength.reshape(1, -1))
+    b, pair, other, *kept = call(
         start_kernel,
-        (field, row, row),
-        [pltpu.with_memory_space_constraint(x, pltpu.HBM) for x in placed],
+        (field, row, row, *[jax.ShapeDtypeStruct(x.shape, x.dtype) for x in given[1:]]),
+        [pltpu.with_memory_space_constraint(x, pltpu.HBM) for x in given],
         work,
-        [*[pltpu.VMEM(x.shape, x.dtype) for x in placed], padded, pltpu.SemaphoreType.DMA((4,))],
-        [HBM] * 4,
-    )
+        [pltpu.VMEM(seismic.shape, seismic.dtype), padded, pltpu.SemaphoreType.DMA((6,))],
+        [HBM] * 6,
+    )
+    strength = kept[-1]
     other = swap("inline", other, 1)
     pair = swap("inline", pair, 0)
     part, top, bottom = call(
         part_kernel,
         (field, row, row),
-        (b, validity, avo_coeffs, wavelets, prior_weight, strength),
+        (b, *kept),
         2 * work,
         [padded],
     )
@@ -399,16 +409,22 @@
     one, two, gram = call(
         image_kernel,
         (field, field, shape(lax.axis_size(axes), 1, LANES)),
-        (
-            b, image, over, other, pair,
-            validity, avo_coeffs, wavelets, prior_weight, strength,
-        ),
+        (b, image, over, other, pair, *kept),
         2 * work,
         [padded],
     )
+    gram, under = lax.optimization_barrier((gram, under))
     gram = lax.all_to_all(gram, axes, 0, 0)
-    last = (gram, b, one, two, under, strength)
-    return tuple(call(finish_kernel, (field, field), last, 8 * field.size))
+    return tuple(
+        call(
+            finish_kernel,
+            (field, field),
+            (gram, b, one, two, under, strength),
+            8 * field.size,
+            [*[pltpu.VMEM(field.shape, F32)] * 2, pltpu.SemaphoreType.DMA((2 * contrasts,))],
+            to=HBM,
+        )
+    )
 
 
 def solution(mesh):

time: 34.1 us -> 36.5 us (1.070)
  blocking collectives: 0 us -> 12.1 us
  starting transfers between devices: 20.2 us -> 13.3 us
  waiting for transfers between devices: 7.19 us -> 5.77 us
  local copies, waits for them, and re-layouts: 0.69 us -> 0 us
  Pallas kernels: 5.01 us -> 4.45 us
    all_to_all x0 -> x1, blocking collectives: none -> 12.1 us  [shards(): gram = lax.all_to_all(gram, axes, 0, 0)]
    all_to_all x1 -> x0, waiting for transfers between devices: 7.06 us -> none  [shards(): gram = lax.all_to_all(gram, axes, 0, 0)]
    all_to_all x1 -> x0, starting transfers between devices: 6.95 us -> none  [shards(): gram = lax.all_to_all(gram, axes, 0, 0)]
    ppermute x2, waiting for transfers between devices: 0.01 us -> 4.99 us  [shift(): lax.ppermute(value, axis, [(i, i + step) for i in range(size) if 0 <= i +...]
    unnamed x10 -> x0, local copies, waits for them, and re-layouts: 0.69 us -> none
    ppermute x4, waiting for transfers between devices: 0.12 us -> 0.79 us  [swap(): lax.ppermute(value, axis, [(i + d, i + 1 - d) for i in starts for d in (0...]
    pallas_call x5, Pallas kernels: 5.01 us -> 4.45 us  [call(): pl.pallas_call(kernel, out_shape=outs, in_specs=[VMEM] * len(ins) if plac...]
  transfers between devices with their start and end apart: 7 -> 6, of which waited for: 2 -> 2; matrix products, arithmetic and copies ran while one was open for 0% -> 0% of each run, Pallas kernels for 8% -> 6%
where the time goes in v7:
time: 36.5 us; the launch traced here: 36.3 us
  starting transfers between devices  13.3 us (36%)
  blocking collectives  12.1 us (33%)
  waiting for transfers between devices  5.77 us (16%)
  Pallas kernels  4.45 us (12%)
  between operations  0.72 us (2%)
    all_to_all x1, blocking collectives, shards(): gram = lax.all_to_all(gram, axes, 0, 0)  12.1 us
    ppermute x4, starting transfers between devices, swap(): lax.ppermute(value, axis, [(i + d, i + 1 - d) for i in starts for d in (0...  10.1 us
    ppermute x2, waiting for transfers between devices, shift(): lax.ppermute(value, axis, [(i, i + step) for i in range(size) if 0 <= i +...  4.99 us
    pallas_call x5, Pallas kernels, call(): pl.pallas_call(kernel, out_shape=outs, in_specs=[VMEM] * len(ins) if plac...  4.45 us
    ppermute x2, starting transfers between devices, shift(): lax.ppermute(value, axis, [(i, i + step) for i in range(size) if 0 <= i +...  3.21 us
    ppermute x4, waiting for transfers between devices, swap(): lax.ppermute(value, axis, [(i + d, i + 1 - d) for i in starts for d in (0...  0.79 us
  transfers between devices with their start and end apart: 6, of which 2 were waited for; matrix products, arithmetic and copies ran while one was open for 0% of the time, Pallas kernels for 6%

profile of v7, /device:TPU:0, one launch (start us, length us, event | category | flops | bytes accessed | tf_op | source)
XLA Modules:
  0.0 36.3 jit_solution(14222340923909071920)
XLA Ops:
  0.6 1.4 %start_kernel.1 = (f32[3,2,8,1024]{3,2,1,0:T(8,128)S(1)}, f32[3,8,1024]{2,1,0:T(8,128)S(1)}, f32[3,8,1024]{2,1,0:T(8,128)S(1)}, s32[4,2,8]{2,1,0:T(2,128)S(1)}, ...) custom-call(bf16[4,2,8,1024]{3,2,1,0:T(8,128)(2,1)} %seis_hbm.1, ...), custom_call_target="tpu_custom_call" | custom-call | flops 134217728 | bytes 627384 | tf_op jit(solution)/shard_map/start_kernel/pallas_call | solution.py:345
  2.1 0.7 %collective-permute-start = (f32[3,8,1024]{2,1,0:T(8,128)S(1)}, f32[3,8,1024]{2,1,0:T(8,128)S(1)}, u32[]{:S(2)}, u32[]{:S(2)}) collective-permute-start(f32[3,8,1024]{2,1,0:T(8,128)S(1)} %get-tuple-element.31), channel_id=1, source_target_pairs={{4,8},{8,4},{12,16},{16,12},{20,24},{24,20},{5,9},{9,5},{13,17},{1... | collective-permute-start | bytes 294920 | tf_op jit(solution)/shard_map/ppermute | solution.py:364
  2.7 5.8 %collective-permute-start.1 = (f32[3,8,1024]{2,1,0:T(8,128)S(1)}, f32[3,8,1024]{2,1,0:T(8,128)S(1)}, u32[]{:S(2)}, u32[]{:S(2)}) collective-permute-start(f32[3,8,1024]{2,1,0:T(8,128)S(1)} %get-tuple-element.32), channel_id=1, source_target_pairs={{0,4},{4,0},{8,12},{12,8},{16,20},{20,16},{24,28},{28,24},{1,5},{5... | collective-permute-start | bytes 294920 | tf_op jit(solution)/shard_map/ppermute | solution.py:364
  8.5 0.8 %part_kernel.1 = (f32[3,2,8,1024]{3,2,1,0:T(8,128)S(1)}, f32[3,8,1024]{2,1,0:T(8,128)S(1)}, f32[3,8,1024]{2,1,0:T(8,128)S(1)}) custom-call(f32[3,2,8,1024]{3,2,1,0:T(8,128)S(1)} %get-tuple-element.23.b_ref, s32[4,2,8]{2,1,0:T(2,128)S(1)} %get-tuple-element.24.valid_ref, f32[3,4,1024]{2,1,0:T(4,128)S(1)} %get-tuple-element.25.avo_ref, ...), custom_call_target="tpu_custom_call" | custom-call | flops 268435456 | bytes 641372 | tf_op jit(solution)/shard_map/part_kernel/pallas_call | solution.py:345
  9.4 1.9 %collective-permute-start.2 = (f32[3,8,1024]{2,1,0:T(8,128)S(1)}, f32[3,8,1024]{2,1,0:T(8,128)S(1)}, u32[]{:S(2)}, u32[]{:S(2)}) collective-permute-start(f32[3,8,1024]{2,1,0:T(8,128)S(1)} %get-tuple-element.35), channel_id=1, source_target_pairs={{0,4},{4,8},{8,12},{12,16},{16,20},{20,24},{24,28},{1,5},{5,9},{9,... | collective-permute-start | bytes 294920 | tf_op jit(solution)/shard_map/ppermute | solution.py:359
  11.3 0.0 collective-permute-done.next_ref
  11.3 0.8 %collective-permute-done.1.mate_ref = f32[3,8,1024]{2,1,0:T(8,128)S(1)} collective-permute-done((f32[3,8,1024]{2,1,0:T(8,128)S(1)}, f32[3,8,1024]{2,1,0:T(8,128)S(1)}, u32[]{:S(2)}, u32[]{:S(2)}) %collective-permute-start.1) | collective-permute-done | bytes 98336 | tf_op jit(solution)/shard_map/ppermute | solution.py:364
  12.1 0.2 rows_kernel.1
  12.3 0.7 %collective-permute-start.3 = (f32[18,1024]{1,0:T(8,128)S(1)}, f32[18,1024]{1,0:T(8,128)S(1)}, u32[]{:S(2)}, u32[]{:S(2)}) collective-permute-start(f32[18,1024]{1,0:T(8,128)S(1)} %get-tuple-element.36), channel_id=1, source_target_pairs={{1,2},{2,1},{5,6},{6,5},{9,10},{10,9},{13,14},{14,13},{17,18},{18,... | collective-permute-start | bytes 221192 | tf_op jit(solution)/shard_map/ppermute | solution.py:364
  12.9 2.9 %collective-permute-start.4 = (f32[18,1024]{1,0:T(8,128)S(1)}, f32[18,1024]{1,0:T(8,128)S(1)}, u32[]{:S(2)}, u32[]{:S(2)}) collective-permute-start(f32[18,1024]{1,0:T(8,128)S(1)} %get-tuple-element.37), channel_id=1, source_target_pairs={{0,1},{1,0},{2,3},{3,2},{4,5},{5,4},{6,7},{7,6},{8,9},{9,8},{10,11... | collective-permute-start | bytes 221192 | tf_op jit(solution)/shard_map/ppermute | solution.py:364
  15.9 1.3 %collective-permute-start.5 = (f32[3,8,1024]{2,1,0:T(8,128)S(1)}, f32[3,8,1024]{2,1,0:T(8,128)S(1)}, u32[]{:S(2)}, u32[]{:S(2)}) collective-permute-start(f32[3,8,1024]{2,1,0:T(8,128)S(1)} %get-tuple-element.39), channel_id=1, source_target_pairs={{4,0},{8,4},{12,8},{16,12},{20,16},{24,20},{28,24},{5,1},{9,5},{13... | collective-permute-start | bytes 294920 | tf_op jit(solution)/shard_map/ppermute | solution.py:359
  17.2 0.0 collective-permute-done.2.over_ref
  17.2 0.0 collective-permute-done.3.other_ref
  17.2 0.0 collective-permute-done.4.pair_ref
  17.2 1.0 %image_kernel.1 = (f32[3,2,8,1024]{3,2,1,0:T(8,128)S(1)}, f32[3,2,8,1024]{3,2,1,0:T(8,128)S(1)}, f32[32,1,128]{2,1,0:T(1,128)S(1)}) custom-call(f32[3,2,8,1024]{3,2,1,0:T(8,128)S(1)} %get-tuple-element.23.b_ref, f32[3,2,8,1024]{3,2,1,0:T(8,128)S(1)} %get-tuple-element.34.v_ref, f32[3,8,1024]{2,1,0:T(8,128)S(1)} %collective-permute-done.2.over_ref, ...), custom_call_target="tpu_custom_call" | custom-call | flops 268435456 | bytes 1100124 | tf_op jit(solution)/shard_map/image_kernel/pallas_call | solution.py:345
  18.3 5.0 %collective-permute-done.5.under_ref = f32[3,8,1024]{2,1,0:T(8,128)S(1)} collective-permute-done((f32[3,8,1024]{2,1,0:T(8,128)S(1)}, f32[3,8,1024]{2,1,0:T(8,128)S(1)}, u32[]{:S(2)}, u32[]{:S(2)}) %collective-permute-start.5) | collective-permute-done | bytes 98336 | tf_op jit(solution)/shard_map/ppermute | solution.py:359
  23.2 12.1 %all_to_all.5.gram_ref = f32[32,1,128]{2,1,0:T(1,128)S(1)} all-to-all(f32[32,1,128]{2,1,0:T(1,128)S(1)} %get-tuple-element.40), channel_id=1, replica_groups=mesh['inline'=8,'col'=4] {'inline','col'}, dimensions={0} | all-to-all | bytes 32768 | tf_op jit(solution)/shard_map/all_to_all | solution.py:417
  35.3 1.0 %finish_kernel.1 = (f32[3,2,8,1024]{3,2,1,0:T(8,128)}, f32[3,2,8,1024]{3,2,1,0:T(8,128)}) custom-call(f32[32,1,128]{2,1,0:T(1,128)S(1)} %all_to_all.5.gram_ref, f32[3,2,8,1024]{3,2,1,0:T(8,128)S(1)} %get-tuple-element.23.b_ref, f32[3,2,8,1024]{3,2,1,0:T(8,128)S(1)} %get-tuple-element.41.one_ref, f32[3,2,8,1024]{3,2,1,0:T(8,128)S(1)} %get-tuple-element.42.two_ref, ...), custom_call_target="tpu_custom_call" | custom-call | flops 393216 | bytes 1097740 | tf_op jit(solution)/shard_map/finish_kernel/pallas_call | solution.py:345
Async XLA Ops:
  2.1 9.2 %collective-permute-start = (f32[3,8,1024]{2,1,0:T(8,128)S(1)}, f32[3,8,1024]{2,1,0:T(8,128)S(1)}, u32[]{:S(2)}, u32[]{:S(2)}) collective-permute-start(f32[3,8,1024]{2,1,0:T(8,128)S(1)} %get-tuple-element.31), channel_id=1, source_target_pairs={{4,8},{8,4},{12,16},{16,12},{20,24},{24,20},{5,9},{9,5},{13,17},{1... | collective-permute-start | bytes 294920 | tf_op jit(solution)/shard_map/ppermute | solution.py:364
  2.7 9.3 %collective-permute-start.1 = (f32[3,8,1024]{2,1,0:T(8,128)S(1)}, f32[3,8,1024]{2,1,0:T(8,128)S(1)}, u32[]{:S(2)}, u32[]{:S(2)}) collective-permute-start(f32[3,8,1024]{2,1,0:T(8,128)S(1)} %get-tuple-element.32), channel_id=1, source_target_pairs={{0,4},{4,0},{8,12},{12,8},{16,20},{20,16},{24,28},{28,24},{1,5},{5... | collective-permute-start | bytes 294920 | tf_op jit(solution)/shard_map/ppermute | solution.py:364
  9.4 7.8 %collective-permute-start.2 = (f32[3,8,1024]{2,1,0:T(8,128)S(1)}, f32[3,8,1024]{2,1,0:T(8,128)S(1)}, u32[]{:S(2)}, u32[]{:S(2)}) collective-permute-start(f32[3,8,1024]{2,1,0:T(8,128)S(1)} %get-tuple-element.35), channel_id=1, source_target_pairs={{0,4},{4,8},{8,12},{12,16},{16,20},{20,24},{24,28},{1,5},{5,9},{9,... | collective-permute-start | bytes 294920 | tf_op jit(solution)/shard_map/ppermute | solution.py:359
  12.3 4.9 %collective-permute-start.3 = (f32[18,1024]{1,0:T(8,128)S(1)}, f32[18,1024]{1,0:T(8,128)S(1)}, u32[]{:S(2)}, u32[]{:S(2)}) collective-permute-start(f32[18,1024]{1,0:T(8,128)S(1)} %get-tuple-element.36), channel_id=1, source_target_pairs={{1,2},{2,1},{5,6},{6,5},{9,10},{10,9},{13,14},{14,13},{17,18},{18,... | collective-permute-start | bytes 221192 | tf_op jit(solution)/shard_map/ppermute | solution.py:364
  12.9 4.3 %collective-permute-start.4 = (f32[18,1024]{1,0:T(8,128)S(1)}, f32[18,1024]{1,0:T(8,128)S(1)}, u32[]{:S(2)}, u32[]{:S(2)}) collective-permute-start(f32[18,1024]{1,0:T(8,128)S(1)} %get-tuple-element.37), channel_id=1, source_target_pairs={{0,1},{1,0},{2,3},{3,2},{4,5},{5,4},{6,7},{7,6},{8,9},{9,8},{10,11... | collective-permute-start | bytes 221192 | tf_op jit(solution)/shard_map/ppermute | solution.py:364
  15.9 7.4 %collective-permute-start.5 = (f32[3,8,1024]{2,1,0:T(8,128)S(1)}, f32[3,8,1024]{2,1,0:T(8,128)S(1)}, u32[]{:S(2)}, u32[]{:S(2)}) collective-permute-start(f32[3,8,1024]{2,1,0:T(8,128)S(1)} %get-tuple-element.39), channel_id=1, source_target_pairs={{4,0},{8,4},{12,8},{16,12},{20,16},{24,20},{28,24},{5,1},{9,5},{13... | collective-permute-start | bytes 294920 | tf_op jit(solution)/shard_map/ppermute | solution.py:359

commit v8 on v6

--- a/solution.py
+++ b/solution.py
@@ -154,9 +154,9 @@
 
 
 def start_kernel(
-    seis_hbm, valid_hbm, avo_hbm, taps_hbm,
-    b_ref, pair_ref, other_ref,
-    seis_ref, valid_ref, avo_ref, taps_ref, padded, sems,
+    seis_hbm, valid_hbm, avo_hbm, taps_hbm, prior_hbm, strength_hbm,
+    b_ref, mate_ref, next_ref, valid_ref, avo_ref, taps_ref, prior_ref, strength_ref,
+    seis_ref, padded, sems,
 ):
     copies = copy_in(
         (
@@ -164,28 +164,39 @@
             (valid_hbm, valid_ref),
             (avo_hbm, avo_ref),
             (seis_hbm, seis_ref),
+            (prior_hbm, prior_ref),
+            (strength_hbm, strength_ref),
         ),
         sems,
     )
     for copy in copies[:2]:
         copy.wait()
     fill_taps(taps_ref, padded)
-    contrasts, angles, _ = avo_ref.shape
-    rows = seis_ref.shape[1]
+    angles = avo_ref.shape[1]
     circs = [circulant(padded, a) for a in range(angles)]
     masks = [trace_columns(valid_ref, a) for a in range(angles)]
     for copy in copies[2:]:
         copy.wait()
     store_tiles(b_ref, right_side(seis_ref, masks, avo_ref, circs))
+    send_rows(b_ref, mate_ref, next_ref)
+
+
+def send_rows(field_ref, mate_ref, next_ref):
     first = starts_pair("inline")
-    for c in range(contrasts):
-        top, bottom = b_ref[c, 0], b_ref[c, rows - 1]
-        pair_ref[c] = jnp.where(first, bottom, top)
-        other_ref[c] = jnp.where(first, top, bottom)
+    for c in range(field_ref.shape[0]):
+        top, bottom = field_ref[c, 0], field_ref[c, field_ref.shape[1] - 1]
+        mate_ref[c] = jnp.where(first, bottom, top)
+        next_ref[c] = jnp.where(first, top, bottom)
+
+
+def halo_rows(mate_ref, next_ref, c):
+    first = starts_pair("inline")
+    mate, other = mate_ref[c], next_ref[c]
+    return jnp.where(first, other, mate), jnp.where(first, mate, other)
 
 
 def part_kernel(
-    b_ref, valid_ref, avo_ref, taps_ref, prior_ref, strength_ref, p_ref, top_ref, bottom_ref, padded
+    b_ref, valid_ref, avo_ref, taps_ref, prior_ref, strength_ref, p_ref, mate_ref, next_ref, padded
 ):
     contrasts, rows = b_ref.shape[:2]
     fill_taps(taps_ref, padded)
@@ -202,8 +213,7 @@
             south = b_ref[c, r + 1] if r < rows - 1 else None
             around = lateral(here, north, south, None, None)
             p_ref[c, r] = p_ref[c, r] + strength * (weights[r] * here - around)
-        top_ref[c] = p_ref[c, 0]
-        bottom_ref[c] = p_ref[c, rows - 1]
+    send_rows(p_ref, mate_ref, next_ref)
 
 
 def stack_tiles(ref):
@@ -229,11 +239,10 @@
 
 def rows_kernel(b_ref, p_ref, next_ref, mate_ref, strength_ref, v_ref, pair_ref, other_ref):
     contrasts, rows, traces, _ = b_ref.shape
-    first_row, first_col = starts_pair("inline"), starts_pair("col")
+    first_col = starts_pair("col")
     for c in range(contrasts):
         strength = strength_ref[:, c : c + 1]
-        above = jnp.where(first_row, next_ref[c], mate_ref[c])
-        below = jnp.where(first_row, mate_ref[c], next_ref[c])
+        above, below = halo_rows(mate_ref, next_ref, c)
         own = [p_ref[c, r] for r in range(rows)]
         own[0] = own[0] - strength * above
         own[-1] = own[-1] - strength * below
@@ -248,7 +257,7 @@
 
 
 def image_kernel(
-    b_ref, v_ref, over_ref, other_ref, pair_ref,
+    b_ref, v_ref, next_ref, mate_ref, other_ref, pair_ref,
     valid_ref, avo_ref, taps_ref, prior_ref, strength_ref,
     one_ref, two_ref, gram_ref, padded,
 ):
@@ -280,8 +289,9 @@
     sums = [jnp.zeros((traces, LANES), F32) for _ in range(4)]
     for c in range(contrasts):
         strength = strength_ref[:, c : c + 1]
-        over = over_ref[c] - strength * (has_above * b_ref[c, 0] + beside(c, 0))
-        under = -strength * (has_below * b_ref[c, rows - 1] + beside(c, ext - 1))
+        over, under = halo_rows(mate_ref, next_ref, c)
+        over = over - strength * (has_above * b_ref[c, 0] + beside(c, 0))
+        under = under - strength * (has_below * b_ref[c, rows - 1] + beside(c, ext - 1))
         for r in range(rows):
             here, b = one_ref[c, r], b_ref[c, r]
             edge = c * stride + ext + r
@@ -290,12 +300,11 @@
                 right[edge : edge + 1, :] - strength * b[traces - 1 : traces, :]
             )
             north = one_ref[c, r - 1] if r else over
-            south = one_ref[c, r + 1] if r < rows - 1 else None
+            south = one_ref[c, r + 1] if r < rows - 1 else under
             around = lateral(here, north, south, west, east)
             two = two_ref[c, r] + strength * (weights[r] * here - around)
-            twice = two if r else two - strength * over
-            two_ref[c, r] = two if r < rows - 1 else two - strength * under
-            for q, product in enumerate((b * b, b * here, here * here, here * twice)):
+            two_ref[c, r] = two
+            for q, product in enumerate((b * b, b * here, here * here, here * two)):
                 tiles = [product[:, k : k + LANES] for k in range(0, samples, LANES)]
                 sums[q] = sums[q] + functools.reduce(jnp.add, tiles)
     lane = lax.broadcasted_iota(jnp.int32, (1, LANES), 1)
@@ -306,9 +315,7 @@
     gram_ref[...] = jnp.broadcast_to(packed[None], gram_ref.shape)
 
 
-def finish_kernel(
-    gram_ref, b_ref, one_ref, two_ref, under_ref, strength_ref, solution_ref, residual_ref
-):
+def finish_kernel(gram_ref, b_ref, one_ref, two_ref, solution_ref, residual_ref):
     sums = jnp.sum(gram_ref[...], axis=0)
     g00, g01, g11, g12 = (sums[:, q : q + 1] for q in range(4))
     first = g00 / g01
@@ -316,12 +323,9 @@
     second = (ratio - 1.0) * g01 / (first * g12 - ratio * g11)
     near = first + second * ratio
     far = first * second
-    rows = b_ref.shape[1]
     for c in range(b_ref.shape[0]):
-        for r in range(rows):
+        for r in range(b_ref.shape[1]):
             b, one, two = b_ref[c, r], one_ref[c, r], two_ref[c, r]
-            if r == rows - 1:
-                two = two - strength_ref[:, c : c + 1] * under_ref[c]
             solution_ref[c, r] = near * b - far * one
             residual_ref[c, r] = b - near * one + far * two
 
@@ -344,11 +348,6 @@
     )(*ins)
 
 
-def shift(axis, value, step):
-    size = lax.axis_size(axis)
-    return lax.ppermute(value, axis, [(i, i + step) for i in range(size) if 0 <= i + step < size])
-
-
 def swap(axis, value, first):
     starts = range(first, lax.axis_size(axis) - 1, 2)
     return lax.ppermute(value, axis, [(i + d, i + 1 - d) for i in starts for d in (0, 1)])
@@ -358,7 +357,6 @@
     angles, rows, traces, samples = seismic.shape
     contrasts = avo_coeffs.shape[1]
     avo_coeffs = jnp.swapaxes(avo_coeffs, 0, 1)
-    strength = lateral_strength.reshape(1, -1)
     shape = lambda *dims: jax.ShapeDtypeStruct(dims, F32)
     field = shape(contrasts, rows, traces, samples)
     row = shape(contrasts, traces, samples)
@@ -366,49 +364,37 @@
     padded = pltpu.VMEM((8, 2 * LANES), F32)
     work = 2 * angles * rows * traces * samples * 256 * 4
 
-    placed = (seismic, validity, avo_coeffs, wavelets)
-    b, pair, other = call(
+    given = (seismic, validity, avo_coeffs, wavelets, prior_weight, lateral_strength.reshape(1, -1))
+    b, mate, other, *kept = call(
         start_kernel,
-        (field, row, row),
-        [pltpu.with_memory_space_constraint(x, pltpu.HBM) for x in placed],
+        (field, row, row, *[jax.ShapeDtypeStruct(x.shape, x.dtype) for x in given[1:]]),
+        [pltpu.with_memory_space_constraint(x, pltpu.HBM) for x in given],
         work,
-        [*[pltpu.VMEM(x.shape, x.dtype) for x in placed], padded, pltpu.SemaphoreType.DMA((4,))],
-        [HBM] * 4,
+        [pltpu.VMEM(seismic.shape, seismic.dtype), padded, pltpu.SemaphoreType.DMA((6,))],
+        [HBM] * 6,
     )
     other = swap("inline", other, 1)
-    pair = swap("inline", pair, 0)
-    part, top, bottom = call(
-        part_kernel,
-        (field, row, row),
-        (b, validity, avo_coeffs, wavelets, prior_weight, strength),
-        2 * work,
-        [padded],
-    )
-    over = shift("inline", bottom, 1)
-    image, pair, other = call(
-        rows_kernel,
-        (field, side, side),
-        (b, part, other, pair, strength),
-        4 * field.size,
-    )
-    other = swap("col", other, 1)
-    pair = swap("col", pair, 0)
-    top, image = lax.optimization_barrier((top, image))
-    under = shift("inline", top, -1)
+    mate = swap("inline", mate, 0)
+    part, part_mate, part_other = call(
+        part_kernel, (field, row, row), (b, *kept), 2 * work, [padded]
+    )
+    part_other = swap("inline", part_other, 1)
+    part_mate = swap("inline", part_mate, 0)
+    image, col_pair, col_other = call(
+        rows_kernel, (field, side, side), (b, part, other, mate, kept[-1]), 4 * field.size
+    )
+    col_other = swap("col", col_other, 1)
+    col_pair = swap("col", col_pair, 0)
     axes = ("inline", "col")
     one, two, gram = call(
         image_kernel,
         (field, field, shape(lax.axis_size(axes), 1, LANES)),
-        (
-            b, image, over, other, pair,
-            validity, avo_coeffs, wavelets, prior_weight, strength,
-        ),
+        (b, image, part_other, part_mate, col_other, col_pair, *kept),
         2 * work,
         [padded],
     )
     gram = lax.all_to_all(gram, axes, 0, 0)
-    last = (gram, b, one, two, under, strength)
-    return tuple(call(finish_kernel, (field, field), last, 8 * field.size))
+    return tuple(call(finish_kernel, (field, field), (gram, b, one, two), 8 * field.size))
 
 
 def solution(mesh):

time: 34.1 us -> 35.4 us (1.038)
  blocking collectives: 0 us -> 14.1 us
  waiting for transfers between devices: 7.19 us -> 0.95 us
  starting transfers between devices: 20.2 us -> 15.1 us
  local copies, waits for them, and re-layouts: 0.69 us -> 0 us
  Pallas kernels: 5.01 us -> 4.39 us
    all_to_all x0 -> x1, blocking collectives: none -> 14.1 us  [shards(): gram = lax.all_to_all(gram, axes, 0, 0)]
    all_to_all x1 -> x0, waiting for transfers between devices: 7.06 us -> none  [shards(): gram = lax.all_to_all(gram, axes, 0, 0)]
    all_to_all x1 -> x0, starting transfers between devices: 6.95 us -> none  [shards(): gram = lax.all_to_all(gram, axes, 0, 0)]
    ppermute x4 -> x6, starting transfers between devices: 10.1 us -> 15.1 us  [swap(): lax.ppermute(value, axis, [(i + d, i + 1 - d) for i in starts for d in (0...]
    ppermute x2 -> x0, starting transfers between devices: 3.2 us -> none  [shift(): lax.ppermute(value, axis, [(i, i + step) for i in range(size) if 0 <= i +...]
    ppermute x4 -> x6, waiting for transfers between devices: 0.12 us -> 0.95 us  [swap(): lax.ppermute(value, axis, [(i + d, i + 1 - d) for i in starts for d in (0...]
    unnamed x10 -> x0, local copies, waits for them, and re-layouts: 0.69 us -> none
    pallas_call x5, Pallas kernels: 5.01 us -> 4.39 us  [call(): pl.pallas_call(kernel, out_shape=outs, in_specs=[VMEM] * len(ins) if plac...]
  transfers between devices with their start and end apart: 7 -> 6, of which waited for: 2 -> 1; matrix products, arithmetic and copies ran while one was open for 0% -> 0% of each run, Pallas kernels for 8% -> 3%
where the time goes in v8:
time: 35.4 us; the launch traced here: 35.2 us
  starting transfers between devices  15.1 us (43%)
  blocking collectives  14.1 us (40%)
  Pallas kernels  4.39 us (12%)
  waiting for transfers between devices  0.95 us (3%)
  between operations  0.68 us (2%)
    ppermute x6, starting transfers between devices, swap(): lax.ppermute(value, axis, [(i + d, i + 1 - d) for i in starts for d in (0...  15.1 us
    all_to_all x1, blocking collectives, shards(): gram = lax.all_to_all(gram, axes, 0, 0)  14.1 us
    pallas_call x5, Pallas kernels, call(): pl.pallas_call(kernel, out_shape=outs, in_specs=[VMEM] * len(ins) if plac...  4.39 us
    ppermute x6, waiting for transfers between devices, swap(): lax.ppermute(value, axis, [(i + d, i + 1 - d) for i in starts for d in (0...  0.95 us
  transfers between devices with their start and end apart: 6, of which 1 were waited for; matrix products, arithmetic and copies ran while one was open for 0% of the time, Pallas kernels for 3%

profile of v8, /device:TPU:0, one launch (start us, length us, event | category | flops | bytes accessed | tf_op | source)
XLA Modules:
  0.0 35.2 jit_solution(2029337553676195365)
XLA Ops:
  0.6 1.4 %start_kernel.1 = (f32[3,2,8,1024]{3,2,1,0:T(8,128)S(1)}, f32[3,8,1024]{2,1,0:T(8,128)S(1)}, f32[3,8,1024]{2,1,0:T(8,128)S(1)}, s32[4,2,8]{2,1,0:T(2,128)S(1)}, ...) custom-call(bf16[4,2,8,1024]{3,2,1,0:T(8,128)(2,1)} %seis_hbm.1, ...), custom_call_target="tpu_custom_call" | custom-call | flops 134217728 | bytes 627384 | tf_op jit(solution)/shard_map/start_kernel/pallas_call | solution.py:339
  2.1 0.7 %collective-permute-start = (f32[3,8,1024]{2,1,0:T(8,128)S(1)}, f32[3,8,1024]{2,1,0:T(8,128)S(1)}, u32[]{:S(2)}, u32[]{:S(2)}) collective-permute-start(f32[3,8,1024]{2,1,0:T(8,128)S(1)} %get-tuple-element.26), channel_id=1, source_target_pairs={{4,8},{8,4},{12,16},{16,12},{20,24},{24,20},{5,9},{9,5},{13,17},{1... | collective-permute-start | bytes 294920 | tf_op jit(solution)/shard_map/ppermute | solution.py:353
  2.7 5.8 %collective-permute-start.1 = (f32[3,8,1024]{2,1,0:T(8,128)S(1)}, f32[3,8,1024]{2,1,0:T(8,128)S(1)}, u32[]{:S(2)}, u32[]{:S(2)}) collective-permute-start(f32[3,8,1024]{2,1,0:T(8,128)S(1)} %get-tuple-element.27), channel_id=1, source_target_pairs={{0,4},{4,0},{8,12},{12,8},{16,20},{20,16},{24,28},{28,24},{1,5},{5... | collective-permute-start | bytes 294920 | tf_op jit(solution)/shard_map/ppermute | solution.py:353
  8.5 0.8 %part_kernel.1 = (f32[3,2,8,1024]{3,2,1,0:T(8,128)S(1)}, f32[3,8,1024]{2,1,0:T(8,128)S(1)}, f32[3,8,1024]{2,1,0:T(8,128)S(1)}) custom-call(f32[3,2,8,1024]{3,2,1,0:T(8,128)S(1)} %get-tuple-element.19.b_ref, s32[4,2,8]{2,1,0:T(2,128)S(1)} %get-tuple-element.20.valid_ref, f32[3,4,1024]{2,1,0:T(4,128)S(1)} %get-tuple-element.21.avo_ref, ...), custom_call_target="tpu_custom_call" | custom-call | flops 268435456 | bytes 641372 | tf_op jit(solution)/shard_map/part_kernel/pallas_call | solution.py:339
  9.4 0.7 %collective-permute-start.2 = (f32[3,8,1024]{2,1,0:T(8,128)S(1)}, f32[3,8,1024]{2,1,0:T(8,128)S(1)}, u32[]{:S(2)}, u32[]{:S(2)}) collective-permute-start(f32[3,8,1024]{2,1,0:T(8,128)S(1)} %get-tuple-element.29), channel_id=1, source_target_pairs={{4,8},{8,4},{12,16},{16,12},{20,24},{24,20},{5,9},{9,5},{13,17},{1... | collective-permute-start | bytes 294920 | tf_op jit(solution)/shard_map/ppermute | solution.py:353
  10.0 4.3 %collective-permute-start.3 = (f32[3,8,1024]{2,1,0:T(8,128)S(1)}, f32[3,8,1024]{2,1,0:T(8,128)S(1)}, u32[]{:S(2)}, u32[]{:S(2)}) collective-permute-start(f32[3,8,1024]{2,1,0:T(8,128)S(1)} %get-tuple-element.30), channel_id=1, source_target_pairs={{0,4},{4,0},{8,12},{12,8},{16,20},{20,16},{24,28},{28,24},{1,5},{5... | collective-permute-start | bytes 294920 | tf_op jit(solution)/shard_map/ppermute | solution.py:353
  14.4 0.0 collective-permute-done.next_ref
  14.4 0.0 collective-permute-done.1.mate_ref
  14.4 0.2 rows_kernel.1
  14.6 0.7 %collective-permute-start.4 = (f32[18,1024]{1,0:T(8,128)S(1)}, f32[18,1024]{1,0:T(8,128)S(1)}, u32[]{:S(2)}, u32[]{:S(2)}) collective-permute-start(f32[18,1024]{1,0:T(8,128)S(1)} %get-tuple-element.31), channel_id=1, source_target_pairs={{1,2},{2,1},{5,6},{6,5},{9,10},{10,9},{13,14},{14,13},{17,18},{18,... | collective-permute-start | bytes 221192 | tf_op jit(solution)/shard_map/ppermute | solution.py:353
  15.2 2.9 %collective-permute-start.5 = (f32[18,1024]{1,0:T(8,128)S(1)}, f32[18,1024]{1,0:T(8,128)S(1)}, u32[]{:S(2)}, u32[]{:S(2)}) collective-permute-start(f32[18,1024]{1,0:T(8,128)S(1)} %get-tuple-element.32), channel_id=1, source_target_pairs={{0,1},{1,0},{2,3},{3,2},{4,5},{5,4},{6,7},{7,6},{8,9},{9,8},{10,11... | collective-permute-start | bytes 221192 | tf_op jit(solution)/shard_map/ppermute | solution.py:353
  18.2 0.0 collective-permute-done.2.next_ref
  18.2 0.0 collective-permute-done.3.mate_ref
  18.2 0.0 collective-permute-done.4.other_ref
  18.2 0.9 %collective-permute-done.5.pair_ref = f32[18,1024]{1,0:T(8,128)S(1)} collective-permute-done((f32[18,1024]{1,0:T(8,128)S(1)}, f32[18,1024]{1,0:T(8,128)S(1)}, u32[]{:S(2)}, u32[]{:S(2)}) %collective-permute-start.5) | collective-permute-done | bytes 73760 | tf_op jit(solution)/shard_map/ppermute | solution.py:353
  19.1 1.0 %image_kernel.1 = (f32[3,2,8,1024]{3,2,1,0:T(8,128)S(1)}, f32[3,2,8,1024]{3,2,1,0:T(8,128)S(1)}, f32[32,1,128]{2,1,0:T(1,128)S(1)}) custom-call(f32[3,2,8,1024]{3,2,1,0:T(8,128)S(1)} %get-tuple-element.19.b_ref, f32[3,2,8,1024]{3,2,1,0:T(8,128)S(1)} %get-tuple-element.28.v_ref, f32[3,8,1024]{2,1,0:T(8,128)S(1)} %collective-permute-done.2.next_ref, ...), custom_call_target="tpu_custom_call" | custom-call | flops 268435456 | bytes 1198428 | tf_op jit(solution)/shard_map/image_kernel/pallas_call | solution.py:339
  20.2 14.1 %all_to_all.5.gram_ref = f32[32,1,128]{2,1,0:T(1,128)S(1)} all-to-all(f32[32,1,128]{2,1,0:T(1,128)S(1)} %get-tuple-element.33), channel_id=1, replica_groups=mesh['inline'=8,'col'=4] {'inline','col'}, dimensions={0} | all-to-all | bytes 32768 | tf_op jit(solution)/shard_map/all_to_all | solution.py:396
  34.2 0.9 %finish_kernel.1 = (f32[3,2,8,1024]{3,2,1,0:T(8,128)}, f32[3,2,8,1024]{3,2,1,0:T(8,128)}) custom-call(f32[32,1,128]{2,1,0:T(1,128)S(1)} %all_to_all.5.gram_ref, f32[3,2,8,1024]{3,2,1,0:T(8,128)S(1)} %get-tuple-element.19.b_ref, f32[3,2,8,1024]{3,2,1,0:T(8,128)S(1)} %get-tuple-element.34.one_ref, f32[3,2,8,1024]{3,2,1,0:T(8,128)S(1)} %get-tuple-element.35.two_ref), custom_call_target="tpu_custom_call" | custom-call | flops 393216 | bytes 999424 | tf_op jit(solution)/shard_map/finish_kernel/pallas_call | solution.py:339
Async XLA Ops:
  2.1 12.3 %collective-permute-start = (f32[3,8,1024]{2,1,0:T(8,128)S(1)}, f32[3,8,1024]{2,1,0:T(8,128)S(1)}, u32[]{:S(2)}, u32[]{:S(2)}) collective-permute-start(f32[3,8,1024]{2,1,0:T(8,128)S(1)} %get-tuple-element.26), channel_id=1, source_target_pairs={{4,8},{8,4},{12,16},{16,12},{20,24},{24,20},{5,9},{9,5},{13,17},{1... | collective-permute-start | bytes 294920 | tf_op jit(solution)/shard_map/ppermute | solution.py:353
  2.7 11.6 %collective-permute-start.1 = (f32[3,8,1024]{2,1,0:T(8,128)S(1)}, f32[3,8,1024]{2,1,0:T(8,128)S(1)}, u32[]{:S(2)}, u32[]{:S(2)}) collective-permute-start(f32[3,8,1024]{2,1,0:T(8,128)S(1)} %get-tuple-element.27), channel_id=1, source_target_pairs={{0,4},{4,0},{8,12},{12,8},{16,20},{20,16},{24,28},{28,24},{1,5},{5... | collective-permute-start | bytes 294920 | tf_op jit(solution)/shard_map/ppermute | solution.py:353
  9.4 8.8 %collective-permute-start.2 = (f32[3,8,1024]{2,1,0:T(8,128)S(1)}, f32[3,8,1024]{2,1,0:T(8,128)S(1)}, u32[]{:S(2)}, u32[]{:S(2)}) collective-permute-start(f32[3,8,1024]{2,1,0:T(8,128)S(1)} %get-tuple-element.29), channel_id=1, source_target_pairs={{4,8},{8,4},{12,16},{16,12},{20,24},{24,20},{5,9},{9,5},{13,17},{1... | collective-permute-start | bytes 294920 | tf_op jit(solution)/shard_map/ppermute | solution.py:353
  10.0 8.2 %collective-permute-start.3 = (f32[3,8,1024]{2,1,0:T(8,128)S(1)}, f32[3,8,1024]{2,1,0:T(8,128)S(1)}, u32[]{:S(2)}, u32[]{:S(2)}) collective-permute-start(f32[3,8,1024]{2,1,0:T(8,128)S(1)} %get-tuple-element.30), channel_id=1, source_target_pairs={{0,4},{4,0},{8,12},{12,8},{16,20},{20,16},{24,28},{28,24},{1,5},{5... | collective-permute-start | bytes 294920 | tf_op jit(solution)/shard_map/ppermute | solution.py:353
  14.6 3.6 %collective-permute-start.4 = (f32[18,1024]{1,0:T(8,128)S(1)}, f32[18,1024]{1,0:T(8,128)S(1)}, u32[]{:S(2)}, u32[]{:S(2)}) collective-permute-start(f32[18,1024]{1,0:T(8,128)S(1)} %get-tuple-element.31), channel_id=1, source_target_pairs={{1,2},{2,1},{5,6},{6,5},{9,10},{10,9},{13,14},{14,13},{17,18},{18,... | collective-permute-start | bytes 221192 | tf_op jit(solution)/shard_map/ppermute | solution.py:353
  15.2 3.9 %collective-permute-start.5 = (f32[18,1024]{1,0:T(8,128)S(1)}, f32[18,1024]{1,0:T(8,128)S(1)}, u32[]{:S(2)}, u32[]{:S(2)}) collective-permute-start(f32[18,1024]{1,0:T(8,128)S(1)} %get-tuple-element.32), channel_id=1, source_target_pairs={{0,1},{1,0},{2,3},{3,2},{4,5},{5,4},{6,7},{7,6},{8,9},{9,8},{10,11... | collective-permute-start | bytes 221192 | tf_op jit(solution)/shard_map/ppermute | solution.py:353

commit v9 on v8

--- a/solution.py
+++ b/solution.py
@@ -155,7 +155,7 @@
 
 def start_kernel(
     seis_hbm, valid_hbm, avo_hbm, taps_hbm, prior_hbm, strength_hbm,
-    b_ref, mate_ref, next_ref, valid_ref, avo_ref, taps_ref, prior_ref, strength_ref,
+    b_ref, near_ref, far_ref, valid_ref, avo_ref, taps_ref, prior_ref, strength_ref,
     seis_ref, padded, sems,
 ):
     copies = copy_in(
@@ -178,25 +178,33 @@
     for copy in copies[2:]:
         copy.wait()
     store_tiles(b_ref, right_side(seis_ref, masks, avo_ref, circs))
-    send_rows(b_ref, mate_ref, next_ref)
-
-
-def send_rows(field_ref, mate_ref, next_ref):
+    contrasts, rows, traces, samples = b_ref.shape
+    n = samples // LANES
     first = starts_pair("inline")
-    for c in range(field_ref.shape[0]):
-        top, bottom = field_ref[c, 0], field_ref[c, field_ref.shape[1] - 1]
-        mate_ref[c] = jnp.where(first, bottom, top)
-        next_ref[c] = jnp.where(first, top, bottom)
-
-
-def halo_rows(mate_ref, next_ref, c):
+    lane = lax.broadcasted_iota(jnp.int32, (traces, LANES), 1)
+    notes = []
+    for r in (0, rows - 1):
+        note = jnp.where(lane == angles, column(prior_ref[r : r + 1, :]), 0.0)
+        for a in range(angles):
+            note = jnp.where(lane == a, masks[a][r * traces : (r + 1) * traces], note)
+        notes.append(note)
+    edges = [
+        [*[b_ref[c, r, :, pl.ds(k * LANES, LANES)] for c in range(contrasts) for k in range(n)], note]
+        for r, note in zip((0, rows - 1), notes)
+    ]
+    for e, (top, bottom) in enumerate(zip(*edges)):
+        near_ref[e] = jnp.where(first, bottom, top)
+        far_ref[e] = jnp.where(first, top, bottom)
+
+
+def either_side(pair_ref, next_ref, *where):
     first = starts_pair("inline")
-    mate, other = mate_ref[c], next_ref[c]
-    return jnp.where(first, other, mate), jnp.where(first, mate, other)
+    pair, other = pair_ref[where], next_ref[where]
+    return jnp.where(first, other, pair), jnp.where(first, pair, other)
 
 
 def part_kernel(
-    b_ref, valid_ref, avo_ref, taps_ref, prior_ref, strength_ref, p_ref, mate_ref, next_ref, padded
+    b_ref, valid_ref, avo_ref, taps_ref, prior_ref, strength_ref, p_ref, padded
 ):
     contrasts, rows = b_ref.shape[:2]
     fill_taps(taps_ref, padded)
@@ -213,7 +221,41 @@
             south = b_ref[c, r + 1] if r < rows - 1 else None
             around = lateral(here, north, south, None, None)
             p_ref[c, r] = p_ref[c, r] + strength * (weights[r] * here - around)
-    send_rows(p_ref, mate_ref, next_ref)
+
+
+def halo_kernel(
+    b_ref, near_ref, far_ref, near_next_ref, far_next_ref, avo_ref, taps_ref, strength_ref,
+    out_ref, padded,
+):
+    contrasts, rows, traces, samples = b_ref.shape
+    angles, n = avo_ref.shape[1], samples // LANES
+    has = inside("inline")
+    fill_taps(taps_ref, padded)
+    circs = [circulant(padded, a) for a in range(angles)]
+    notes = either_side(near_ref, near_next_ref, contrasts * n)
+    masks = [
+        jnp.concatenate([note[:, a : a + 1] for note in notes], axis=0) for a in range(angles)
+    ]
+    field = [
+        [
+            jnp.concatenate(either_side(near_ref, near_next_ref, c * n + k), axis=0)
+            for k in range(n)
+        ]
+        for c in range(contrasts)
+    ]
+    total = normal(field, masks, avo_ref, circs)
+    for c in range(contrasts):
+        strength = strength_ref[:, c : c + 1]
+        for side, own in ((0, 0), (1, rows - 1)):
+            weight = notes[side][:, angles : angles + 1] + 4.0
+            lines = slice(side * traces, (side + 1) * traces)
+            here = jnp.concatenate([tile[lines] for tile in field[c]], axis=1)
+            beyond = jnp.concatenate(
+                [either_side(far_ref, far_next_ref, c * n + k)[side] for k in range(n)], axis=1
+            )
+            around = lateral(here, beyond, has[side] * b_ref[c, own], None, None)
+            data = jnp.concatenate([tile[lines] for tile in total[c]], axis=1)
+            out_ref[side, c] = data + strength * (weight * here - around)
 
 
 def stack_tiles(ref):
@@ -237,12 +279,14 @@
     return lax.axis_index(axis) % 2 == 0
 
 
-def rows_kernel(b_ref, p_ref, next_ref, mate_ref, strength_ref, v_ref, pair_ref, other_ref):
-    contrasts, rows, traces, _ = b_ref.shape
+def rows_kernel(b_ref, p_ref, near_ref, near_next_ref, strength_ref, v_ref, pair_ref, other_ref):
+    contrasts, rows, traces, samples = b_ref.shape
     first_col = starts_pair("col")
+    n = samples // LANES
     for c in range(contrasts):
         strength = strength_ref[:, c : c + 1]
-        above, below = halo_rows(mate_ref, next_ref, c)
+        tiles = [either_side(near_ref, near_next_ref, c * n + k) for k in range(n)]
+        above, below = (jnp.concatenate(side, axis=1) for side in zip(*tiles))
         own = [p_ref[c, r] for r in range(rows)]
         own[0] = own[0] - strength * above
         own[-1] = own[-1] - strength * below
@@ -257,14 +301,13 @@
 
 
 def image_kernel(
-    b_ref, v_ref, next_ref, mate_ref, other_ref, pair_ref,
+    b_ref, v_ref, halo_ref, other_ref, pair_ref,
     valid_ref, avo_ref, taps_ref, prior_ref, strength_ref,
     one_ref, two_ref, gram_ref, padded,
 ):
     contrasts, rows, traces, samples = b_ref.shape
     angles = avo_ref.shape[1]
     has_left, has_right = inside("col")
-    has_above, has_below = inside("inline")
     first_col = starts_pair("col")
     left = jnp.where(first_col, other_ref[...], pair_ref[...])
     right = jnp.where(first_col, pair_ref[...], other_ref[...])
@@ -289,9 +332,8 @@
     sums = [jnp.zeros((traces, LANES), F32) for _ in range(4)]
     for c in range(contrasts):
         strength = strength_ref[:, c : c + 1]
-        over, under = halo_rows(mate_ref, next_ref, c)
-        over = over - strength * (has_above * b_ref[c, 0] + beside(c, 0))
-        under = under - strength * (has_below * b_ref[c, rows - 1] + beside(c, ext - 1))
+        over = halo_ref[0, c] - strength * beside(c, 0)
+        under = halo_ref[1, c] - strength * beside(c, ext - 1)
         for r in range(rows):
             here, b = one_ref[c, r], b_ref[c, r]
             edge = c * stride + ext + r
@@ -353,43 +395,55 @@
     return lax.ppermute(value, axis, [(i + d, i + 1 - d) for i in starts for d in (0, 1)])
 
 
+def hand_on(axis, value):
+    size = lax.axis_size(axis)
+    steps = [(i, i + 2 - 4 * (i % 2)) for i in range(size)]
+    return lax.ppermute(value, axis, [(i, j) for i, j in steps if 0 <= j < size])
+
+
 def shards(seismic, validity, prior_weight, lateral_strength, avo_coeffs, wavelets):
     angles, rows, traces, samples = seismic.shape
     contrasts = avo_coeffs.shape[1]
     avo_coeffs = jnp.swapaxes(avo_coeffs, 0, 1)
     shape = lambda *dims: jax.ShapeDtypeStruct(dims, F32)
     field = shape(contrasts, rows, traces, samples)
-    row = shape(contrasts, traces, samples)
     side = shape(contrasts * (2 * rows + 2), samples)
     padded = pltpu.VMEM((8, 2 * LANES), F32)
     work = 2 * angles * rows * traces * samples * 256 * 4
 
     given = (seismic, validity, avo_coeffs, wavelets, prior_weight, lateral_strength.reshape(1, -1))
-    b, mate, other, *kept = call(
+    edge = shape(contrasts * samples // LANES + 1, traces, LANES)
+    b, near, far, *kept = call(
         start_kernel,
-        (field, row, row, *[jax.ShapeDtypeStruct(x.shape, x.dtype) for x in given[1:]]),
+        (field, edge, edge, *[jax.ShapeDtypeStruct(x.shape, x.dtype) for x in given[1:]]),
         [pltpu.with_memory_space_constraint(x, pltpu.HBM) for x in given],
         work,
         [pltpu.VMEM(seismic.shape, seismic.dtype), padded, pltpu.SemaphoreType.DMA((6,))],
         [HBM] * 6,
     )
-    other = swap("inline", other, 1)
-    mate = swap("inline", mate, 0)
-    part, part_mate, part_other = call(
-        part_kernel, (field, row, row), (b, *kept), 2 * work, [padded]
-    )
-    part_other = swap("inline", part_other, 1)
-    part_mate = swap("inline", part_mate, 0)
+    avo, taps, strength = kept[1], kept[2], kept[-1]
+    far = swap("inline", far, 0)
+    near = swap("inline", near, 0)
+    near_next = hand_on("inline", far)
+    far_next = hand_on("inline", near)
+    (part,) = call(part_kernel, (field,), (b, *kept), 2 * work, [padded])
     image, col_pair, col_other = call(
-        rows_kernel, (field, side, side), (b, part, other, mate, kept[-1]), 4 * field.size
+        rows_kernel, (field, side, side), (b, part, near, near_next, strength), 4 * field.size
     )
     col_other = swap("col", col_other, 1)
     col_pair = swap("col", col_pair, 0)
+    (halo,) = call(
+        halo_kernel,
+        (shape(2, contrasts, traces, samples),),
+        (b, near, far, near_next, far_next, avo, taps, strength),
+        2 * work,
+        [padded],
+    )
     axes = ("inline", "col")
     one, two, gram = call(
         image_kernel,
         (field, field, shape(lax.axis_size(axes), 1, LANES)),
-        (b, image, part_other, part_mate, col_other, col_pair, *kept),
+        (b, image, halo, col_other, col_pair, *kept),
         2 * work,
         [padded],
     )

time: 35.4 us -> 36.4 us (1.028)
  waiting for transfers between devices: 0.95 us -> 3.78 us
  blocking collectives: 14.1 us -> 12.4 us
  starting transfers between devices: 15.1 us -> 14.2 us
  Pallas kernels: 4.39 us -> 5.14 us
    ppermute x6 -> x4, starting transfers between devices: 15.1 us -> 6.69 us  [swap(): lax.ppermute(value, axis, [(i + d, i + 1 - d) for i in starts for d in (0...]
    ppermute x0 -> x2, starting transfers between devices: none -> 7.48 us  [hand_on(): lax.ppermute(value, axis, [(i, j) for i, j in steps if 0 <= j < size])]
    ppermute x6 -> x4, waiting for transfers between devices: 0.95 us -> 3.78 us  [swap(): lax.ppermute(value, axis, [(i + d, i + 1 - d) for i in starts for d in (0...]
    all_to_all x1, blocking collectives: 14.1 us -> 12.4 us  [shards(): gram = lax.all_to_all(gram, axes, 0, 0)]
    pallas_call x5 -> x6, Pallas kernels: 4.39 us -> 5.14 us  [call(): pl.pallas_call(kernel, out_shape=outs, in_specs=[VMEM] * len(ins) if plac...]
  transfers between devices with their start and end apart: 6 -> 6, of which waited for: 1 -> 2; matrix products, arithmetic and copies ran while one was open for 0% -> 0% of each run, Pallas kernels for 3% -> 5%
where the time goes in v9:
time: 36.4 us; the launch traced here: 36.2 us
  starting transfers between devices  14.2 us (39%)
  blocking collectives  12.4 us (34%)
  Pallas kernels  5.14 us (14%)
  waiting for transfers between devices  3.78 us (10%)
  between operations  0.71 us (2%)
    all_to_all x1, blocking collectives, shards(): gram = lax.all_to_all(gram, axes, 0, 0)  12.4 us
    ppermute x2, starting transfers between devices, hand_on(): lax.ppermute(value, axis, [(i, j) for i, j in steps if 0 <= j < size])  7.48 us
    ppermute x4, starting transfers between devices, swap(): lax.ppermute(value, axis, [(i + d, i + 1 - d) for i in starts for d in (0...  6.69 us
    pallas_call x6, Pallas kernels, call(): pl.pallas_call(kernel, out_shape=outs, in_specs=[VMEM] * len(ins) if plac...  5.14 us
    ppermute x4, waiting for transfers between devices, swap(): lax.ppermute(value, axis, [(i + d, i + 1 - d) for i in starts for d in (0...  3.78 us
  transfers between devices with their start and end apart: 6, of which 2 were waited for; matrix products, arithmetic and copies ran while one was open for 0% of the time, Pallas kernels for 5%

profile of v9, /device:TPU:0, one launch (start us, length us, event | category | flops | bytes accessed | tf_op | source)
XLA Modules:
  0.0 36.2 jit_solution(15168802859047385166)
XLA Ops:
  0.6 1.4 %start_kernel.1 = (f32[3,2,8,1024]{3,2,1,0:T(8,128)S(1)}, f32[25,8,128]{2,1,0:T(8,128)S(1)}, f32[25,8,128]{2,1,0:T(8,128)S(1)}, s32[4,2,8]{2,1,0:T(2,128)S(1)}, ...) custom-call(bf16[4,2,8,1024]{3,2,1,0:T(8,128)(2,1)} %seis_hbm.1, ...), custom_call_target="tpu_custom_call" | custom-call | flops 134217728 | bytes 635576 | tf_op jit(solution)/shard_map/start_kernel/pallas_call | solution.py:381
  2.1 3.0 %collective-permute-start.1 = (f32[25,8,128]{2,1,0:T(8,128)S(1)}, f32[25,8,128]{2,1,0:T(8,128)S(1)}, u32[]{:S(2)}, u32[]{:S(2)}) collective-permute-start(f32[25,8,128]{2,1,0:T(8,128)S(1)} %get-tuple-element.23), channel_id=1, source_target_pairs={{0,4},{4,0},{8,12},{12,8},{16,20},{20,16},{24,28},{28,24},{1,5},{5... | collective-permute-start | bytes 307208 | tf_op jit(solution)/shard_map/ppermute | solution.py:395
  5.1 0.1 collective-permute-start
  5.2 3.6 %collective-permute-done.1.far_ref = f32[25,8,128]{2,1,0:T(8,128)S(1)} collective-permute-done((f32[25,8,128]{2,1,0:T(8,128)S(1)}, f32[25,8,128]{2,1,0:T(8,128)S(1)}, u32[]{:S(2)}, u32[]{:S(2)}) %collective-permute-start.1) | collective-permute-done | bytes 102432 | tf_op jit(solution)/shard_map/ppermute | solution.py:395
  8.7 4.0 %collective-permute-start.2 = (f32[25,8,128]{2,1,0:T(8,128)S(1)}, f32[25,8,128]{2,1,0:T(8,128)S(1)}, u32[]{:S(2)}, u32[]{:S(2)}) collective-permute-start(f32[25,8,128]{2,1,0:T(8,128)S(1)} %collective-permute-done.1.far_ref), channel_id=1, source_target_pairs={{0,8},{8,16},{12,4},{16,24},{20,12},{28,20},{1,9},{9,17},{13,5},{1... | collective-permute-start | bytes 307208 | tf_op jit(solution)/shard_map/ppermute | solution.py:401
  12.8 0.0 collective-permute-done.near_ref
  12.8 3.5 %collective-permute-start.3 = (f32[25,8,128]{2,1,0:T(8,128)S(1)}, f32[25,8,128]{2,1,0:T(8,128)S(1)}, u32[]{:S(2)}, u32[]{:S(2)}) collective-permute-start(f32[25,8,128]{2,1,0:T(8,128)S(1)} %collective-permute-done.near_ref), channel_id=1, source_target_pairs={{0,8},{8,16},{12,4},{16,24},{20,12},{28,20},{1,9},{9,17},{13,5},{1... | collective-permute-start | bytes 307208 | tf_op jit(solution)/shard_map/ppermute | solution.py:401
  16.3 0.8 %part_kernel.1.p_ref = f32[3,2,8,1024]{3,2,1,0:T(8,128)S(1)} custom-call(f32[3,2,8,1024]{3,2,1,0:T(8,128)S(1)} %get-tuple-element.16.b_ref, s32[4,2,8]{2,1,0:T(2,128)S(1)} %get-tuple-element.17.valid_ref, f32[3,4,1024]{2,1,0:T(4,128)S(1)} %get-tuple-element.18.avo_ref, f32[4,129]{1,0:T(4,128)S(1)} %get-tuple-element.19.taps_ref, ...), custom_call_target="tpu_custom_call" | custom-call | flops 268435456 | bytes 444764 | tf_op jit(solution)/shard_map/part_kernel/pallas_call | solution.py:381
  17.1 0.0 collective-permute-done.2.near_next_ref
  17.1 0.2 rows_kernel.1
  17.3 0.7 %collective-permute-start.4 = (f32[18,1024]{1,0:T(8,128)S(1)}, f32[18,1024]{1,0:T(8,128)S(1)}, u32[]{:S(2)}, u32[]{:S(2)}) collective-permute-start(f32[18,1024]{1,0:T(8,128)S(1)} %get-tuple-element.25), channel_id=1, source_target_pairs={{1,2},{2,1},{5,6},{6,5},{9,10},{10,9},{13,14},{14,13},{17,18},{18,... | collective-permute-start | bytes 221192 | tf_op jit(solution)/shard_map/ppermute | solution.py:395
  17.9 2.9 %collective-permute-start.5 = (f32[18,1024]{1,0:T(8,128)S(1)}, f32[18,1024]{1,0:T(8,128)S(1)}, u32[]{:S(2)}, u32[]{:S(2)}) collective-permute-start(f32[18,1024]{1,0:T(8,128)S(1)} %get-tuple-element.26), channel_id=1, source_target_pairs={{0,1},{1,0},{2,3},{3,2},{4,5},{5,4},{6,7},{7,6},{8,9},{9,8},{10,11... | collective-permute-start | bytes 221192 | tf_op jit(solution)/shard_map/ppermute | solution.py:395
  20.9 0.0 collective-permute-done.3.far_next_ref
  20.9 0.7 %halo_kernel.1.halo_ref = f32[2,3,8,1024]{3,2,1,0:T(8,128)S(1)} custom-call(f32[3,2,8,1024]{3,2,1,0:T(8,128)S(1)} %get-tuple-element.16.b_ref, f32[25,8,128]{2,1,0:T(8,128)S(1)} %collective-permute-done.near_ref, f32[25,8,128]{2,1,0:T(8,128)S(1)} %collective-permute-done.1.far_ref, f32[25,8,128]{2,1,0:T(8,128)S(1)} %collective-permute-done.2.near_next_ref, ...), custom_call_target="tpu_custom_call" | custom-call | flops 268435456 | bytes 854044 | tf_op jit(solution)/shard_map/halo_kernel/pallas_call | solution.py:381
  21.6 0.0 collective-permute-done.4.other_ref
  21.6 0.2 collective-permute-done.5.pair_ref
  21.8 1.0 %image_kernel.1 = (f32[3,2,8,1024]{3,2,1,0:T(8,128)S(1)}, f32[3,2,8,1024]{3,2,1,0:T(8,128)S(1)}, f32[32,1,128]{2,1,0:T(1,128)S(1)}) custom-call(f32[3,2,8,1024]{3,2,1,0:T(8,128)S(1)} %get-tuple-element.16.b_ref, f32[3,2,8,1024]{3,2,1,0:T(8,128)S(1)} %get-tuple-element.24.v_ref, f32[2,3,8,1024]{3,2,1,0:T(8,128)S(1)} %halo_kernel.1.halo_ref, ...), custom_call_target="tpu_custom_call" | custom-call | flops 268435456 | bytes 1198428 | tf_op jit(solution)/shard_map/image_kernel/pallas_call | solution.py:381
  22.9 12.4 %all_to_all.5.gram_ref = f32[32,1,128]{2,1,0:T(1,128)S(1)} all-to-all(f32[32,1,128]{2,1,0:T(1,128)S(1)} %get-tuple-element.27), channel_id=1, replica_groups=mesh['inline'=8,'col'=4] {'inline','col'}, dimensions={0} | all-to-all | bytes 32768 | tf_op jit(solution)/shard_map/all_to_all | solution.py:450
  35.2 0.9 %finish_kernel.1 = (f32[3,2,8,1024]{3,2,1,0:T(8,128)}, f32[3,2,8,1024]{3,2,1,0:T(8,128)}) custom-call(f32[32,1,128]{2,1,0:T(1,128)S(1)} %all_to_all.5.gram_ref, f32[3,2,8,1024]{3,2,1,0:T(8,128)S(1)} %get-tuple-element.16.b_ref, f32[3,2,8,1024]{3,2,1,0:T(8,128)S(1)} %get-tuple-element.28.one_ref, f32[3,2,8,1024]{3,2,1,0:T(8,128)S(1)} %get-tuple-element.29.two_ref), custom_call_target="tpu_custom_call" | custom-call | flops 393216 | bytes 999424 | tf_op jit(solution)/shard_map/finish_kernel/pallas_call | solution.py:381
Async XLA Ops:
  2.1 6.7 %collective-permute-start.1 = (f32[25,8,128]{2,1,0:T(8,128)S(1)}, f32[25,8,128]{2,1,0:T(8,128)S(1)}, u32[]{:S(2)}, u32[]{:S(2)}) collective-permute-start(f32[25,8,128]{2,1,0:T(8,128)S(1)} %get-tuple-element.23), channel_id=1, source_target_pairs={{0,4},{4,0},{8,12},{12,8},{16,20},{20,16},{24,28},{28,24},{1,5},{5... | collective-permute-start | bytes 307208 | tf_op jit(solution)/shard_map/ppermute | solution.py:395
  5.1 7.7 %collective-permute-start = (f32[25,8,128]{2,1,0:T(8,128)S(1)}, f32[25,8,128]{2,1,0:T(8,128)S(1)}, u32[]{:S(2)}, u32[]{:S(2)}) collective-permute-start(f32[25,8,128]{2,1,0:T(8,128)S(1)} %get-tuple-element.22), channel_id=1, source_target_pairs={{0,4},{4,0},{8,12},{12,8},{16,20},{20,16},{24,28},{28,24},{1,5},{5... | collective-permute-start | bytes 307208 | tf_op jit(solution)/shard_map/ppermute | solution.py:395
  8.7 8.3 %collective-permute-start.2 = (f32[25,8,128]{2,1,0:T(8,128)S(1)}, f32[25,8,128]{2,1,0:T(8,128)S(1)}, u32[]{:S(2)}, u32[]{:S(2)}) collective-permute-start(f32[25,8,128]{2,1,0:T(8,128)S(1)} %collective-permute-done.1.far_ref), channel_id=1, source_target_pairs={{0,8},{8,16},{12,4},{16,24},{20,12},{28,20},{1,9},{9,17},{13,5},{1... | collective-permute-start | bytes 307208 | tf_op jit(solution)/shard_map/ppermute | solution.py:401
  12.8 8.1 %collective-permute-start.3 = (f32[25,8,128]{2,1,0:T(8,128)S(1)}, f32[25,8,128]{2,1,0:T(8,128)S(1)}, u32[]{:S(2)}, u32[]{:S(2)}) collective-permute-start(f32[25,8,128]{2,1,0:T(8,128)S(1)} %collective-permute-done.near_ref), channel_id=1, source_target_pairs={{0,8},{8,16},{12,4},{16,24},{20,12},{28,20},{1,9},{9,17},{13,5},{1... | collective-permute-start | bytes 307208 | tf_op jit(solution)/shard_map/ppermute | solution.py:401
  17.3 4.4 %collective-permute-start.4 = (f32[18,1024]{1,0:T(8,128)S(1)}, f32[18,1024]{1,0:T(8,128)S(1)}, u32[]{:S(2)}, u32[]{:S(2)}) collective-permute-start(f32[18,1024]{1,0:T(8,128)S(1)} %get-tuple-element.25), channel_id=1, source_target_pairs={{1,2},{2,1},{5,6},{6,5},{9,10},{10,9},{13,14},{14,13},{17,18},{18,... | collective-permute-start | bytes 221192 | tf_op jit(solution)/shard_map/ppermute | solution.py:395
  17.9 3.9 %collective-permute-start.5 = (f32[18,1024]{1,0:T(8,128)S(1)}, f32[18,1024]{1,0:T(8,128)S(1)}, u32[]{:S(2)}, u32[]{:S(2)}) collective-permute-start(f32[18,1024]{1,0:T(8,128)S(1)} %get-tuple-element.26), channel_id=1, source_target_pairs={{0,1},{1,0},{2,3},{3,2},{4,5},{5,4},{6,7},{7,6},{8,9},{9,8},{10,11... | collective-permute-start | bytes 221192 | tf_op jit(solution)/shard_map/ppermute | solution.py:395

commit v10 on v8

--- a/solution.py
+++ b/solution.py
@@ -237,7 +237,7 @@
     return lax.axis_index(axis) % 2 == 0
 
 
-def rows_kernel(b_ref, p_ref, next_ref, mate_ref, strength_ref, v_ref, pair_ref, other_ref):
+def rows_kernel(b_ref, p_ref, mate_ref, next_ref, strength_ref, v_ref, pair_ref, other_ref):
     contrasts, rows, traces, _ = b_ref.shape
     first_col = starts_pair("col")
     for c in range(contrasts):
@@ -373,15 +373,15 @@
         [pltpu.VMEM(seismic.shape, seismic.dtype), padded, pltpu.SemaphoreType.DMA((6,))],
         [HBM] * 6,
     )
+    mate = swap("inline", mate, 0)
     other = swap("inline", other, 1)
-    mate = swap("inline", mate, 0)
     part, part_mate, part_other = call(
         part_kernel, (field, row, row), (b, *kept), 2 * work, [padded]
     )
     part_other = swap("inline", part_other, 1)
     part_mate = swap("inline", part_mate, 0)
     image, col_pair, col_other = call(
-        rows_kernel, (field, side, side), (b, part, other, mate, kept[-1]), 4 * field.size
+        rows_kernel, (field, side, side), (b, part, mate, other, kept[-1]), 4 * field.size
     )
     col_other = swap("col", col_other, 1)
     col_pair = swap("col", col_pair, 0)

time: 35.4 us -> 34.4 us (0.972)
  starting transfers between devices: 15.1 us -> 13.9 us
    ppermute x6, starting transfers between devices: 15.1 us -> 13.9 us  [swap(): lax.ppermute(value, axis, [(i + d, i + 1 - d) for i in starts for d in (0...]
where the time goes in v10:
time: 34.4 us; the launch traced here: 34.1 us
  blocking collectives  14.2 us (41%)
  starting transfers between devices  13.9 us (40%)
  Pallas kernels  4.39 us (13%)
  waiting for transfers between devices  0.95 us (3%)
  between operations  0.68 us (2%)
    all_to_all x1, blocking collectives, shards(): gram = lax.all_to_all(gram, axes, 0, 0)  14.2 us
    ppermute x6, starting transfers between devices, swap(): lax.ppermute(value, axis, [(i + d, i + 1 - d) for i in starts for d in (0...  13.9 us
    pallas_call x5, Pallas kernels, call(): pl.pallas_call(kernel, out_shape=outs, in_specs=[VMEM] * len(ins) if plac...  4.39 us
    ppermute x6, waiting for transfers between devices, swap(): lax.ppermute(value, axis, [(i + d, i + 1 - d) for i in starts for d in (0...  0.95 us
  transfers between devices with their start and end apart: 6, of which 1 were waited for; matrix products, arithmetic and copies ran while one was open for 0% of the time, Pallas kernels for 3%

profile of v10, /device:TPU:0, one launch (start us, length us, event | category | flops | bytes accessed | tf_op | source)
XLA Modules:
  0.0 34.1 jit_solution(6161574817141708402)
XLA Ops:
  0.6 1.4 %start_kernel.1 = (f32[3,2,8,1024]{3,2,1,0:T(8,128)S(1)}, f32[3,8,1024]{2,1,0:T(8,128)S(1)}, f32[3,8,1024]{2,1,0:T(8,128)S(1)}, s32[4,2,8]{2,1,0:T(2,128)S(1)}, ...) custom-call(bf16[4,2,8,1024]{3,2,1,0:T(8,128)(2,1)} %seis_hbm.1, ...), custom_call_target="tpu_custom_call" | custom-call | flops 134217728 | bytes 627384 | tf_op jit(solution)/shard_map/start_kernel/pallas_call | solution.py:339
  2.1 3.0 %collective-permute-start = (f32[3,8,1024]{2,1,0:T(8,128)S(1)}, f32[3,8,1024]{2,1,0:T(8,128)S(1)}, u32[]{:S(2)}, u32[]{:S(2)}) collective-permute-start(f32[3,8,1024]{2,1,0:T(8,128)S(1)} %get-tuple-element.26), channel_id=1, source_target_pairs={{0,4},{4,0},{8,12},{12,8},{16,20},{20,16},{24,28},{28,24},{1,5},{5... | collective-permute-start | bytes 294920 | tf_op jit(solution)/shard_map/ppermute | solution.py:353
  5.1 0.7 %collective-permute-start.1 = (f32[3,8,1024]{2,1,0:T(8,128)S(1)}, f32[3,8,1024]{2,1,0:T(8,128)S(1)}, u32[]{:S(2)}, u32[]{:S(2)}) collective-permute-start(f32[3,8,1024]{2,1,0:T(8,128)S(1)} %get-tuple-element.27), channel_id=1, source_target_pairs={{4,8},{8,4},{12,16},{16,12},{20,24},{24,20},{5,9},{9,5},{13,17},{1... | collective-permute-start | bytes 294920 | tf_op jit(solution)/shard_map/ppermute | solution.py:353
  5.7 0.8 %part_kernel.1 = (f32[3,2,8,1024]{3,2,1,0:T(8,128)S(1)}, f32[3,8,1024]{2,1,0:T(8,128)S(1)}, f32[3,8,1024]{2,1,0:T(8,128)S(1)}) custom-call(f32[3,2,8,1024]{3,2,1,0:T(8,128)S(1)} %get-tuple-element.19.b_ref, s32[4,2,8]{2,1,0:T(2,128)S(1)} %get-tuple-element.20.valid_ref, f32[3,4,1024]{2,1,0:T(4,128)S(1)} %get-tuple-element.21.avo_ref, ...), custom_call_target="tpu_custom_call" | custom-call | flops 268435456 | bytes 641372 | tf_op jit(solution)/shard_map/part_kernel/pallas_call | solution.py:339
  6.6 0.7 %collective-permute-start.2 = (f32[3,8,1024]{2,1,0:T(8,128)S(1)}, f32[3,8,1024]{2,1,0:T(8,128)S(1)}, u32[]{:S(2)}, u32[]{:S(2)}) collective-permute-start(f32[3,8,1024]{2,1,0:T(8,128)S(1)} %get-tuple-element.29), channel_id=1, source_target_pairs={{4,8},{8,4},{12,16},{16,12},{20,24},{24,20},{5,9},{9,5},{13,17},{1... | collective-permute-start | bytes 294920 | tf_op jit(solution)/shard_map/ppermute | solution.py:353
  7.2 5.6 %collective-permute-start.3 = (f32[3,8,1024]{2,1,0:T(8,128)S(1)}, f32[3,8,1024]{2,1,0:T(8,128)S(1)}, u32[]{:S(2)}, u32[]{:S(2)}) collective-permute-start(f32[3,8,1024]{2,1,0:T(8,128)S(1)} %get-tuple-element.30), channel_id=1, source_target_pairs={{0,4},{4,0},{8,12},{12,8},{16,20},{20,16},{24,28},{28,24},{1,5},{5... | collective-permute-start | bytes 294920 | tf_op jit(solution)/shard_map/ppermute | solution.py:353
  12.8 0.0 collective-permute-done.mate_ref
  12.8 0.0 collective-permute-done.1.next_ref
  12.8 0.2 rows_kernel.1
  13.0 0.7 %collective-permute-start.4 = (f32[18,1024]{1,0:T(8,128)S(1)}, f32[18,1024]{1,0:T(8,128)S(1)}, u32[]{:S(2)}, u32[]{:S(2)}) collective-permute-start(f32[18,1024]{1,0:T(8,128)S(1)} %get-tuple-element.31), channel_id=1, source_target_pairs={{1,2},{2,1},{5,6},{6,5},{9,10},{10,9},{13,14},{14,13},{17,18},{18,... | collective-permute-start | bytes 221192 | tf_op jit(solution)/shard_map/ppermute | solution.py:353
  13.7 3.4 %collective-permute-start.5 = (f32[18,1024]{1,0:T(8,128)S(1)}, f32[18,1024]{1,0:T(8,128)S(1)}, u32[]{:S(2)}, u32[]{:S(2)}) collective-permute-start(f32[18,1024]{1,0:T(8,128)S(1)} %get-tuple-element.32), channel_id=1, source_target_pairs={{0,1},{1,0},{2,3},{3,2},{4,5},{5,4},{6,7},{7,6},{8,9},{9,8},{10,11... | collective-permute-start | bytes 221192 | tf_op jit(solution)/shard_map/ppermute | solution.py:353
  17.0 0.0 collective-permute-done.2.next_ref
  17.1 0.0 collective-permute-done.3.mate_ref
  17.1 0.0 collective-permute-done.4.other_ref
  17.1 0.9 %collective-permute-done.5.pair_ref = f32[18,1024]{1,0:T(8,128)S(1)} collective-permute-done((f32[18,1024]{1,0:T(8,128)S(1)}, f32[18,1024]{1,0:T(8,128)S(1)}, u32[]{:S(2)}, u32[]{:S(2)}) %collective-permute-start.5) | collective-permute-done | bytes 73760 | tf_op jit(solution)/shard_map/ppermute | solution.py:353
  18.0 1.0 %image_kernel.1 = (f32[3,2,8,1024]{3,2,1,0:T(8,128)S(1)}, f32[3,2,8,1024]{3,2,1,0:T(8,128)S(1)}, f32[32,1,128]{2,1,0:T(1,128)S(1)}) custom-call(f32[3,2,8,1024]{3,2,1,0:T(8,128)S(1)} %get-tuple-element.19.b_ref, f32[3,2,8,1024]{3,2,1,0:T(8,128)S(1)} %get-tuple-element.28.v_ref, f32[3,8,1024]{2,1,0:T(8,128)S(1)} %collective-permute-done.2.next_ref, ...), custom_call_target="tpu_custom_call" | custom-call | flops 268435456 | bytes 1198428 | tf_op jit(solution)/shard_map/image_kernel/pallas_call | solution.py:339
  19.0 14.2 %all_to_all.5.gram_ref = f32[32,1,128]{2,1,0:T(1,128)S(1)} all-to-all(f32[32,1,128]{2,1,0:T(1,128)S(1)} %get-tuple-element.33), channel_id=1, replica_groups=mesh['inline'=8,'col'=4] {'inline','col'}, dimensions={0} | all-to-all | bytes 32768 | tf_op jit(solution)/shard_map/all_to_all | solution.py:396
  33.2 0.9 %finish_kernel.1 = (f32[3,2,8,1024]{3,2,1,0:T(8,128)}, f32[3,2,8,1024]{3,2,1,0:T(8,128)}) custom-call(f32[32,1,128]{2,1,0:T(1,128)S(1)} %all_to_all.5.gram_ref, f32[3,2,8,1024]{3,2,1,0:T(8,128)S(1)} %get-tuple-element.19.b_ref, f32[3,2,8,1024]{3,2,1,0:T(8,128)S(1)} %get-tuple-element.34.one_ref, f32[3,2,8,1024]{3,2,1,0:T(8,128)S(1)} %get-tuple-element.35.two_ref), custom_call_target="tpu_custom_call" | custom-call | flops 393216 | bytes 999424 | tf_op jit(solution)/shard_map/finish_kernel/pallas_call | solution.py:339
Async XLA Ops:
  2.1 10.8 %collective-permute-start = (f32[3,8,1024]{2,1,0:T(8,128)S(1)}, f32[3,8,1024]{2,1,0:T(8,128)S(1)}, u32[]{:S(2)}, u32[]{:S(2)}) collective-permute-start(f32[3,8,1024]{2,1,0:T(8,128)S(1)} %get-tuple-element.26), channel_id=1, source_target_pairs={{0,4},{4,0},{8,12},{12,8},{16,20},{20,16},{24,28},{28,24},{1,5},{5... | collective-permute-start | bytes 294920 | tf_op jit(solution)/shard_map/ppermute | solution.py:353
  5.1 7.8 %collective-permute-start.1 = (f32[3,8,1024]{2,1,0:T(8,128)S(1)}, f32[3,8,1024]{2,1,0:T(8,128)S(1)}, u32[]{:S(2)}, u32[]{:S(2)}) collective-permute-start(f32[3,8,1024]{2,1,0:T(8,128)S(1)} %get-tuple-element.27), channel_id=1, source_target_pairs={{4,8},{8,4},{12,16},{16,12},{20,24},{24,20},{5,9},{9,5},{13,17},{1... | collective-permute-start | bytes 294920 | tf_op jit(solution)/shard_map/ppermute | solution.py:353
  6.6 10.5 %collective-permute-start.2 = (f32[3,8,1024]{2,1,0:T(8,128)S(1)}, f32[3,8,1024]{2,1,0:T(8,128)S(1)}, u32[]{:S(2)}, u32[]{:S(2)}) collective-permute-start(f32[3,8,1024]{2,1,0:T(8,128)S(1)} %get-tuple-element.29), channel_id=1, source_target_pairs={{4,8},{8,4},{12,16},{16,12},{20,24},{24,20},{5,9},{9,5},{13,17},{1... | collective-permute-start | bytes 294920 | tf_op jit(solution)/shard_map/ppermute | solution.py:353
  7.2 9.8 %collective-permute-start.3 = (f32[3,8,1024]{2,1,0:T(8,128)S(1)}, f32[3,8,1024]{2,1,0:T(8,128)S(1)}, u32[]{:S(2)}, u32[]{:S(2)}) collective-permute-start(f32[3,8,1024]{2,1,0:T(8,128)S(1)} %get-tuple-element.30), channel_id=1, source_target_pairs={{0,4},{4,0},{8,12},{12,8},{16,20},{20,16},{24,28},{28,24},{1,5},{5... | collective-permute-start | bytes 294920 | tf_op jit(solution)/shard_map/ppermute | solution.py:353
  13.0 4.0 %collective-permute-start.4 = (f32[18,1024]{1,0:T(8,128)S(1)}, f32[18,1024]{1,0:T(8,128)S(1)}, u32[]{:S(2)}, u32[]{:S(2)}) collective-permute-start(f32[18,1024]{1,0:T(8,128)S(1)} %get-tuple-element.31), channel_id=1, source_target_pairs={{1,2},{2,1},{5,6},{6,5},{9,10},{10,9},{13,14},{14,13},{17,18},{18,... | collective-permute-start | bytes 221192 | tf_op jit(solution)/shard_map/ppermute | solution.py:353
  13.7 4.3 %collective-permute-start.5 = (f32[18,1024]{1,0:T(8,128)S(1)}, f32[18,1024]{1,0:T(8,128)S(1)}, u32[]{:S(2)}, u32[]{:S(2)}) collective-permute-start(f32[18,1024]{1,0:T(8,128)S(1)} %get-tuple-element.32), channel_id=1, source_target_pairs={{0,1},{1,0},{2,3},{3,2},{4,5},{5,4},{6,7},{7,6},{8,9},{9,8},{10,11... | collective-permute-start | bytes 221192 | tf_op jit(solution)/shard_map/ppermute | solution.py:353

commit v11 on v10

--- a/solution.py
+++ b/solution.py
@@ -393,7 +393,8 @@
         2 * work,
         [padded],
     )
-    gram = lax.all_to_all(gram, axes, 0, 0)
+    group = list(range(lax.axis_size(axes)))[::-1]
+    gram = lax.all_to_all(gram, axes, 0, 0, axis_index_groups=[group])
     return tuple(call(finish_kernel, (field, field), (gram, b, one, two), 8 * field.size))
 
 

time: 34.4 us -> 34.3 us (level)
  no operation moved by 1% of the time
where the time goes in v11:
time: 34.3 us; the launch traced here: 34.1 us
  blocking collectives  14.2 us (41%)
  starting transfers between devices  13.9 us (41%)
  Pallas kernels  4.39 us (13%)
  waiting for transfers between devices  0.95 us (3%)
  between operations  0.68 us (2%)
    all_to_all x1, blocking collectives, shards(): gram = lax.all_to_all(gram, axes, 0, 0, axis_index_groups=[group])  14.2 us
    ppermute x6, starting transfers between devices, swap(): lax.ppermute(value, axis, [(i + d, i + 1 - d) for i in starts for d in (0...  13.9 us
    pallas_call x5, Pallas kernels, call(): pl.pallas_call(kernel, out_shape=outs, in_specs=[VMEM] * len(ins) if plac...  4.39 us
    ppermute x6, waiting for transfers between devices, swap(): lax.ppermute(value, axis, [(i + d, i + 1 - d) for i in starts for d in (0...  0.95 us
  transfers between devices with their start and end apart: 6, of which 1 were waited for; matrix products, arithmetic and copies ran while one was open for 0% of the time, Pallas kernels for 3%

profile of v11, /device:TPU:0, one launch (start us, length us, event | category | flops | bytes accessed | tf_op | source)
XLA Modules:
  0.0 34.1 jit_solution(6555984755740569772)
XLA Ops:
  0.6 1.4 %start_kernel.1 = (f32[3,2,8,1024]{3,2,1,0:T(8,128)S(1)}, f32[3,8,1024]{2,1,0:T(8,128)S(1)}, f32[3,8,1024]{2,1,0:T(8,128)S(1)}, s32[4,2,8]{2,1,0:T(2,128)S(1)}, ...) custom-call(bf16[4,2,8,1024]{3,2,1,0:T(8,128)(2,1)} %seis_hbm.1, ...), custom_call_target="tpu_custom_call" | custom-call | flops 134217728 | bytes 627384 | tf_op jit(solution)/shard_map/start_kernel/pallas_call | solution.py:339
  2.1 3.0 %collective-permute-start = (f32[3,8,1024]{2,1,0:T(8,128)S(1)}, f32[3,8,1024]{2,1,0:T(8,128)S(1)}, u32[]{:S(2)}, u32[]{:S(2)}) collective-permute-start(f32[3,8,1024]{2,1,0:T(8,128)S(1)} %get-tuple-element.26), channel_id=1, source_target_pairs={{0,4},{4,0},{8,12},{12,8},{16,20},{20,16},{24,28},{28,24},{1,5},{5... | collective-permute-start | bytes 294920 | tf_op jit(solution)/shard_map/ppermute | solution.py:353
  5.1 0.7 %collective-permute-start.1 = (f32[3,8,1024]{2,1,0:T(8,128)S(1)}, f32[3,8,1024]{2,1,0:T(8,128)S(1)}, u32[]{:S(2)}, u32[]{:S(2)}) collective-permute-start(f32[3,8,1024]{2,1,0:T(8,128)S(1)} %get-tuple-element.27), channel_id=1, source_target_pairs={{4,8},{8,4},{12,16},{16,12},{20,24},{24,20},{5,9},{9,5},{13,17},{1... | collective-permute-start | bytes 294920 | tf_op jit(solution)/shard_map/ppermute | solution.py:353
  5.7 0.8 %part_kernel.1 = (f32[3,2,8,1024]{3,2,1,0:T(8,128)S(1)}, f32[3,8,1024]{2,1,0:T(8,128)S(1)}, f32[3,8,1024]{2,1,0:T(8,128)S(1)}) custom-call(f32[3,2,8,1024]{3,2,1,0:T(8,128)S(1)} %get-tuple-element.19.b_ref, s32[4,2,8]{2,1,0:T(2,128)S(1)} %get-tuple-element.20.valid_ref, f32[3,4,1024]{2,1,0:T(4,128)S(1)} %get-tuple-element.21.avo_ref, ...), custom_call_target="tpu_custom_call" | custom-call | flops 268435456 | bytes 641372 | tf_op jit(solution)/shard_map/part_kernel/pallas_call | solution.py:339
  6.6 0.7 %collective-permute-start.2 = (f32[3,8,1024]{2,1,0:T(8,128)S(1)}, f32[3,8,1024]{2,1,0:T(8,128)S(1)}, u32[]{:S(2)}, u32[]{:S(2)}) collective-permute-start(f32[3,8,1024]{2,1,0:T(8,128)S(1)} %get-tuple-element.29), channel_id=1, source_target_pairs={{4,8},{8,4},{12,16},{16,12},{20,24},{24,20},{5,9},{9,5},{13,17},{1... | collective-permute-start | bytes 294920 | tf_op jit(solution)/shard_map/ppermute | solution.py:353
  7.2 5.6 %collective-permute-start.3 = (f32[3,8,1024]{2,1,0:T(8,128)S(1)}, f32[3,8,1024]{2,1,0:T(8,128)S(1)}, u32[]{:S(2)}, u32[]{:S(2)}) collective-permute-start(f32[3,8,1024]{2,1,0:T(8,128)S(1)} %get-tuple-element.30), channel_id=1, source_target_pairs={{0,4},{4,0},{8,12},{12,8},{16,20},{20,16},{24,28},{28,24},{1,5},{5... | collective-permute-start | bytes 294920 | tf_op jit(solution)/shard_map/ppermute | solution.py:353
  12.8 0.0 collective-permute-done.mate_ref
  12.8 0.0 collective-permute-done.1.next_ref
  12.8 0.2 rows_kernel.1
  13.0 0.7 %collective-permute-start.4 = (f32[18,1024]{1,0:T(8,128)S(1)}, f32[18,1024]{1,0:T(8,128)S(1)}, u32[]{:S(2)}, u32[]{:S(2)}) collective-permute-start(f32[18,1024]{1,0:T(8,128)S(1)} %get-tuple-element.31), channel_id=1, source_target_pairs={{1,2},{2,1},{5,6},{6,5},{9,10},{10,9},{13,14},{14,13},{17,18},{18,... | collective-permute-start | bytes 221192 | tf_op jit(solution)/shard_map/ppermute | solution.py:353
  13.7 3.4 %collective-permute-start.5 = (f32[18,1024]{1,0:T(8,128)S(1)}, f32[18,1024]{1,0:T(8,128)S(1)}, u32[]{:S(2)}, u32[]{:S(2)}) collective-permute-start(f32[18,1024]{1,0:T(8,128)S(1)} %get-tuple-element.32), channel_id=1, source_target_pairs={{0,1},{1,0},{2,3},{3,2},{4,5},{5,4},{6,7},{7,6},{8,9},{9,8},{10,11... | collective-permute-start | bytes 221192 | tf_op jit(solution)/shard_map/ppermute | solution.py:353
  17.0 0.0 collective-permute-done.2.next_ref
  17.1 0.0 collective-permute-done.3.mate_ref
  17.1 0.0 collective-permute-done.4.other_ref
  17.1 0.9 %collective-permute-done.5.pair_ref = f32[18,1024]{1,0:T(8,128)S(1)} collective-permute-done((f32[18,1024]{1,0:T(8,128)S(1)}, f32[18,1024]{1,0:T(8,128)S(1)}, u32[]{:S(2)}, u32[]{:S(2)}) %collective-permute-start.5) | collective-permute-done | bytes 73760 | tf_op jit(solution)/shard_map/ppermute | solution.py:353
  18.0 1.0 %image_kernel.1 = (f32[3,2,8,1024]{3,2,1,0:T(8,128)S(1)}, f32[3,2,8,1024]{3,2,1,0:T(8,128)S(1)}, f32[32,1,128]{2,1,0:T(1,128)S(1)}) custom-call(f32[3,2,8,1024]{3,2,1,0:T(8,128)S(1)} %get-tuple-element.19.b_ref, f32[3,2,8,1024]{3,2,1,0:T(8,128)S(1)} %get-tuple-element.28.v_ref, f32[3,8,1024]{2,1,0:T(8,128)S(1)} %collective-permute-done.2.next_ref, ...), custom_call_target="tpu_custom_call" | custom-call | flops 268435456 | bytes 1198428 | tf_op jit(solution)/shard_map/image_kernel/pallas_call | solution.py:339
  19.0 14.2 %all_to_all.5.gram_ref = f32[32,1,128]{2,1,0:T(1,128)S(1)} all-to-all(f32[32,1,128]{2,1,0:T(1,128)S(1)} %get-tuple-element.33), channel_id=1, replica_groups={{31,30,29,28,27,26,25,24,23,22,21,20,19,18,17,16,15,14,13,12,11,10,9,8,..., dimensions={0} | all-to-all | bytes 32768 | tf_op jit(solution)/shard_map/all_to_all | solution.py:397
  33.2 0.9 %finish_kernel.1 = (f32[3,2,8,1024]{3,2,1,0:T(8,128)}, f32[3,2,8,1024]{3,2,1,0:T(8,128)}) custom-call(f32[32,1,128]{2,1,0:T(1,128)S(1)} %all_to_all.5.gram_ref, f32[3,2,8,1024]{3,2,1,0:T(8,128)S(1)} %get-tuple-element.19.b_ref, f32[3,2,8,1024]{3,2,1,0:T(8,128)S(1)} %get-tuple-element.34.one_ref, f32[3,2,8,1024]{3,2,1,0:T(8,128)S(1)} %get-tuple-element.35.two_ref), custom_call_target="tpu_custom_call" | custom-call | flops 393216 | bytes 999424 | tf_op jit(solution)/shard_map/finish_kernel/pallas_call | solution.py:339
Async XLA Ops:
  2.1 10.8 %collective-permute-start = (f32[3,8,1024]{2,1,0:T(8,128)S(1)}, f32[3,8,1024]{2,1,0:T(8,128)S(1)}, u32[]{:S(2)}, u32[]{:S(2)}) collective-permute-start(f32[3,8,1024]{2,1,0:T(8,128)S(1)} %get-tuple-element.26), channel_id=1, source_target_pairs={{0,4},{4,0},{8,12},{12,8},{16,20},{20,16},{24,28},{28,24},{1,5},{5... | collective-permute-start | bytes 294920 | tf_op jit(solution)/shard_map/ppermute | solution.py:353
  5.1 7.8 %collective-permute-start.1 = (f32[3,8,1024]{2,1,0:T(8,128)S(1)}, f32[3,8,1024]{2,1,0:T(8,128)S(1)}, u32[]{:S(2)}, u32[]{:S(2)}) collective-permute-start(f32[3,8,1024]{2,1,0:T(8,128)S(1)} %get-tuple-element.27), channel_id=1, source_target_pairs={{4,8},{8,4},{12,16},{16,12},{20,24},{24,20},{5,9},{9,5},{13,17},{1... | collective-permute-start | bytes 294920 | tf_op jit(solution)/shard_map/ppermute | solution.py:353
  6.6 10.5 %collective-permute-start.2 = (f32[3,8,1024]{2,1,0:T(8,128)S(1)}, f32[3,8,1024]{2,1,0:T(8,128)S(1)}, u32[]{:S(2)}, u32[]{:S(2)}) collective-permute-start(f32[3,8,1024]{2,1,0:T(8,128)S(1)} %get-tuple-element.29), channel_id=1, source_target_pairs={{4,8},{8,4},{12,16},{16,12},{20,24},{24,20},{5,9},{9,5},{13,17},{1... | collective-permute-start | bytes 294920 | tf_op jit(solution)/shard_map/ppermute | solution.py:353
  7.2 9.8 %collective-permute-start.3 = (f32[3,8,1024]{2,1,0:T(8,128)S(1)}, f32[3,8,1024]{2,1,0:T(8,128)S(1)}, u32[]{:S(2)}, u32[]{:S(2)}) collective-permute-start(f32[3,8,1024]{2,1,0:T(8,128)S(1)} %get-tuple-element.30), channel_id=1, source_target_pairs={{0,4},{4,0},{8,12},{12,8},{16,20},{20,16},{24,28},{28,24},{1,5},{5... | collective-permute-start | bytes 294920 | tf_op jit(solution)/shard_map/ppermute | solution.py:353
  13.0 4.0 %collective-permute-start.4 = (f32[18,1024]{1,0:T(8,128)S(1)}, f32[18,1024]{1,0:T(8,128)S(1)}, u32[]{:S(2)}, u32[]{:S(2)}) collective-permute-start(f32[18,1024]{1,0:T(8,128)S(1)} %get-tuple-element.31), channel_id=1, source_target_pairs={{1,2},{2,1},{5,6},{6,5},{9,10},{10,9},{13,14},{14,13},{17,18},{18,... | collective-permute-start | bytes 221192 | tf_op jit(solution)/shard_map/ppermute | solution.py:353
  13.7 4.3 %collective-permute-start.5 = (f32[18,1024]{1,0:T(8,128)S(1)}, f32[18,1024]{1,0:T(8,128)S(1)}, u32[]{:S(2)}, u32[]{:S(2)}) collective-permute-start(f32[18,1024]{1,0:T(8,128)S(1)} %get-tuple-element.32), channel_id=1, source_target_pairs={{0,1},{1,0},{2,3},{3,2},{4,5},{5,4},{6,7},{7,6},{8,9},{9,8},{10,11... | collective-permute-start | bytes 221192 | tf_op jit(solution)/shard_map/ppermute | solution.py:353

commit v12 on v9

--- a/solution.py
+++ b/solution.py
@@ -224,7 +224,7 @@
 
 
 def halo_kernel(
-    b_ref, near_ref, far_ref, near_next_ref, far_next_ref, avo_ref, taps_ref, strength_ref,
+    b_ref, near_ref, near_next_ref, far_next_ref, far_ref, avo_ref, taps_ref, strength_ref,
     out_ref, padded,
 ):
     contrasts, rows, traces, samples = b_ref.shape
@@ -422,10 +422,10 @@
         [HBM] * 6,
     )
     avo, taps, strength = kept[1], kept[2], kept[-1]
+    near = swap("inline", near, 0)
+    near_next = swap("inline", far, 1)
+    far_next = hand_on("inline", near)
     far = swap("inline", far, 0)
-    near = swap("inline", near, 0)
-    near_next = hand_on("inline", far)
-    far_next = hand_on("inline", near)
     (part,) = call(part_kernel, (field,), (b, *kept), 2 * work, [padded])
     image, col_pair, col_other = call(
         rows_kernel, (field, side, side), (b, part, near, near_next, strength), 4 * field.size
@@ -435,7 +435,7 @@
     (halo,) = call(
         halo_kernel,
         (shape(2, contrasts, traces, samples),),
-        (b, near, far, near_next, far_next, avo, taps, strength),
+        (b, near, near_next, far_next, far, avo, taps, strength),
         2 * work,
         [padded],
     )

time: 36.4 us -> 33 us (0.907)
  waiting for transfers between devices: 3.78 us -> 0.19 us
  starting transfers between devices: 14.2 us -> 15.1 us
  blocking collectives: 12.4 us -> 11.6 us
    ppermute x4 -> x5, starting transfers between devices: 6.69 us -> 11.6 us  [swap(): lax.ppermute(value, axis, [(i + d, i + 1 - d) for i in starts for d in (0...]
    ppermute x2 -> x1, starting transfers between devices: 7.48 us -> 3.48 us  [hand_on(): lax.ppermute(value, axis, [(i, j) for i, j in steps if 0 <= j < size])]
    ppermute x4 -> x5, waiting for transfers between devices: 3.78 us -> 0.19 us  [swap(): lax.ppermute(value, axis, [(i + d, i + 1 - d) for i in starts for d in (0...]
    all_to_all x1, blocking collectives: 12.4 us -> 11.6 us  [shards(): gram = lax.all_to_all(gram, axes, 0, 0)]
  transfers between devices with their start and end apart: 6 -> 6, of which waited for: 2 -> 1; matrix products, arithmetic and copies ran while one was open for 0% -> 0% of each run, Pallas kernels for 5% -> 5%
where the time goes in v12:
time: 33 us; the launch traced here: 32.7 us
  starting transfers between devices  15.1 us (46%)
  blocking collectives  11.6 us (35%)
  Pallas kernels  5.13 us (16%)
  between operations  0.7 us (2%)
    ppermute x5, starting transfers between devices, swap(): lax.ppermute(value, axis, [(i + d, i + 1 - d) for i in starts for d in (0...  11.6 us
    all_to_all x1, blocking collectives, shards(): gram = lax.all_to_all(gram, axes, 0, 0)  11.6 us
    pallas_call x6, Pallas kernels, call(): pl.pallas_call(kernel, out_shape=outs, in_specs=[VMEM] * len(ins) if plac...  5.13 us
    ppermute x1, starting transfers between devices, hand_on(): lax.ppermute(value, axis, [(i, j) for i, j in steps if 0 <= j < size])  3.48 us
  transfers between devices with their start and end apart: 6, of which 1 were waited for; matrix products, arithmetic and copies ran while one was open for 0% of the time, Pallas kernels for 5%

profile of v12, /device:TPU:0, one launch (start us, length us, event | category | flops | bytes accessed | tf_op | source)
XLA Modules:
  0.0 32.7 jit_solution(13994561546622433388)
XLA Ops:
  0.6 1.4 %start_kernel.1 = (f32[3,2,8,1024]{3,2,1,0:T(8,128)S(1)}, f32[25,8,128]{2,1,0:T(8,128)S(1)}, f32[25,8,128]{2,1,0:T(8,128)S(1)}, s32[4,2,8]{2,1,0:T(2,128)S(1)}, ...) custom-call(bf16[4,2,8,1024]{3,2,1,0:T(8,128)(2,1)} %seis_hbm.1, ...), custom_call_target="tpu_custom_call" | custom-call | flops 134217728 | bytes 635576 | tf_op jit(solution)/shard_map/start_kernel/pallas_call | solution.py:381
  2.1 3.0 %collective-permute-start = (f32[25,8,128]{2,1,0:T(8,128)S(1)}, f32[25,8,128]{2,1,0:T(8,128)S(1)}, u32[]{:S(2)}, u32[]{:S(2)}) collective-permute-start(f32[25,8,128]{2,1,0:T(8,128)S(1)} %get-tuple-element.22), channel_id=1, source_target_pairs={{0,4},{4,0},{8,12},{12,8},{16,20},{20,16},{24,28},{28,24},{1,5},{5... | collective-permute-start | bytes 307208 | tf_op jit(solution)/shard_map/ppermute | solution.py:395
  5.1 0.7 %collective-permute-start.1 = (f32[25,8,128]{2,1,0:T(8,128)S(1)}, f32[25,8,128]{2,1,0:T(8,128)S(1)}, u32[]{:S(2)}, u32[]{:S(2)}) collective-permute-start(f32[25,8,128]{2,1,0:T(8,128)S(1)} %get-tuple-element.23), channel_id=1, source_target_pairs={{4,8},{8,4},{12,16},{16,12},{20,24},{24,20},{5,9},{9,5},{13,17},{1... | collective-permute-start | bytes 307208 | tf_op jit(solution)/shard_map/ppermute | solution.py:395
  5.7 4.3 %collective-permute-start.3 = (f32[25,8,128]{2,1,0:T(8,128)S(1)}, f32[25,8,128]{2,1,0:T(8,128)S(1)}, u32[]{:S(2)}, u32[]{:S(2)}) collective-permute-start(f32[25,8,128]{2,1,0:T(8,128)S(1)} %get-tuple-element.23), channel_id=1, source_target_pairs={{0,4},{4,0},{8,12},{12,8},{16,20},{20,16},{24,28},{28,24},{1,5},{5... | collective-permute-start | bytes 307208 | tf_op jit(solution)/shard_map/ppermute | solution.py:395
  10.1 0.0 collective-permute-done.near_ref
  10.1 3.5 %collective-permute-start.2 = (f32[25,8,128]{2,1,0:T(8,128)S(1)}, f32[25,8,128]{2,1,0:T(8,128)S(1)}, u32[]{:S(2)}, u32[]{:S(2)}) collective-permute-start(f32[25,8,128]{2,1,0:T(8,128)S(1)} %collective-permute-done.near_ref), channel_id=1, source_target_pairs={{0,8},{8,16},{12,4},{16,24},{20,12},{28,20},{1,9},{9,17},{13,5},{1... | collective-permute-start | bytes 307208 | tf_op jit(solution)/shard_map/ppermute | solution.py:401
  13.6 0.8 %part_kernel.1.p_ref = f32[3,2,8,1024]{3,2,1,0:T(8,128)S(1)} custom-call(f32[3,2,8,1024]{3,2,1,0:T(8,128)S(1)} %get-tuple-element.16.b_ref, s32[4,2,8]{2,1,0:T(2,128)S(1)} %get-tuple-element.17.valid_ref, f32[3,4,1024]{2,1,0:T(4,128)S(1)} %get-tuple-element.18.avo_ref, f32[4,129]{1,0:T(4,128)S(1)} %get-tuple-element.19.taps_ref, ...), custom_call_target="tpu_custom_call" | custom-call | flops 268435456 | bytes 444764 | tf_op jit(solution)/shard_map/part_kernel/pallas_call | solution.py:381
  14.4 0.0 collective-permute-done.1.near_next_ref
  14.4 0.2 rows_kernel.1
  14.6 0.7 %collective-permute-start.4 = (f32[18,1024]{1,0:T(8,128)S(1)}, f32[18,1024]{1,0:T(8,128)S(1)}, u32[]{:S(2)}, u32[]{:S(2)}) collective-permute-start(f32[18,1024]{1,0:T(8,128)S(1)} %get-tuple-element.25), channel_id=1, source_target_pairs={{1,2},{2,1},{5,6},{6,5},{9,10},{10,9},{13,14},{14,13},{17,18},{18,... | collective-permute-start | bytes 221192 | tf_op jit(solution)/shard_map/ppermute | solution.py:395
  15.3 2.9 %collective-permute-start.5 = (f32[18,1024]{1,0:T(8,128)S(1)}, f32[18,1024]{1,0:T(8,128)S(1)}, u32[]{:S(2)}, u32[]{:S(2)}) collective-permute-start(f32[18,1024]{1,0:T(8,128)S(1)} %get-tuple-element.26), channel_id=1, source_target_pairs={{0,1},{1,0},{2,3},{3,2},{4,5},{5,4},{6,7},{7,6},{8,9},{9,8},{10,11... | collective-permute-start | bytes 221192 | tf_op jit(solution)/shard_map/ppermute | solution.py:395
  18.2 0.0 collective-permute-done.3.far_ref
  18.2 0.0 collective-permute-done.2.far_next_ref
  18.2 0.7 %halo_kernel.1.halo_ref = f32[2,3,8,1024]{3,2,1,0:T(8,128)S(1)} custom-call(f32[3,2,8,1024]{3,2,1,0:T(8,128)S(1)} %get-tuple-element.16.b_ref, f32[25,8,128]{2,1,0:T(8,128)S(1)} %collective-permute-done.near_ref, f32[25,8,128]{2,1,0:T(8,128)S(1)} %collective-permute-done.1.near_next_ref, f32[25,8,128]{2,1,0:T(8,128)S(1)} %collective-permute-done.2.far_next_ref, ...), custom_call_target="tpu_custom_call" | custom-call | flops 268435456 | bytes 854044 | tf_op jit(solution)/shard_map/halo_kernel/pallas_call | solution.py:381
  19.0 0.0 collective-permute-done.4.other_ref
  19.0 0.2 collective-permute-done.5.pair_ref
  19.1 1.0 %image_kernel.1 = (f32[3,2,8,1024]{3,2,1,0:T(8,128)S(1)}, f32[3,2,8,1024]{3,2,1,0:T(8,128)S(1)}, f32[32,1,128]{2,1,0:T(1,128)S(1)}) custom-call(f32[3,2,8,1024]{3,2,1,0:T(8,128)S(1)} %get-tuple-element.16.b_ref, f32[3,2,8,1024]{3,2,1,0:T(8,128)S(1)} %get-tuple-element.24.v_ref, f32[2,3,8,1024]{3,2,1,0:T(8,128)S(1)} %halo_kernel.1.halo_ref, ...), custom_call_target="tpu_custom_call" | custom-call | flops 268435456 | bytes 1198428 | tf_op jit(solution)/shard_map/image_kernel/pallas_call | solution.py:381
  20.2 11.6 %all_to_all.5.gram_ref = f32[32,1,128]{2,1,0:T(1,128)S(1)} all-to-all(f32[32,1,128]{2,1,0:T(1,128)S(1)} %get-tuple-element.27), channel_id=1, replica_groups=mesh['inline'=8,'col'=4] {'inline','col'}, dimensions={0} | all-to-all | bytes 32768 | tf_op jit(solution)/shard_map/all_to_all | solution.py:450
  31.8 0.9 %finish_kernel.1 = (f32[3,2,8,1024]{3,2,1,0:T(8,128)}, f32[3,2,8,1024]{3,2,1,0:T(8,128)}) custom-call(f32[32,1,128]{2,1,0:T(1,128)S(1)} %all_to_all.5.gram_ref, f32[3,2,8,1024]{3,2,1,0:T(8,128)S(1)} %get-tuple-element.16.b_ref, f32[3,2,8,1024]{3,2,1,0:T(8,128)S(1)} %get-tuple-element.28.one_ref, f32[3,2,8,1024]{3,2,1,0:T(8,128)S(1)} %get-tuple-element.29.two_ref), custom_call_target="tpu_custom_call" | custom-call | flops 393216 | bytes 999424 | tf_op jit(solution)/shard_map/finish_kernel/pallas_call | solution.py:381
Async XLA Ops:
  2.1 8.0 %collective-permute-start = (f32[25,8,128]{2,1,0:T(8,128)S(1)}, f32[25,8,128]{2,1,0:T(8,128)S(1)}, u32[]{:S(2)}, u32[]{:S(2)}) collective-permute-start(f32[25,8,128]{2,1,0:T(8,128)S(1)} %get-tuple-element.22), channel_id=1, source_target_pairs={{0,4},{4,0},{8,12},{12,8},{16,20},{20,16},{24,28},{28,24},{1,5},{5... | collective-permute-start | bytes 307208 | tf_op jit(solution)/shard_map/ppermute | solution.py:395
  5.1 9.3 %collective-permute-start.1 = (f32[25,8,128]{2,1,0:T(8,128)S(1)}, f32[25,8,128]{2,1,0:T(8,128)S(1)}, u32[]{:S(2)}, u32[]{:S(2)}) collective-permute-start(f32[25,8,128]{2,1,0:T(8,128)S(1)} %get-tuple-element.23), channel_id=1, source_target_pairs={{4,8},{8,4},{12,16},{16,12},{20,24},{24,20},{5,9},{9,5},{13,17},{1... | collective-permute-start | bytes 307208 | tf_op jit(solution)/shard_map/ppermute | solution.py:395
  5.7 12.5 %collective-permute-start.3 = (f32[25,8,128]{2,1,0:T(8,128)S(1)}, f32[25,8,128]{2,1,0:T(8,128)S(1)}, u32[]{:S(2)}, u32[]{:S(2)}) collective-permute-start(f32[25,8,128]{2,1,0:T(8,128)S(1)} %get-tuple-element.23), channel_id=1, source_target_pairs={{0,4},{4,0},{8,12},{12,8},{16,20},{20,16},{24,28},{28,24},{1,5},{5... | collective-permute-start | bytes 307208 | tf_op jit(solution)/shard_map/ppermute | solution.py:395
  10.1 8.1 %collective-permute-start.2 = (f32[25,8,128]{2,1,0:T(8,128)S(1)}, f32[25,8,128]{2,1,0:T(8,128)S(1)}, u32[]{:S(2)}, u32[]{:S(2)}) collective-permute-start(f32[25,8,128]{2,1,0:T(8,128)S(1)} %collective-permute-done.near_ref), channel_id=1, source_target_pairs={{0,8},{8,16},{12,4},{16,24},{20,12},{28,20},{1,9},{9,17},{13,5},{1... | collective-permute-start | bytes 307208 | tf_op jit(solution)/shard_map/ppermute | solution.py:401
  14.6 4.4 %collective-permute-start.4 = (f32[18,1024]{1,0:T(8,128)S(1)}, f32[18,1024]{1,0:T(8,128)S(1)}, u32[]{:S(2)}, u32[]{:S(2)}) collective-permute-start(f32[18,1024]{1,0:T(8,128)S(1)} %get-tuple-element.25), channel_id=1, source_target_pairs={{1,2},{2,1},{5,6},{6,5},{9,10},{10,9},{13,14},{14,13},{17,18},{18,... | collective-permute-start | bytes 221192 | tf_op jit(solution)/shard_map/ppermute | solution.py:395
  15.3 3.9 %collective-permute-start.5 = (f32[18,1024]{1,0:T(8,128)S(1)}, f32[18,1024]{1,0:T(8,128)S(1)}, u32[]{:S(2)}, u32[]{:S(2)}) collective-permute-start(f32[18,1024]{1,0:T(8,128)S(1)} %get-tuple-element.26), channel_id=1, source_target_pairs={{0,1},{1,0},{2,3},{3,2},{4,5},{5,4},{6,7},{7,6},{8,9},{9,8},{10,11... | collective-permute-start | bytes 221192 | tf_op jit(solution)/shard_map/ppermute | solution.py:395

commit v13 on v12

--- a/solution.py
+++ b/solution.py
@@ -201,26 +201,6 @@
     first = starts_pair("inline")
     pair, other = pair_ref[where], next_ref[where]
     return jnp.where(first, other, pair), jnp.where(first, pair, other)
-
-
-def part_kernel(
-    b_ref, valid_ref, avo_ref, taps_ref, prior_ref, strength_ref, p_ref, padded
-):
-    contrasts, rows = b_ref.shape[:2]
-    fill_taps(taps_ref, padded)
-    angles = avo_ref.shape[1]
-    circs = [circulant(padded, a) for a in range(angles)]
-    masks = [trace_columns(valid_ref, a) for a in range(angles)]
-    store_tiles(p_ref, normal(stack_tiles(b_ref), masks, avo_ref, circs))
-    weights = [column(prior_ref[r : r + 1, :]) + 4.0 for r in range(rows)]
-    for c in range(contrasts):
-        strength = strength_ref[:, c : c + 1]
-        for r in range(rows):
-            here = b_ref[c, r]
-            north = b_ref[c, r - 1] if r else None
-            south = b_ref[c, r + 1] if r < rows - 1 else None
-            around = lateral(here, north, south, None, None)
-            p_ref[c, r] = p_ref[c, r] + strength * (weights[r] * here - around)
 
 
 def halo_kernel(
@@ -279,72 +259,136 @@
     return lax.axis_index(axis) % 2 == 0
 
 
-def rows_kernel(b_ref, p_ref, near_ref, near_next_ref, strength_ref, v_ref, pair_ref, other_ref):
+def row_pair(near_ref, next_ref, c, n):
+    tiles = [either_side(near_ref, next_ref, c * n + k) for k in range(n)]
+    return [jnp.concatenate(side, axis=1) for side in zip(*tiles)]
+
+
+def column_kernel(b_ref, near_ref, near_next_ref, valid_ref, prior_ref, pair_ref, other_ref):
     contrasts, rows, traces, samples = b_ref.shape
+    angles = valid_ref.shape[0]
     first_col = starts_pair("col")
-    n = samples // LANES
+    lines = []
+    for c in range(contrasts):
+        above, below = row_pair(near_ref, near_next_ref, c, samples // LANES)
+        own = [b_ref[c, r] for r in range(rows)]
+        lines += [(line[0:1], line[traces - 1 :]) for line in (above, *own, below)]
+        lines += [(line[1:2], line[traces - 2 : traces - 1]) for line in own]
+    for e, (left, right) in enumerate(lines):
+        place = (slice(e % rows, e % rows + 1), pl.ds(e // rows * samples, samples))
+        pair_ref[place] = jnp.where(first_col, right, left)
+        other_ref[place] = jnp.where(first_col, left, right)
+    lane = lax.broadcasted_iota(jnp.int32, (1, LANES), 1)
+    for r in range(rows):
+        notes = []
+        for t in (0, traces - 1):
+            note = jnp.where(lane == angles, prior_ref[r : r + 1, t : t + 1], 0.0)
+            for a in range(angles):
+                note = jnp.where(lane == a, valid_ref[a, r : r + 1, t : t + 1].astype(F32), note)
+            notes.append(note)
+        left, right = notes
+        place = (slice(r, r + 1), pl.ds(len(lines) // rows * samples, LANES))
+        pair_ref[place] = jnp.where(first_col, right, left)
+        other_ref[place] = jnp.where(first_col, left, right)
+
+
+def inner_kernel(
+    b_ref, near_ref, near_next_ref, valid_ref, avo_ref, taps_ref, prior_ref, strength_ref,
+    v_ref, data_ref, padded,
+):
+    contrasts, rows, _, samples = b_ref.shape
+    fill_taps(taps_ref, padded)
+    angles = avo_ref.shape[1]
+    circs = [circulant(padded, a) for a in range(angles)]
+    masks = [trace_columns(valid_ref, a) for a in range(angles)]
+    store_tiles(v_ref, normal(stack_tiles(b_ref), masks, avo_ref, circs))
+    weights = [column(prior_ref[r : r + 1, :]) + 4.0 for r in range(rows)]
     for c in range(contrasts):
         strength = strength_ref[:, c : c + 1]
-        tiles = [either_side(near_ref, near_next_ref, c * n + k) for k in range(n)]
-        above, below = (jnp.concatenate(side, axis=1) for side in zip(*tiles))
-        own = [p_ref[c, r] for r in range(rows)]
-        own[0] = own[0] - strength * above
-        own[-1] = own[-1] - strength * below
-        for r, line in enumerate(own):
-            v_ref[c, r] = line
-        lines = [above, *[b_ref[c, r] for r in range(rows)], below, *own]
-        base = c * len(lines)
-        for e, line in enumerate(lines):
-            left, right = line[0:1, :], line[traces - 1 : traces, :]
-            pair_ref[base + e : base + e + 1, :] = jnp.where(first_col, right, left)
-            other_ref[base + e : base + e + 1, :] = jnp.where(first_col, left, right)
+        above, below = row_pair(near_ref, near_next_ref, c, samples // LANES)
+        for r in range(rows):
+            here = b_ref[c, r]
+            north = b_ref[c, r - 1] if r else above
+            south = b_ref[c, r + 1] if r < rows - 1 else below
+            around = lateral(here, north, south, None, None)
+            v_ref[c, r] = v_ref[c, r] + strength * (weights[r] * here - around)
+    store_tiles(data_ref, normal(stack_tiles(v_ref), masks, avo_ref, circs))
 
 
 def image_kernel(
-    b_ref, v_ref, halo_ref, other_ref, pair_ref,
+    b_ref, v_ref, data_ref, halo_ref, other_ref, pair_ref,
     valid_ref, avo_ref, taps_ref, prior_ref, strength_ref,
     one_ref, two_ref, gram_ref, padded,
 ):
     contrasts, rows, traces, samples = b_ref.shape
-    angles = avo_ref.shape[1]
+    angles, n = avo_ref.shape[1], samples // LANES
     has_left, has_right = inside("col")
     first_col = starts_pair("col")
     left = jnp.where(first_col, other_ref[...], pair_ref[...])
     right = jnp.where(first_col, pair_ref[...], other_ref[...])
     place = lax.broadcasted_iota(jnp.int32, (traces, samples), 0)
     ext = rows + 2
-    stride = ext + rows
-
-    def beside(c, r):
-        edge = c * stride + r
-        west, east = left[edge : edge + 1, :], right[edge : edge + 1, :]
+
+    def trace(side, c, i):
+        e = c * (ext + rows) + i
+        return side[e % rows : e % rows + 1, e // rows * samples : (e // rows + 1) * samples]
+
+    def note(side, r, i):
+        at = contrasts * (ext + rows) // rows * samples + i
+        return side[r : r + 1, at : at + 1]
+
+    def beside(c, i):
+        west, east = trace(left, c, i), trace(right, c, i)
         return jnp.where(place == 0, west, jnp.where(place == traces - 1, east, 0.0))
 
+    def spread(values):
+        total = values[-1]
+        for t in range(traces - 2, -1, -1):
+            total = jnp.where(place[:, : values[0].shape[1]] == t, values[t], total)
+        return total
+
+    fill_taps(taps_ref, padded)
+    circs = [circulant(padded, a) for a in range(angles)]
+    masks = []
+    for a in range(angles):
+        own = [
+            [valid_ref[a, r : r + 1, t : t + 1].astype(F32) for r in range(rows)]
+            for t in (0, traces - 1)
+        ]
+        west, east = ([note(side, r, a) for r in range(rows)] for side in (left, right))
+        masks.append(spread([*own[0], *west, *east[::-1], *own[1][::-1]]))
+    tile = []
     for c in range(contrasts):
         strength = strength_ref[:, c : c + 1]
-        for r in range(rows):
-            one_ref[c, r] = v_ref[c, r] - strength * beside(c, r + 1)
-    fill_taps(taps_ref, padded)
-    circs = [circulant(padded, a) for a in range(angles)]
-    masks = [trace_columns(valid_ref, a) for a in range(angles)]
-    store_tiles(two_ref, normal(stack_tiles(one_ref), masks, avo_ref, circs))
+        west, east = ([trace(side, c, r + 1) for r in range(rows)] for side in (left, right))
+        less = [-strength * line for line in west], [-strength * line for line in east]
+        whole = spread([*less[0], *west, *east[::-1], *less[1][::-1]])
+        tile.append([whole[:, k * LANES : (k + 1) * LANES] for k in range(n)])
+    edge = [jnp.concatenate(line, axis=1) for line in normal(tile, masks, avo_ref, circs)]
+
     weights = [column(prior_ref[r : r + 1, :]) + 4.0 for r in range(rows)]
     sums = [jnp.zeros((traces, LANES), F32) for _ in range(4)]
     for c in range(contrasts):
         strength = strength_ref[:, c : c + 1]
-        over = halo_ref[0, c] - strength * beside(c, 0)
-        under = halo_ref[1, c] - strength * beside(c, ext - 1)
+        lines = [halo_ref[0, c], *[v_ref[c, r] for r in range(rows)], halo_ref[1, c]]
+        lines = [line - strength * beside(c, i) for i, line in enumerate(lines)]
         for r in range(rows):
-            here, b = one_ref[c, r], b_ref[c, r]
-            edge = c * stride + ext + r
-            west = has_left * (left[edge : edge + 1, :] - strength * b[0:1, :])
-            east = has_right * (
-                right[edge : edge + 1, :] - strength * b[traces - 1 : traces, :]
-            )
-            north = one_ref[c, r - 1] if r else over
-            south = one_ref[c, r + 1] if r < rows - 1 else under
-            around = lateral(here, north, south, west, east)
-            two = two_ref[c, r] + strength * (weights[r] * here - around)
+            here, b = lines[r + 1], b_ref[c, r]
+            beyond = []
+            for side, has, t, u in (
+                (left, has_left, 0, rows + r),
+                (right, has_right, traces - 1, traces - rows - 1 - r),
+            ):
+                weight = note(side, r, angles) + 4.0
+                around = trace(side, c, r) + trace(side, c, r + 2) + trace(side, c, ext + r)
+                around = around + has * b[t : t + 1]
+                prior = strength * (weight * trace(side, c, r + 1) - around)
+                beyond.append(edge[c][u : u + 1] + prior)
+            around = lateral(here, lines[r], lines[r + 2], *beyond)
+            first, last = edge[c][r : r + 1], edge[c][traces - 1 - r : traces - r]
+            mend = jnp.where(place == 0, first, jnp.where(place == traces - 1, last, 0.0))
+            two = data_ref[c, r] + mend + strength * (weights[r] * here - around)
+            one_ref[c, r] = here
             two_ref[c, r] = two
             for q, product in enumerate((b * b, b * here, here * here, here * two)):
                 tiles = [product[:, k : k + LANES] for k in range(0, samples, LANES)]
@@ -407,7 +451,7 @@
     avo_coeffs = jnp.swapaxes(avo_coeffs, 0, 1)
     shape = lambda *dims: jax.ShapeDtypeStruct(dims, F32)
     field = shape(contrasts, rows, traces, samples)
-    side = shape(contrasts * (2 * rows + 2), samples)
+    side = shape(rows, contrasts * (2 * rows + 2) // rows * samples + LANES)
     padded = pltpu.VMEM((8, 2 * LANES), F32)
     work = 2 * angles * rows * traces * samples * 256 * 4
 
@@ -426,12 +470,14 @@
     near_next = swap("inline", far, 1)
     far_next = hand_on("inline", near)
     far = swap("inline", far, 0)
-    (part,) = call(part_kernel, (field,), (b, *kept), 2 * work, [padded])
-    image, col_pair, col_other = call(
-        rows_kernel, (field, side, side), (b, part, near, near_next, strength), 4 * field.size
+    col_pair, col_other = call(
+        column_kernel, (side, side), (b, near, near_next, kept[0], kept[3]), 2 * field.size
     )
     col_other = swap("col", col_other, 1)
     col_pair = swap("col", col_pair, 0)
+    image, data = call(
+        inner_kernel, (field, field), (b, near, near_next, *kept), 4 * work, [padded]
+    )
     (halo,) = call(
         halo_kernel,
         (shape(2, contrasts, traces, samples),),
@@ -443,7 +489,7 @@
     one, two, gram = call(
         image_kernel,
         (field, field, shape(lax.axis_size(axes), 1, LANES)),
-        (b, image, halo, col_other, col_pair, *kept),
+        (b, image, data, halo, col_other, col_pair, *kept),
         2 * work,
         [padded],
     )

time: 33 us -> 32.7 us (level)
  blocking collectives: 11.6 us -> 10.3 us
  Pallas kernels: 5.13 us -> 6.29 us
    all_to_all x1, blocking collectives: 11.6 us -> 10.3 us  [shards(): gram = lax.all_to_all(gram, axes, 0, 0)]
    pallas_call x6, Pallas kernels: 5.13 us -> 6.29 us  [call(): pl.pallas_call(kernel, out_shape=outs, in_specs=[VMEM] * len(ins) if plac...]
  transfers between devices with their start and end apart: 6 -> 6, of which waited for: 1 -> 0; matrix products, arithmetic and copies ran while one was open for 0% -> 0% of each run, Pallas kernels for 5% -> 9%
where the time goes in v13:
time: 32.7 us; the launch traced here: 32.4 us
  starting transfers between devices  15.1 us (46%)
  blocking collectives  10.3 us (31%)
  Pallas kernels  6.29 us (19%)
  between operations  0.72 us (2%)
    ppermute x5, starting transfers between devices, swap(): lax.ppermute(value, axis, [(i + d, i + 1 - d) for i in starts for d in (0...  11.6 us
    all_to_all x1, blocking collectives, shards(): gram = lax.all_to_all(gram, axes, 0, 0)  10.3 us
    pallas_call x6, Pallas kernels, call(): pl.pallas_call(kernel, out_shape=outs, in_specs=[VMEM] * len(ins) if plac...  6.29 us
    ppermute x1, starting transfers between devices, hand_on(): lax.ppermute(value, axis, [(i, j) for i, j in steps if 0 <= j < size])  3.48 us
  transfers between devices with their start and end apart: 6, of which 0 were waited for; matrix products, arithmetic and copies ran while one was open for 0% of the time, Pallas kernels for 9%

profile of v13, /device:TPU:0, one launch (start us, length us, event | category | flops | bytes accessed | tf_op | source)
XLA Modules:
  0.0 32.4 jit_solution(14458667692181242233)
XLA Ops:
  0.6 1.4 %start_kernel.1 = (f32[3,2,8,1024]{3,2,1,0:T(8,128)S(1)}, f32[25,8,128]{2,1,0:T(8,128)S(1)}, f32[25,8,128]{2,1,0:T(8,128)S(1)}, s32[4,2,8]{2,1,0:T(2,128)S(1)}, ...) custom-call(bf16[4,2,8,1024]{3,2,1,0:T(8,128)(2,1)} %seis_hbm.1, ...), custom_call_target="tpu_custom_call" | custom-call | flops 134217728 | bytes 635576 | tf_op jit(solution)/shard_map/start_kernel/pallas_call | solution.py:425
  2.1 3.0 %collective-permute-start = (f32[25,8,128]{2,1,0:T(8,128)S(1)}, f32[25,8,128]{2,1,0:T(8,128)S(1)}, u32[]{:S(2)}, u32[]{:S(2)}) collective-permute-start(f32[25,8,128]{2,1,0:T(8,128)S(1)} %get-tuple-element.18), channel_id=1, source_target_pairs={{0,4},{4,0},{8,12},{12,8},{16,20},{20,16},{24,28},{28,24},{1,5},{5... | collective-permute-start | bytes 307208 | tf_op jit(solution)/shard_map/ppermute | solution.py:439
  5.1 0.7 %collective-permute-start.1 = (f32[25,8,128]{2,1,0:T(8,128)S(1)}, f32[25,8,128]{2,1,0:T(8,128)S(1)}, u32[]{:S(2)}, u32[]{:S(2)}) collective-permute-start(f32[25,8,128]{2,1,0:T(8,128)S(1)} %get-tuple-element.19), channel_id=1, source_target_pairs={{4,8},{8,4},{12,16},{16,12},{20,24},{24,20},{5,9},{9,5},{13,17},{1... | collective-permute-start | bytes 307208 | tf_op jit(solution)/shard_map/ppermute | solution.py:439
  5.7 4.3 %collective-permute-start.3 = (f32[25,8,128]{2,1,0:T(8,128)S(1)}, f32[25,8,128]{2,1,0:T(8,128)S(1)}, u32[]{:S(2)}, u32[]{:S(2)}) collective-permute-start(f32[25,8,128]{2,1,0:T(8,128)S(1)} %get-tuple-element.19), channel_id=1, source_target_pairs={{0,4},{4,0},{8,12},{12,8},{16,20},{20,16},{24,28},{28,24},{1,5},{5... | collective-permute-start | bytes 307208 | tf_op jit(solution)/shard_map/ppermute | solution.py:439
  10.1 0.0 collective-permute-done.near_ref
  10.1 3.5 %collective-permute-start.2 = (f32[25,8,128]{2,1,0:T(8,128)S(1)}, f32[25,8,128]{2,1,0:T(8,128)S(1)}, u32[]{:S(2)}, u32[]{:S(2)}) collective-permute-start(f32[25,8,128]{2,1,0:T(8,128)S(1)} %collective-permute-done.near_ref), channel_id=1, source_target_pairs={{0,8},{8,16},{12,4},{16,24},{20,12},{28,20},{1,9},{9,17},{13,5},{1... | collective-permute-start | bytes 307208 | tf_op jit(solution)/shard_map/ppermute | solution.py:445
  13.6 0.0 collective-permute-done.1.near_next_ref
  13.6 0.2 column_kernel.1
  13.8 0.7 %collective-permute-start.4 = (f32[2,9344]{1,0:T(2,128)S(1)}, f32[2,9344]{1,0:T(2,128)S(1)}, u32[]{:S(2)}, u32[]{:S(2)}) collective-permute-start(f32[2,9344]{1,0:T(2,128)S(1)} %get-tuple-element.27), channel_id=1, source_target_pairs={{1,2},{2,1},{5,6},{6,5},{9,10},{10,9},{13,14},{14,13},{17,18},{18,... | collective-permute-start | bytes 224264 | tf_op jit(solution)/shard_map/ppermute | solution.py:439
  14.4 2.9 %collective-permute-start.5 = (f32[2,9344]{1,0:T(2,128)S(1)}, f32[2,9344]{1,0:T(2,128)S(1)}, u32[]{:S(2)}, u32[]{:S(2)}) collective-permute-start(f32[2,9344]{1,0:T(2,128)S(1)} %get-tuple-element.28), channel_id=1, source_target_pairs={{0,1},{1,0},{2,3},{3,2},{4,5},{5,4},{6,7},{7,6},{8,9},{9,8},{10,11... | collective-permute-start | bytes 224264 | tf_op jit(solution)/shard_map/ppermute | solution.py:439
  17.4 1.9 %inner_kernel.1 = (f32[3,2,8,1024]{3,2,1,0:T(8,128)S(1)}, f32[3,2,8,1024]{3,2,1,0:T(8,128)S(1)}) custom-call(f32[3,2,8,1024]{3,2,1,0:T(8,128)S(1)} %get-tuple-element.17.b_ref, f32[25,8,128]{2,1,0:T(8,128)S(1)} %collective-permute-done.near_ref, f32[25,8,128]{2,1,0:T(8,128)S(1)} %collective-permute-done.1.near_next_ref, ...), custom_call_target="tpu_custom_call" | custom-call | flops 536870912 | bytes 846172 | tf_op jit(solution)/shard_map/inner_kernel/pallas_call | solution.py:425
  19.2 0.0 collective-permute-done.3.far_ref
  19.2 0.0 collective-permute-done.2.far_next_ref
  19.3 0.7 %halo_kernel.1.halo_ref = f32[2,3,8,1024]{3,2,1,0:T(8,128)S(1)} custom-call(f32[3,2,8,1024]{3,2,1,0:T(8,128)S(1)} %get-tuple-element.17.b_ref, f32[25,8,128]{2,1,0:T(8,128)S(1)} %collective-permute-done.near_ref, f32[25,8,128]{2,1,0:T(8,128)S(1)} %collective-permute-done.1.near_next_ref, f32[25,8,128]{2,1,0:T(8,128)S(1)} %collective-permute-done.2.far_next_ref, ...), custom_call_target="tpu_custom_call" | custom-call | flops 268435456 | bytes 854044 | tf_op jit(solution)/shard_map/halo_kernel/pallas_call | solution.py:425
  20.0 0.0 collective-permute-done.4.other_ref
  20.0 0.0 collective-permute-done.5.pair_ref
  20.0 1.2 %image_kernel.1 = (f32[3,2,8,1024]{3,2,1,0:T(8,128)S(1)}, f32[3,2,8,1024]{3,2,1,0:T(8,128)S(1)}, f32[32,1,128]{2,1,0:T(1,128)S(1)}) custom-call(f32[3,2,8,1024]{3,2,1,0:T(8,128)S(1)} %get-tuple-element.17.b_ref, f32[3,2,8,1024]{3,2,1,0:T(8,128)S(1)} %get-tuple-element.25.v_ref, f32[3,2,8,1024]{3,2,1,0:T(8,128)S(1)} %get-tuple-element.26.data_ref, ...), custom_call_target="tpu_custom_call" | custom-call | flops 268435456 | bytes 1397084 | tf_op jit(solution)/shard_map/image_kernel/pallas_call | solution.py:425
  21.2 10.3 %all_to_all.5.gram_ref = f32[32,1,128]{2,1,0:T(1,128)S(1)} all-to-all(f32[32,1,128]{2,1,0:T(1,128)S(1)} %get-tuple-element.29), channel_id=1, replica_groups=mesh['inline'=8,'col'=4] {'inline','col'}, dimensions={0} | all-to-all | bytes 32768 | tf_op jit(solution)/shard_map/all_to_all | solution.py:496
  31.5 0.9 %finish_kernel.1 = (f32[3,2,8,1024]{3,2,1,0:T(8,128)}, f32[3,2,8,1024]{3,2,1,0:T(8,128)}) custom-call(f32[32,1,128]{2,1,0:T(1,128)S(1)} %all_to_all.5.gram_ref, f32[3,2,8,1024]{3,2,1,0:T(8,128)S(1)} %get-tuple-element.17.b_ref, f32[3,2,8,1024]{3,2,1,0:T(8,128)S(1)} %get-tuple-element.30.one_ref, f32[3,2,8,1024]{3,2,1,0:T(8,128)S(1)} %get-tuple-element.31.two_ref), custom_call_target="tpu_custom_call" | custom-call | flops 393216 | bytes 999424 | tf_op jit(solution)/shard_map/finish_kernel/pallas_call | solution.py:425
Async XLA Ops:
  2.1 8.0 %collective-permute-start = (f32[25,8,128]{2,1,0:T(8,128)S(1)}, f32[25,8,128]{2,1,0:T(8,128)S(1)}, u32[]{:S(2)}, u32[]{:S(2)}) collective-permute-start(f32[25,8,128]{2,1,0:T(8,128)S(1)} %get-tuple-element.18), channel_id=1, source_target_pairs={{0,4},{4,0},{8,12},{12,8},{16,20},{20,16},{24,28},{28,24},{1,5},{5... | collective-permute-start | bytes 307208 | tf_op jit(solution)/shard_map/ppermute | solution.py:439
  5.1 8.5 %collective-permute-start.1 = (f32[25,8,128]{2,1,0:T(8,128)S(1)}, f32[25,8,128]{2,1,0:T(8,128)S(1)}, u32[]{:S(2)}, u32[]{:S(2)}) collective-permute-start(f32[25,8,128]{2,1,0:T(8,128)S(1)} %get-tuple-element.19), channel_id=1, source_target_pairs={{4,8},{8,4},{12,16},{16,12},{20,24},{24,20},{5,9},{9,5},{13,17},{1... | collective-permute-start | bytes 307208 | tf_op jit(solution)/shard_map/ppermute | solution.py:439
  5.7 13.5 %collective-permute-start.3 = (f32[25,8,128]{2,1,0:T(8,128)S(1)}, f32[25,8,128]{2,1,0:T(8,128)S(1)}, u32[]{:S(2)}, u32[]{:S(2)}) collective-permute-start(f32[25,8,128]{2,1,0:T(8,128)S(1)} %get-tuple-element.19), channel_id=1, source_target_pairs={{0,4},{4,0},{8,12},{12,8},{16,20},{20,16},{24,28},{28,24},{1,5},{5... | collective-permute-start | bytes 307208 | tf_op jit(solution)/shard_map/ppermute | solution.py:439
  10.1 9.2 %collective-permute-start.2 = (f32[25,8,128]{2,1,0:T(8,128)S(1)}, f32[25,8,128]{2,1,0:T(8,128)S(1)}, u32[]{:S(2)}, u32[]{:S(2)}) collective-permute-start(f32[25,8,128]{2,1,0:T(8,128)S(1)} %collective-permute-done.near_ref), channel_id=1, source_target_pairs={{0,8},{8,16},{12,4},{16,24},{20,12},{28,20},{1,9},{9,17},{13,5},{1... | collective-permute-start | bytes 307208 | tf_op jit(solution)/shard_map/ppermute | solution.py:445
  13.8 6.2 %collective-permute-start.4 = (f32[2,9344]{1,0:T(2,128)S(1)}, f32[2,9344]{1,0:T(2,128)S(1)}, u32[]{:S(2)}, u32[]{:S(2)}) collective-permute-start(f32[2,9344]{1,0:T(2,128)S(1)} %get-tuple-element.27), channel_id=1, source_target_pairs={{1,2},{2,1},{5,6},{6,5},{9,10},{10,9},{13,14},{14,13},{17,18},{18,... | collective-permute-start | bytes 224264 | tf_op jit(solution)/shard_map/ppermute | solution.py:439
  14.4 5.6 %collective-permute-start.5 = (f32[2,9344]{1,0:T(2,128)S(1)}, f32[2,9344]{1,0:T(2,128)S(1)}, u32[]{:S(2)}, u32[]{:S(2)}) collective-permute-start(f32[2,9344]{1,0:T(2,128)S(1)} %get-tuple-element.28), channel_id=1, source_target_pairs={{0,1},{1,0},{2,3},{3,2},{4,5},{5,4},{6,7},{7,6},{8,9},{9,8},{10,11... | collective-permute-start | bytes 224264 | tf_op jit(solution)/shard_map/ppermute | solution.py:439

commit v14 on v13

--- a/solution.py
+++ b/solution.py
@@ -116,19 +116,19 @@
     return total
 
 
-def normal(field, masks, avo_ref, circs):
+def normal(field, masks, avo_ref, bands):
     contrasts, n = len(field), len(field[0])
     total = [[None] * n for _ in range(contrasts)]
-    for a, circ in enumerate(circs):
+    for a, (ahead, back) in enumerate(bands):
         mixed = []
         for k in range(n):
             parts = [coeff(avo_ref, a, c, k) * field[c][k] for c in range(contrasts)]
             mixed.append(functools.reduce(jnp.add, parts))
-        synth = [tile * masks[a] for tile in forward(mixed, forward_band(circ))]
+        synth = [tile * masks[a] for tile in forward(mixed, ahead)]
         left_half = lax.broadcasted_iota(jnp.int32, synth[0].shape, 1) < LANES // 2
         synth[0] = jnp.where(left_half, 0.0, synth[0])
         synth[n] = jnp.where(left_half, synth[n], 0.0)
-        result = backward(list(zip(*[split(t) for t in synth])), backward_band(circ))
+        result = backward(list(zip(*[split(t) for t in synth])), back)
         add_terms(total, avo_ref, a, result)
     return total
 
@@ -203,41 +203,6 @@
     return jnp.where(first, other, pair), jnp.where(first, pair, other)
 
 
-def halo_kernel(
-    b_ref, near_ref, near_next_ref, far_next_ref, far_ref, avo_ref, taps_ref, strength_ref,
-    out_ref, padded,
-):
-    contrasts, rows, traces, samples = b_ref.shape
-    angles, n = avo_ref.shape[1], samples // LANES
-    has = inside("inline")
-    fill_taps(taps_ref, padded)
-    circs = [circulant(padded, a) for a in range(angles)]
-    notes = either_side(near_ref, near_next_ref, contrasts * n)
-    masks = [
-        jnp.concatenate([note[:, a : a + 1] for note in notes], axis=0) for a in range(angles)
-    ]
-    field = [
-        [
-            jnp.concatenate(either_side(near_ref, near_next_ref, c * n + k), axis=0)
-            for k in range(n)
-        ]
-        for c in range(contrasts)
-    ]
-    total = normal(field, masks, avo_ref, circs)
-    for c in range(contrasts):
-        strength = strength_ref[:, c : c + 1]
-        for side, own in ((0, 0), (1, rows - 1)):
-            weight = notes[side][:, angles : angles + 1] + 4.0
-            lines = slice(side * traces, (side + 1) * traces)
-            here = jnp.concatenate([tile[lines] for tile in field[c]], axis=1)
-            beyond = jnp.concatenate(
-                [either_side(far_ref, far_next_ref, c * n + k)[side] for k in range(n)], axis=1
-            )
-            around = lateral(here, beyond, has[side] * b_ref[c, own], None, None)
-            data = jnp.concatenate([tile[lines] for tile in total[c]], axis=1)
-            out_ref[side, c] = data + strength * (weight * here - around)
-
-
 def stack_tiles(ref):
     contrasts, rows, _, samples = ref.shape
     return [
@@ -294,31 +259,56 @@
 
 def inner_kernel(
     b_ref, near_ref, near_next_ref, valid_ref, avo_ref, taps_ref, prior_ref, strength_ref,
-    v_ref, data_ref, padded,
+    v_ref, data_ref, halo_ref, ahead_ref, back_ref, padded,
 ):
-    contrasts, rows, _, samples = b_ref.shape
+    contrasts, rows, traces, samples = b_ref.shape
+    angles, n = avo_ref.shape[1], samples // LANES
     fill_taps(taps_ref, padded)
-    angles = avo_ref.shape[1]
-    circs = [circulant(padded, a) for a in range(angles)]
+    bands = []
+    for a in range(angles):
+        circ = circulant(padded, a)
+        bands.append((forward_band(circ), backward_band(circ)))
+        ahead_ref[a], back_ref[a] = bands[a]
     masks = [trace_columns(valid_ref, a) for a in range(angles)]
-    store_tiles(v_ref, normal(stack_tiles(b_ref), masks, avo_ref, circs))
     weights = [column(prior_ref[r : r + 1, :]) + 4.0 for r in range(rows)]
+    above, below = either_side(near_ref, near_next_ref, contrasts * n)
+    wide = [
+        jnp.concatenate([above[:, a : a + 1], mask, below[:, a : a + 1]], axis=0)
+        for a, mask in enumerate(masks)
+    ]
+    weights = [above[:, angles : angles + 1] + 4.0, *weights, below[:, angles : angles + 1] + 4.0]
+    field = []
+    for c, line in enumerate(stack_tiles(b_ref)):
+        ends = [either_side(near_ref, near_next_ref, c * n + k) for k in range(n)]
+        field.append(
+            [jnp.concatenate([up, own, low], axis=0) for (up, low), own in zip(ends, line)]
+        )
+    total = normal(field, wide, avo_ref, bands)
+    has_above, has_below = inside("inline")
     for c in range(contrasts):
         strength = strength_ref[:, c : c + 1]
-        above, below = row_pair(near_ref, near_next_ref, c, samples // LANES)
-        for r in range(rows):
-            here = b_ref[c, r]
-            north = b_ref[c, r - 1] if r else above
-            south = b_ref[c, r + 1] if r < rows - 1 else below
+        whole, data = jnp.concatenate(field[c], axis=1), jnp.concatenate(total[c], axis=1)
+        lines = [whole[r * traces : (r + 1) * traces] for r in range(rows + 2)]
+        for r, here in enumerate(lines):
+            north = lines[r - 1] if r else None
+            south = lines[r + 1] if r < rows + 1 else None
+            if r == 0:
+                south = has_above * south
+            if r == rows + 1:
+                north = has_below * north
             around = lateral(here, north, south, None, None)
-            v_ref[c, r] = v_ref[c, r] + strength * (weights[r] * here - around)
-    store_tiles(data_ref, normal(stack_tiles(v_ref), masks, avo_ref, circs))
+            image = data[r * traces : (r + 1) * traces] + strength * (weights[r] * here - around)
+            if 0 < r <= rows:
+                v_ref[c, r - 1] = image
+            else:
+                halo_ref[min(r, 1), c] = image
+    store_tiles(data_ref, normal(stack_tiles(v_ref), masks, avo_ref, bands))
 
 
 def image_kernel(
-    b_ref, v_ref, data_ref, halo_ref, other_ref, pair_ref,
-    valid_ref, avo_ref, taps_ref, prior_ref, strength_ref,
-    one_ref, two_ref, gram_ref, padded,
+    b_ref, v_ref, data_ref, halo_ref, far_next_ref, far_ref, other_ref, pair_ref,
+    valid_ref, avo_ref, prior_ref, strength_ref, ahead_ref, back_ref,
+    one_ref, two_ref, gram_ref,
 ):
     contrasts, rows, traces, samples = b_ref.shape
     angles, n = avo_ref.shape[1], samples // LANES
@@ -347,8 +337,7 @@
             total = jnp.where(place[:, : values[0].shape[1]] == t, values[t], total)
         return total
 
-    fill_taps(taps_ref, padded)
-    circs = [circulant(padded, a) for a in range(angles)]
+    bands = [(ahead_ref[a], back_ref[a]) for a in range(angles)]
     masks = []
     for a in range(angles):
         own = [
@@ -364,13 +353,15 @@
         less = [-strength * line for line in west], [-strength * line for line in east]
         whole = spread([*less[0], *west, *east[::-1], *less[1][::-1]])
         tile.append([whole[:, k * LANES : (k + 1) * LANES] for k in range(n)])
-    edge = [jnp.concatenate(line, axis=1) for line in normal(tile, masks, avo_ref, circs)]
+    edge = [jnp.concatenate(line, axis=1) for line in normal(tile, masks, avo_ref, bands)]
 
     weights = [column(prior_ref[r : r + 1, :]) + 4.0 for r in range(rows)]
     sums = [jnp.zeros((traces, LANES), F32) for _ in range(4)]
     for c in range(contrasts):
         strength = strength_ref[:, c : c + 1]
-        lines = [halo_ref[0, c], *[v_ref[c, r] for r in range(rows)], halo_ref[1, c]]
+        beyond = row_pair(far_ref, far_next_ref, c, n)
+        over, under = (halo_ref[i, c] - strength * beyond[i] for i in (0, 1))
+        lines = [over, *[v_ref[c, r] for r in range(rows)], under]
         lines = [line - strength * beside(c, i) for i, line in enumerate(lines)]
         for r in range(rows):
             here, b = lines[r + 1], b_ref[c, r]
@@ -465,7 +456,6 @@
         [pltpu.VMEM(seismic.shape, seismic.dtype), padded, pltpu.SemaphoreType.DMA((6,))],
         [HBM] * 6,
     )
-    avo, taps, strength = kept[1], kept[2], kept[-1]
     near = swap("inline", near, 0)
     near_next = swap("inline", far, 1)
     far_next = hand_on("inline", near)
@@ -475,23 +465,23 @@
     )
     col_other = swap("col", col_other, 1)
     col_pair = swap("col", col_pair, 0)
-    image, data = call(
-        inner_kernel, (field, field), (b, near, near_next, *kept), 4 * work, [padded]
-    )
-    (halo,) = call(
-        halo_kernel,
-        (shape(2, contrasts, traces, samples),),
-        (b, near, near_next, far_next, far, avo, taps, strength),
-        2 * work,
+    band = jax.ShapeDtypeStruct((angles, 2 * LANES, 2 * LANES), BF16)
+    image, data, halo, ahead, back = call(
+        inner_kernel,
+        (field, field, shape(2, contrasts, traces, samples), band, band),
+        (b, near, near_next, *kept),
+        6 * work,
         [padded],
     )
     axes = ("inline", "col")
     one, two, gram = call(
         image_kernel,
         (field, field, shape(lax.axis_size(axes), 1, LANES)),
-        (b, image, data, halo, col_other, col_pair, *kept),
-        2 * work,
-        [padded],
+        (
+            b, image, data, halo, far_next, far, col_other, col_pair,
+            kept[0], kept[1], kept[3], kept[4], ahead, back,
+        ),
+        work,
     )
     gram = lax.all_to_all(gram, axes, 0, 0)
     return tuple(call(finish_kernel, (field, field), (gram, b, one, two), 8 * field.size))

time: 32.7 us -> 32.6 us (level)
    pallas_call x6 -> x5, Pallas kernels: 6.29 us -> 5.98 us  [call(): pl.pallas_call(kernel, out_shape=outs, in_specs=[VMEM] * len(ins) if plac...]
  transfers between devices with their start and end apart: 6 -> 6, of which waited for: 0 -> 0; matrix products, arithmetic and copies ran while one was open for 0% -> 0% of each run, Pallas kernels for 9% -> 8%
where the time goes in v14:
time: 32.6 us; the launch traced here: 32.3 us
  starting transfers between devices  15.1 us (46%)
  blocking collectives  10.5 us (32%)
  Pallas kernels  5.98 us (18%)
  between operations  0.72 us (2%)
    ppermute x5, starting transfers between devices, swap(): lax.ppermute(value, axis, [(i + d, i + 1 - d) for i in starts for d in (0...  11.6 us
    all_to_all x1, blocking collectives, shards(): gram = lax.all_to_all(gram, axes, 0, 0)  10.5 us
    pallas_call x5, Pallas kernels, call(): pl.pallas_call(kernel, out_shape=outs, in_specs=[VMEM] * len(ins) if plac...  5.98 us
    ppermute x1, starting transfers between devices, hand_on(): lax.ppermute(value, axis, [(i, j) for i, j in steps if 0 <= j < size])  3.48 us
  transfers between devices with their start and end apart: 6, of which 0 were waited for; matrix products, arithmetic and copies ran while one was open for 0% of the time, Pallas kernels for 8%

profile of v14, /device:TPU:0, one launch (start us, length us, event | category | flops | bytes accessed | tf_op | source)
XLA Modules:
  0.0 32.3 jit_solution(13810780174376150275)
XLA Ops:
  0.6 1.4 %start_kernel.1 = (f32[3,2,8,1024]{3,2,1,0:T(8,128)S(1)}, f32[25,8,128]{2,1,0:T(8,128)S(1)}, f32[25,8,128]{2,1,0:T(8,128)S(1)}, s32[4,2,8]{2,1,0:T(2,128)S(1)}, ...) custom-call(bf16[4,2,8,1024]{3,2,1,0:T(8,128)(2,1)} %seis_hbm.1, ...), custom_call_target="tpu_custom_call" | custom-call | flops 134217728 | bytes 635576 | tf_op jit(solution)/shard_map/start_kernel/pallas_call | solution.py:416
  2.1 3.0 %collective-permute-start = (f32[25,8,128]{2,1,0:T(8,128)S(1)}, f32[25,8,128]{2,1,0:T(8,128)S(1)}, u32[]{:S(2)}, u32[]{:S(2)}) collective-permute-start(f32[25,8,128]{2,1,0:T(8,128)S(1)} %get-tuple-element.21), channel_id=1, source_target_pairs={{0,4},{4,0},{8,12},{12,8},{16,20},{20,16},{24,28},{28,24},{1,5},{5... | collective-permute-start | bytes 307208 | tf_op jit(solution)/shard_map/ppermute | solution.py:430
  5.1 0.7 %collective-permute-start.1 = (f32[25,8,128]{2,1,0:T(8,128)S(1)}, f32[25,8,128]{2,1,0:T(8,128)S(1)}, u32[]{:S(2)}, u32[]{:S(2)}) collective-permute-start(f32[25,8,128]{2,1,0:T(8,128)S(1)} %get-tuple-element.22), channel_id=1, source_target_pairs={{4,8},{8,4},{12,16},{16,12},{20,24},{24,20},{5,9},{9,5},{13,17},{1... | collective-permute-start | bytes 307208 | tf_op jit(solution)/shard_map/ppermute | solution.py:430
  5.7 4.3 %collective-permute-start.3 = (f32[25,8,128]{2,1,0:T(8,128)S(1)}, f32[25,8,128]{2,1,0:T(8,128)S(1)}, u32[]{:S(2)}, u32[]{:S(2)}) collective-permute-start(f32[25,8,128]{2,1,0:T(8,128)S(1)} %get-tuple-element.22), channel_id=1, source_target_pairs={{0,4},{4,0},{8,12},{12,8},{16,20},{20,16},{24,28},{28,24},{1,5},{5... | collective-permute-start | bytes 307208 | tf_op jit(solution)/shard_map/ppermute | solution.py:430
  10.1 0.0 collective-permute-done.near_ref
  10.1 3.5 %collective-permute-start.2 = (f32[25,8,128]{2,1,0:T(8,128)S(1)}, f32[25,8,128]{2,1,0:T(8,128)S(1)}, u32[]{:S(2)}, u32[]{:S(2)}) collective-permute-start(f32[25,8,128]{2,1,0:T(8,128)S(1)} %collective-permute-done.near_ref), channel_id=1, source_target_pairs={{0,8},{8,16},{12,4},{16,24},{20,12},{28,20},{1,9},{9,17},{13,5},{1... | collective-permute-start | bytes 307208 | tf_op jit(solution)/shard_map/ppermute | solution.py:436
  13.6 0.0 collective-permute-done.1.near_next_ref
  13.6 0.2 column_kernel.1
  13.8 0.7 %collective-permute-start.4 = (f32[2,9344]{1,0:T(2,128)S(1)}, f32[2,9344]{1,0:T(2,128)S(1)}, u32[]{:S(2)}, u32[]{:S(2)}) collective-permute-start(f32[2,9344]{1,0:T(2,128)S(1)} %get-tuple-element.31), channel_id=1, source_target_pairs={{1,2},{2,1},{5,6},{6,5},{9,10},{10,9},{13,14},{14,13},{17,18},{18,... | collective-permute-start | bytes 224264 | tf_op jit(solution)/shard_map/ppermute | solution.py:430
  14.4 2.9 %collective-permute-start.5 = (f32[2,9344]{1,0:T(2,128)S(1)}, f32[2,9344]{1,0:T(2,128)S(1)}, u32[]{:S(2)}, u32[]{:S(2)}) collective-permute-start(f32[2,9344]{1,0:T(2,128)S(1)} %get-tuple-element.32), channel_id=1, source_target_pairs={{0,1},{1,0},{2,3},{3,2},{4,5},{5,4},{6,7},{7,6},{8,9},{9,8},{10,11... | collective-permute-start | bytes 224264 | tf_op jit(solution)/shard_map/ppermute | solution.py:430
  17.4 2.4 %inner_kernel.1 = (f32[3,2,8,1024]{3,2,1,0:T(8,128)S(1)}, f32[3,2,8,1024]{3,2,1,0:T(8,128)S(1)}, f32[2,3,8,1024]{3,2,1,0:T(8,128)S(1)}, bf16[4,256,256]{2,1,0:T(8,128)(2,1)S(1)}, bf16[4,256,256]{2,1,0:T(8,128)(2,1)S(1)}) custom-call(f32[3,2,8,1024]{3,2,1,0:T(8,128)S(1)} %get-tuple-element.20.b_ref, f32[25,8,128]{2,1,0:T(8,128)S(1)} %collective-permute-done.near_ref, ...), custom_call_target="tpu_custom_call" | custom-call | flops 805306368 | bytes 2091356 | tf_op jit(solution)/shard_map/inner_kernel/pallas_call | solution.py:416
  19.7 0.0 collective-permute-done.3.far_ref
  19.7 0.0 collective-permute-done.4.other_ref
  19.8 0.0 collective-permute-done.5.pair_ref
  19.8 0.0 collective-permute-done.2.far_next_ref
  19.8 1.1 %image_kernel.1 = (f32[3,2,8,1024]{3,2,1,0:T(8,128)S(1)}, f32[3,2,8,1024]{3,2,1,0:T(8,128)S(1)}, f32[32,1,128]{2,1,0:T(1,128)S(1)}) custom-call(f32[3,2,8,1024]{3,2,1,0:T(8,128)S(1)} %get-tuple-element.20.b_ref, f32[3,2,8,1024]{3,2,1,0:T(8,128)S(1)} %get-tuple-element.28.v_ref, f32[3,2,8,1024]{3,2,1,0:T(8,128)S(1)} %get-tuple-element.29.data_ref, ...), custom_call_target="tpu_custom_call" | custom-call | flops 134217728 | bytes 2648396 | tf_op jit(solution)/shard_map/image_kernel/pallas_call | solution.py:416
  20.9 10.5 %all_to_all.5.gram_ref = f32[32,1,128]{2,1,0:T(1,128)S(1)} all-to-all(f32[32,1,128]{2,1,0:T(1,128)S(1)} %get-tuple-element.35), channel_id=1, replica_groups=mesh['inline'=8,'col'=4] {'inline','col'}, dimensions={0} | all-to-all | bytes 32768 | tf_op jit(solution)/shard_map/all_to_all | solution.py:486
  31.4 0.9 %finish_kernel.1 = (f32[3,2,8,1024]{3,2,1,0:T(8,128)}, f32[3,2,8,1024]{3,2,1,0:T(8,128)}) custom-call(f32[32,1,128]{2,1,0:T(1,128)S(1)} %all_to_all.5.gram_ref, f32[3,2,8,1024]{3,2,1,0:T(8,128)S(1)} %get-tuple-element.20.b_ref, f32[3,2,8,1024]{3,2,1,0:T(8,128)S(1)} %get-tuple-element.36.one_ref, f32[3,2,8,1024]{3,2,1,0:T(8,128)S(1)} %get-tuple-element.37.two_ref), custom_call_target="tpu_custom_call" | custom-call | flops 393216 | bytes 999424 | tf_op jit(solution)/shard_map/finish_kernel/pallas_call | solution.py:416
Async XLA Ops:
  2.1 8.0 %collective-permute-start = (f32[25,8,128]{2,1,0:T(8,128)S(1)}, f32[25,8,128]{2,1,0:T(8,128)S(1)}, u32[]{:S(2)}, u32[]{:S(2)}) collective-permute-start(f32[25,8,128]{2,1,0:T(8,128)S(1)} %get-tuple-element.21), channel_id=1, source_target_pairs={{0,4},{4,0},{8,12},{12,8},{16,20},{20,16},{24,28},{28,24},{1,5},{5... | collective-permute-start | bytes 307208 | tf_op jit(solution)/shard_map/ppermute | solution.py:430
  5.1 8.5 %collective-permute-start.1 = (f32[25,8,128]{2,1,0:T(8,128)S(1)}, f32[25,8,128]{2,1,0:T(8,128)S(1)}, u32[]{:S(2)}, u32[]{:S(2)}) collective-permute-start(f32[25,8,128]{2,1,0:T(8,128)S(1)} %get-tuple-element.22), channel_id=1, source_target_pairs={{4,8},{8,4},{12,16},{16,12},{20,24},{24,20},{5,9},{9,5},{13,17},{1... | collective-permute-start | bytes 307208 | tf_op jit(solution)/shard_map/ppermute | solution.py:430
  5.7 14.0 %collective-permute-start.3 = (f32[25,8,128]{2,1,0:T(8,128)S(1)}, f32[25,8,128]{2,1,0:T(8,128)S(1)}, u32[]{:S(2)}, u32[]{:S(2)}) collective-permute-start(f32[25,8,128]{2,1,0:T(8,128)S(1)} %get-tuple-element.22), channel_id=1, source_target_pairs={{0,4},{4,0},{8,12},{12,8},{16,20},{20,16},{24,28},{28,24},{1,5},{5... | collective-permute-start | bytes 307208 | tf_op jit(solution)/shard_map/ppermute | solution.py:430
  10.1 9.7 %collective-permute-start.2 = (f32[25,8,128]{2,1,0:T(8,128)S(1)}, f32[25,8,128]{2,1,0:T(8,128)S(1)}, u32[]{:S(2)}, u32[]{:S(2)}) collective-permute-start(f32[25,8,128]{2,1,0:T(8,128)S(1)} %collective-permute-done.near_ref), channel_id=1, source_target_pairs={{0,8},{8,16},{12,4},{16,24},{20,12},{28,20},{1,9},{9,17},{13,5},{1... | collective-permute-start | bytes 307208 | tf_op jit(solution)/shard_map/ppermute | solution.py:436
  13.8 6.0 %collective-permute-start.4 = (f32[2,9344]{1,0:T(2,128)S(1)}, f32[2,9344]{1,0:T(2,128)S(1)}, u32[]{:S(2)}, u32[]{:S(2)}) collective-permute-start(f32[2,9344]{1,0:T(2,128)S(1)} %get-tuple-element.31), channel_id=1, source_target_pairs={{1,2},{2,1},{5,6},{6,5},{9,10},{10,9},{13,14},{14,13},{17,18},{18,... | collective-permute-start | bytes 224264 | tf_op jit(solution)/shard_map/ppermute | solution.py:430
  14.4 5.3 %collective-permute-start.5 = (f32[2,9344]{1,0:T(2,128)S(1)}, f32[2,9344]{1,0:T(2,128)S(1)}, u32[]{:S(2)}, u32[]{:S(2)}) collective-permute-start(f32[2,9344]{1,0:T(2,128)S(1)} %get-tuple-element.32), channel_id=1, source_target_pairs={{0,1},{1,0},{2,3},{3,2},{4,5},{5,4},{6,7},{7,6},{8,9},{9,8},{10,11... | collective-permute-start | bytes 224264 | tf_op jit(solution)/shard_map/ppermute | solution.py:430

commit v15 on v14

--- a/solution.py
+++ b/solution.py
@@ -17,22 +17,27 @@
     return high, (value - high.astype(F32)).astype(BF16)
 
 
-def circulant(padded_ref, angle):
-    line = jnp.broadcast_to(padded_ref[angle : angle + 1, :], (2 * LANES, 2 * LANES))
-    return pltpu.roll(line, LANES, 1, stride=1, stride_axis=0)
-
-
-def fill_taps(taps_ref, padded_ref):
+def band(taps_ref, angle):
+    line = jnp.broadcast_to(taps_ref[angle : angle + 1, :], (2 * LANES, 2 * LANES))
+    rolled = pltpu.roll(line, LANES, 1, stride=1, stride_axis=0)
+    return jnp.concatenate(split(rolled[:, :LANES]), axis=1)
+
+
+def fill_taps(taps_ref, padded_ref, turned_ref):
     padded_ref[...] = jnp.zeros_like(padded_ref)
     padded_ref[0 : taps_ref.shape[0], 0 : taps_ref.shape[1]] = taps_ref[...]
-
-
-def forward_band(circ):
-    return jnp.concatenate(split(circ[:, :LANES]), axis=1)
-
-
-def backward_band(circ):
-    return jnp.concatenate(split(circ[LANES:, :]), axis=0)
+    rest, parts = padded_ref[...], []
+    for _ in range(3):
+        parts.append(rest.astype(BF16).astype(F32))
+        rest = rest - parts[-1]
+    size = 2 * LANES
+    rows = lax.broadcasted_iota(jnp.int32, (size, size), 0)
+    cols = lax.broadcasted_iota(jnp.int32, (size, size), 1)
+    flip = jnp.where(rows + cols == taps_ref.shape[1] - 1, 1.0, 0.0).astype(BF16)
+    lines = jnp.concatenate(parts, axis=0).astype(BF16)
+    turned = jnp.dot(lines, flip, preferred_element_type=F32)
+    n = padded_ref.shape[0]
+    turned_ref[...] = turned[:n] + turned[n : 2 * n] + turned[2 * n :]
 
 
 def column(row):
@@ -69,7 +74,7 @@
 def backward(parts, band):
     n, size = len(parts[0]) - 1, parts[0][0].shape[0]
     rows = jnp.concatenate([windows(part) for part in parts], axis=0)
-    out = lax.dot_general(rows, band, (((1,), (1,)), ((), ())), preferred_element_type=F32)
+    out = jnp.dot(rows, band, preferred_element_type=F32)
     out = halves_sum(out)
     total = out[: n * size]
     for p in range(1, len(parts)):
@@ -96,7 +101,7 @@
                 out_ref[c, r, :, pl.ds(k * LANES, LANES)] = tile[r * size : (r + 1) * size]
 
 
-def right_side(seis_ref, masks, avo_ref, circs):
+def right_side(seis_ref, masks, avo_ref, turned_ref):
     angles, rows, _, samples = seis_ref.shape
     n = samples // LANES
     total = [[None] * n for _ in range(avo_ref.shape[0])]
@@ -112,7 +117,7 @@
             jnp.where(left_half, before, here).astype(BF16)
             for before, here in zip([zero, *turned], [*turned, zero])
         ]
-        add_terms(total, avo_ref, a, backward([shifted], backward_band(circs[a])))
+        add_terms(total, avo_ref, a, backward([shifted], band(turned_ref, a)))
     return total
 
 
@@ -155,8 +160,8 @@
 
 def start_kernel(
     seis_hbm, valid_hbm, avo_hbm, taps_hbm, prior_hbm, strength_hbm,
-    b_ref, near_ref, far_ref, valid_ref, avo_ref, taps_ref, prior_ref, strength_ref,
-    seis_ref, padded, sems,
+    b_ref, near_ref, far_ref, padded_ref, turned_ref, valid_ref, avo_ref, prior_ref, strength_ref,
+    seis_ref, taps_ref, sems,
 ):
     copies = copy_in(
         (
@@ -171,13 +176,12 @@
     )
     for copy in copies[:2]:
         copy.wait()
-    fill_taps(taps_ref, padded)
+    fill_taps(taps_ref, padded_ref, turned_ref)
     angles = avo_ref.shape[1]
-    circs = [circulant(padded, a) for a in range(angles)]
     masks = [trace_columns(valid_ref, a) for a in range(angles)]
     for copy in copies[2:]:
         copy.wait()
-    store_tiles(b_ref, right_side(seis_ref, masks, avo_ref, circs))
+    store_tiles(b_ref, right_side(seis_ref, masks, avo_ref, turned_ref))
     contrasts, rows, traces, samples = b_ref.shape
     n = samples // LANES
     first = starts_pair("inline")
@@ -258,16 +262,14 @@
 
 
 def inner_kernel(
-    b_ref, near_ref, near_next_ref, valid_ref, avo_ref, taps_ref, prior_ref, strength_ref,
-    v_ref, data_ref, halo_ref, ahead_ref, back_ref, padded,
+    b_ref, near_ref, near_next_ref, padded_ref, turned_ref, valid_ref, avo_ref, prior_ref,
+    strength_ref, v_ref, data_ref, halo_ref, ahead_ref, back_ref,
 ):
     contrasts, rows, traces, samples = b_ref.shape
     angles, n = avo_ref.shape[1], samples // LANES
-    fill_taps(taps_ref, padded)
     bands = []
     for a in range(angles):
-        circ = circulant(padded, a)
-        bands.append((forward_band(circ), backward_band(circ)))
+        bands.append((band(padded_ref, a), band(turned_ref, a)))
         ahead_ref[a], back_ref[a] = bands[a]
     masks = [trace_columns(valid_ref, a) for a in range(angles)]
     weights = [column(prior_ref[r : r + 1, :]) + 4.0 for r in range(rows)]
@@ -443,17 +445,25 @@
     shape = lambda *dims: jax.ShapeDtypeStruct(dims, F32)
     field = shape(contrasts, rows, traces, samples)
     side = shape(rows, contrasts * (2 * rows + 2) // rows * samples + LANES)
-    padded = pltpu.VMEM((8, 2 * LANES), F32)
+    lines = shape(8, 2 * LANES)
     work = 2 * angles * rows * traces * samples * 256 * 4
 
     given = (seismic, validity, avo_coeffs, wavelets, prior_weight, lateral_strength.reshape(1, -1))
+    kept = [given[i] for i in (1, 2, 4, 5)]
     edge = shape(contrasts * samples // LANES + 1, traces, LANES)
-    b, near, far, *kept = call(
+    b, near, far, padded, turned, *kept = call(
         start_kernel,
-        (field, edge, edge, *[jax.ShapeDtypeStruct(x.shape, x.dtype) for x in given[1:]]),
+        (
+            field, edge, edge, lines, lines,
+            *[jax.ShapeDtypeStruct(x.shape, x.dtype) for x in kept],
+        ),
         [pltpu.with_memory_space_constraint(x, pltpu.HBM) for x in given],
         work,
-        [pltpu.VMEM(seismic.shape, seismic.dtype), padded, pltpu.SemaphoreType.DMA((6,))],
+        [
+            pltpu.VMEM(seismic.shape, seismic.dtype),
+            pltpu.VMEM(wavelets.shape, F32),
+            pltpu.SemaphoreType.DMA((6,)),
+        ],
         [HBM] * 6,
     )
     near = swap("inline", near, 0)
@@ -461,17 +471,16 @@
     far_next = hand_on("inline", near)
     far = swap("inline", far, 0)
     col_pair, col_other = call(
-        column_kernel, (side, side), (b, near, near_next, kept[0], kept[3]), 2 * field.size
+        column_kernel, (side, side), (b, near, near_next, kept[0], kept[2]), 2 * field.size
     )
     col_other = swap("col", col_other, 1)
     col_pair = swap("col", col_pair, 0)
-    band = jax.ShapeDtypeStruct((angles, 2 * LANES, 2 * LANES), BF16)
+    bands = jax.ShapeDtypeStruct((angles, 2 * LANES, 2 * LANES), BF16)
     image, data, halo, ahead, back = call(
         inner_kernel,
-        (field, field, shape(2, contrasts, traces, samples), band, band),
-        (b, near, near_next, *kept),
+        (field, field, shape(2, contrasts, traces, samples), bands, bands),
+        (b, near, near_next, padded, turned, *kept),
         6 * work,
-        [padded],
     )
     axes = ("inline", "col")
     one, two, gram = call(
@@ -479,7 +488,7 @@
         (field, field, shape(lax.axis_size(axes), 1, LANES)),
         (
             b, image, data, halo, far_next, far, col_other, col_pair,
-            kept[0], kept[1], kept[3], kept[4], ahead, back,
+            *kept, ahead, back,
         ),
         work,
     )

time: 32.6 us -> 32.9 us (level)
  Pallas kernels: 5.98 us -> 6.62 us
    pallas_call x5, Pallas kernels: 5.98 us -> 6.62 us  [call(): pl.pallas_call(kernel, out_shape=outs, in_specs=[VMEM] * len(ins) if plac...]
    all_to_all x1, blocking collectives: 10.5 us -> 10.2 us  [shards(): gram = lax.all_to_all(gram, axes, 0, 0)]
  transfers between devices with their start and end apart: 6 -> 6, of which waited for: 0 -> 0; matrix products, arithmetic and copies ran while one was open for 0% -> 0% of each run, Pallas kernels for 8% -> 9%
where the time goes in v15:
time: 32.9 us; the launch traced here: 32.6 us
  starting transfers between devices  15.1 us (46%)
  blocking collectives  10.2 us (31%)
  Pallas kernels  6.62 us (20%)
  between operations  0.72 us (2%)
    ppermute x5, starting transfers between devices, swap(): lax.ppermute(value, axis, [(i + d, i + 1 - d) for i in starts for d in (0...  11.6 us
    all_to_all x1, blocking collectives, shards(): gram = lax.all_to_all(gram, axes, 0, 0)  10.2 us
    pallas_call x5, Pallas kernels, call(): pl.pallas_call(kernel, out_shape=outs, in_specs=[VMEM] * len(ins) if plac...  6.62 us
    ppermute x1, starting transfers between devices, hand_on(): lax.ppermute(value, axis, [(i, j) for i, j in steps if 0 <= j < size])  3.48 us
  transfers between devices with their start and end apart: 6, of which 0 were waited for; matrix products, arithmetic and copies ran while one was open for 0% of the time, Pallas kernels for 9%

profile of v15, /device:TPU:0, one launch (start us, length us, event | category | flops | bytes accessed | tf_op | source)
XLA Modules:
  0.0 32.6 jit_solution(13932010251211303447)
XLA Ops:
  0.6 1.4 %start_kernel.1 = (f32[3,2,8,1024]{3,2,1,0:T(8,128)S(1)}, f32[25,8,128]{2,1,0:T(8,128)S(1)}, f32[25,8,128]{2,1,0:T(8,128)S(1)}, f32[8,256]{1,0:T(8,128)S(1)}, f3...) custom-call(bf16[4,2,8,1024]{3,2,1,0:T(8,128)(2,1)} %seis_hbm.1, ...), custom_call_target="tpu_custom_call" | custom-call | flops 134217728 | bytes 649896 | tf_op jit(solution)/shard_map/start_kernel/pallas_call | solution.py:418
  2.1 3.0 %collective-permute-start = (f32[25,8,128]{2,1,0:T(8,128)S(1)}, f32[25,8,128]{2,1,0:T(8,128)S(1)}, u32[]{:S(2)}, u32[]{:S(2)}) collective-permute-start(f32[25,8,128]{2,1,0:T(8,128)S(1)} %get-tuple-element.22), channel_id=1, source_target_pairs={{0,4},{4,0},{8,12},{12,8},{16,20},{20,16},{24,28},{28,24},{1,5},{5... | collective-permute-start | bytes 307208 | tf_op jit(solution)/shard_map/ppermute | solution.py:432
  5.1 0.7 %collective-permute-start.1 = (f32[25,8,128]{2,1,0:T(8,128)S(1)}, f32[25,8,128]{2,1,0:T(8,128)S(1)}, u32[]{:S(2)}, u32[]{:S(2)}) collective-permute-start(f32[25,8,128]{2,1,0:T(8,128)S(1)} %get-tuple-element.23), channel_id=1, source_target_pairs={{4,8},{8,4},{12,16},{16,12},{20,24},{24,20},{5,9},{9,5},{13,17},{1... | collective-permute-start | bytes 307208 | tf_op jit(solution)/shard_map/ppermute | solution.py:432
  5.8 4.3 %collective-permute-start.3 = (f32[25,8,128]{2,1,0:T(8,128)S(1)}, f32[25,8,128]{2,1,0:T(8,128)S(1)}, u32[]{:S(2)}, u32[]{:S(2)}) collective-permute-start(f32[25,8,128]{2,1,0:T(8,128)S(1)} %get-tuple-element.23), channel_id=1, source_target_pairs={{0,4},{4,0},{8,12},{12,8},{16,20},{20,16},{24,28},{28,24},{1,5},{5... | collective-permute-start | bytes 307208 | tf_op jit(solution)/shard_map/ppermute | solution.py:432
  10.1 0.0 collective-permute-done.near_ref
  10.1 3.5 %collective-permute-start.2 = (f32[25,8,128]{2,1,0:T(8,128)S(1)}, f32[25,8,128]{2,1,0:T(8,128)S(1)}, u32[]{:S(2)}, u32[]{:S(2)}) collective-permute-start(f32[25,8,128]{2,1,0:T(8,128)S(1)} %collective-permute-done.near_ref), channel_id=1, source_target_pairs={{0,8},{8,16},{12,4},{16,24},{20,12},{28,20},{1,9},{9,17},{13,5},{1... | collective-permute-start | bytes 307208 | tf_op jit(solution)/shard_map/ppermute | solution.py:438
  13.6 0.0 collective-permute-done.1.near_next_ref
  13.6 0.2 column_kernel.1
  13.8 0.7 %collective-permute-start.4 = (f32[2,9344]{1,0:T(2,128)S(1)}, f32[2,9344]{1,0:T(2,128)S(1)}, u32[]{:S(2)}, u32[]{:S(2)}) collective-permute-start(f32[2,9344]{1,0:T(2,128)S(1)} %get-tuple-element.33), channel_id=1, source_target_pairs={{1,2},{2,1},{5,6},{6,5},{9,10},{10,9},{13,14},{14,13},{17,18},{18,... | collective-permute-start | bytes 224264 | tf_op jit(solution)/shard_map/ppermute | solution.py:432
  14.4 2.9 %collective-permute-start.5 = (f32[2,9344]{1,0:T(2,128)S(1)}, f32[2,9344]{1,0:T(2,128)S(1)}, u32[]{:S(2)}, u32[]{:S(2)}) collective-permute-start(f32[2,9344]{1,0:T(2,128)S(1)} %get-tuple-element.34), channel_id=1, source_target_pairs={{0,1},{1,0},{2,3},{3,2},{4,5},{5,4},{6,7},{7,6},{8,9},{9,8},{10,11... | collective-permute-start | bytes 224264 | tf_op jit(solution)/shard_map/ppermute | solution.py:432
  17.4 2.7 %inner_kernel.1 = (f32[3,2,8,1024]{3,2,1,0:T(8,128)S(1)}, f32[3,2,8,1024]{3,2,1,0:T(8,128)S(1)}, f32[2,3,8,1024]{3,2,1,0:T(8,128)S(1)}, bf16[4,256,256]{2,1,0:T(8,128)(2,1)S(1)}, bf16[4,256,256]{2,1,0:T(8,128)(2,1)S(1)}) custom-call(f32[3,2,8,1024]{3,2,1,0:T(8,128)S(1)} %get-tuple-element.21.b_ref, f32[25,8,128]{2,1,0:T(8,128)S(1)} %collective-permute-done.near_ref, ...), custom_call_target="tpu_custom_call" | custom-call | flops 805306368 | bytes 2105676 | tf_op jit(solution)/shard_map/inner_kernel/pallas_call | solution.py:418
  20.1 0.0 collective-permute-done.3.far_ref
  20.1 0.0 collective-permute-done.4.other_ref
  20.1 0.0 collective-permute-done.5.pair_ref
  20.1 0.0 collective-permute-done.2.far_next_ref
  20.2 1.3 %image_kernel.1 = (f32[3,2,8,1024]{3,2,1,0:T(8,128)S(1)}, f32[3,2,8,1024]{3,2,1,0:T(8,128)S(1)}, f32[32,1,128]{2,1,0:T(1,128)S(1)}) custom-call(f32[3,2,8,1024]{3,2,1,0:T(8,128)S(1)} %get-tuple-element.21.b_ref, f32[3,2,8,1024]{3,2,1,0:T(8,128)S(1)} %get-tuple-element.30.v_ref, f32[3,2,8,1024]{3,2,1,0:T(8,128)S(1)} %get-tuple-element.31.data_ref, ...), custom_call_target="tpu_custom_call" | custom-call | flops 134217728 | bytes 2648396 | tf_op jit(solution)/shard_map/image_kernel/pallas_call | solution.py:418
  21.5 10.2 %all_to_all.5.gram_ref = f32[32,1,128]{2,1,0:T(1,128)S(1)} all-to-all(f32[32,1,128]{2,1,0:T(1,128)S(1)} %get-tuple-element.37), channel_id=1, replica_groups=mesh['inline'=8,'col'=4] {'inline','col'}, dimensions={0} | all-to-all | bytes 32768 | tf_op jit(solution)/shard_map/all_to_all | solution.py:495
  31.7 0.9 %finish_kernel.1 = (f32[3,2,8,1024]{3,2,1,0:T(8,128)}, f32[3,2,8,1024]{3,2,1,0:T(8,128)}) custom-call(f32[32,1,128]{2,1,0:T(1,128)S(1)} %all_to_all.5.gram_ref, f32[3,2,8,1024]{3,2,1,0:T(8,128)S(1)} %get-tuple-element.21.b_ref, f32[3,2,8,1024]{3,2,1,0:T(8,128)S(1)} %get-tuple-element.38.one_ref, f32[3,2,8,1024]{3,2,1,0:T(8,128)S(1)} %get-tuple-element.39.two_ref), custom_call_target="tpu_custom_call" | custom-call | flops 393216 | bytes 999424 | tf_op jit(solution)/shard_map/finish_kernel/pallas_call | solution.py:418
Async XLA Ops:
  2.1 8.0 %collective-permute-start = (f32[25,8,128]{2,1,0:T(8,128)S(1)}, f32[25,8,128]{2,1,0:T(8,128)S(1)}, u32[]{:S(2)}, u32[]{:S(2)}) collective-permute-start(f32[25,8,128]{2,1,0:T(8,128)S(1)} %get-tuple-element.22), channel_id=1, source_target_pairs={{0,4},{4,0},{8,12},{12,8},{16,20},{20,16},{24,28},{28,24},{1,5},{5... | collective-permute-start | bytes 307208 | tf_op jit(solution)/shard_map/ppermute | solution.py:432
  5.1 8.5 %collective-permute-start.1 = (f32[25,8,128]{2,1,0:T(8,128)S(1)}, f32[25,8,128]{2,1,0:T(8,128)S(1)}, u32[]{:S(2)}, u32[]{:S(2)}) collective-permute-start(f32[25,8,128]{2,1,0:T(8,128)S(1)} %get-tuple-element.23), channel_id=1, source_target_pairs={{4,8},{8,4},{12,16},{16,12},{20,24},{24,20},{5,9},{9,5},{13,17},{1... | collective-permute-start | bytes 307208 | tf_op jit(solution)/shard_map/ppermute | solution.py:432
  5.8 14.4 %collective-permute-start.3 = (f32[25,8,128]{2,1,0:T(8,128)S(1)}, f32[25,8,128]{2,1,0:T(8,128)S(1)}, u32[]{:S(2)}, u32[]{:S(2)}) collective-permute-start(f32[25,8,128]{2,1,0:T(8,128)S(1)} %get-tuple-element.23), channel_id=1, source_target_pairs={{0,4},{4,0},{8,12},{12,8},{16,20},{20,16},{24,28},{28,24},{1,5},{5... | collective-permute-start | bytes 307208 | tf_op jit(solution)/shard_map/ppermute | solution.py:432
  10.1 10.0 %collective-permute-start.2 = (f32[25,8,128]{2,1,0:T(8,128)S(1)}, f32[25,8,128]{2,1,0:T(8,128)S(1)}, u32[]{:S(2)}, u32[]{:S(2)}) collective-permute-start(f32[25,8,128]{2,1,0:T(8,128)S(1)} %collective-permute-done.near_ref), channel_id=1, source_target_pairs={{0,8},{8,16},{12,4},{16,24},{20,12},{28,20},{1,9},{9,17},{13,5},{1... | collective-permute-start | bytes 307208 | tf_op jit(solution)/shard_map/ppermute | solution.py:438
  13.8 6.3 %collective-permute-start.4 = (f32[2,9344]{1,0:T(2,128)S(1)}, f32[2,9344]{1,0:T(2,128)S(1)}, u32[]{:S(2)}, u32[]{:S(2)}) collective-permute-start(f32[2,9344]{1,0:T(2,128)S(1)} %get-tuple-element.33), channel_id=1, source_target_pairs={{1,2},{2,1},{5,6},{6,5},{9,10},{10,9},{13,14},{14,13},{17,18},{18,... | collective-permute-start | bytes 224264 | tf_op jit(solution)/shard_map/ppermute | solution.py:432
  14.4 5.7 %collective-permute-start.5 = (f32[2,9344]{1,0:T(2,128)S(1)}, f32[2,9344]{1,0:T(2,128)S(1)}, u32[]{:S(2)}, u32[]{:S(2)}) collective-permute-start(f32[2,9344]{1,0:T(2,128)S(1)} %get-tuple-element.34), channel_id=1, source_target_pairs={{0,1},{1,0},{2,3},{3,2},{4,5},{5,4},{6,7},{7,6},{8,9},{9,8},{10,11... | collective-permute-start | bytes 224264 | tf_op jit(solution)/shard_map/ppermute | solution.py:432

commit v16 on v15

--- a/solution.py
+++ b/solution.py
@@ -17,27 +17,33 @@
     return high, (value - high.astype(F32)).astype(BF16)
 
 
-def band(taps_ref, angle):
-    line = jnp.broadcast_to(taps_ref[angle : angle + 1, :], (2 * LANES, 2 * LANES))
-    rolled = pltpu.roll(line, LANES, 1, stride=1, stride_axis=0)
-    return jnp.concatenate(split(rolled[:, :LANES]), axis=1)
-
-
-def fill_taps(taps_ref, padded_ref, turned_ref):
+def pad_taps(taps_ref, padded_ref):
     padded_ref[...] = jnp.zeros_like(padded_ref)
     padded_ref[0 : taps_ref.shape[0], 0 : taps_ref.shape[1]] = taps_ref[...]
-    rest, parts = padded_ref[...], []
+
+
+def turn(lines, count):
+    n, size = lines.shape
+    parts = []
     for _ in range(3):
-        parts.append(rest.astype(BF16).astype(F32))
-        rest = rest - parts[-1]
-    size = 2 * LANES
+        parts.append(lines.astype(BF16).astype(F32))
+        lines = lines - parts[-1]
     rows = lax.broadcasted_iota(jnp.int32, (size, size), 0)
     cols = lax.broadcasted_iota(jnp.int32, (size, size), 1)
-    flip = jnp.where(rows + cols == taps_ref.shape[1] - 1, 1.0, 0.0).astype(BF16)
-    lines = jnp.concatenate(parts, axis=0).astype(BF16)
-    turned = jnp.dot(lines, flip, preferred_element_type=F32)
-    n = padded_ref.shape[0]
-    turned_ref[...] = turned[:n] + turned[n : 2 * n] + turned[2 * n :]
+    flip = jnp.where(rows + cols == count - 1, 1.0, 0.0).astype(BF16)
+    whole = jnp.concatenate(parts, axis=0).astype(BF16)
+    turned = jnp.dot(whole, flip, preferred_element_type=F32)
+    return turned[:n] + turned[n : 2 * n] + turned[2 * n :]
+
+
+def band(line):
+    lines = jnp.broadcast_to(line, (LANES, line.shape[1]))
+    return jnp.concatenate(split(pltpu.roll(lines, 0, 1, stride=1, stride_axis=0)), axis=0)
+
+
+def convolve(rows, bands):
+    out = lax.dot_general(rows, bands, (((1,), (1,)), ((), ())), preferred_element_type=F32)
+    return out[:, :LANES] + out[:, LANES:]
 
 
 def column(row):
@@ -56,26 +62,20 @@
     return jnp.concatenate(pairs, axis=0)
 
 
-def halves_sum(wide):
-    return wide[:, :LANES] + wide[:, LANES:]
-
-
-def forward(tiles, band):
+def forward(tiles, bands):
     zero = jnp.zeros_like(tiles[0]).astype(BF16)
     highs, lows = zip(*[split(t) for t in tiles])
     n, size = len(tiles) + 1, tiles[0].shape[0]
     rows = [windows([zero, *part, zero]) for part in (highs, lows)]
-    out = jnp.dot(jnp.concatenate(rows, axis=0), band, preferred_element_type=F32)
-    out = halves_sum(out)
+    out = convolve(jnp.concatenate(rows, axis=0), bands)
     out = out[: n * size] + out[n * size :]
     return [out[k * size : (k + 1) * size] for k in range(n)]
 
 
-def backward(parts, band):
+def backward(parts, bands):
     n, size = len(parts[0]) - 1, parts[0][0].shape[0]
     rows = jnp.concatenate([windows(part) for part in parts], axis=0)
-    out = jnp.dot(rows, band, preferred_element_type=F32)
-    out = halves_sum(out)
+    out = convolve(rows, bands)
     total = out[: n * size]
     for p in range(1, len(parts)):
         total = total + out[p * n * size : (p + 1) * n * size]
@@ -101,7 +101,7 @@
                 out_ref[c, r, :, pl.ds(k * LANES, LANES)] = tile[r * size : (r + 1) * size]
 
 
-def right_side(seis_ref, masks, avo_ref, turned_ref):
+def right_side(seis_ref, masks, avo_ref, padded_ref):
     angles, rows, _, samples = seis_ref.shape
     n = samples // LANES
     total = [[None] * n for _ in range(avo_ref.shape[0])]
@@ -117,7 +117,7 @@
             jnp.where(left_half, before, here).astype(BF16)
             for before, here in zip([zero, *turned], [*turned, zero])
         ]
-        add_terms(total, avo_ref, a, backward([shifted], band(turned_ref, a)))
+        add_terms(total, avo_ref, a, backward([shifted], band(padded_ref[a : a + 1, :])))
     return total
 
 
@@ -160,7 +160,7 @@
 
 def start_kernel(
     seis_hbm, valid_hbm, avo_hbm, taps_hbm, prior_hbm, strength_hbm,
-    b_ref, near_ref, far_ref, padded_ref, turned_ref, valid_ref, avo_ref, prior_ref, strength_ref,
+    b_ref, near_ref, far_ref, padded_ref, valid_ref, avo_ref, prior_ref, strength_ref,
     seis_ref, taps_ref, sems,
 ):
     copies = copy_in(
@@ -176,12 +176,12 @@
     )
     for copy in copies[:2]:
         copy.wait()
-    fill_taps(taps_ref, padded_ref, turned_ref)
+    pad_taps(taps_ref, padded_ref)
     angles = avo_ref.shape[1]
     masks = [trace_columns(valid_ref, a) for a in range(angles)]
     for copy in copies[2:]:
         copy.wait()
-    store_tiles(b_ref, right_side(seis_ref, masks, avo_ref, turned_ref))
+    store_tiles(b_ref, right_side(seis_ref, masks, avo_ref, padded_ref))
     contrasts, rows, traces, samples = b_ref.shape
     n = samples // LANES
     first = starts_pair("inline")
@@ -262,14 +262,15 @@
 
 
 def inner_kernel(
-    b_ref, near_ref, near_next_ref, padded_ref, turned_ref, valid_ref, avo_ref, prior_ref,
-    strength_ref, v_ref, data_ref, halo_ref, ahead_ref, back_ref,
+    count, b_ref, near_ref, near_next_ref, padded_ref, valid_ref, avo_ref, prior_ref, strength_ref,
+    v_ref, data_ref, halo_ref, ahead_ref, back_ref,
 ):
     contrasts, rows, traces, samples = b_ref.shape
     angles, n = avo_ref.shape[1], samples // LANES
+    turned = turn(padded_ref[...], count)
     bands = []
     for a in range(angles):
-        bands.append((band(padded_ref, a), band(turned_ref, a)))
+        bands.append((band(turned[a : a + 1]), band(padded_ref[a : a + 1, :])))
         ahead_ref[a], back_ref[a] = bands[a]
     masks = [trace_columns(valid_ref, a) for a in range(angles)]
     weights = [column(prior_ref[r : r + 1, :]) + 4.0 for r in range(rows)]
@@ -423,7 +424,7 @@
         scratch_shapes=list(scratch),
         compiler_params=pltpu.CompilerParams(vmem_limit_bytes=24 * 1024 * 1024),
         cost_estimate=pl.CostEstimate(flops=flops, bytes_accessed=moved, transcendentals=0),
-        name=kernel.__name__,
+        name=getattr(kernel, "func", kernel).__name__,
     )(*ins)
 
 
@@ -451,10 +452,10 @@
     given = (seismic, validity, avo_coeffs, wavelets, prior_weight, lateral_strength.reshape(1, -1))
     kept = [given[i] for i in (1, 2, 4, 5)]
     edge = shape(contrasts * samples // LANES + 1, traces, LANES)
-    b, near, far, padded, turned, *kept = call(
+    b, near, far, padded, *kept = call(
         start_kernel,
         (
-            field, edge, edge, lines, lines,
+            field, edge, edge, lines,
             *[jax.ShapeDtypeStruct(x.shape, x.dtype) for x in kept],
         ),
         [pltpu.with_memory_space_constraint(x, pltpu.HBM) for x in given],
@@ -477,9 +478,9 @@
     col_pair = swap("col", col_pair, 0)
     bands = jax.ShapeDtypeStruct((angles, 2 * LANES, 2 * LANES), BF16)
     image, data, halo, ahead, back = call(
-        inner_kernel,
+        functools.partial(inner_kernel, wavelets.shape[1]),
         (field, field, shape(2, contrasts, traces, samples), bands, bands),
-        (b, near, near_next, padded, turned, *kept),
+        (b, near, near_next, padded, *kept),
         6 * work,
     )
     axes = ("inline", "col")

time: 32.9 us -> 32.6 us (level)
  Pallas kernels: 6.62 us -> 6.25 us
    pallas_call x5, Pallas kernels: 6.62 us -> 6.25 us  [call(): pl.pallas_call(kernel, out_shape=outs, in_specs=[VMEM] * len(ins) if plac...]
  transfers between devices with their start and end apart: 6 -> 6, of which waited for: 0 -> 0; matrix products, arithmetic and copies ran while one was open for 0% -> 0% of each run, Pallas kernels for 9% -> 8%
where the time goes in v16:
time: 32.6 us; the launch traced here: 32.4 us
  starting transfers between devices  15.1 us (46%)
  blocking collectives  10.3 us (32%)
  Pallas kernels  6.25 us (19%)
  between operations  0.72 us (2%)
    ppermute x5, starting transfers between devices, swap(): lax.ppermute(value, axis, [(i + d, i + 1 - d) for i in starts for d in (0...  11.6 us
    all_to_all x1, blocking collectives, shards(): gram = lax.all_to_all(gram, axes, 0, 0)  10.3 us
    pallas_call x5, Pallas kernels, call(): pl.pallas_call(kernel, out_shape=outs, in_specs=[VMEM] * len(ins) if plac...  6.25 us
    ppermute x1, starting transfers between devices, hand_on(): lax.ppermute(value, axis, [(i, j) for i, j in steps if 0 <= j < size])  3.48 us
  transfers between devices with their start and end apart: 6, of which 0 were waited for; matrix products, arithmetic and copies ran while one was open for 0% of the time, Pallas kernels for 8%

profile of v16, /device:TPU:0, one launch (start us, length us, event | category | flops | bytes accessed | tf_op | source)
XLA Modules:
  0.0 32.4 jit_solution(13741599231934770261)
XLA Ops:
  0.6 1.5 %start_kernel.1 = (f32[3,2,8,1024]{3,2,1,0:T(8,128)S(1)}, f32[25,8,128]{2,1,0:T(8,128)S(1)}, f32[25,8,128]{2,1,0:T(8,128)S(1)}, f32[8,256]{1,0:T(8,128)S(1)}, s3...) custom-call(bf16[4,2,8,1024]{3,2,1,0:T(8,128)(2,1)} %seis_hbm.1, ...), custom_call_target="tpu_custom_call" | custom-call | flops 134217728 | bytes 641704 | tf_op jit(solution)/shard_map/start_kernel/pallas_call | solution.py:419
  2.2 3.0 %collective-permute-start = (f32[25,8,128]{2,1,0:T(8,128)S(1)}, f32[25,8,128]{2,1,0:T(8,128)S(1)}, u32[]{:S(2)}, u32[]{:S(2)}) collective-permute-start(f32[25,8,128]{2,1,0:T(8,128)S(1)} %get-tuple-element.21), channel_id=1, source_target_pairs={{0,4},{4,0},{8,12},{12,8},{16,20},{20,16},{24,28},{28,24},{1,5},{5... | collective-permute-start | bytes 307208 | tf_op jit(solution)/shard_map/ppermute | solution.py:433
  5.2 0.7 %collective-permute-start.1 = (f32[25,8,128]{2,1,0:T(8,128)S(1)}, f32[25,8,128]{2,1,0:T(8,128)S(1)}, u32[]{:S(2)}, u32[]{:S(2)}) collective-permute-start(f32[25,8,128]{2,1,0:T(8,128)S(1)} %get-tuple-element.22), channel_id=1, source_target_pairs={{4,8},{8,4},{12,16},{16,12},{20,24},{24,20},{5,9},{9,5},{13,17},{1... | collective-permute-start | bytes 307208 | tf_op jit(solution)/shard_map/ppermute | solution.py:433
  5.9 4.3 %collective-permute-start.3 = (f32[25,8,128]{2,1,0:T(8,128)S(1)}, f32[25,8,128]{2,1,0:T(8,128)S(1)}, u32[]{:S(2)}, u32[]{:S(2)}) collective-permute-start(f32[25,8,128]{2,1,0:T(8,128)S(1)} %get-tuple-element.22), channel_id=1, source_target_pairs={{0,4},{4,0},{8,12},{12,8},{16,20},{20,16},{24,28},{28,24},{1,5},{5... | collective-permute-start | bytes 307208 | tf_op jit(solution)/shard_map/ppermute | solution.py:433
  10.2 0.0 collective-permute-done.near_ref
  10.2 3.5 %collective-permute-start.2 = (f32[25,8,128]{2,1,0:T(8,128)S(1)}, f32[25,8,128]{2,1,0:T(8,128)S(1)}, u32[]{:S(2)}, u32[]{:S(2)}) collective-permute-start(f32[25,8,128]{2,1,0:T(8,128)S(1)} %collective-permute-done.near_ref), channel_id=1, source_target_pairs={{0,8},{8,16},{12,4},{16,24},{20,12},{28,20},{1,9},{9,17},{13,5},{1... | collective-permute-start | bytes 307208 | tf_op jit(solution)/shard_map/ppermute | solution.py:439
  13.7 0.0 collective-permute-done.1.near_next_ref
  13.7 0.2 column_kernel.1
  13.9 0.7 %collective-permute-start.4 = (f32[2,9344]{1,0:T(2,128)S(1)}, f32[2,9344]{1,0:T(2,128)S(1)}, u32[]{:S(2)}, u32[]{:S(2)}) collective-permute-start(f32[2,9344]{1,0:T(2,128)S(1)} %get-tuple-element.31), channel_id=1, source_target_pairs={{1,2},{2,1},{5,6},{6,5},{9,10},{10,9},{13,14},{14,13},{17,18},{18,... | collective-permute-start | bytes 224264 | tf_op jit(solution)/shard_map/ppermute | solution.py:433
  14.5 2.9 %collective-permute-start.5 = (f32[2,9344]{1,0:T(2,128)S(1)}, f32[2,9344]{1,0:T(2,128)S(1)}, u32[]{:S(2)}, u32[]{:S(2)}) collective-permute-start(f32[2,9344]{1,0:T(2,128)S(1)} %get-tuple-element.32), channel_id=1, source_target_pairs={{0,1},{1,0},{2,3},{3,2},{4,5},{5,4},{6,7},{7,6},{8,9},{9,8},{10,11... | collective-permute-start | bytes 224264 | tf_op jit(solution)/shard_map/ppermute | solution.py:433
  17.5 2.6 %inner_kernel.1 = (f32[3,2,8,1024]{3,2,1,0:T(8,128)S(1)}, f32[3,2,8,1024]{3,2,1,0:T(8,128)S(1)}, f32[2,3,8,1024]{3,2,1,0:T(8,128)S(1)}, bf16[4,256,256]{2,1,0:T(8,128)(2,1)S(1)}, bf16[4,256,256]{2,1,0:T(8,128)(2,1)S(1)}) custom-call(f32[3,2,8,1024]{3,2,1,0:T(8,128)S(1)} %get-tuple-element.20.b_ref, f32[25,8,128]{2,1,0:T(8,128)S(1)} %collective-permute-done.near_ref, ...), custom_call_target="tpu_custom_call" | custom-call | flops 805306368 | bytes 2097484 | tf_op jit(solution)/shard_map/inner_kernel/pallas_call | solution.py:419
  20.1 0.0 collective-permute-done.3.far_ref
  20.1 0.0 collective-permute-done.4.other_ref
  20.1 0.0 collective-permute-done.5.pair_ref
  20.1 0.0 collective-permute-done.2.far_next_ref
  20.1 1.0 %image_kernel.1 = (f32[3,2,8,1024]{3,2,1,0:T(8,128)S(1)}, f32[3,2,8,1024]{3,2,1,0:T(8,128)S(1)}, f32[32,1,128]{2,1,0:T(1,128)S(1)}) custom-call(f32[3,2,8,1024]{3,2,1,0:T(8,128)S(1)} %get-tuple-element.20.b_ref, f32[3,2,8,1024]{3,2,1,0:T(8,128)S(1)} %get-tuple-element.28.v_ref, f32[3,2,8,1024]{3,2,1,0:T(8,128)S(1)} %get-tuple-element.29.data_ref, ...), custom_call_target="tpu_custom_call" | custom-call | flops 134217728 | bytes 2648396 | tf_op jit(solution)/shard_map/image_kernel/pallas_call | solution.py:419
  21.1 10.3 %all_to_all.5.gram_ref = f32[32,1,128]{2,1,0:T(1,128)S(1)} all-to-all(f32[32,1,128]{2,1,0:T(1,128)S(1)} %get-tuple-element.35), channel_id=1, replica_groups=mesh['inline'=8,'col'=4] {'inline','col'}, dimensions={0} | all-to-all | bytes 32768 | tf_op jit(solution)/shard_map/all_to_all | solution.py:496
  31.5 0.9 %finish_kernel.1 = (f32[3,2,8,1024]{3,2,1,0:T(8,128)}, f32[3,2,8,1024]{3,2,1,0:T(8,128)}) custom-call(f32[32,1,128]{2,1,0:T(1,128)S(1)} %all_to_all.5.gram_ref, f32[3,2,8,1024]{3,2,1,0:T(8,128)S(1)} %get-tuple-element.20.b_ref, f32[3,2,8,1024]{3,2,1,0:T(8,128)S(1)} %get-tuple-element.36.one_ref, f32[3,2,8,1024]{3,2,1,0:T(8,128)S(1)} %get-tuple-element.37.two_ref), custom_call_target="tpu_custom_call" | custom-call | flops 393216 | bytes 999424 | tf_op jit(solution)/shard_map/finish_kernel/pallas_call | solution.py:419
Async XLA Ops:
  2.2 8.0 %collective-permute-start = (f32[25,8,128]{2,1,0:T(8,128)S(1)}, f32[25,8,128]{2,1,0:T(8,128)S(1)}, u32[]{:S(2)}, u32[]{:S(2)}) collective-permute-start(f32[25,8,128]{2,1,0:T(8,128)S(1)} %get-tuple-element.21), channel_id=1, source_target_pairs={{0,4},{4,0},{8,12},{12,8},{16,20},{20,16},{24,28},{28,24},{1,5},{5... | collective-permute-start | bytes 307208 | tf_op jit(solution)/shard_map/ppermute | solution.py:433
  5.2 8.5 %collective-permute-start.1 = (f32[25,8,128]{2,1,0:T(8,128)S(1)}, f32[25,8,128]{2,1,0:T(8,128)S(1)}, u32[]{:S(2)}, u32[]{:S(2)}) collective-permute-start(f32[25,8,128]{2,1,0:T(8,128)S(1)} %get-tuple-element.22), channel_id=1, source_target_pairs={{4,8},{8,4},{12,16},{16,12},{20,24},{24,20},{5,9},{9,5},{13,17},{1... | collective-permute-start | bytes 307208 | tf_op jit(solution)/shard_map/ppermute | solution.py:433
  5.9 14.2 %collective-permute-start.3 = (f32[25,8,128]{2,1,0:T(8,128)S(1)}, f32[25,8,128]{2,1,0:T(8,128)S(1)}, u32[]{:S(2)}, u32[]{:S(2)}) collective-permute-start(f32[25,8,128]{2,1,0:T(8,128)S(1)} %get-tuple-element.22), channel_id=1, source_target_pairs={{0,4},{4,0},{8,12},{12,8},{16,20},{20,16},{24,28},{28,24},{1,5},{5... | collective-permute-start | bytes 307208 | tf_op jit(solution)/shard_map/ppermute | solution.py:433
  10.2 9.9 %collective-permute-start.2 = (f32[25,8,128]{2,1,0:T(8,128)S(1)}, f32[25,8,128]{2,1,0:T(8,128)S(1)}, u32[]{:S(2)}, u32[]{:S(2)}) collective-permute-start(f32[25,8,128]{2,1,0:T(8,128)S(1)} %collective-permute-done.near_ref), channel_id=1, source_target_pairs={{0,8},{8,16},{12,4},{16,24},{20,12},{28,20},{1,9},{9,17},{13,5},{1... | collective-permute-start | bytes 307208 | tf_op jit(solution)/shard_map/ppermute | solution.py:439
  13.9 6.2 %collective-permute-start.4 = (f32[2,9344]{1,0:T(2,128)S(1)}, f32[2,9344]{1,0:T(2,128)S(1)}, u32[]{:S(2)}, u32[]{:S(2)}) collective-permute-start(f32[2,9344]{1,0:T(2,128)S(1)} %get-tuple-element.31), channel_id=1, source_target_pairs={{1,2},{2,1},{5,6},{6,5},{9,10},{10,9},{13,14},{14,13},{17,18},{18,... | collective-permute-start | bytes 224264 | tf_op jit(solution)/shard_map/ppermute | solution.py:433
  14.5 5.5 %collective-permute-start.5 = (f32[2,9344]{1,0:T(2,128)S(1)}, f32[2,9344]{1,0:T(2,128)S(1)}, u32[]{:S(2)}, u32[]{:S(2)}) collective-permute-start(f32[2,9344]{1,0:T(2,128)S(1)} %get-tuple-element.32), channel_id=1, source_target_pairs={{0,1},{1,0},{2,3},{3,2},{4,5},{5,4},{6,7},{7,6},{8,9},{9,8},{10,11... | collective-permute-start | bytes 224264 | tf_op jit(solution)/shard_map/ppermute | solution.py:433

commit v17 on v16

--- a/solution.py
+++ b/solution.py
@@ -101,7 +101,7 @@
                 out_ref[c, r, :, pl.ds(k * LANES, LANES)] = tile[r * size : (r + 1) * size]
 
 
-def right_side(seis_ref, masks, avo_ref, padded_ref):
+def right_side(seis_ref, masks, avo_ref, bands):
     angles, rows, _, samples = seis_ref.shape
     n = samples // LANES
     total = [[None] * n for _ in range(avo_ref.shape[0])]
@@ -117,7 +117,7 @@
             jnp.where(left_half, before, here).astype(BF16)
             for before, here in zip([zero, *turned], [*turned, zero])
         ]
-        add_terms(total, avo_ref, a, backward([shifted], band(padded_ref[a : a + 1, :])))
+        add_terms(total, avo_ref, a, backward([shifted], bands[a]))
     return total
 
 
@@ -178,10 +178,11 @@
         copy.wait()
     pad_taps(taps_ref, padded_ref)
     angles = avo_ref.shape[1]
+    bands = [band(padded_ref[a : a + 1, :]) for a in range(angles)]
     masks = [trace_columns(valid_ref, a) for a in range(angles)]
     for copy in copies[2:]:
         copy.wait()
-    store_tiles(b_ref, right_side(seis_ref, masks, avo_ref, padded_ref))
+    store_tiles(b_ref, right_side(seis_ref, masks, avo_ref, bands))
     contrasts, rows, traces, samples = b_ref.shape
     n = samples // LANES
     first = starts_pair("inline")
@@ -233,45 +234,59 @@
     return [jnp.concatenate(side, axis=1) for side in zip(*tiles)]
 
 
-def column_kernel(b_ref, near_ref, near_next_ref, valid_ref, prior_ref, pair_ref, other_ref):
+def column_kernel(
+    b_ref, near_ref, near_next_ref, valid_ref, prior_ref,
+    pair_ref, other_ref, own_ref, note_ref, second_ref,
+):
     contrasts, rows, traces, samples = b_ref.shape
     angles = valid_ref.shape[0]
     first_col = starts_pair("col")
-    lines = []
+    half = rows + 2
+    second_ref[...] = jnp.zeros_like(second_ref)
+    note_ref[...] = jnp.zeros_like(note_ref)
     for c in range(contrasts):
-        above, below = row_pair(near_ref, near_next_ref, c, samples // LANES)
         own = [b_ref[c, r] for r in range(rows)]
-        lines += [(line[0:1], line[traces - 1 :]) for line in (above, *own, below)]
-        lines += [(line[1:2], line[traces - 2 : traces - 1]) for line in own]
-    for e, (left, right) in enumerate(lines):
-        place = (slice(e % rows, e % rows + 1), pl.ds(e // rows * samples, samples))
-        pair_ref[place] = jnp.where(first_col, right, left)
-        other_ref[place] = jnp.where(first_col, left, right)
+        for i, line in enumerate([*own, *row_pair(near_ref, near_next_ref, c, samples // LANES)]):
+            own_ref[c, i : i + 1, :] = line[0:1]
+            own_ref[c, half + i : half + i + 1, :] = line[traces - 1 :]
+        for r, line in enumerate(own):
+            at = c * rows + r
+            second_ref[0, at : at + 1, :] = line[1:2]
+            second_ref[1, at : at + 1, :] = line[traces - 2 : traces - 1]
     lane = lax.broadcasted_iota(jnp.int32, (1, LANES), 1)
     for r in range(rows):
-        notes = []
-        for t in (0, traces - 1):
+        for side, t in enumerate((0, traces - 1)):
             note = jnp.where(lane == angles, prior_ref[r : r + 1, t : t + 1], 0.0)
             for a in range(angles):
                 note = jnp.where(lane == a, valid_ref[a, r : r + 1, t : t + 1].astype(F32), note)
-            notes.append(note)
-        left, right = notes
-        place = (slice(r, r + 1), pl.ds(len(lines) // rows * samples, LANES))
-        pair_ref[place] = jnp.where(first_col, right, left)
-        other_ref[place] = jnp.where(first_col, left, right)
+            at = contrasts * rows + r
+            second_ref[side, at : at + 1, 0:LANES] = note
+            at = r + side * (traces - rows)
+            note_ref[at : at + 1, :] = note
+    for c in range(contrasts):
+        left, right = own_ref[c, 0:half], own_ref[c, half:]
+        pair_ref[c] = jnp.where(first_col, right, left)
+        other_ref[c] = jnp.where(first_col, left, right)
+    for i in range(2):
+        left, right = (second_ref[side, i * half : (i + 1) * half] for side in (0, 1))
+        pair_ref[contrasts + i] = jnp.where(first_col, right, left)
+        other_ref[contrasts + i] = jnp.where(first_col, left, right)
+
+
+def bands_kernel(count, padded_ref, near_ref, ahead_ref, back_ref):
+    turned = turn(padded_ref[...], count)
+    for a in range(ahead_ref.shape[0]):
+        ahead_ref[a] = band(turned[a : a + 1])
+        back_ref[a] = band(padded_ref[a : a + 1, :])
 
 
 def inner_kernel(
-    count, b_ref, near_ref, near_next_ref, padded_ref, valid_ref, avo_ref, prior_ref, strength_ref,
-    v_ref, data_ref, halo_ref, ahead_ref, back_ref,
+    b_ref, near_ref, near_next_ref, valid_ref, avo_ref, prior_ref, strength_ref, ahead_ref, back_ref,
+    v_ref, data_ref, halo_ref,
 ):
     contrasts, rows, traces, samples = b_ref.shape
     angles, n = avo_ref.shape[1], samples // LANES
-    turned = turn(padded_ref[...], count)
-    bands = []
-    for a in range(angles):
-        bands.append((band(turned[a : a + 1]), band(padded_ref[a : a + 1, :])))
-        ahead_ref[a], back_ref[a] = bands[a]
+    bands = [(ahead_ref[a], back_ref[a]) for a in range(angles)]
     masks = [trace_columns(valid_ref, a) for a in range(angles)]
     weights = [column(prior_ref[r : r + 1, :]) + 4.0 for r in range(rows)]
     above, below = either_side(near_ref, near_next_ref, contrasts * n)
@@ -309,78 +324,71 @@
 
 
 def image_kernel(
-    b_ref, v_ref, data_ref, halo_ref, far_next_ref, far_ref, other_ref, pair_ref,
-    valid_ref, avo_ref, prior_ref, strength_ref, ahead_ref, back_ref,
+    b_ref, v_ref, data_ref, halo_ref, own_ref, note_ref, far_next_ref, far_ref, other_ref, pair_ref,
+    avo_ref, prior_ref, strength_ref, ahead_ref, back_ref,
     one_ref, two_ref, gram_ref,
 ):
     contrasts, rows, traces, samples = b_ref.shape
     angles, n = avo_ref.shape[1], samples // LANES
     has_left, has_right = inside("col")
     first_col = starts_pair("col")
-    left = jnp.where(first_col, other_ref[...], pair_ref[...])
-    right = jnp.where(first_col, pair_ref[...], other_ref[...])
     place = lax.broadcasted_iota(jnp.int32, (traces, samples), 0)
-    ext = rows + 2
-
-    def trace(side, c, i):
-        e = c * (ext + rows) + i
-        return side[e % rows : e % rows + 1, e // rows * samples : (e // rows + 1) * samples]
-
-    def note(side, r, i):
-        at = contrasts * (ext + rows) // rows * samples + i
-        return side[r : r + 1, at : at + 1]
-
-    def beside(c, i):
-        west, east = trace(left, c, i), trace(right, c, i)
-        return jnp.where(place == 0, west, jnp.where(place == traces - 1, east, 0.0))
-
-    def spread(values):
-        total = values[-1]
-        for t in range(traces - 2, -1, -1):
-            total = jnp.where(place[:, : values[0].shape[1]] == t, values[t], total)
-        return total
-
-    bands = [(ahead_ref[a], back_ref[a]) for a in range(angles)]
-    masks = []
-    for a in range(angles):
-        own = [
-            [valid_ref[a, r : r + 1, t : t + 1].astype(F32) for r in range(rows)]
-            for t in (0, traces - 1)
-        ]
-        west, east = ([note(side, r, a) for r in range(rows)] for side in (left, right))
-        masks.append(spread([*own[0], *west, *east[::-1], *own[1][::-1]]))
+    west, east = place == 0, place == traces - 1
+    half = traces // 2
+
+    def turned(value, k):
+        return pltpu.roll(value, k % traces, 0) if k % traces else value
+
+    def sides(i):
+        pair, other = pair_ref[i], other_ref[i]
+        left, right = jnp.where(first_col, other, pair), jnp.where(first_col, pair, other)
+        return jnp.concatenate([left, right], axis=0)
+
+    def at_ends(value, left, right, inner):
+        return jnp.where(west, turned(value, left), jnp.where(east, turned(value, right), inner))
+
+    beside = [sides(c) for c in range(contrasts)]
+    seconds = [sides(contrasts), sides(contrasts + 1)]
+    notes = seconds[1][:, :LANES]
+    line = place[:, :LANES]
+    theirs = turned(notes, -rows)
+    mixed = jnp.where((line == 2) | (line == 3), notes, note_ref[...])
+    mixed = jnp.where((line == 4) | (line == 5), theirs, mixed)
+    masks = [mixed[:, a : a + 1] for a in range(angles)]
+    mine = (place[:, :1] < 2) | (place[:, :1] >= traces - 2)
     tile = []
     for c in range(contrasts):
-        strength = strength_ref[:, c : c + 1]
-        west, east = ([trace(side, c, r + 1) for r in range(rows)] for side in (left, right))
-        less = [-strength * line for line in west], [-strength * line for line in east]
-        whole = spread([*less[0], *west, *east[::-1], *less[1][::-1]])
+        scale = jnp.where(mine, -strength_ref[:, c : c + 1], 1.0)
+        whole = jnp.where(place % half < rows, beside[c], turned(beside[c], rows)) * scale
         tile.append([whole[:, k * LANES : (k + 1) * LANES] for k in range(n)])
-    edge = [jnp.concatenate(line, axis=1) for line in normal(tile, masks, avo_ref, bands)]
-
+    bands = [(ahead_ref[a], back_ref[a]) for a in range(angles)]
+    edge = [jnp.concatenate(tiles, axis=1) for tiles in normal(tile, masks, avo_ref, bands)]
+
+    has = jnp.where(place[:, :1] < half, has_left, has_right)
+    far_weight = theirs[:, angles : angles + 1] + 4.0
     weights = [column(prior_ref[r : r + 1, :]) + 4.0 for r in range(rows)]
     sums = [jnp.zeros((traces, LANES), F32) for _ in range(4)]
     for c in range(contrasts):
         strength = strength_ref[:, c : c + 1]
-        beyond = row_pair(far_ref, far_next_ref, c, n)
-        over, under = (halo_ref[i, c] - strength * beyond[i] for i in (0, 1))
+        theirs = beside[c]
+        around = turned(seconds[c // 2], -rows * (c % 2)) + turned(theirs, -rows)
+        around = around + jnp.where(place % 2 == 1, turned(theirs, 1), turned(theirs, -1))
+        prior = far_weight * theirs - (around + has * own_ref[c])
+        beyond = jnp.where(place < half, turned(edge[c], -rows), edge[c]) + strength * prior
+
+        far_rows = row_pair(far_ref, far_next_ref, c, n)
+        over, under = (halo_ref[i, c] - strength * far_rows[i] for i in (0, 1))
         lines = [over, *[v_ref[c, r] for r in range(rows)], under]
-        lines = [line - strength * beside(c, i) for i, line in enumerate(lines)]
+        lines = [
+            here - strength * at_ends(theirs, -k, half - 1 - k, 0.0)
+            for here, k in zip(lines, (rows, *range(rows), rows + 1))
+        ]
         for r in range(rows):
             here, b = lines[r + 1], b_ref[c, r]
-            beyond = []
-            for side, has, t, u in (
-                (left, has_left, 0, rows + r),
-                (right, has_right, traces - 1, traces - rows - 1 - r),
-            ):
-                weight = note(side, r, angles) + 4.0
-                around = trace(side, c, r) + trace(side, c, r + 2) + trace(side, c, ext + r)
-                around = around + has * b[t : t + 1]
-                prior = strength * (weight * trace(side, c, r + 1) - around)
-                beyond.append(edge[c][u : u + 1] + prior)
-            around = lateral(here, lines[r], lines[r + 2], *beyond)
-            first, last = edge[c][r : r + 1], edge[c][traces - 1 - r : traces - r]
-            mend = jnp.where(place == 0, first, jnp.where(place == traces - 1, last, 0.0))
+            ends = jnp.where(west, turned(beyond, -r), turned(beyond, half - 1 - r))
+            around = jnp.where(west, ends, turned(here, 1)) + jnp.where(east, ends, turned(here, -1))
+            around = around + lines[r] + lines[r + 2]
+            mend = at_ends(edge[c], -r, 1 - r, 0.0)
             two = data_ref[c, r] + mend + strength * (weights[r] * here - around)
             one_ref[c, r] = here
             two_ref[c, r] = two
@@ -445,7 +453,7 @@
     avo_coeffs = jnp.swapaxes(avo_coeffs, 0, 1)
     shape = lambda *dims: jax.ShapeDtypeStruct(dims, F32)
     field = shape(contrasts, rows, traces, samples)
-    side = shape(rows, contrasts * (2 * rows + 2) // rows * samples + LANES)
+    side = shape(contrasts + 2, rows + 2, samples)
     lines = shape(8, 2 * LANES)
     work = 2 * angles * rows * traces * samples * 256 * 4
 
@@ -471,16 +479,23 @@
     near_next = swap("inline", far, 1)
     far_next = hand_on("inline", near)
     far = swap("inline", far, 0)
-    col_pair, col_other = call(
-        column_kernel, (side, side), (b, near, near_next, kept[0], kept[2]), 2 * field.size
+    bands = jax.ShapeDtypeStruct((angles, 2 * LANES, 2 * LANES), BF16)
+    ahead, back = call(
+        functools.partial(bands_kernel, wavelets.shape[1]), (bands, bands), (padded, near), work // 8
+    )
+    col_pair, col_other, own, note = call(
+        column_kernel,
+        (side, side, shape(contrasts, 2 * rows + 4, samples), shape(traces, LANES)),
+        (b, near, near_next, kept[0], kept[2]),
+        2 * field.size,
+        [pltpu.VMEM((2, 2 * rows + 4, samples), F32)],
     )
     col_other = swap("col", col_other, 1)
     col_pair = swap("col", col_pair, 0)
-    bands = jax.ShapeDtypeStruct((angles, 2 * LANES, 2 * LANES), BF16)
-    image, data, halo, ahead, back = call(
-        functools.partial(inner_kernel, wavelets.shape[1]),
-        (field, field, shape(2, contrasts, traces, samples), bands, bands),
-        (b, near, near_next, padded, *kept),
+    image, data, halo = call(
+        inner_kernel,
+        (field, field, shape(2, contrasts, traces, samples)),
+        (b, near, near_next, *kept, ahead, back),
         6 * work,
     )
     axes = ("inline", "col")
@@ -488,8 +503,8 @@
         image_kernel,
         (field, field, shape(lax.axis_size(axes), 1, LANES)),
         (
-            b, image, data, halo, far_next, far, col_other, col_pair,
-            *kept, ahead, back,
+            b, image, data, halo, own, note, far_next, far, col_other, col_pair,
+            *kept[1:], ahead, back,
         ),
         work,
     )

time: 32.6 us -> 32.6 us (level)
  blocking collectives: 10.3 us -> 9.92 us
    all_to_all x1, blocking collectives: 10.3 us -> 9.92 us  [shards(): gram = lax.all_to_all(gram, axes, 0, 0)]
    pallas_call x5 -> x6, Pallas kernels: 6.25 us -> 6.57 us  [call(): pl.pallas_call(kernel, out_shape=outs, in_specs=[VMEM] * len(ins) if plac...]
  transfers between devices with their start and end apart: 6 -> 6, of which waited for: 0 -> 0; matrix products, arithmetic and copies ran while one was open for 0% -> 0% of each run, Pallas kernels for 8% -> 10%
where the time goes in v17:
time: 32.6 us; the launch traced here: 32.3 us
  starting transfers between devices  15.1 us (46%)
  blocking collectives  9.92 us (30%)
  Pallas kernels  6.57 us (20%)
  between operations  0.72 us (2%)
    ppermute x5, starting transfers between devices, swap(): lax.ppermute(value, axis, [(i + d, i + 1 - d) for i in starts for d in (0...  11.6 us
    all_to_all x1, blocking collectives, shards(): gram = lax.all_to_all(gram, axes, 0, 0)  9.92 us
    pallas_call x6, Pallas kernels, call(): pl.pallas_call(kernel, out_shape=outs, in_specs=[VMEM] * len(ins) if plac...  6.57 us
    ppermute x1, starting transfers between devices, hand_on(): lax.ppermute(value, axis, [(i, j) for i, j in steps if 0 <= j < size])  3.48 us
  transfers between devices with their start and end apart: 6, of which 0 were waited for; matrix products, arithmetic and copies ran while one was open for 0% of the time, Pallas kernels for 10%

profile of v17, /device:TPU:0, one launch (start us, length us, event | category | flops | bytes accessed | tf_op | source)
XLA Modules:
  0.0 32.3 jit_solution(18283711579623466572)
XLA Ops:
  0.6 1.4 %start_kernel.1 = (f32[3,2,8,1024]{3,2,1,0:T(8,128)S(1)}, f32[25,8,128]{2,1,0:T(8,128)S(1)}, f32[25,8,128]{2,1,0:T(8,128)S(1)}, f32[8,256]{1,0:T(8,128)S(1)}, s3...) custom-call(bf16[4,2,8,1024]{3,2,1,0:T(8,128)(2,1)} %seis_hbm.1, ...), custom_call_target="tpu_custom_call" | custom-call | flops 134217728 | bytes 641704 | tf_op jit(solution)/shard_map/start_kernel/pallas_call | solution.py:427
  2.1 3.0 %collective-permute-start = (f32[25,8,128]{2,1,0:T(8,128)S(1)}, f32[25,8,128]{2,1,0:T(8,128)S(1)}, u32[]{:S(2)}, u32[]{:S(2)}) collective-permute-start(f32[25,8,128]{2,1,0:T(8,128)S(1)} %get-tuple-element.23), channel_id=1, source_target_pairs={{0,4},{4,0},{8,12},{12,8},{16,20},{20,16},{24,28},{28,24},{1,5},{5... | collective-permute-start | bytes 307208 | tf_op jit(solution)/shard_map/ppermute | solution.py:441
  5.1 0.7 %collective-permute-start.1 = (f32[25,8,128]{2,1,0:T(8,128)S(1)}, f32[25,8,128]{2,1,0:T(8,128)S(1)}, u32[]{:S(2)}, u32[]{:S(2)}) collective-permute-start(f32[25,8,128]{2,1,0:T(8,128)S(1)} %get-tuple-element.24), channel_id=1, source_target_pairs={{4,8},{8,4},{12,16},{16,12},{20,24},{24,20},{5,9},{9,5},{13,17},{1... | collective-permute-start | bytes 307208 | tf_op jit(solution)/shard_map/ppermute | solution.py:441
  5.7 4.3 %collective-permute-start.3 = (f32[25,8,128]{2,1,0:T(8,128)S(1)}, f32[25,8,128]{2,1,0:T(8,128)S(1)}, u32[]{:S(2)}, u32[]{:S(2)}) collective-permute-start(f32[25,8,128]{2,1,0:T(8,128)S(1)} %get-tuple-element.24), channel_id=1, source_target_pairs={{0,4},{4,0},{8,12},{12,8},{16,20},{20,16},{24,28},{28,24},{1,5},{5... | collective-permute-start | bytes 307208 | tf_op jit(solution)/shard_map/ppermute | solution.py:441
  10.1 0.0 collective-permute-done.near_ref
  10.1 3.5 %collective-permute-start.2 = (f32[25,8,128]{2,1,0:T(8,128)S(1)}, f32[25,8,128]{2,1,0:T(8,128)S(1)}, u32[]{:S(2)}, u32[]{:S(2)}) collective-permute-start(f32[25,8,128]{2,1,0:T(8,128)S(1)} %collective-permute-done.near_ref), channel_id=1, source_target_pairs={{0,8},{8,16},{12,4},{16,24},{20,12},{28,20},{1,9},{9,17},{13,5},{1... | collective-permute-start | bytes 307208 | tf_op jit(solution)/shard_map/ppermute | solution.py:447
  13.6 0.0 collective-permute-done.1.near_next_ref
  13.6 0.1 column_kernel.1
  13.7 0.7 %collective-permute-start.4 = (f32[5,4,1024]{2,1,0:T(4,128)S(1)}, f32[5,4,1024]{2,1,0:T(4,128)S(1)}, u32[]{:S(2)}, u32[]{:S(2)}) collective-permute-start(f32[5,4,1024]{2,1,0:T(4,128)S(1)} %get-tuple-element.37), channel_id=1, source_target_pairs={{1,2},{2,1},{5,6},{6,5},{9,10},{10,9},{13,14},{14,13},{17,18},{18,... | collective-permute-start | bytes 245768 | tf_op jit(solution)/shard_map/ppermute | solution.py:441
  14.4 2.9 %collective-permute-start.5 = (f32[5,4,1024]{2,1,0:T(4,128)S(1)}, f32[5,4,1024]{2,1,0:T(4,128)S(1)}, u32[]{:S(2)}, u32[]{:S(2)}) collective-permute-start(f32[5,4,1024]{2,1,0:T(4,128)S(1)} %get-tuple-element.38), channel_id=1, source_target_pairs={{0,1},{1,0},{2,3},{3,2},{4,5},{5,4},{6,7},{7,6},{8,9},{9,8},{10,11... | collective-permute-start | bytes 245768 | tf_op jit(solution)/shard_map/ppermute | solution.py:441
  17.3 0.4 %bands_kernel.1 = (bf16[4,256,256]{2,1,0:T(8,128)(2,1)S(1)}, bf16[4,256,256]{2,1,0:T(8,128)(2,1)S(1)}) custom-call(f32[8,256]{1,0:T(8,128)S(1)} %get-tuple-element.29.padded_ref, f32[25,8,128]{2,1,0:T(8,128)S(1)} %collective-permute-done.near_ref), custom_call_target="tpu_custom_call" | custom-call | flops 16777216 | bytes 1159168 | tf_op jit(solution)/shard_map/bands_kernel/pallas_call | solution.py:427
  17.7 2.7 %inner_kernel.1 = (f32[3,2,8,1024]{3,2,1,0:T(8,128)S(1)}, f32[3,2,8,1024]{3,2,1,0:T(8,128)S(1)}, f32[2,3,8,1024]{3,2,1,0:T(8,128)S(1)}) custom-call(f32[3,2,8,1024]{3,2,1,0:T(8,128)S(1)} %get-tuple-element.22.b_ref, f32[25,8,128]{2,1,0:T(8,128)S(1)} %collective-permute-done.near_ref, f32[25,8,128]{2,1,0:T(8,128)S(1)} %collective-permute-done.1.near_next_ref, ...), custom_call_target="tpu_custom_call" | custom-call | flops 805306368 | bytes 2089292 | tf_op jit(solution)/shard_map/inner_kernel/pallas_call | solution.py:427
  20.4 0.0 collective-permute-done.3.far_ref
  20.4 0.0 collective-permute-done.4.other_ref
  20.5 0.0 collective-permute-done.5.pair_ref
  20.5 0.0 collective-permute-done.2.far_next_ref
  20.5 1.0 %image_kernel.1 = (f32[3,2,8,1024]{3,2,1,0:T(8,128)S(1)}, f32[3,2,8,1024]{3,2,1,0:T(8,128)S(1)}, f32[32,1,128]{2,1,0:T(1,128)S(1)}) custom-call(f32[3,2,8,1024]{3,2,1,0:T(8,128)S(1)} %get-tuple-element.22.b_ref, f32[3,2,8,1024]{3,2,1,0:T(8,128)S(1)} %get-tuple-element.32.v_ref, f32[3,2,8,1024]{3,2,1,0:T(8,128)S(1)} %get-tuple-element.33.data_ref, ...), custom_call_target="tpu_custom_call" | custom-call | flops 134217728 | bytes 2764876 | tf_op jit(solution)/shard_map/image_kernel/pallas_call | solution.py:427
  21.4 9.9 %all_to_all.5.gram_ref = f32[32,1,128]{2,1,0:T(1,128)S(1)} all-to-all(f32[32,1,128]{2,1,0:T(1,128)S(1)} %get-tuple-element.39), channel_id=1, replica_groups=mesh['inline'=8,'col'=4] {'inline','col'}, dimensions={0} | all-to-all | bytes 32768 | tf_op jit(solution)/shard_map/all_to_all | solution.py:511
  31.4 0.9 %finish_kernel.1 = (f32[3,2,8,1024]{3,2,1,0:T(8,128)}, f32[3,2,8,1024]{3,2,1,0:T(8,128)}) custom-call(f32[32,1,128]{2,1,0:T(1,128)S(1)} %all_to_all.5.gram_ref, f32[3,2,8,1024]{3,2,1,0:T(8,128)S(1)} %get-tuple-element.22.b_ref, f32[3,2,8,1024]{3,2,1,0:T(8,128)S(1)} %get-tuple-element.40.one_ref, f32[3,2,8,1024]{3,2,1,0:T(8,128)S(1)} %get-tuple-element.41.two_ref), custom_call_target="tpu_custom_call" | custom-call | flops 393216 | bytes 999424 | tf_op jit(solution)/shard_map/finish_kernel/pallas_call | solution.py:427
Async XLA Ops:
  2.1 8.0 %collective-permute-start = (f32[25,8,128]{2,1,0:T(8,128)S(1)}, f32[25,8,128]{2,1,0:T(8,128)S(1)}, u32[]{:S(2)}, u32[]{:S(2)}) collective-permute-start(f32[25,8,128]{2,1,0:T(8,128)S(1)} %get-tuple-element.23), channel_id=1, source_target_pairs={{0,4},{4,0},{8,12},{12,8},{16,20},{20,16},{24,28},{28,24},{1,5},{5... | collective-permute-start | bytes 307208 | tf_op jit(solution)/shard_map/ppermute | solution.py:441
  5.1 8.5 %collective-permute-start.1 = (f32[25,8,128]{2,1,0:T(8,128)S(1)}, f32[25,8,128]{2,1,0:T(8,128)S(1)}, u32[]{:S(2)}, u32[]{:S(2)}) collective-permute-start(f32[25,8,128]{2,1,0:T(8,128)S(1)} %get-tuple-element.24), channel_id=1, source_target_pairs={{4,8},{8,4},{12,16},{16,12},{20,24},{24,20},{5,9},{9,5},{13,17},{1... | collective-permute-start | bytes 307208 | tf_op jit(solution)/shard_map/ppermute | solution.py:441
  5.7 14.7 %collective-permute-start.3 = (f32[25,8,128]{2,1,0:T(8,128)S(1)}, f32[25,8,128]{2,1,0:T(8,128)S(1)}, u32[]{:S(2)}, u32[]{:S(2)}) collective-permute-start(f32[25,8,128]{2,1,0:T(8,128)S(1)} %get-tuple-element.24), channel_id=1, source_target_pairs={{0,4},{4,0},{8,12},{12,8},{16,20},{20,16},{24,28},{28,24},{1,5},{5... | collective-permute-start | bytes 307208 | tf_op jit(solution)/shard_map/ppermute | solution.py:441
  10.1 10.4 %collective-permute-start.2 = (f32[25,8,128]{2,1,0:T(8,128)S(1)}, f32[25,8,128]{2,1,0:T(8,128)S(1)}, u32[]{:S(2)}, u32[]{:S(2)}) collective-permute-start(f32[25,8,128]{2,1,0:T(8,128)S(1)} %collective-permute-done.near_ref), channel_id=1, source_target_pairs={{0,8},{8,16},{12,4},{16,24},{20,12},{28,20},{1,9},{9,17},{13,5},{1... | collective-permute-start | bytes 307208 | tf_op jit(solution)/shard_map/ppermute | solution.py:447
  13.7 6.8 %collective-permute-start.4 = (f32[5,4,1024]{2,1,0:T(4,128)S(1)}, f32[5,4,1024]{2,1,0:T(4,128)S(1)}, u32[]{:S(2)}, u32[]{:S(2)}) collective-permute-start(f32[5,4,1024]{2,1,0:T(4,128)S(1)} %get-tuple-element.37), channel_id=1, source_target_pairs={{1,2},{2,1},{5,6},{6,5},{9,10},{10,9},{13,14},{14,13},{17,18},{18,... | collective-permute-start | bytes 245768 | tf_op jit(solution)/shard_map/ppermute | solution.py:441
  14.4 6.1 %collective-permute-start.5 = (f32[5,4,1024]{2,1,0:T(4,128)S(1)}, f32[5,4,1024]{2,1,0:T(4,128)S(1)}, u32[]{:S(2)}, u32[]{:S(2)}) collective-permute-start(f32[5,4,1024]{2,1,0:T(4,128)S(1)} %get-tuple-element.38), channel_id=1, source_target_pairs={{0,1},{1,0},{2,3},{3,2},{4,5},{5,4},{6,7},{7,6},{8,9},{9,8},{10,11... | collective-permute-start | bytes 245768 | tf_op jit(solution)/shard_map/ppermute | solution.py:441

commit v18 on v17

--- a/solution.py
+++ b/solution.py
@@ -38,11 +38,12 @@
 
 def band(line):
     lines = jnp.broadcast_to(line, (LANES, line.shape[1]))
-    return jnp.concatenate(split(pltpu.roll(lines, 0, 1, stride=1, stride_axis=0)), axis=0)
-
-
-def convolve(rows, bands):
-    out = lax.dot_general(rows, bands, (((1,), (1,)), ((), ())), preferred_element_type=F32)
+    return pltpu.roll(lines, 0, 1, stride=1, stride_axis=0)
+
+
+def convolve(rows, line_band):
+    halves = jnp.concatenate(split(line_band), axis=0)
+    out = lax.dot_general(rows, halves, (((1,), (1,)), ((), ())), preferred_element_type=F32)
     return out[:, :LANES] + out[:, LANES:]
 
 
@@ -479,7 +480,7 @@
     near_next = swap("inline", far, 1)
     far_next = hand_on("inline", near)
     far = swap("inline", far, 0)
-    bands = jax.ShapeDtypeStruct((angles, 2 * LANES, 2 * LANES), BF16)
+    bands = shape(angles, LANES, 2 * LANES)
     ahead, back = call(
         functools.partial(bands_kernel, wavelets.shape[1]), (bands, bands), (padded, near), work // 8
     )

time: 32.6 us -> 32.6 us (level)
  no operation moved by 1% of the time
where the time goes in v18:
time: 32.6 us; the launch traced here: 32.3 us
  starting transfers between devices  15.1 us (46%)
  blocking collectives  9.92 us (30%)
  Pallas kernels  6.58 us (20%)
  between operations  0.72 us (2%)
    ppermute x5, starting transfers between devices, swap(): lax.ppermute(value, axis, [(i + d, i + 1 - d) for i in starts for d in (0...  11.6 us
    all_to_all x1, blocking collectives, shards(): gram = lax.all_to_all(gram, axes, 0, 0)  9.92 us
    pallas_call x6, Pallas kernels, call(): pl.pallas_call(kernel, out_shape=outs, in_specs=[VMEM] * len(ins) if plac...  6.58 us
    ppermute x1, starting transfers between devices, hand_on(): lax.ppermute(value, axis, [(i, j) for i, j in steps if 0 <= j < size])  3.48 us
  transfers between devices with their start and end apart: 6, of which 0 were waited for; matrix products, arithmetic and copies ran while one was open for 0% of the time, Pallas kernels for 10%

profile of v18, /device:TPU:0, one launch (start us, length us, event | category | flops | bytes accessed | tf_op | source)
XLA Modules:
  0.0 32.3 jit_solution(12040386482233542897)
XLA Ops:
  0.6 1.4 %start_kernel.1 = (f32[3,2,8,1024]{3,2,1,0:T(8,128)S(1)}, f32[25,8,128]{2,1,0:T(8,128)S(1)}, f32[25,8,128]{2,1,0:T(8,128)S(1)}, f32[8,256]{1,0:T(8,128)S(1)}, s3...) custom-call(bf16[4,2,8,1024]{3,2,1,0:T(8,128)(2,1)} %seis_hbm.1, ...), custom_call_target="tpu_custom_call" | custom-call | flops 134217728 | bytes 641704 | tf_op jit(solution)/shard_map/start_kernel/pallas_call | solution.py:428
  2.1 3.0 %collective-permute-start = (f32[25,8,128]{2,1,0:T(8,128)S(1)}, f32[25,8,128]{2,1,0:T(8,128)S(1)}, u32[]{:S(2)}, u32[]{:S(2)}) collective-permute-start(f32[25,8,128]{2,1,0:T(8,128)S(1)} %get-tuple-element.23), channel_id=1, source_target_pairs={{0,4},{4,0},{8,12},{12,8},{16,20},{20,16},{24,28},{28,24},{1,5},{5... | collective-permute-start | bytes 307208 | tf_op jit(solution)/shard_map/ppermute | solution.py:442
  5.1 0.7 %collective-permute-start.1 = (f32[25,8,128]{2,1,0:T(8,128)S(1)}, f32[25,8,128]{2,1,0:T(8,128)S(1)}, u32[]{:S(2)}, u32[]{:S(2)}) collective-permute-start(f32[25,8,128]{2,1,0:T(8,128)S(1)} %get-tuple-element.24), channel_id=1, source_target_pairs={{4,8},{8,4},{12,16},{16,12},{20,24},{24,20},{5,9},{9,5},{13,17},{1... | collective-permute-start | bytes 307208 | tf_op jit(solution)/shard_map/ppermute | solution.py:442
  5.7 4.3 %collective-permute-start.3 = (f32[25,8,128]{2,1,0:T(8,128)S(1)}, f32[25,8,128]{2,1,0:T(8,128)S(1)}, u32[]{:S(2)}, u32[]{:S(2)}) collective-permute-start(f32[25,8,128]{2,1,0:T(8,128)S(1)} %get-tuple-element.24), channel_id=1, source_target_pairs={{0,4},{4,0},{8,12},{12,8},{16,20},{20,16},{24,28},{28,24},{1,5},{5... | collective-permute-start | bytes 307208 | tf_op jit(solution)/shard_map/ppermute | solution.py:442
  10.1 0.0 collective-permute-done.near_ref
  10.1 3.5 %collective-permute-start.2 = (f32[25,8,128]{2,1,0:T(8,128)S(1)}, f32[25,8,128]{2,1,0:T(8,128)S(1)}, u32[]{:S(2)}, u32[]{:S(2)}) collective-permute-start(f32[25,8,128]{2,1,0:T(8,128)S(1)} %collective-permute-done.near_ref), channel_id=1, source_target_pairs={{0,8},{8,16},{12,4},{16,24},{20,12},{28,20},{1,9},{9,17},{13,5},{1... | collective-permute-start | bytes 307208 | tf_op jit(solution)/shard_map/ppermute | solution.py:448
  13.6 0.0 collective-permute-done.1.near_next_ref
  13.6 0.1 column_kernel.1
  13.7 0.7 %collective-permute-start.4 = (f32[5,4,1024]{2,1,0:T(4,128)S(1)}, f32[5,4,1024]{2,1,0:T(4,128)S(1)}, u32[]{:S(2)}, u32[]{:S(2)}) collective-permute-start(f32[5,4,1024]{2,1,0:T(4,128)S(1)} %get-tuple-element.37), channel_id=1, source_target_pairs={{1,2},{2,1},{5,6},{6,5},{9,10},{10,9},{13,14},{14,13},{17,18},{18,... | collective-permute-start | bytes 245768 | tf_op jit(solution)/shard_map/ppermute | solution.py:442
  14.4 2.9 %collective-permute-start.5 = (f32[5,4,1024]{2,1,0:T(4,128)S(1)}, f32[5,4,1024]{2,1,0:T(4,128)S(1)}, u32[]{:S(2)}, u32[]{:S(2)}) collective-permute-start(f32[5,4,1024]{2,1,0:T(4,128)S(1)} %get-tuple-element.38), channel_id=1, source_target_pairs={{0,1},{1,0},{2,3},{3,2},{4,5},{5,4},{6,7},{7,6},{8,9},{9,8},{10,11... | collective-permute-start | bytes 245768 | tf_op jit(solution)/shard_map/ppermute | solution.py:442
  17.3 0.4 %bands_kernel.1 = (f32[4,128,256]{2,1,0:T(8,128)S(1)}, f32[4,128,256]{2,1,0:T(8,128)S(1)}) custom-call(f32[8,256]{1,0:T(8,128)S(1)} %get-tuple-element.29.padded_ref, f32[25,8,128]{2,1,0:T(8,128)S(1)} %collective-permute-done.near_ref), custom_call_target="tpu_custom_call" | custom-call | flops 16777216 | bytes 1159168 | tf_op jit(solution)/shard_map/bands_kernel/pallas_call | solution.py:428
  17.7 2.7 %inner_kernel.1 = (f32[3,2,8,1024]{3,2,1,0:T(8,128)S(1)}, f32[3,2,8,1024]{3,2,1,0:T(8,128)S(1)}, f32[2,3,8,1024]{3,2,1,0:T(8,128)S(1)}) custom-call(f32[3,2,8,1024]{3,2,1,0:T(8,128)S(1)} %get-tuple-element.22.b_ref, f32[25,8,128]{2,1,0:T(8,128)S(1)} %collective-permute-done.near_ref, f32[25,8,128]{2,1,0:T(8,128)S(1)} %collective-permute-done.1.near_next_ref, ...), custom_call_target="tpu_custom_call" | custom-call | flops 805306368 | bytes 2089292 | tf_op jit(solution)/shard_map/inner_kernel/pallas_call | solution.py:428
  20.4 0.0 collective-permute-done.3.far_ref
  20.4 0.0 collective-permute-done.4.other_ref
  20.5 0.0 collective-permute-done.5.pair_ref
  20.5 0.0 collective-permute-done.2.far_next_ref
  20.5 1.0 %image_kernel.1 = (f32[3,2,8,1024]{3,2,1,0:T(8,128)S(1)}, f32[3,2,8,1024]{3,2,1,0:T(8,128)S(1)}, f32[32,1,128]{2,1,0:T(1,128)S(1)}) custom-call(f32[3,2,8,1024]{3,2,1,0:T(8,128)S(1)} %get-tuple-element.22.b_ref, f32[3,2,8,1024]{3,2,1,0:T(8,128)S(1)} %get-tuple-element.32.v_ref, f32[3,2,8,1024]{3,2,1,0:T(8,128)S(1)} %get-tuple-element.33.data_ref, ...), custom_call_target="tpu_custom_call" | custom-call | flops 134217728 | bytes 2764876 | tf_op jit(solution)/shard_map/image_kernel/pallas_call | solution.py:428
  21.5 9.9 %all_to_all.5.gram_ref = f32[32,1,128]{2,1,0:T(1,128)S(1)} all-to-all(f32[32,1,128]{2,1,0:T(1,128)S(1)} %get-tuple-element.39), channel_id=1, replica_groups=mesh['inline'=8,'col'=4] {'inline','col'}, dimensions={0} | all-to-all | bytes 32768 | tf_op jit(solution)/shard_map/all_to_all | solution.py:512
  31.4 0.9 %finish_kernel.1 = (f32[3,2,8,1024]{3,2,1,0:T(8,128)}, f32[3,2,8,1024]{3,2,1,0:T(8,128)}) custom-call(f32[32,1,128]{2,1,0:T(1,128)S(1)} %all_to_all.5.gram_ref, f32[3,2,8,1024]{3,2,1,0:T(8,128)S(1)} %get-tuple-element.22.b_ref, f32[3,2,8,1024]{3,2,1,0:T(8,128)S(1)} %get-tuple-element.40.one_ref, f32[3,2,8,1024]{3,2,1,0:T(8,128)S(1)} %get-tuple-element.41.two_ref), custom_call_target="tpu_custom_call" | custom-call | flops 393216 | bytes 999424 | tf_op jit(solution)/shard_map/finish_kernel/pallas_call | solution.py:428
Async XLA Ops:
  2.1 8.0 %collective-permute-start = (f32[25,8,128]{2,1,0:T(8,128)S(1)}, f32[25,8,128]{2,1,0:T(8,128)S(1)}, u32[]{:S(2)}, u32[]{:S(2)}) collective-permute-start(f32[25,8,128]{2,1,0:T(8,128)S(1)} %get-tuple-element.23), channel_id=1, source_target_pairs={{0,4},{4,0},{8,12},{12,8},{16,20},{20,16},{24,28},{28,24},{1,5},{5... | collective-permute-start | bytes 307208 | tf_op jit(solution)/shard_map/ppermute | solution.py:442
  5.1 8.5 %collective-permute-start.1 = (f32[25,8,128]{2,1,0:T(8,128)S(1)}, f32[25,8,128]{2,1,0:T(8,128)S(1)}, u32[]{:S(2)}, u32[]{:S(2)}) collective-permute-start(f32[25,8,128]{2,1,0:T(8,128)S(1)} %get-tuple-element.24), channel_id=1, source_target_pairs={{4,8},{8,4},{12,16},{16,12},{20,24},{24,20},{5,9},{9,5},{13,17},{1... | collective-permute-start | bytes 307208 | tf_op jit(solution)/shard_map/ppermute | solution.py:442
  5.7 14.7 %collective-permute-start.3 = (f32[25,8,128]{2,1,0:T(8,128)S(1)}, f32[25,8,128]{2,1,0:T(8,128)S(1)}, u32[]{:S(2)}, u32[]{:S(2)}) collective-permute-start(f32[25,8,128]{2,1,0:T(8,128)S(1)} %get-tuple-element.24), channel_id=1, source_target_pairs={{0,4},{4,0},{8,12},{12,8},{16,20},{20,16},{24,28},{28,24},{1,5},{5... | collective-permute-start | bytes 307208 | tf_op jit(solution)/shard_map/ppermute | solution.py:442
  10.1 10.4 %collective-permute-start.2 = (f32[25,8,128]{2,1,0:T(8,128)S(1)}, f32[25,8,128]{2,1,0:T(8,128)S(1)}, u32[]{:S(2)}, u32[]{:S(2)}) collective-permute-start(f32[25,8,128]{2,1,0:T(8,128)S(1)} %collective-permute-done.near_ref), channel_id=1, source_target_pairs={{0,8},{8,16},{12,4},{16,24},{20,12},{28,20},{1,9},{9,17},{13,5},{1... | collective-permute-start | bytes 307208 | tf_op jit(solution)/shard_map/ppermute | solution.py:448
  13.7 6.8 %collective-permute-start.4 = (f32[5,4,1024]{2,1,0:T(4,128)S(1)}, f32[5,4,1024]{2,1,0:T(4,128)S(1)}, u32[]{:S(2)}, u32[]{:S(2)}) collective-permute-start(f32[5,4,1024]{2,1,0:T(4,128)S(1)} %get-tuple-element.37), channel_id=1, source_target_pairs={{1,2},{2,1},{5,6},{6,5},{9,10},{10,9},{13,14},{14,13},{17,18},{18,... | collective-permute-start | bytes 245768 | tf_op jit(solution)/shard_map/ppermute | solution.py:442
  14.4 6.1 %collective-permute-start.5 = (f32[5,4,1024]{2,1,0:T(4,128)S(1)}, f32[5,4,1024]{2,1,0:T(4,128)S(1)}, u32[]{:S(2)}, u32[]{:S(2)}) collective-permute-start(f32[5,4,1024]{2,1,0:T(4,128)S(1)} %get-tuple-element.38), channel_id=1, source_target_pairs={{0,1},{1,0},{2,3},{3,2},{4,5},{5,4},{6,7},{7,6},{8,9},{9,8},{10,11... | collective-permute-start | bytes 245768 | tf_op jit(solution)/shard_map/ppermute | solution.py:442

commit v19 on v17

--- a/solution.py
+++ b/solution.py
@@ -273,20 +273,17 @@
         other_ref[contrasts + i] = jnp.where(first_col, left, right)
 
 
-def bands_kernel(count, padded_ref, near_ref, ahead_ref, back_ref):
-    turned = turn(padded_ref[...], count)
-    for a in range(ahead_ref.shape[0]):
-        ahead_ref[a] = band(turned[a : a + 1])
-        back_ref[a] = band(padded_ref[a : a + 1, :])
-
-
 def inner_kernel(
-    b_ref, near_ref, near_next_ref, valid_ref, avo_ref, prior_ref, strength_ref, ahead_ref, back_ref,
-    v_ref, data_ref, halo_ref,
+    count, b_ref, near_ref, near_next_ref, padded_ref, valid_ref, avo_ref, prior_ref, strength_ref,
+    v_ref, data_ref, halo_ref, ahead_ref, back_ref,
 ):
     contrasts, rows, traces, samples = b_ref.shape
     angles, n = avo_ref.shape[1], samples // LANES
-    bands = [(ahead_ref[a], back_ref[a]) for a in range(angles)]
+    turned = turn(padded_ref[...], count)
+    bands = []
+    for a in range(angles):
+        bands.append((band(turned[a : a + 1]), band(padded_ref[a : a + 1, :])))
+        ahead_ref[a], back_ref[a] = (half.astype(F32) for half in bands[a])
     masks = [trace_columns(valid_ref, a) for a in range(angles)]
     weights = [column(prior_ref[r : r + 1, :]) + 4.0 for r in range(rows)]
     above, below = either_side(near_ref, near_next_ref, contrasts * n)
@@ -361,7 +358,7 @@
         scale = jnp.where(mine, -strength_ref[:, c : c + 1], 1.0)
         whole = jnp.where(place % half < rows, beside[c], turned(beside[c], rows)) * scale
         tile.append([whole[:, k * LANES : (k + 1) * LANES] for k in range(n)])
-    bands = [(ahead_ref[a], back_ref[a]) for a in range(angles)]
+    bands = [(ahead_ref[a].astype(BF16), back_ref[a].astype(BF16)) for a in range(angles)]
     edge = [jnp.concatenate(tiles, axis=1) for tiles in normal(tile, masks, avo_ref, bands)]
 
     has = jnp.where(place[:, :1] < half, has_left, has_right)
@@ -479,10 +476,6 @@
     near_next = swap("inline", far, 1)
     far_next = hand_on("inline", near)
     far = swap("inline", far, 0)
-    bands = jax.ShapeDtypeStruct((angles, 2 * LANES, 2 * LANES), BF16)
-    ahead, back = call(
-        functools.partial(bands_kernel, wavelets.shape[1]), (bands, bands), (padded, near), work // 8
-    )
     col_pair, col_other, own, note = call(
         column_kernel,
         (side, side, shape(contrasts, 2 * rows + 4, samples), shape(traces, LANES)),
@@ -492,10 +485,11 @@
     )
     col_other = swap("col", col_other, 1)
     col_pair = swap("col", col_pair, 0)
-    image, data, halo = call(
-        inner_kernel,
-        (field, field, shape(2, contrasts, traces, samples)),
-        (b, near, near_next, *kept, ahead, back),
+    bands = shape(angles, 2 * LANES, 2 * LANES)
+    image, data, halo, ahead, back = call(
+        functools.partial(inner_kernel, wavelets.shape[1]),
+        (field, field, shape(2, contrasts, traces, samples), bands, bands),
+        (b, near, near_next, padded, *kept),
         6 * work,
     )
     axes = ("inline", "col")

time: 32.6 us -> 32.5 us (level)
  Pallas kernels: 6.57 us -> 6.07 us
  blocking collectives: 9.92 us -> 10.4 us
    pallas_call x6 -> x5, Pallas kernels: 6.57 us -> 6.07 us  [call(): pl.pallas_call(kernel, out_shape=outs, in_specs=[VMEM] * len(ins) if plac...]
    all_to_all x1, blocking collectives: 9.92 us -> 10.4 us  [shards(): gram = lax.all_to_all(gram, axes, 0, 0)]
  transfers between devices with their start and end apart: 6 -> 6, of which waited for: 0 -> 0; matrix products, arithmetic and copies ran while one was open for 0% -> 0% of each run, Pallas kernels for 10% -> 8%
where the time goes in v19:
time: 32.5 us; the launch traced here: 32.3 us
  starting transfers between devices  15.1 us (46%)
  blocking collectives  10.4 us (32%)
  Pallas kernels  6.07 us (19%)
  between operations  0.71 us (2%)
    ppermute x5, starting transfers between devices, swap(): lax.ppermute(value, axis, [(i + d, i + 1 - d) for i in starts for d in (0...  11.6 us
    all_to_all x1, blocking collectives, shards(): gram = lax.all_to_all(gram, axes, 0, 0)  10.4 us
    pallas_call x5, Pallas kernels, call(): pl.pallas_call(kernel, out_shape=outs, in_specs=[VMEM] * len(ins) if plac...  6.07 us
    ppermute x1, starting transfers between devices, hand_on(): lax.ppermute(value, axis, [(i, j) for i, j in steps if 0 <= j < size])  3.48 us
  transfers between devices with their start and end apart: 6, of which 0 were waited for; matrix products, arithmetic and copies ran while one was open for 0% of the time, Pallas kernels for 8%

profile of v19, /device:TPU:0, one launch (start us, length us, event | category | flops | bytes accessed | tf_op | source)
XLA Modules:
  0.0 32.3 jit_solution(14663281999328144872)
XLA Ops:
  0.6 1.4 %start_kernel.1 = (f32[3,2,8,1024]{3,2,1,0:T(8,128)S(1)}, f32[25,8,128]{2,1,0:T(8,128)S(1)}, f32[25,8,128]{2,1,0:T(8,128)S(1)}, f32[8,256]{1,0:T(8,128)S(1)}, s3...) custom-call(bf16[4,2,8,1024]{3,2,1,0:T(8,128)(2,1)} %seis_hbm.1, ...), custom_call_target="tpu_custom_call" | custom-call | flops 134217728 | bytes 641704 | tf_op jit(solution)/shard_map/start_kernel/pallas_call | solution.py:424
  2.1 3.0 %collective-permute-start = (f32[25,8,128]{2,1,0:T(8,128)S(1)}, f32[25,8,128]{2,1,0:T(8,128)S(1)}, u32[]{:S(2)}, u32[]{:S(2)}) collective-permute-start(f32[25,8,128]{2,1,0:T(8,128)S(1)} %get-tuple-element.23), channel_id=1, source_target_pairs={{0,4},{4,0},{8,12},{12,8},{16,20},{20,16},{24,28},{28,24},{1,5},{5... | collective-permute-start | bytes 307208 | tf_op jit(solution)/shard_map/ppermute | solution.py:438
  5.1 0.7 %collective-permute-start.1 = (f32[25,8,128]{2,1,0:T(8,128)S(1)}, f32[25,8,128]{2,1,0:T(8,128)S(1)}, u32[]{:S(2)}, u32[]{:S(2)}) collective-permute-start(f32[25,8,128]{2,1,0:T(8,128)S(1)} %get-tuple-element.24), channel_id=1, source_target_pairs={{4,8},{8,4},{12,16},{16,12},{20,24},{24,20},{5,9},{9,5},{13,17},{1... | collective-permute-start | bytes 307208 | tf_op jit(solution)/shard_map/ppermute | solution.py:438
  5.7 4.3 %collective-permute-start.3 = (f32[25,8,128]{2,1,0:T(8,128)S(1)}, f32[25,8,128]{2,1,0:T(8,128)S(1)}, u32[]{:S(2)}, u32[]{:S(2)}) collective-permute-start(f32[25,8,128]{2,1,0:T(8,128)S(1)} %get-tuple-element.24), channel_id=1, source_target_pairs={{0,4},{4,0},{8,12},{12,8},{16,20},{20,16},{24,28},{28,24},{1,5},{5... | collective-permute-start | bytes 307208 | tf_op jit(solution)/shard_map/ppermute | solution.py:438
  10.1 0.0 collective-permute-done.near_ref
  10.1 3.5 %collective-permute-start.2 = (f32[25,8,128]{2,1,0:T(8,128)S(1)}, f32[25,8,128]{2,1,0:T(8,128)S(1)}, u32[]{:S(2)}, u32[]{:S(2)}) collective-permute-start(f32[25,8,128]{2,1,0:T(8,128)S(1)} %collective-permute-done.near_ref), channel_id=1, source_target_pairs={{0,8},{8,16},{12,4},{16,24},{20,12},{28,20},{1,9},{9,17},{13,5},{1... | collective-permute-start | bytes 307208 | tf_op jit(solution)/shard_map/ppermute | solution.py:444
  13.6 0.0 collective-permute-done.1.near_next_ref
  13.6 0.1 column_kernel.1
  13.7 0.7 %collective-permute-start.4 = (f32[5,4,1024]{2,1,0:T(4,128)S(1)}, f32[5,4,1024]{2,1,0:T(4,128)S(1)}, u32[]{:S(2)}, u32[]{:S(2)}) collective-permute-start(f32[5,4,1024]{2,1,0:T(4,128)S(1)} %get-tuple-element.35), channel_id=1, source_target_pairs={{1,2},{2,1},{5,6},{6,5},{9,10},{10,9},{13,14},{14,13},{17,18},{18,... | collective-permute-start | bytes 245768 | tf_op jit(solution)/shard_map/ppermute | solution.py:438
  14.4 2.9 %collective-permute-start.5 = (f32[5,4,1024]{2,1,0:T(4,128)S(1)}, f32[5,4,1024]{2,1,0:T(4,128)S(1)}, u32[]{:S(2)}, u32[]{:S(2)}) collective-permute-start(f32[5,4,1024]{2,1,0:T(4,128)S(1)} %get-tuple-element.36), channel_id=1, source_target_pairs={{0,1},{1,0},{2,3},{3,2},{4,5},{5,4},{6,7},{7,6},{8,9},{9,8},{10,11... | collective-permute-start | bytes 245768 | tf_op jit(solution)/shard_map/ppermute | solution.py:438
  17.3 2.6 %inner_kernel.1 = (f32[3,2,8,1024]{3,2,1,0:T(8,128)S(1)}, f32[3,2,8,1024]{3,2,1,0:T(8,128)S(1)}, f32[2,3,8,1024]{3,2,1,0:T(8,128)S(1)}, f32[4,256,256]{2,1,0:T(8,128)S(1)}, f32[4,256,256]{2,1,0:T(8,128)S(1)}) custom-call(f32[3,2,8,1024]{3,2,1,0:T(8,128)S(1)} %get-tuple-element.22.b_ref, f32[25,8,128]{2,1,0:T(8,128)S(1)} %collective-permute-done.near_ref, ...), custom_call_target="tpu_custom_call" | custom-call | flops 805306368 | bytes 3146060 | tf_op jit(solution)/shard_map/inner_kernel/pallas_call | solution.py:424
  19.9 0.0 collective-permute-done.3.far_ref
  19.9 0.0 collective-permute-done.4.other_ref
  19.9 0.0 collective-permute-done.5.pair_ref
  19.9 0.0 collective-permute-done.2.far_next_ref
  19.9 1.0 %image_kernel.1 = (f32[3,2,8,1024]{3,2,1,0:T(8,128)S(1)}, f32[3,2,8,1024]{3,2,1,0:T(8,128)S(1)}, f32[32,1,128]{2,1,0:T(1,128)S(1)}) custom-call(f32[3,2,8,1024]{3,2,1,0:T(8,128)S(1)} %get-tuple-element.22.b_ref, f32[3,2,8,1024]{3,2,1,0:T(8,128)S(1)} %get-tuple-element.30.v_ref, f32[3,2,8,1024]{3,2,1,0:T(8,128)S(1)} %get-tuple-element.31.data_ref, ...), custom_call_target="tpu_custom_call" | custom-call | flops 134217728 | bytes 3813452 | tf_op jit(solution)/shard_map/image_kernel/pallas_call | solution.py:424
  20.9 10.4 %all_to_all.5.gram_ref = f32[32,1,128]{2,1,0:T(1,128)S(1)} all-to-all(f32[32,1,128]{2,1,0:T(1,128)S(1)} %get-tuple-element.39), channel_id=1, replica_groups=mesh['inline'=8,'col'=4] {'inline','col'}, dimensions={0} | all-to-all | bytes 32768 | tf_op jit(solution)/shard_map/all_to_all | solution.py:505
  31.3 0.9 %finish_kernel.1 = (f32[3,2,8,1024]{3,2,1,0:T(8,128)}, f32[3,2,8,1024]{3,2,1,0:T(8,128)}) custom-call(f32[32,1,128]{2,1,0:T(1,128)S(1)} %all_to_all.5.gram_ref, f32[3,2,8,1024]{3,2,1,0:T(8,128)S(1)} %get-tuple-element.22.b_ref, f32[3,2,8,1024]{3,2,1,0:T(8,128)S(1)} %get-tuple-element.40.one_ref, f32[3,2,8,1024]{3,2,1,0:T(8,128)S(1)} %get-tuple-element.41.two_ref), custom_call_target="tpu_custom_call" | custom-call | flops 393216 | bytes 999424 | tf_op jit(solution)/shard_map/finish_kernel/pallas_call | solution.py:424
Async XLA Ops:
  2.1 8.0 %collective-permute-start = (f32[25,8,128]{2,1,0:T(8,128)S(1)}, f32[25,8,128]{2,1,0:T(8,128)S(1)}, u32[]{:S(2)}, u32[]{:S(2)}) collective-permute-start(f32[25,8,128]{2,1,0:T(8,128)S(1)} %get-tuple-element.23), channel_id=1, source_target_pairs={{0,4},{4,0},{8,12},{12,8},{16,20},{20,16},{24,28},{28,24},{1,5},{5... | collective-permute-start | bytes 307208 | tf_op jit(solution)/shard_map/ppermute | solution.py:438
  5.1 8.5 %collective-permute-start.1 = (f32[25,8,128]{2,1,0:T(8,128)S(1)}, f32[25,8,128]{2,1,0:T(8,128)S(1)}, u32[]{:S(2)}, u32[]{:S(2)}) collective-permute-start(f32[25,8,128]{2,1,0:T(8,128)S(1)} %get-tuple-element.24), channel_id=1, source_target_pairs={{4,8},{8,4},{12,16},{16,12},{20,24},{24,20},{5,9},{9,5},{13,17},{1... | collective-permute-start | bytes 307208 | tf_op jit(solution)/shard_map/ppermute | solution.py:438
  5.7 14.2 %collective-permute-start.3 = (f32[25,8,128]{2,1,0:T(8,128)S(1)}, f32[25,8,128]{2,1,0:T(8,128)S(1)}, u32[]{:S(2)}, u32[]{:S(2)}) collective-permute-start(f32[25,8,128]{2,1,0:T(8,128)S(1)} %get-tuple-element.24), channel_id=1, source_target_pairs={{0,4},{4,0},{8,12},{12,8},{16,20},{20,16},{24,28},{28,24},{1,5},{5... | collective-permute-start | bytes 307208 | tf_op jit(solution)/shard_map/ppermute | solution.py:438
  10.1 9.9 %collective-permute-start.2 = (f32[25,8,128]{2,1,0:T(8,128)S(1)}, f32[25,8,128]{2,1,0:T(8,128)S(1)}, u32[]{:S(2)}, u32[]{:S(2)}) collective-permute-start(f32[25,8,128]{2,1,0:T(8,128)S(1)} %collective-permute-done.near_ref), channel_id=1, source_target_pairs={{0,8},{8,16},{12,4},{16,24},{20,12},{28,20},{1,9},{9,17},{13,5},{1... | collective-permute-start | bytes 307208 | tf_op jit(solution)/shard_map/ppermute | solution.py:444
  13.7 6.2 %collective-permute-start.4 = (f32[5,4,1024]{2,1,0:T(4,128)S(1)}, f32[5,4,1024]{2,1,0:T(4,128)S(1)}, u32[]{:S(2)}, u32[]{:S(2)}) collective-permute-start(f32[5,4,1024]{2,1,0:T(4,128)S(1)} %get-tuple-element.35), channel_id=1, source_target_pairs={{1,2},{2,1},{5,6},{6,5},{9,10},{10,9},{13,14},{14,13},{17,18},{18,... | collective-permute-start | bytes 245768 | tf_op jit(solution)/shard_map/ppermute | solution.py:438
  14.4 5.6 %collective-permute-start.5 = (f32[5,4,1024]{2,1,0:T(4,128)S(1)}, f32[5,4,1024]{2,1,0:T(4,128)S(1)}, u32[]{:S(2)}, u32[]{:S(2)}) collective-permute-start(f32[5,4,1024]{2,1,0:T(4,128)S(1)} %get-tuple-element.36), channel_id=1, source_target_pairs={{0,1},{1,0},{2,3},{3,2},{4,5},{5,4},{6,7},{7,6},{8,9},{9,8},{10,11... | collective-permute-start | bytes 245768 | tf_op jit(solution)/shard_map/ppermute | solution.py:438

commit v20 on v19

--- a/solution.py
+++ b/solution.py
@@ -163,24 +163,24 @@
     b_ref, near_ref, far_ref, padded_ref, valid_ref, avo_ref, prior_ref, strength_ref,
     seis_ref, taps_ref, sems,
 ):
-    copies = copy_in(
+    taps, seis, valid, avo, prior, strength = copy_in(
         (
             (taps_hbm, taps_ref),
+            (seis_hbm, seis_ref),
             (valid_hbm, valid_ref),
             (avo_hbm, avo_ref),
-            (seis_hbm, seis_ref),
             (prior_hbm, prior_ref),
             (strength_hbm, strength_ref),
         ),
         sems,
     )
-    for copy in copies[:2]:
-        copy.wait()
+    taps.wait()
     pad_taps(taps_ref, padded_ref)
     angles = avo_ref.shape[1]
     bands = [band(padded_ref[a : a + 1, :]) for a in range(angles)]
+    valid.wait()
     masks = [trace_columns(valid_ref, a) for a in range(angles)]
-    for copy in copies[2:]:
+    for copy in (seis, avo, prior, strength):
         copy.wait()
     store_tiles(b_ref, right_side(seis_ref, masks, avo_ref, bands))
     contrasts, rows, traces, samples = b_ref.shape
@@ -275,7 +275,7 @@
 
 def inner_kernel(
     count, b_ref, near_ref, near_next_ref, padded_ref, valid_ref, avo_ref, prior_ref, strength_ref,
-    v_ref, data_ref, halo_ref, ahead_ref, back_ref,
+    v_ref, data_ref, halo_ref, ahead_ref, back_ref, norm_ref,
 ):
     contrasts, rows, traces, samples = b_ref.shape
     angles, n = avo_ref.shape[1], samples // LANES
@@ -318,10 +318,25 @@
             else:
                 halo_ref[min(r, 1), c] = image
     store_tiles(data_ref, normal(stack_tiles(v_ref), masks, avo_ref, bands))
+    norm_ref[...] = functools.reduce(
+        jnp.add, [lane_tiles(b_ref[c, r] * b_ref[c, r]) for c in range(contrasts) for r in range(rows)]
+    )
+
+
+def lane_tiles(product):
+    tiles = [product[:, k : k + LANES] for k in range(0, product.shape[1], LANES)]
+    return functools.reduce(jnp.add, tiles)
+
+
+def halo_kernel(halo_ref, far_next_ref, far_ref, strength_ref, out_ref):
+    contrasts, samples = halo_ref.shape[1], halo_ref.shape[3]
+    for c in range(contrasts):
+        for i, line in enumerate(row_pair(far_ref, far_next_ref, c, samples // LANES)):
+            out_ref[i, c] = halo_ref[i, c] - strength_ref[:, c : c + 1] * line
 
 
 def image_kernel(
-    b_ref, v_ref, data_ref, halo_ref, own_ref, note_ref, far_next_ref, far_ref, other_ref, pair_ref,
+    b_ref, v_ref, data_ref, halo_ref, norm_ref, own_ref, note_ref, other_ref, pair_ref,
     avo_ref, prior_ref, strength_ref, ahead_ref, back_ref,
     one_ref, two_ref, gram_ref,
 ):
@@ -364,7 +379,7 @@
     has = jnp.where(place[:, :1] < half, has_left, has_right)
     far_weight = theirs[:, angles : angles + 1] + 4.0
     weights = [column(prior_ref[r : r + 1, :]) + 4.0 for r in range(rows)]
-    sums = [jnp.zeros((traces, LANES), F32) for _ in range(4)]
+    sums = [norm_ref[...], *[jnp.zeros((traces, LANES), F32) for _ in range(3)]]
     for c in range(contrasts):
         strength = strength_ref[:, c : c + 1]
         theirs = beside[c]
@@ -373,9 +388,7 @@
         prior = far_weight * theirs - (around + has * own_ref[c])
         beyond = jnp.where(place < half, turned(edge[c], -rows), edge[c]) + strength * prior
 
-        far_rows = row_pair(far_ref, far_next_ref, c, n)
-        over, under = (halo_ref[i, c] - strength * far_rows[i] for i in (0, 1))
-        lines = [over, *[v_ref[c, r] for r in range(rows)], under]
+        lines = [halo_ref[0, c], *[v_ref[c, r] for r in range(rows)], halo_ref[1, c]]
         lines = [
             here - strength * at_ends(theirs, -k, half - 1 - k, 0.0)
             for here, k in zip(lines, (rows, *range(rows), rows + 1))
@@ -389,9 +402,8 @@
             two = data_ref[c, r] + mend + strength * (weights[r] * here - around)
             one_ref[c, r] = here
             two_ref[c, r] = two
-            for q, product in enumerate((b * b, b * here, here * here, here * two)):
-                tiles = [product[:, k : k + LANES] for k in range(0, samples, LANES)]
-                sums[q] = sums[q] + functools.reduce(jnp.add, tiles)
+            for q, product in enumerate((b * here, here * here, here * two), 1):
+                sums[q] = sums[q] + lane_tiles(product)
     lane = lax.broadcasted_iota(jnp.int32, (1, LANES), 1)
     packed = jnp.zeros((1, LANES), F32)
     for q, total in enumerate(sums):
@@ -401,11 +413,13 @@
 
 
 def finish_kernel(gram_ref, b_ref, one_ref, two_ref, solution_ref, residual_ref):
-    sums = jnp.sum(gram_ref[...], axis=0)
+    sums = jnp.sum(gram_ref[...], axis=0, keepdims=True)
     g00, g01, g11, g12 = (sums[:, q : q + 1] for q in range(4))
-    first = g00 / g01
-    ratio = first * g11 / g01
-    second = (ratio - 1.0) * g01 / (first * g12 - ratio * g11)
+    inverse = 1.0 / g01
+    first = g00 * inverse
+    quotient = g11 * inverse
+    ratio = first * quotient
+    second = (ratio - 1.0) * g01 / (first * (g12 - quotient * g11))
     near = first + second * ratio
     far = first * second
     for c in range(b_ref.shape[0]):
@@ -486,23 +500,25 @@
     col_other = swap("col", col_other, 1)
     col_pair = swap("col", col_pair, 0)
     bands = shape(angles, 2 * LANES, 2 * LANES)
-    image, data, halo, ahead, back = call(
+    halo = shape(2, contrasts, traces, samples)
+    image, data, part, ahead, back, norm = call(
         functools.partial(inner_kernel, wavelets.shape[1]),
-        (field, field, shape(2, contrasts, traces, samples), bands, bands),
+        (field, field, halo, bands, bands, shape(traces, LANES)),
         (b, near, near_next, padded, *kept),
         6 * work,
     )
+    (halo,) = call(halo_kernel, (halo,), (part, far_next, far, kept[-1]), field.size)
     axes = ("inline", "col")
     one, two, gram = call(
         image_kernel,
         (field, field, shape(lax.axis_size(axes), 1, LANES)),
         (
-            b, image, data, halo, own, note, far_next, far, col_other, col_pair,
+            b, image, data, halo, norm, own, note, col_other, col_pair,
             *kept[1:], ahead, back,
         ),
         work,
     )
-    gram = lax.all_to_all(gram, axes, 0, 0)
+    gram = lax.all_to_all(gram, axes, 0, 0).reshape(-1, LANES)
     return tuple(call(finish_kernel, (field, field), (gram, b, one, two), 8 * field.size))
 
 

time: 32.5 us -> 32.6 us (level)
    pallas_call x5 -> x6, Pallas kernels: 6.07 us -> 6.2 us  [call(): pl.pallas_call(kernel, out_shape=outs, in_specs=[VMEM] * len(ins) if plac...]
  transfers between devices with their start and end apart: 6 -> 6, of which waited for: 0 -> 0; matrix products, arithmetic and copies ran while one was open for 0% -> 0% of each run, Pallas kernels for 8% -> 9%
where the time goes in v20:
time: 32.6 us; the launch traced here: 32.3 us
  starting transfers between devices  15.1 us (46%)
  blocking collectives  10.3 us (32%)
  Pallas kernels  6.2 us (19%)
  between operations  0.72 us (2%)
    ppermute x5, starting transfers between devices, swap(): lax.ppermute(value, axis, [(i + d, i + 1 - d) for i in starts for d in (0...  11.6 us
    all_to_all x1, blocking collectives, shards(): gram = lax.all_to_all(gram, axes, 0, 0).reshape(-1, LANES)  10.3 us
    pallas_call x6, Pallas kernels, call(): pl.pallas_call(kernel, out_shape=outs, in_specs=[VMEM] * len(ins) if plac...  6.2 us
    ppermute x1, starting transfers between devices, hand_on(): lax.ppermute(value, axis, [(i, j) for i, j in steps if 0 <= j < size])  3.48 us
  transfers between devices with their start and end apart: 6, of which 0 were waited for; matrix products, arithmetic and copies ran while one was open for 0% of the time, Pallas kernels for 9%

profile of v20, /device:TPU:0, one launch (start us, length us, event | category | flops | bytes accessed | tf_op | source)
XLA Modules:
  0.0 32.3 jit_solution(10914928655006228717)
XLA Ops:
  0.6 1.4 %start_kernel.1 = (f32[3,2,8,1024]{3,2,1,0:T(8,128)S(1)}, f32[25,8,128]{2,1,0:T(8,128)S(1)}, f32[25,8,128]{2,1,0:T(8,128)S(1)}, f32[8,256]{1,0:T(8,128)S(1)}, s3...) custom-call(bf16[4,2,8,1024]{3,2,1,0:T(8,128)(2,1)} %seis_hbm.1, ...), custom_call_target="tpu_custom_call" | custom-call | flops 134217728 | bytes 641704 | tf_op jit(solution)/shard_map/start_kernel/pallas_call | solution.py:438
  2.1 3.0 %collective-permute-start = (f32[25,8,128]{2,1,0:T(8,128)S(1)}, f32[25,8,128]{2,1,0:T(8,128)S(1)}, u32[]{:S(2)}, u32[]{:S(2)}) collective-permute-start(f32[25,8,128]{2,1,0:T(8,128)S(1)} %get-tuple-element.24), channel_id=1, source_target_pairs={{0,4},{4,0},{8,12},{12,8},{16,20},{20,16},{24,28},{28,24},{1,5},{5... | collective-permute-start | bytes 307208 | tf_op jit(solution)/shard_map/ppermute | solution.py:452
  5.1 0.7 %collective-permute-start.1 = (f32[25,8,128]{2,1,0:T(8,128)S(1)}, f32[25,8,128]{2,1,0:T(8,128)S(1)}, u32[]{:S(2)}, u32[]{:S(2)}) collective-permute-start(f32[25,8,128]{2,1,0:T(8,128)S(1)} %get-tuple-element.25), channel_id=1, source_target_pairs={{4,8},{8,4},{12,16},{16,12},{20,24},{24,20},{5,9},{9,5},{13,17},{1... | collective-permute-start | bytes 307208 | tf_op jit(solution)/shard_map/ppermute | solution.py:452
  5.8 4.3 %collective-permute-start.3 = (f32[25,8,128]{2,1,0:T(8,128)S(1)}, f32[25,8,128]{2,1,0:T(8,128)S(1)}, u32[]{:S(2)}, u32[]{:S(2)}) collective-permute-start(f32[25,8,128]{2,1,0:T(8,128)S(1)} %get-tuple-element.25), channel_id=1, source_target_pairs={{0,4},{4,0},{8,12},{12,8},{16,20},{20,16},{24,28},{28,24},{1,5},{5... | collective-permute-start | bytes 307208 | tf_op jit(solution)/shard_map/ppermute | solution.py:452
  10.1 0.0 collective-permute-done.near_ref
  10.1 3.5 %collective-permute-start.2 = (f32[25,8,128]{2,1,0:T(8,128)S(1)}, f32[25,8,128]{2,1,0:T(8,128)S(1)}, u32[]{:S(2)}, u32[]{:S(2)}) collective-permute-start(f32[25,8,128]{2,1,0:T(8,128)S(1)} %collective-permute-done.near_ref), channel_id=1, source_target_pairs={{0,8},{8,16},{12,4},{16,24},{20,12},{28,20},{1,9},{9,17},{13,5},{1... | collective-permute-start | bytes 307208 | tf_op jit(solution)/shard_map/ppermute | solution.py:458
  13.6 0.0 collective-permute-done.1.near_next_ref
  13.6 0.1 column_kernel.1
  13.7 0.7 %collective-permute-start.4 = (f32[5,4,1024]{2,1,0:T(4,128)S(1)}, f32[5,4,1024]{2,1,0:T(4,128)S(1)}, u32[]{:S(2)}, u32[]{:S(2)}) collective-permute-start(f32[5,4,1024]{2,1,0:T(4,128)S(1)} %get-tuple-element.37), channel_id=1, source_target_pairs={{1,2},{2,1},{5,6},{6,5},{9,10},{10,9},{13,14},{14,13},{17,18},{18,... | collective-permute-start | bytes 245768 | tf_op jit(solution)/shard_map/ppermute | solution.py:452
  14.4 2.9 %collective-permute-start.5 = (f32[5,4,1024]{2,1,0:T(4,128)S(1)}, f32[5,4,1024]{2,1,0:T(4,128)S(1)}, u32[]{:S(2)}, u32[]{:S(2)}) collective-permute-start(f32[5,4,1024]{2,1,0:T(4,128)S(1)} %get-tuple-element.38), channel_id=1, source_target_pairs={{0,1},{1,0},{2,3},{3,2},{4,5},{5,4},{6,7},{7,6},{8,9},{9,8},{10,11... | collective-permute-start | bytes 245768 | tf_op jit(solution)/shard_map/ppermute | solution.py:452
  17.3 2.5 %inner_kernel.1 = (f32[3,2,8,1024]{3,2,1,0:T(8,128)S(1)}, f32[3,2,8,1024]{3,2,1,0:T(8,128)S(1)}, f32[2,3,8,1024]{3,2,1,0:T(8,128)S(1)}, f32[4,256,256]{2,1,0:T(8...) custom-call(f32[3,2,8,1024]{3,2,1,0:T(8,128)S(1)} %get-tuple-element.23.b_ref, ...), custom_call_target="tpu_custom_call" | custom-call | flops 805306368 | bytes 3150156 | tf_op jit(solution)/shard_map/inner_kernel/pallas_call | solution.py:438
  19.9 0.0 collective-permute-done.3.far_ref
  19.9 0.0 collective-permute-done.2.far_next_ref
  19.9 0.1 halo_kernel.1.halo_ref
  20.0 0.0 collective-permute-done.4.other_ref
  20.0 0.0 collective-permute-done.5.pair_ref
  20.0 0.9 %image_kernel.1 = (f32[3,2,8,1024]{3,2,1,0:T(8,128)S(1)}, f32[3,2,8,1024]{3,2,1,0:T(8,128)S(1)}, f32[32,1,128]{2,1,0:T(1,128)S(1)}) custom-call(f32[3,2,8,1024]{3,2,1,0:T(8,128)S(1)} %get-tuple-element.23.b_ref, f32[3,2,8,1024]{3,2,1,0:T(8,128)S(1)} %get-tuple-element.31.v_ref, f32[3,2,8,1024]{3,2,1,0:T(8,128)S(1)} %get-tuple-element.32.data_ref, ...), custom_call_target="tpu_custom_call" | custom-call | flops 134217728 | bytes 3612748 | tf_op jit(solution)/shard_map/image_kernel/pallas_call | solution.py:438
  21.0 10.3 %all_to_all.5 = f32[32,1,128]{2,1,0:T(1,128)S(1)} all-to-all(f32[32,1,128]{2,1,0:T(1,128)S(1)} %get-tuple-element.41), channel_id=1, replica_groups=mesh['inline'=8,'col'=4] {'inline','col'}, dimensions={0} | all-to-all | bytes 32768 | tf_op jit(solution)/shard_map/all_to_all | solution.py:521
  31.3 1.1 %finish_kernel.1 = (f32[3,2,8,1024]{3,2,1,0:T(8,128)}, f32[3,2,8,1024]{3,2,1,0:T(8,128)}) custom-call(f32[32,128]{1,0:T(8,128)S(1)} %bitcast.3, f32[3,2,8,1024]{3,2,1,0:T(8,128)S(1)} %get-tuple-element.23.b_ref, f32[3,2,8,1024]{3,2,1,0:T(8,128)S(1)} %get-tuple-element.42.one_ref, f32[3,2,8,1024]{3,2,1,0:T(8,128)S(1)} %get-tuple-element.43.two_ref), custom_call_target="tpu_custom_call" | custom-call | flops 393216 | bytes 999424 | tf_op jit(solution)/shard_map/finish_kernel/pallas_call | solution.py:438
Async XLA Ops:
  2.1 8.0 %collective-permute-start = (f32[25,8,128]{2,1,0:T(8,128)S(1)}, f32[25,8,128]{2,1,0:T(8,128)S(1)}, u32[]{:S(2)}, u32[]{:S(2)}) collective-permute-start(f32[25,8,128]{2,1,0:T(8,128)S(1)} %get-tuple-element.24), channel_id=1, source_target_pairs={{0,4},{4,0},{8,12},{12,8},{16,20},{20,16},{24,28},{28,24},{1,5},{5... | collective-permute-start | bytes 307208 | tf_op jit(solution)/shard_map/ppermute | solution.py:452
  5.1 8.5 %collective-permute-start.1 = (f32[25,8,128]{2,1,0:T(8,128)S(1)}, f32[25,8,128]{2,1,0:T(8,128)S(1)}, u32[]{:S(2)}, u32[]{:S(2)}) collective-permute-start(f32[25,8,128]{2,1,0:T(8,128)S(1)} %get-tuple-element.25), channel_id=1, source_target_pairs={{4,8},{8,4},{12,16},{16,12},{20,24},{24,20},{5,9},{9,5},{13,17},{1... | collective-permute-start | bytes 307208 | tf_op jit(solution)/shard_map/ppermute | solution.py:452
  5.8 14.1 %collective-permute-start.3 = (f32[25,8,128]{2,1,0:T(8,128)S(1)}, f32[25,8,128]{2,1,0:T(8,128)S(1)}, u32[]{:S(2)}, u32[]{:S(2)}) collective-permute-start(f32[25,8,128]{2,1,0:T(8,128)S(1)} %get-tuple-element.25), channel_id=1, source_target_pairs={{0,4},{4,0},{8,12},{12,8},{16,20},{20,16},{24,28},{28,24},{1,5},{5... | collective-permute-start | bytes 307208 | tf_op jit(solution)/shard_map/ppermute | solution.py:452
  10.1 9.8 %collective-permute-start.2 = (f32[25,8,128]{2,1,0:T(8,128)S(1)}, f32[25,8,128]{2,1,0:T(8,128)S(1)}, u32[]{:S(2)}, u32[]{:S(2)}) collective-permute-start(f32[25,8,128]{2,1,0:T(8,128)S(1)} %collective-permute-done.near_ref), channel_id=1, source_target_pairs={{0,8},{8,16},{12,4},{16,24},{20,12},{28,20},{1,9},{9,17},{13,5},{1... | collective-permute-start | bytes 307208 | tf_op jit(solution)/shard_map/ppermute | solution.py:458
  13.7 6.3 %collective-permute-start.4 = (f32[5,4,1024]{2,1,0:T(4,128)S(1)}, f32[5,4,1024]{2,1,0:T(4,128)S(1)}, u32[]{:S(2)}, u32[]{:S(2)}) collective-permute-start(f32[5,4,1024]{2,1,0:T(4,128)S(1)} %get-tuple-element.37), channel_id=1, source_target_pairs={{1,2},{2,1},{5,6},{6,5},{9,10},{10,9},{13,14},{14,13},{17,18},{18,... | collective-permute-start | bytes 245768 | tf_op jit(solution)/shard_map/ppermute | solution.py:452
  14.4 5.6 %collective-permute-start.5 = (f32[5,4,1024]{2,1,0:T(4,128)S(1)}, f32[5,4,1024]{2,1,0:T(4,128)S(1)}, u32[]{:S(2)}, u32[]{:S(2)}) collective-permute-start(f32[5,4,1024]{2,1,0:T(4,128)S(1)} %get-tuple-element.38), channel_id=1, source_target_pairs={{0,1},{1,0},{2,3},{3,2},{4,5},{5,4},{6,7},{7,6},{8,9},{9,8},{10,11... | collective-permute-start | bytes 245768 | tf_op jit(solution)/shard_map/ppermute | solution.py:452

commit v21 on v20

--- a/solution.py
+++ b/solution.py
@@ -101,11 +101,12 @@
                 out_ref[c, r, :, pl.ds(k * LANES, LANES)] = tile[r * size : (r + 1) * size]
 
 
-def right_side(seis_ref, masks, avo_ref, bands):
+def right_side(seis_ref, masks, avo_ref, bands, copies):
     angles, rows, _, samples = seis_ref.shape
     n = samples // LANES
     total = [[None] * n for _ in range(avo_ref.shape[0])]
     for a in range(angles):
+        copies[a].wait()
         data = jnp.concatenate([seis_ref[a, r].astype(F32) for r in range(rows)], axis=0)
         data = data * masks[a]
         turned = [
@@ -163,12 +164,13 @@
     b_ref, near_ref, far_ref, padded_ref, valid_ref, avo_ref, prior_ref, strength_ref,
     seis_ref, taps_ref, sems,
 ):
-    taps, seis, valid, avo, prior, strength = copy_in(
+    contrasts, angles, _ = avo_ref.shape
+    taps, *rest = copy_in(
         (
             (taps_hbm, taps_ref),
-            (seis_hbm, seis_ref),
+            *((seis_hbm.at[a], seis_ref.at[a]) for a in range(angles)),
+            *((avo_hbm.at[c], avo_ref.at[c]) for c in range(contrasts)),
             (valid_hbm, valid_ref),
-            (avo_hbm, avo_ref),
             (prior_hbm, prior_ref),
             (strength_hbm, strength_ref),
         ),
@@ -176,14 +178,12 @@
     )
     taps.wait()
     pad_taps(taps_ref, padded_ref)
-    angles = avo_ref.shape[1]
     bands = [band(padded_ref[a : a + 1, :]) for a in range(angles)]
-    valid.wait()
+    for copy in rest[angles:]:
+        copy.wait()
     masks = [trace_columns(valid_ref, a) for a in range(angles)]
-    for copy in (seis, avo, prior, strength):
-        copy.wait()
-    store_tiles(b_ref, right_side(seis_ref, masks, avo_ref, bands))
-    contrasts, rows, traces, samples = b_ref.shape
+    store_tiles(b_ref, right_side(seis_ref, masks, avo_ref, bands, rest[:angles]))
+    _, rows, traces, samples = b_ref.shape
     n = samples // LANES
     first = starts_pair("inline")
     lane = lax.broadcasted_iota(jnp.int32, (traces, LANES), 1)
@@ -413,7 +413,7 @@
 
 
 def finish_kernel(gram_ref, b_ref, one_ref, two_ref, solution_ref, residual_ref):
-    sums = jnp.sum(gram_ref[...], axis=0, keepdims=True)
+    sums = jnp.sum(gram_ref[...], axis=0)
     g00, g01, g11, g12 = (sums[:, q : q + 1] for q in range(4))
     inverse = 1.0 / g01
     first = g00 * inverse
@@ -482,7 +482,7 @@
         [
             pltpu.VMEM(seismic.shape, seismic.dtype),
             pltpu.VMEM(wavelets.shape, F32),
-            pltpu.SemaphoreType.DMA((6,)),
+            pltpu.SemaphoreType.DMA((angles + contrasts + 4,)),
         ],
         [HBM] * 6,
     )
@@ -518,7 +518,7 @@
         ),
         work,
     )
-    gram = lax.all_to_all(gram, axes, 0, 0).reshape(-1, LANES)
+    gram = lax.all_to_all(gram, axes, 0, 0)
     return tuple(call(finish_kernel, (field, field), (gram, b, one, two), 8 * field.size))
 
 

time: 32.6 us -> 33.4 us (1.025)
  Pallas kernels: 6.2 us -> 7.06 us
    pallas_call x6, Pallas kernels: 6.2 us -> 7.06 us  [call(): pl.pallas_call(kernel, out_shape=outs, in_specs=[VMEM] * len(ins) if plac...]
  transfers between devices with their start and end apart: 6 -> 6, of which waited for: 0 -> 0; matrix products, arithmetic and copies ran while one was open for 0% -> 0% of each run, Pallas kernels for 9% -> 8%
where the time goes in v21:
time: 33.4 us; the launch traced here: 33.2 us
  starting transfers between devices  15.1 us (45%)
  blocking collectives  10.3 us (31%)
  Pallas kernels  7.06 us (21%)
  between operations  0.72 us (2%)
    ppermute x5, starting transfers between devices, swap(): lax.ppermute(value, axis, [(i + d, i + 1 - d) for i in starts for d in (0...  11.6 us
    all_to_all x1, blocking collectives, shards(): gram = lax.all_to_all(gram, axes, 0, 0)  10.3 us
    pallas_call x6, Pallas kernels, call(): pl.pallas_call(kernel, out_shape=outs, in_specs=[VMEM] * len(ins) if plac...  7.06 us
    ppermute x1, starting transfers between devices, hand_on(): lax.ppermute(value, axis, [(i, j) for i, j in steps if 0 <= j < size])  3.48 us
  transfers between devices with their start and end apart: 6, of which 0 were waited for; matrix products, arithmetic and copies ran while one was open for 0% of the time, Pallas kernels for 8%

profile of v21, /device:TPU:0, one launch (start us, length us, event | category | flops | bytes accessed | tf_op | source)
XLA Modules:
  0.0 33.2 jit_solution(10751773405891330075)
XLA Ops:
  0.6 2.3 %start_kernel.1 = (f32[3,2,8,1024]{3,2,1,0:T(8,128)S(1)}, f32[25,8,128]{2,1,0:T(8,128)S(1)}, f32[25,8,128]{2,1,0:T(8,128)S(1)}, f32[8,256]{1,0:T(8,128)S(1)}, s3...) custom-call(bf16[4,2,8,1024]{3,2,1,0:T(8,128)(2,1)} %seis_hbm.1, ...), custom_call_target="tpu_custom_call" | custom-call | flops 134217728 | bytes 641704 | tf_op jit(solution)/shard_map/start_kernel/pallas_call | solution.py:438
  2.9 3.0 %collective-permute-start = (f32[25,8,128]{2,1,0:T(8,128)S(1)}, f32[25,8,128]{2,1,0:T(8,128)S(1)}, u32[]{:S(2)}, u32[]{:S(2)}) collective-permute-start(f32[25,8,128]{2,1,0:T(8,128)S(1)} %get-tuple-element.24), channel_id=1, source_target_pairs={{0,4},{4,0},{8,12},{12,8},{16,20},{20,16},{24,28},{28,24},{1,5},{5... | collective-permute-start | bytes 307208 | tf_op jit(solution)/shard_map/ppermute | solution.py:452
  5.9 0.7 %collective-permute-start.1 = (f32[25,8,128]{2,1,0:T(8,128)S(1)}, f32[25,8,128]{2,1,0:T(8,128)S(1)}, u32[]{:S(2)}, u32[]{:S(2)}) collective-permute-start(f32[25,8,128]{2,1,0:T(8,128)S(1)} %get-tuple-element.25), channel_id=1, source_target_pairs={{4,8},{8,4},{12,16},{16,12},{20,24},{24,20},{5,9},{9,5},{13,17},{1... | collective-permute-start | bytes 307208 | tf_op jit(solution)/shard_map/ppermute | solution.py:452
  6.6 4.3 %collective-permute-start.3 = (f32[25,8,128]{2,1,0:T(8,128)S(1)}, f32[25,8,128]{2,1,0:T(8,128)S(1)}, u32[]{:S(2)}, u32[]{:S(2)}) collective-permute-start(f32[25,8,128]{2,1,0:T(8,128)S(1)} %get-tuple-element.25), channel_id=1, source_target_pairs={{0,4},{4,0},{8,12},{12,8},{16,20},{20,16},{24,28},{28,24},{1,5},{5... | collective-permute-start | bytes 307208 | tf_op jit(solution)/shard_map/ppermute | solution.py:452
  10.9 0.0 collective-permute-done.near_ref
  10.9 3.5 %collective-permute-start.2 = (f32[25,8,128]{2,1,0:T(8,128)S(1)}, f32[25,8,128]{2,1,0:T(8,128)S(1)}, u32[]{:S(2)}, u32[]{:S(2)}) collective-permute-start(f32[25,8,128]{2,1,0:T(8,128)S(1)} %collective-permute-done.near_ref), channel_id=1, source_target_pairs={{0,8},{8,16},{12,4},{16,24},{20,12},{28,20},{1,9},{9,17},{13,5},{1... | collective-permute-start | bytes 307208 | tf_op jit(solution)/shard_map/ppermute | solution.py:458
  14.4 0.0 collective-permute-done.1.near_next_ref
  14.4 0.1 column_kernel.1
  14.6 0.7 %collective-permute-start.4 = (f32[5,4,1024]{2,1,0:T(4,128)S(1)}, f32[5,4,1024]{2,1,0:T(4,128)S(1)}, u32[]{:S(2)}, u32[]{:S(2)}) collective-permute-start(f32[5,4,1024]{2,1,0:T(4,128)S(1)} %get-tuple-element.37), channel_id=1, source_target_pairs={{1,2},{2,1},{5,6},{6,5},{9,10},{10,9},{13,14},{14,13},{17,18},{18,... | collective-permute-start | bytes 245768 | tf_op jit(solution)/shard_map/ppermute | solution.py:452
  15.2 2.9 %collective-permute-start.5 = (f32[5,4,1024]{2,1,0:T(4,128)S(1)}, f32[5,4,1024]{2,1,0:T(4,128)S(1)}, u32[]{:S(2)}, u32[]{:S(2)}) collective-permute-start(f32[5,4,1024]{2,1,0:T(4,128)S(1)} %get-tuple-element.38), channel_id=1, source_target_pairs={{0,1},{1,0},{2,3},{3,2},{4,5},{5,4},{6,7},{7,6},{8,9},{9,8},{10,11... | collective-permute-start | bytes 245768 | tf_op jit(solution)/shard_map/ppermute | solution.py:452
  18.2 2.5 %inner_kernel.1 = (f32[3,2,8,1024]{3,2,1,0:T(8,128)S(1)}, f32[3,2,8,1024]{3,2,1,0:T(8,128)S(1)}, f32[2,3,8,1024]{3,2,1,0:T(8,128)S(1)}, f32[4,256,256]{2,1,0:T(8...) custom-call(f32[3,2,8,1024]{3,2,1,0:T(8,128)S(1)} %get-tuple-element.23.b_ref, ...), custom_call_target="tpu_custom_call" | custom-call | flops 805306368 | bytes 3150156 | tf_op jit(solution)/shard_map/inner_kernel/pallas_call | solution.py:438
  20.7 0.0 collective-permute-done.3.far_ref
  20.7 0.0 collective-permute-done.2.far_next_ref
  20.7 0.1 halo_kernel.1.halo_ref
  20.8 0.0 collective-permute-done.4.other_ref
  20.8 0.0 collective-permute-done.5.pair_ref
  20.9 0.9 %image_kernel.1 = (f32[3,2,8,1024]{3,2,1,0:T(8,128)S(1)}, f32[3,2,8,1024]{3,2,1,0:T(8,128)S(1)}, f32[32,1,128]{2,1,0:T(1,128)S(1)}) custom-call(f32[3,2,8,1024]{3,2,1,0:T(8,128)S(1)} %get-tuple-element.23.b_ref, f32[3,2,8,1024]{3,2,1,0:T(8,128)S(1)} %get-tuple-element.31.v_ref, f32[3,2,8,1024]{3,2,1,0:T(8,128)S(1)} %get-tuple-element.32.data_ref, ...), custom_call_target="tpu_custom_call" | custom-call | flops 134217728 | bytes 3612748 | tf_op jit(solution)/shard_map/image_kernel/pallas_call | solution.py:438
  21.8 10.3 %all_to_all.5.gram_ref = f32[32,1,128]{2,1,0:T(1,128)S(1)} all-to-all(f32[32,1,128]{2,1,0:T(1,128)S(1)} %get-tuple-element.41), channel_id=1, replica_groups=mesh['inline'=8,'col'=4] {'inline','col'}, dimensions={0} | all-to-all | bytes 32768 | tf_op jit(solution)/shard_map/all_to_all | solution.py:521
  32.1 1.1 %finish_kernel.1 = (f32[3,2,8,1024]{3,2,1,0:T(8,128)}, f32[3,2,8,1024]{3,2,1,0:T(8,128)}) custom-call(f32[32,1,128]{2,1,0:T(1,128)S(1)} %all_to_all.5.gram_ref, f32[3,2,8,1024]{3,2,1,0:T(8,128)S(1)} %get-tuple-element.23.b_ref, f32[3,2,8,1024]{3,2,1,0:T(8,128)S(1)} %get-tuple-element.42.one_ref, f32[3,2,8,1024]{3,2,1,0:T(8,128)S(1)} %get-tuple-element.43.two_ref), custom_call_target="tpu_custom_call" | custom-call | flops 393216 | bytes 999424 | tf_op jit(solution)/shard_map/finish_kernel/pallas_call | solution.py:438
Async XLA Ops:
  2.9 8.0 %collective-permute-start = (f32[25,8,128]{2,1,0:T(8,128)S(1)}, f32[25,8,128]{2,1,0:T(8,128)S(1)}, u32[]{:S(2)}, u32[]{:S(2)}) collective-permute-start(f32[25,8,128]{2,1,0:T(8,128)S(1)} %get-tuple-element.24), channel_id=1, source_target_pairs={{0,4},{4,0},{8,12},{12,8},{16,20},{20,16},{24,28},{28,24},{1,5},{5... | collective-permute-start | bytes 307208 | tf_op jit(solution)/shard_map/ppermute | solution.py:452
  5.9 8.5 %collective-permute-start.1 = (f32[25,8,128]{2,1,0:T(8,128)S(1)}, f32[25,8,128]{2,1,0:T(8,128)S(1)}, u32[]{:S(2)}, u32[]{:S(2)}) collective-permute-start(f32[25,8,128]{2,1,0:T(8,128)S(1)} %get-tuple-element.25), channel_id=1, source_target_pairs={{4,8},{8,4},{12,16},{16,12},{20,24},{24,20},{5,9},{9,5},{13,17},{1... | collective-permute-start | bytes 307208 | tf_op jit(solution)/shard_map/ppermute | solution.py:452
  6.6 14.1 %collective-permute-start.3 = (f32[25,8,128]{2,1,0:T(8,128)S(1)}, f32[25,8,128]{2,1,0:T(8,128)S(1)}, u32[]{:S(2)}, u32[]{:S(2)}) collective-permute-start(f32[25,8,128]{2,1,0:T(8,128)S(1)} %get-tuple-element.25), channel_id=1, source_target_pairs={{0,4},{4,0},{8,12},{12,8},{16,20},{20,16},{24,28},{28,24},{1,5},{5... | collective-permute-start | bytes 307208 | tf_op jit(solution)/shard_map/ppermute | solution.py:452
  10.9 9.8 %collective-permute-start.2 = (f32[25,8,128]{2,1,0:T(8,128)S(1)}, f32[25,8,128]{2,1,0:T(8,128)S(1)}, u32[]{:S(2)}, u32[]{:S(2)}) collective-permute-start(f32[25,8,128]{2,1,0:T(8,128)S(1)} %collective-permute-done.near_ref), channel_id=1, source_target_pairs={{0,8},{8,16},{12,4},{16,24},{20,12},{28,20},{1,9},{9,17},{13,5},{1... | collective-permute-start | bytes 307208 | tf_op jit(solution)/shard_map/ppermute | solution.py:458
  14.6 6.3 %collective-permute-start.4 = (f32[5,4,1024]{2,1,0:T(4,128)S(1)}, f32[5,4,1024]{2,1,0:T(4,128)S(1)}, u32[]{:S(2)}, u32[]{:S(2)}) collective-permute-start(f32[5,4,1024]{2,1,0:T(4,128)S(1)} %get-tuple-element.37), channel_id=1, source_target_pairs={{1,2},{2,1},{5,6},{6,5},{9,10},{10,9},{13,14},{14,13},{17,18},{18,... | collective-permute-start | bytes 245768 | tf_op jit(solution)/shard_map/ppermute | solution.py:452
  15.2 5.6 %collective-permute-start.5 = (f32[5,4,1024]{2,1,0:T(4,128)S(1)}, f32[5,4,1024]{2,1,0:T(4,128)S(1)}, u32[]{:S(2)}, u32[]{:S(2)}) collective-permute-start(f32[5,4,1024]{2,1,0:T(4,128)S(1)} %get-tuple-element.38), channel_id=1, source_target_pairs={{0,1},{1,0},{2,3},{3,2},{4,5},{5,4},{6,7},{7,6},{8,9},{9,8},{10,11... | collective-permute-start | bytes 245768 | tf_op jit(solution)/shard_map/ppermute | solution.py:452

commit v22 on v20

--- a/solution.py
+++ b/solution.py
@@ -159,18 +159,17 @@
 
 
 def start_kernel(
-    seis_hbm, valid_hbm, avo_hbm, taps_hbm, prior_hbm, strength_hbm,
-    b_ref, near_ref, far_ref, padded_ref, valid_ref, avo_ref, prior_ref, strength_ref,
+    seis_hbm, valid_hbm, avo_hbm, taps_hbm, prior_hbm,
+    b_ref, near_ref, far_ref, padded_ref, valid_ref, avo_ref, prior_ref,
     seis_ref, taps_ref, sems,
 ):
-    taps, seis, valid, avo, prior, strength = copy_in(
+    taps, seis, valid, avo, prior = copy_in(
         (
             (taps_hbm, taps_ref),
             (seis_hbm, seis_ref),
             (valid_hbm, valid_ref),
             (avo_hbm, avo_ref),
             (prior_hbm, prior_ref),
-            (strength_hbm, strength_ref),
         ),
         sems,
     )
@@ -180,7 +179,7 @@
     bands = [band(padded_ref[a : a + 1, :]) for a in range(angles)]
     valid.wait()
     masks = [trace_columns(valid_ref, a) for a in range(angles)]
-    for copy in (seis, avo, prior, strength):
+    for copy in (seis, avo, prior):
         copy.wait()
     store_tiles(b_ref, right_side(seis_ref, masks, avo_ref, bands))
     contrasts, rows, traces, samples = b_ref.shape
@@ -274,11 +273,12 @@
 
 
 def inner_kernel(
-    count, b_ref, near_ref, near_next_ref, padded_ref, valid_ref, avo_ref, prior_ref, strength_ref,
-    v_ref, data_ref, halo_ref, ahead_ref, back_ref, norm_ref,
+    count, strength_hbm, b_ref, near_ref, near_next_ref, padded_ref, valid_ref, avo_ref, prior_ref,
+    v_ref, data_ref, halo_ref, ahead_ref, back_ref, norm_ref, strength_ref, sem,
 ):
     contrasts, rows, traces, samples = b_ref.shape
     angles, n = avo_ref.shape[1], samples // LANES
+    (copy,) = copy_in(((strength_hbm, strength_ref),), sem)
     turned = turn(padded_ref[...], count)
     bands = []
     for a in range(angles):
@@ -299,6 +299,7 @@
             [jnp.concatenate([up, own, low], axis=0) for (up, low), own in zip(ends, line)]
         )
     total = normal(field, wide, avo_ref, bands)
+    copy.wait()
     has_above, has_below = inside("inline")
     for c in range(contrasts):
         strength = strength_ref[:, c : c + 1]
@@ -413,13 +414,11 @@
 
 
 def finish_kernel(gram_ref, b_ref, one_ref, two_ref, solution_ref, residual_ref):
-    sums = jnp.sum(gram_ref[...], axis=0, keepdims=True)
-    g00, g01, g11, g12 = (sums[:, q : q + 1] for q in range(4))
-    inverse = 1.0 / g01
-    first = g00 * inverse
-    quotient = g11 * inverse
-    ratio = first * quotient
-    second = (ratio - 1.0) * g01 / (first * (g12 - quotient * g11))
+    sums = jnp.sum(gram_ref[...], axis=0)
+    shares = sums / sums[:, 1:2]
+    first, middle, last = (shares[:, q : q + 1] for q in (0, 2, 3))
+    ratio = first * middle
+    second = (ratio - 1.0) / (first * last - ratio * middle)
     near = first + second * ratio
     far = first * second
     for c in range(b_ref.shape[0]):
@@ -468,8 +467,8 @@
     lines = shape(8, 2 * LANES)
     work = 2 * angles * rows * traces * samples * 256 * 4
 
-    given = (seismic, validity, avo_coeffs, wavelets, prior_weight, lateral_strength.reshape(1, -1))
-    kept = [given[i] for i in (1, 2, 4, 5)]
+    given = (seismic, validity, avo_coeffs, wavelets, prior_weight)
+    kept = [given[i] for i in (1, 2, 4)]
     edge = shape(contrasts * samples // LANES + 1, traces, LANES)
     b, near, far, padded, *kept = call(
         start_kernel,
@@ -482,9 +481,9 @@
         [
             pltpu.VMEM(seismic.shape, seismic.dtype),
             pltpu.VMEM(wavelets.shape, F32),
-            pltpu.SemaphoreType.DMA((6,)),
+            pltpu.SemaphoreType.DMA((5,)),
         ],
-        [HBM] * 6,
+        [HBM] * 5,
     )
     near = swap("inline", near, 0)
     near_next = swap("inline", far, 1)
@@ -501,24 +500,30 @@
     col_pair = swap("col", col_pair, 0)
     bands = shape(angles, 2 * LANES, 2 * LANES)
     halo = shape(2, contrasts, traces, samples)
-    image, data, part, ahead, back, norm = call(
+    strength = lateral_strength.reshape(1, -1)
+    image, data, part, ahead, back, norm, strength = call(
         functools.partial(inner_kernel, wavelets.shape[1]),
-        (field, field, halo, bands, bands, shape(traces, LANES)),
-        (b, near, near_next, padded, *kept),
+        (field, field, halo, bands, bands, shape(traces, LANES), shape(*strength.shape)),
+        (
+            pltpu.with_memory_space_constraint(strength, pltpu.HBM),
+            b, near, near_next, padded, *kept,
+        ),
         6 * work,
-    )
-    (halo,) = call(halo_kernel, (halo,), (part, far_next, far, kept[-1]), field.size)
+        [pltpu.SemaphoreType.DMA((1,))],
+        [HBM] + [VMEM] * 7,
+    )
+    (halo,) = call(halo_kernel, (halo,), (part, far_next, far, strength), field.size)
     axes = ("inline", "col")
     one, two, gram = call(
         image_kernel,
         (field, field, shape(lax.axis_size(axes), 1, LANES)),
         (
             b, image, data, halo, norm, own, note, col_other, col_pair,
-            *kept[1:], ahead, back,
+            *kept[1:], strength, ahead, back,
         ),
         work,
     )
-    gram = lax.all_to_all(gram, axes, 0, 0).reshape(-1, LANES)
+    gram = lax.all_to_all(gram, axes, 0, 0)
     return tuple(call(finish_kernel, (field, field), (gram, b, one, two), 8 * field.size))
 
 

time: 32.6 us -> 32.5 us (level)
  no operation moved by 1% of the time
where the time goes in v22:
time: 32.5 us; the launch traced here: 32.3 us
  starting transfers between devices  15.1 us (46%)
  blocking collectives  10.2 us (31%)
  Pallas kernels  6.29 us (19%)
  between operations  0.72 us (2%)
    ppermute x5, starting transfers between devices, swap(): lax.ppermute(value, axis, [(i + d, i + 1 - d) for i in starts for d in (0...  11.6 us
    all_to_all x1, blocking collectives, shards(): gram = lax.all_to_all(gram, axes, 0, 0)  10.2 us
    pallas_call x6, Pallas kernels, call(): pl.pallas_call(kernel, out_shape=outs, in_specs=[VMEM] * len(ins) if plac...  6.29 us
    ppermute x1, starting transfers between devices, hand_on(): lax.ppermute(value, axis, [(i, j) for i, j in steps if 0 <= j < size])  3.47 us
  transfers between devices with their start and end apart: 6, of which 0 were waited for; matrix products, arithmetic and copies ran while one was open for 0% of the time, Pallas kernels for 9%

profile of v22, /device:TPU:0, one launch (start us, length us, event | category | flops | bytes accessed | tf_op | source)
XLA Modules:
  0.0 32.3 jit_solution(370352501962356888)
XLA Ops:
  0.6 1.4 %start_kernel.1 = (f32[3,2,8,1024]{3,2,1,0:T(8,128)S(1)}, f32[25,8,128]{2,1,0:T(8,128)S(1)}, f32[25,8,128]{2,1,0:T(8,128)S(1)}, f32[8,256]{1,0:T(8,128)S(1)}, s3...) custom-call(bf16[4,2,8,1024]{3,2,1,0:T(8,128)(2,1)} %seis_hbm.1, s32[4,2,8]{2,1,0:T(2,128)} %valid_hbm.1, ...), custom_call_target="tpu_custom_call" | custom-call | flops 134217728 | bytes 641680 | tf_op jit(solution)/shard_map/start_kernel/pallas_call | solution.py:437
  2.1 3.0 %collective-permute-start = (f32[25,8,128]{2,1,0:T(8,128)S(1)}, f32[25,8,128]{2,1,0:T(8,128)S(1)}, u32[]{:S(2)}, u32[]{:S(2)}) collective-permute-start(f32[25,8,128]{2,1,0:T(8,128)S(1)} %get-tuple-element.24), channel_id=1, source_target_pairs={{0,4},{4,0},{8,12},{12,8},{16,20},{20,16},{24,28},{28,24},{1,5},{5... | collective-permute-start | bytes 307208 | tf_op jit(solution)/shard_map/ppermute | solution.py:451
  5.1 0.7 %collective-permute-start.1 = (f32[25,8,128]{2,1,0:T(8,128)S(1)}, f32[25,8,128]{2,1,0:T(8,128)S(1)}, u32[]{:S(2)}, u32[]{:S(2)}) collective-permute-start(f32[25,8,128]{2,1,0:T(8,128)S(1)} %get-tuple-element.25), channel_id=1, source_target_pairs={{4,8},{8,4},{12,16},{16,12},{20,24},{24,20},{5,9},{9,5},{13,17},{1... | collective-permute-start | bytes 307208 | tf_op jit(solution)/shard_map/ppermute | solution.py:451
  5.7 4.3 %collective-permute-start.3 = (f32[25,8,128]{2,1,0:T(8,128)S(1)}, f32[25,8,128]{2,1,0:T(8,128)S(1)}, u32[]{:S(2)}, u32[]{:S(2)}) collective-permute-start(f32[25,8,128]{2,1,0:T(8,128)S(1)} %get-tuple-element.25), channel_id=1, source_target_pairs={{0,4},{4,0},{8,12},{12,8},{16,20},{20,16},{24,28},{28,24},{1,5},{5... | collective-permute-start | bytes 307208 | tf_op jit(solution)/shard_map/ppermute | solution.py:451
  10.1 0.0 collective-permute-done.near_ref
  10.1 3.5 %collective-permute-start.2 = (f32[25,8,128]{2,1,0:T(8,128)S(1)}, f32[25,8,128]{2,1,0:T(8,128)S(1)}, u32[]{:S(2)}, u32[]{:S(2)}) collective-permute-start(f32[25,8,128]{2,1,0:T(8,128)S(1)} %collective-permute-done.near_ref), channel_id=1, source_target_pairs={{0,8},{8,16},{12,4},{16,24},{20,12},{28,20},{1,9},{9,17},{13,5},{1... | collective-permute-start | bytes 307208 | tf_op jit(solution)/shard_map/ppermute | solution.py:457
  13.6 0.0 collective-permute-done.1.near_next_ref
  13.6 0.1 column_kernel.1
  13.7 0.7 %collective-permute-start.4 = (f32[5,4,1024]{2,1,0:T(4,128)S(1)}, f32[5,4,1024]{2,1,0:T(4,128)S(1)}, u32[]{:S(2)}, u32[]{:S(2)}) collective-permute-start(f32[5,4,1024]{2,1,0:T(4,128)S(1)} %get-tuple-element.37), channel_id=1, source_target_pairs={{1,2},{2,1},{5,6},{6,5},{9,10},{10,9},{13,14},{14,13},{17,18},{18,... | collective-permute-start | bytes 245768 | tf_op jit(solution)/shard_map/ppermute | solution.py:451
  14.4 2.9 %collective-permute-start.5 = (f32[5,4,1024]{2,1,0:T(4,128)S(1)}, f32[5,4,1024]{2,1,0:T(4,128)S(1)}, u32[]{:S(2)}, u32[]{:S(2)}) collective-permute-start(f32[5,4,1024]{2,1,0:T(4,128)S(1)} %get-tuple-element.38), channel_id=1, source_target_pairs={{0,1},{1,0},{2,3},{3,2},{4,5},{5,4},{6,7},{7,6},{8,9},{9,8},{10,11... | collective-permute-start | bytes 245768 | tf_op jit(solution)/shard_map/ppermute | solution.py:451
  17.3 2.7 %inner_kernel.1 = (f32[3,2,8,1024]{3,2,1,0:T(8,128)S(1)}, f32[3,2,8,1024]{3,2,1,0:T(8,128)S(1)}, f32[2,3,8,1024]{3,2,1,0:T(8,128)S(1)}, f32[4,256,256]{2,1,0:T(8...) custom-call(f32[1,3]{1,0:T(1,128)} %bitcast.3, ...), custom_call_target="tpu_custom_call" | custom-call | flops 805306368 | bytes 3150168 | tf_op jit(solution)/shard_map/inner_kernel/pallas_call | solution.py:437
  20.0 0.0 collective-permute-done.3.far_ref
  20.0 0.0 collective-permute-done.2.far_next_ref
  20.0 0.1 halo_kernel.1.halo_ref
  20.1 0.0 collective-permute-done.4.other_ref
  20.1 0.0 collective-permute-done.5.pair_ref
  20.1 1.0 %image_kernel.1 = (f32[3,2,8,1024]{3,2,1,0:T(8,128)S(1)}, f32[3,2,8,1024]{3,2,1,0:T(8,128)S(1)}, f32[32,1,128]{2,1,0:T(1,128)S(1)}) custom-call(f32[3,2,8,1024]{3,2,1,0:T(8,128)S(1)} %get-tuple-element.23.b_ref, f32[3,2,8,1024]{3,2,1,0:T(8,128)S(1)} %get-tuple-element.30.v_ref, f32[3,2,8,1024]{3,2,1,0:T(8,128)S(1)} %get-tuple-element.31.data_ref, ...), custom_call_target="tpu_custom_call" | custom-call | flops 134217728 | bytes 3612748 | tf_op jit(solution)/shard_map/image_kernel/pallas_call | solution.py:437
  21.1 10.2 %all_to_all.5.gram_ref = f32[32,1,128]{2,1,0:T(1,128)S(1)} all-to-all(f32[32,1,128]{2,1,0:T(1,128)S(1)} %get-tuple-element.41), channel_id=1, replica_groups=mesh['inline'=8,'col'=4] {'inline','col'}, dimensions={0} | all-to-all | bytes 32768 | tf_op jit(solution)/shard_map/all_to_all | solution.py:526
  31.3 1.0 %finish_kernel.1 = (f32[3,2,8,1024]{3,2,1,0:T(8,128)}, f32[3,2,8,1024]{3,2,1,0:T(8,128)}) custom-call(f32[32,1,128]{2,1,0:T(1,128)S(1)} %all_to_all.5.gram_ref, f32[3,2,8,1024]{3,2,1,0:T(8,128)S(1)} %get-tuple-element.23.b_ref, f32[3,2,8,1024]{3,2,1,0:T(8,128)S(1)} %get-tuple-element.42.one_ref, f32[3,2,8,1024]{3,2,1,0:T(8,128)S(1)} %get-tuple-element.43.two_ref), custom_call_target="tpu_custom_call" | custom-call | flops 393216 | bytes 999424 | tf_op jit(solution)/shard_map/finish_kernel/pallas_call | solution.py:437
Async XLA Ops:
  2.1 8.0 %collective-permute-start = (f32[25,8,128]{2,1,0:T(8,128)S(1)}, f32[25,8,128]{2,1,0:T(8,128)S(1)}, u32[]{:S(2)}, u32[]{:S(2)}) collective-permute-start(f32[25,8,128]{2,1,0:T(8,128)S(1)} %get-tuple-element.24), channel_id=1, source_target_pairs={{0,4},{4,0},{8,12},{12,8},{16,20},{20,16},{24,28},{28,24},{1,5},{5... | collective-permute-start | bytes 307208 | tf_op jit(solution)/shard_map/ppermute | solution.py:451
  5.1 8.5 %collective-permute-start.1 = (f32[25,8,128]{2,1,0:T(8,128)S(1)}, f32[25,8,128]{2,1,0:T(8,128)S(1)}, u32[]{:S(2)}, u32[]{:S(2)}) collective-permute-start(f32[25,8,128]{2,1,0:T(8,128)S(1)} %get-tuple-element.25), channel_id=1, source_target_pairs={{4,8},{8,4},{12,16},{16,12},{20,24},{24,20},{5,9},{9,5},{13,17},{1... | collective-permute-start | bytes 307208 | tf_op jit(solution)/shard_map/ppermute | solution.py:451
  5.7 14.3 %collective-permute-start.3 = (f32[25,8,128]{2,1,0:T(8,128)S(1)}, f32[25,8,128]{2,1,0:T(8,128)S(1)}, u32[]{:S(2)}, u32[]{:S(2)}) collective-permute-start(f32[25,8,128]{2,1,0:T(8,128)S(1)} %get-tuple-element.25), channel_id=1, source_target_pairs={{0,4},{4,0},{8,12},{12,8},{16,20},{20,16},{24,28},{28,24},{1,5},{5... | collective-permute-start | bytes 307208 | tf_op jit(solution)/shard_map/ppermute | solution.py:451
  10.1 9.9 %collective-permute-start.2 = (f32[25,8,128]{2,1,0:T(8,128)S(1)}, f32[25,8,128]{2,1,0:T(8,128)S(1)}, u32[]{:S(2)}, u32[]{:S(2)}) collective-permute-start(f32[25,8,128]{2,1,0:T(8,128)S(1)} %collective-permute-done.near_ref), channel_id=1, source_target_pairs={{0,8},{8,16},{12,4},{16,24},{20,12},{28,20},{1,9},{9,17},{13,5},{1... | collective-permute-start | bytes 307208 | tf_op jit(solution)/shard_map/ppermute | solution.py:457
  13.7 6.4 %collective-permute-start.4 = (f32[5,4,1024]{2,1,0:T(4,128)S(1)}, f32[5,4,1024]{2,1,0:T(4,128)S(1)}, u32[]{:S(2)}, u32[]{:S(2)}) collective-permute-start(f32[5,4,1024]{2,1,0:T(4,128)S(1)} %get-tuple-element.37), channel_id=1, source_target_pairs={{1,2},{2,1},{5,6},{6,5},{9,10},{10,9},{13,14},{14,13},{17,18},{18,... | collective-permute-start | bytes 245768 | tf_op jit(solution)/shard_map/ppermute | solution.py:451
  14.4 5.8 %collective-permute-start.5 = (f32[5,4,1024]{2,1,0:T(4,128)S(1)}, f32[5,4,1024]{2,1,0:T(4,128)S(1)}, u32[]{:S(2)}, u32[]{:S(2)}) collective-permute-start(f32[5,4,1024]{2,1,0:T(4,128)S(1)} %get-tuple-element.38), channel_id=1, source_target_pairs={{0,1},{1,0},{2,3},{3,2},{4,5},{5,4},{6,7},{7,6},{8,9},{9,8},{10,11... | collective-permute-start | bytes 245768 | tf_op jit(solution)/shard_map/ppermute | solution.py:451

commit v23 on v22

--- a/solution.py
+++ b/solution.py
@@ -163,11 +163,12 @@
     b_ref, near_ref, far_ref, padded_ref, valid_ref, avo_ref, prior_ref,
     seis_ref, taps_ref, sems,
 ):
-    taps, seis, valid, avo, prior = copy_in(
+    angles = avo_ref.shape[1]
+    taps, valid, *rest = copy_in(
         (
             (taps_hbm, taps_ref),
-            (seis_hbm, seis_ref),
             (valid_hbm, valid_ref),
+            *((seis_hbm.at[a], seis_ref.at[a]) for a in range(angles)),
             (avo_hbm, avo_ref),
             (prior_hbm, prior_ref),
         ),
@@ -175,11 +176,10 @@
     )
     taps.wait()
     pad_taps(taps_ref, padded_ref)
-    angles = avo_ref.shape[1]
     bands = [band(padded_ref[a : a + 1, :]) for a in range(angles)]
     valid.wait()
     masks = [trace_columns(valid_ref, a) for a in range(angles)]
-    for copy in (seis, avo, prior):
+    for copy in rest:
         copy.wait()
     store_tiles(b_ref, right_side(seis_ref, masks, avo_ref, bands))
     contrasts, rows, traces, samples = b_ref.shape
@@ -413,32 +413,40 @@
     gram_ref[...] = jnp.broadcast_to(packed[None], gram_ref.shape)
 
 
-def finish_kernel(gram_ref, b_ref, one_ref, two_ref, solution_ref, residual_ref):
+def finish_kernel(
+    gram_ref, b_ref, one_ref, two_ref, solution_hbm, residual_hbm, solution_ref, residual_ref, sems
+):
     sums = jnp.sum(gram_ref[...], axis=0)
-    shares = sums / sums[:, 1:2]
-    first, middle, last = (shares[:, q : q + 1] for q in (0, 2, 3))
-    ratio = first * middle
-    second = (ratio - 1.0) / (first * last - ratio * middle)
+    g00, g01, g11, g12 = (sums[:, q : q + 1] for q in range(4))
+    first = g00 / g01
+    ratio = first * g11 / g01
+    second = (ratio - 1.0) * g01 / (first * g12 - ratio * g11)
     near = first + second * ratio
     far = first * second
-    for c in range(b_ref.shape[0]):
-        for r in range(b_ref.shape[1]):
-            b, one, two = b_ref[c, r], one_ref[c, r], two_ref[c, r]
-            solution_ref[c, r] = near * b - far * one
-            residual_ref[c, r] = b - near * one + far * two
+    blocks = [(c, r) for c in range(b_ref.shape[0]) for r in range(b_ref.shape[1])]
+    for block in blocks:
+        solution_ref[block] = near * b_ref[block] - far * one_ref[block]
+    done = pltpu.make_async_copy(solution_ref, solution_hbm, sems.at[0])
+    done.start()
+    for block in blocks:
+        residual_ref[block] = b_ref[block] - near * one_ref[block] + far * two_ref[block]
+    last = pltpu.make_async_copy(residual_ref, residual_hbm, sems.at[1])
+    last.start()
+    done.wait()
+    last.wait()
 
 
 VMEM = pl.BlockSpec(memory_space=pltpu.VMEM)
 HBM = pl.BlockSpec(memory_space=pltpu.HBM)
 
 
-def call(kernel, outs, ins, flops, scratch=(), places=None):
+def call(kernel, outs, ins, flops, scratch=(), places=None, to=VMEM):
     moved = sum(x.size * x.dtype.itemsize for x in (*ins, *outs))
     return pl.pallas_call(
         kernel,
         out_shape=outs,
         in_specs=[VMEM] * len(ins) if places is None else places,
-        out_specs=jax.tree.map(lambda _: VMEM, outs),
+        out_specs=jax.tree.map(lambda _: to, outs),
         scratch_shapes=list(scratch),
         compiler_params=pltpu.CompilerParams(vmem_limit_bytes=24 * 1024 * 1024),
         cost_estimate=pl.CostEstimate(flops=flops, bytes_accessed=moved, transcendentals=0),
@@ -481,7 +489,7 @@
         [
             pltpu.VMEM(seismic.shape, seismic.dtype),
             pltpu.VMEM(wavelets.shape, F32),
-            pltpu.SemaphoreType.DMA((5,)),
+            pltpu.SemaphoreType.DMA((angles + 4,)),
         ],
         [HBM] * 5,
     )
@@ -524,7 +532,11 @@
         work,
     )
     gram = lax.all_to_all(gram, axes, 0, 0)
-    return tuple(call(finish_kernel, (field, field), (gram, b, one, two), 8 * field.size))
+    work = 8 * field.size
+    room = [pltpu.VMEM(field.shape, F32)] * 2 + [pltpu.SemaphoreType.DMA((2,))]
+    return tuple(
+        call(finish_kernel, (field, field), (gram, b, one, two), work, room, to=HBM)
+    )
 
 
 def solution(mesh):

time: 32.5 us -> 32.5 us (level)
  no operation moved by 1% of the time
where the time goes in v23:
time: 32.5 us; the launch traced here: 32.3 us
  starting transfers between devices  15.1 us (46%)
  blocking collectives  10.2 us (31%)
  Pallas kernels  6.25 us (19%)
  between operations  0.72 us (2%)
    ppermute x5, starting transfers between devices, swap(): lax.ppermute(value, axis, [(i + d, i + 1 - d) for i in starts for d in (0...  11.6 us
    all_to_all x1, blocking collectives, shards(): gram = lax.all_to_all(gram, axes, 0, 0)  10.2 us
    pallas_call x6, Pallas kernels, call(): pl.pallas_call(kernel, out_shape=outs, in_specs=[VMEM] * len(ins) if plac...  6.25 us
    ppermute x1, starting transfers between devices, hand_on(): lax.ppermute(value, axis, [(i, j) for i, j in steps if 0 <= j < size])  3.48 us
  transfers between devices with their start and end apart: 6, of which 0 were waited for; matrix products, arithmetic and copies ran while one was open for 0% of the time, Pallas kernels for 9%

profile of v23, /device:TPU:0, one launch (start us, length us, event | category | flops | bytes accessed | tf_op | source)
XLA Modules:
  0.0 32.3 jit_solution(11576809477832441077)
XLA Ops:
  0.6 1.5 %start_kernel.1 = (f32[3,2,8,1024]{3,2,1,0:T(8,128)S(1)}, f32[25,8,128]{2,1,0:T(8,128)S(1)}, f32[25,8,128]{2,1,0:T(8,128)S(1)}, f32[8,256]{1,0:T(8,128)S(1)}, s3...) custom-call(bf16[4,2,8,1024]{3,2,1,0:T(8,128)(2,1)} %seis_hbm.1, s32[4,2,8]{2,1,0:T(2,128)} %valid_hbm.1, ...), custom_call_target="tpu_custom_call" | custom-call | flops 134217728 | bytes 641680 | tf_op jit(solution)/shard_map/start_kernel/pallas_call | solution.py:445
  2.1 3.0 %collective-permute-start = (f32[25,8,128]{2,1,0:T(8,128)S(1)}, f32[25,8,128]{2,1,0:T(8,128)S(1)}, u32[]{:S(2)}, u32[]{:S(2)}) collective-permute-start(f32[25,8,128]{2,1,0:T(8,128)S(1)} %get-tuple-element.24), channel_id=1, source_target_pairs={{0,4},{4,0},{8,12},{12,8},{16,20},{20,16},{24,28},{28,24},{1,5},{5... | collective-permute-start | bytes 307208 | tf_op jit(solution)/shard_map/ppermute | solution.py:459
  5.1 0.7 %collective-permute-start.1 = (f32[25,8,128]{2,1,0:T(8,128)S(1)}, f32[25,8,128]{2,1,0:T(8,128)S(1)}, u32[]{:S(2)}, u32[]{:S(2)}) collective-permute-start(f32[25,8,128]{2,1,0:T(8,128)S(1)} %get-tuple-element.25), channel_id=1, source_target_pairs={{4,8},{8,4},{12,16},{16,12},{20,24},{24,20},{5,9},{9,5},{13,17},{1... | collective-permute-start | bytes 307208 | tf_op jit(solution)/shard_map/ppermute | solution.py:459
  5.8 4.3 %collective-permute-start.3 = (f32[25,8,128]{2,1,0:T(8,128)S(1)}, f32[25,8,128]{2,1,0:T(8,128)S(1)}, u32[]{:S(2)}, u32[]{:S(2)}) collective-permute-start(f32[25,8,128]{2,1,0:T(8,128)S(1)} %get-tuple-element.25), channel_id=1, source_target_pairs={{0,4},{4,0},{8,12},{12,8},{16,20},{20,16},{24,28},{28,24},{1,5},{5... | collective-permute-start | bytes 307208 | tf_op jit(solution)/shard_map/ppermute | solution.py:459
  10.1 0.0 collective-permute-done.near_ref
  10.1 3.5 %collective-permute-start.2 = (f32[25,8,128]{2,1,0:T(8,128)S(1)}, f32[25,8,128]{2,1,0:T(8,128)S(1)}, u32[]{:S(2)}, u32[]{:S(2)}) collective-permute-start(f32[25,8,128]{2,1,0:T(8,128)S(1)} %collective-permute-done.near_ref), channel_id=1, source_target_pairs={{0,8},{8,16},{12,4},{16,24},{20,12},{28,20},{1,9},{9,17},{13,5},{1... | collective-permute-start | bytes 307208 | tf_op jit(solution)/shard_map/ppermute | solution.py:465
  13.6 0.0 collective-permute-done.1.near_next_ref
  13.6 0.1 column_kernel.1
  13.7 0.7 %collective-permute-start.4 = (f32[5,4,1024]{2,1,0:T(4,128)S(1)}, f32[5,4,1024]{2,1,0:T(4,128)S(1)}, u32[]{:S(2)}, u32[]{:S(2)}) collective-permute-start(f32[5,4,1024]{2,1,0:T(4,128)S(1)} %get-tuple-element.37), channel_id=1, source_target_pairs={{1,2},{2,1},{5,6},{6,5},{9,10},{10,9},{13,14},{14,13},{17,18},{18,... | collective-permute-start | bytes 245768 | tf_op jit(solution)/shard_map/ppermute | solution.py:459
  14.4 2.9 %collective-permute-start.5 = (f32[5,4,1024]{2,1,0:T(4,128)S(1)}, f32[5,4,1024]{2,1,0:T(4,128)S(1)}, u32[]{:S(2)}, u32[]{:S(2)}) collective-permute-start(f32[5,4,1024]{2,1,0:T(4,128)S(1)} %get-tuple-element.38), channel_id=1, source_target_pairs={{0,1},{1,0},{2,3},{3,2},{4,5},{5,4},{6,7},{7,6},{8,9},{9,8},{10,11... | collective-permute-start | bytes 245768 | tf_op jit(solution)/shard_map/ppermute | solution.py:459
  17.4 2.7 %inner_kernel.1 = (f32[3,2,8,1024]{3,2,1,0:T(8,128)S(1)}, f32[3,2,8,1024]{3,2,1,0:T(8,128)S(1)}, f32[2,3,8,1024]{3,2,1,0:T(8,128)S(1)}, f32[4,256,256]{2,1,0:T(8...) custom-call(f32[1,3]{1,0:T(1,128)} %bitcast.3, ...), custom_call_target="tpu_custom_call" | custom-call | flops 805306368 | bytes 3150168 | tf_op jit(solution)/shard_map/inner_kernel/pallas_call | solution.py:445
  20.0 0.0 collective-permute-done.3.far_ref
  20.0 0.0 collective-permute-done.2.far_next_ref
  20.1 0.1 halo_kernel.1.halo_ref
  20.2 0.0 collective-permute-done.4.other_ref
  20.2 0.0 collective-permute-done.5.pair_ref
  20.2 0.9 %image_kernel.1 = (f32[3,2,8,1024]{3,2,1,0:T(8,128)S(1)}, f32[3,2,8,1024]{3,2,1,0:T(8,128)S(1)}, f32[32,1,128]{2,1,0:T(1,128)S(1)}) custom-call(f32[3,2,8,1024]{3,2,1,0:T(8,128)S(1)} %get-tuple-element.23.b_ref, f32[3,2,8,1024]{3,2,1,0:T(8,128)S(1)} %get-tuple-element.30.v_ref, f32[3,2,8,1024]{3,2,1,0:T(8,128)S(1)} %get-tuple-element.31.data_ref, ...), custom_call_target="tpu_custom_call" | custom-call | flops 134217728 | bytes 3612748 | tf_op jit(solution)/shard_map/image_kernel/pallas_call | solution.py:445
  21.1 10.2 %all_to_all.5.gram_ref = f32[32,1,128]{2,1,0:T(1,128)S(1)} all-to-all(f32[32,1,128]{2,1,0:T(1,128)S(1)} %get-tuple-element.41), channel_id=1, replica_groups=mesh['inline'=8,'col'=4] {'inline','col'}, dimensions={0} | all-to-all | bytes 32768 | tf_op jit(solution)/shard_map/all_to_all | solution.py:534
  31.3 0.9 %finish_kernel.1 = (f32[3,2,8,1024]{3,2,1,0:T(8,128)}, f32[3,2,8,1024]{3,2,1,0:T(8,128)}) custom-call(f32[32,1,128]{2,1,0:T(1,128)S(1)} %all_to_all.5.gram_ref, f32[3,2,8,1024]{3,2,1,0:T(8,128)S(1)} %get-tuple-element.23.b_ref, f32[3,2,8,1024]{3,2,1,0:T(8,128)S(1)} %get-tuple-element.42.one_ref, f32[3,2,8,1024]{3,2,1,0:T(8,128)S(1)} %get-tuple-element.43.two_ref), custom_call_target="tpu_custom_call" | custom-call | flops 393216 | bytes 999424 | tf_op jit(solution)/shard_map/finish_kernel/pallas_call | solution.py:445
Async XLA Ops:
  2.1 8.0 %collective-permute-start = (f32[25,8,128]{2,1,0:T(8,128)S(1)}, f32[25,8,128]{2,1,0:T(8,128)S(1)}, u32[]{:S(2)}, u32[]{:S(2)}) collective-permute-start(f32[25,8,128]{2,1,0:T(8,128)S(1)} %get-tuple-element.24), channel_id=1, source_target_pairs={{0,4},{4,0},{8,12},{12,8},{16,20},{20,16},{24,28},{28,24},{1,5},{5... | collective-permute-start | bytes 307208 | tf_op jit(solution)/shard_map/ppermute | solution.py:459
  5.1 8.5 %collective-permute-start.1 = (f32[25,8,128]{2,1,0:T(8,128)S(1)}, f32[25,8,128]{2,1,0:T(8,128)S(1)}, u32[]{:S(2)}, u32[]{:S(2)}) collective-permute-start(f32[25,8,128]{2,1,0:T(8,128)S(1)} %get-tuple-element.25), channel_id=1, source_target_pairs={{4,8},{8,4},{12,16},{16,12},{20,24},{24,20},{5,9},{9,5},{13,17},{1... | collective-permute-start | bytes 307208 | tf_op jit(solution)/shard_map/ppermute | solution.py:459
  5.8 14.3 %collective-permute-start.3 = (f32[25,8,128]{2,1,0:T(8,128)S(1)}, f32[25,8,128]{2,1,0:T(8,128)S(1)}, u32[]{:S(2)}, u32[]{:S(2)}) collective-permute-start(f32[25,8,128]{2,1,0:T(8,128)S(1)} %get-tuple-element.25), channel_id=1, source_target_pairs={{0,4},{4,0},{8,12},{12,8},{16,20},{20,16},{24,28},{28,24},{1,5},{5... | collective-permute-start | bytes 307208 | tf_op jit(solution)/shard_map/ppermute | solution.py:459
  10.1 9.9 %collective-permute-start.2 = (f32[25,8,128]{2,1,0:T(8,128)S(1)}, f32[25,8,128]{2,1,0:T(8,128)S(1)}, u32[]{:S(2)}, u32[]{:S(2)}) collective-permute-start(f32[25,8,128]{2,1,0:T(8,128)S(1)} %collective-permute-done.near_ref), channel_id=1, source_target_pairs={{0,8},{8,16},{12,4},{16,24},{20,12},{28,20},{1,9},{9,17},{13,5},{1... | collective-permute-start | bytes 307208 | tf_op jit(solution)/shard_map/ppermute | solution.py:465
  13.7 6.4 %collective-permute-start.4 = (f32[5,4,1024]{2,1,0:T(4,128)S(1)}, f32[5,4,1024]{2,1,0:T(4,128)S(1)}, u32[]{:S(2)}, u32[]{:S(2)}) collective-permute-start(f32[5,4,1024]{2,1,0:T(4,128)S(1)} %get-tuple-element.37), channel_id=1, source_target_pairs={{1,2},{2,1},{5,6},{6,5},{9,10},{10,9},{13,14},{14,13},{17,18},{18,... | collective-permute-start | bytes 245768 | tf_op jit(solution)/shard_map/ppermute | solution.py:459
  14.4 5.8 %collective-permute-start.5 = (f32[5,4,1024]{2,1,0:T(4,128)S(1)}, f32[5,4,1024]{2,1,0:T(4,128)S(1)}, u32[]{:S(2)}, u32[]{:S(2)}) collective-permute-start(f32[5,4,1024]{2,1,0:T(4,128)S(1)} %get-tuple-element.38), channel_id=1, source_target_pairs={{0,1},{1,0},{2,3},{3,2},{4,5},{5,4},{6,7},{7,6},{8,9},{9,8},{10,11... | collective-permute-start | bytes 245768 | tf_op jit(solution)/shard_map/ppermute | solution.py:459

commit v24 on v23

--- a/solution.py
+++ b/solution.py
@@ -42,6 +42,7 @@
 
 
 def convolve(rows, bands):
+    rows = rows.astype(BF16)
     out = lax.dot_general(rows, bands, (((1,), (1,)), ((), ())), preferred_element_type=F32)
     return out[:, :LANES] + out[:, LANES:]
 
@@ -57,14 +58,21 @@
     return jnp.concatenate([column(rows[r : r + 1, :]) for r in range(rows.shape[0])], axis=0)
 
 
+def halves(value):
+    if value.shape[0] % 16 == 0:
+        return split(value)
+    high = value.astype(BF16).astype(F32)
+    return high, value - high
+
+
 def windows(tiles):
     pairs = [jnp.concatenate(pair, axis=1) for pair in zip(tiles[:-1], tiles[1:])]
     return jnp.concatenate(pairs, axis=0)
 
 
 def forward(tiles, bands):
-    zero = jnp.zeros_like(tiles[0]).astype(BF16)
-    highs, lows = zip(*[split(t) for t in tiles])
+    highs, lows = zip(*[halves(t) for t in tiles])
+    zero = jnp.zeros_like(highs[0])
     n, size = len(tiles) + 1, tiles[0].shape[0]
     rows = [windows([zero, *part, zero]) for part in (highs, lows)]
     out = convolve(jnp.concatenate(rows, axis=0), bands)
@@ -133,7 +141,7 @@
         left_half = lax.broadcasted_iota(jnp.int32, synth[0].shape, 1) < LANES // 2
         synth[0] = jnp.where(left_half, 0.0, synth[0])
         synth[n] = jnp.where(left_half, synth[n], 0.0)
-        result = backward(list(zip(*[split(t) for t in synth])), back)
+        result = backward(list(zip(*[halves(t) for t in synth])), back)
         add_terms(total, avo_ref, a, result)
     return total
 

time: 32.5 us -> 32.5 us (level)
  no operation moved by 1% of the time
where the time goes in v24:
time: 32.5 us; the launch traced here: 32.3 us
  starting transfers between devices  15.1 us (46%)
  blocking collectives  10.2 us (31%)
  Pallas kernels  6.25 us (19%)
  between operations  0.72 us (2%)
    ppermute x5, starting transfers between devices, swap(): lax.ppermute(value, axis, [(i + d, i + 1 - d) for i in starts for d in (0...  11.6 us
    all_to_all x1, blocking collectives, shards(): gram = lax.all_to_all(gram, axes, 0, 0)  10.2 us
    pallas_call x6, Pallas kernels, call(): pl.pallas_call(kernel, out_shape=outs, in_specs=[VMEM] * len(ins) if plac...  6.25 us
    ppermute x1, starting transfers between devices, hand_on(): lax.ppermute(value, axis, [(i, j) for i, j in steps if 0 <= j < size])  3.48 us
  transfers between devices with their start and end apart: 6, of which 0 were waited for; matrix products, arithmetic and copies ran while one was open for 0% of the time, Pallas kernels for 9%

profile of v24, /device:TPU:0, one launch (start us, length us, event | category | flops | bytes accessed | tf_op | source)
XLA Modules:
  0.0 32.3 jit_solution(17237804368907023609)
XLA Ops:
  0.6 1.5 %start_kernel.1 = (f32[3,2,8,1024]{3,2,1,0:T(8,128)S(1)}, f32[25,8,128]{2,1,0:T(8,128)S(1)}, f32[25,8,128]{2,1,0:T(8,128)S(1)}, f32[8,256]{1,0:T(8,128)S(1)}, s3...) custom-call(bf16[4,2,8,1024]{3,2,1,0:T(8,128)(2,1)} %seis_hbm.1, s32[4,2,8]{2,1,0:T(2,128)} %valid_hbm.1, ...), custom_call_target="tpu_custom_call" | custom-call | flops 134217728 | bytes 641680 | tf_op jit(solution)/shard_map/start_kernel/pallas_call | solution.py:453
  2.1 3.0 %collective-permute-start = (f32[25,8,128]{2,1,0:T(8,128)S(1)}, f32[25,8,128]{2,1,0:T(8,128)S(1)}, u32[]{:S(2)}, u32[]{:S(2)}) collective-permute-start(f32[25,8,128]{2,1,0:T(8,128)S(1)} %get-tuple-element.24), channel_id=1, source_target_pairs={{0,4},{4,0},{8,12},{12,8},{16,20},{20,16},{24,28},{28,24},{1,5},{5... | collective-permute-start | bytes 307208 | tf_op jit(solution)/shard_map/ppermute | solution.py:467
  5.1 0.7 %collective-permute-start.1 = (f32[25,8,128]{2,1,0:T(8,128)S(1)}, f32[25,8,128]{2,1,0:T(8,128)S(1)}, u32[]{:S(2)}, u32[]{:S(2)}) collective-permute-start(f32[25,8,128]{2,1,0:T(8,128)S(1)} %get-tuple-element.25), channel_id=1, source_target_pairs={{4,8},{8,4},{12,16},{16,12},{20,24},{24,20},{5,9},{9,5},{13,17},{1... | collective-permute-start | bytes 307208 | tf_op jit(solution)/shard_map/ppermute | solution.py:467
  5.8 4.3 %collective-permute-start.3 = (f32[25,8,128]{2,1,0:T(8,128)S(1)}, f32[25,8,128]{2,1,0:T(8,128)S(1)}, u32[]{:S(2)}, u32[]{:S(2)}) collective-permute-start(f32[25,8,128]{2,1,0:T(8,128)S(1)} %get-tuple-element.25), channel_id=1, source_target_pairs={{0,4},{4,0},{8,12},{12,8},{16,20},{20,16},{24,28},{28,24},{1,5},{5... | collective-permute-start | bytes 307208 | tf_op jit(solution)/shard_map/ppermute | solution.py:467
  10.1 0.0 collective-permute-done.near_ref
  10.1 3.5 %collective-permute-start.2 = (f32[25,8,128]{2,1,0:T(8,128)S(1)}, f32[25,8,128]{2,1,0:T(8,128)S(1)}, u32[]{:S(2)}, u32[]{:S(2)}) collective-permute-start(f32[25,8,128]{2,1,0:T(8,128)S(1)} %collective-permute-done.near_ref), channel_id=1, source_target_pairs={{0,8},{8,16},{12,4},{16,24},{20,12},{28,20},{1,9},{9,17},{13,5},{1... | collective-permute-start | bytes 307208 | tf_op jit(solution)/shard_map/ppermute | solution.py:473
  13.6 0.0 collective-permute-done.1.near_next_ref
  13.6 0.1 column_kernel.1
  13.7 0.7 %collective-permute-start.4 = (f32[5,4,1024]{2,1,0:T(4,128)S(1)}, f32[5,4,1024]{2,1,0:T(4,128)S(1)}, u32[]{:S(2)}, u32[]{:S(2)}) collective-permute-start(f32[5,4,1024]{2,1,0:T(4,128)S(1)} %get-tuple-element.37), channel_id=1, source_target_pairs={{1,2},{2,1},{5,6},{6,5},{9,10},{10,9},{13,14},{14,13},{17,18},{18,... | collective-permute-start | bytes 245768 | tf_op jit(solution)/shard_map/ppermute | solution.py:467
  14.4 2.9 %collective-permute-start.5 = (f32[5,4,1024]{2,1,0:T(4,128)S(1)}, f32[5,4,1024]{2,1,0:T(4,128)S(1)}, u32[]{:S(2)}, u32[]{:S(2)}) collective-permute-start(f32[5,4,1024]{2,1,0:T(4,128)S(1)} %get-tuple-element.38), channel_id=1, source_target_pairs={{0,1},{1,0},{2,3},{3,2},{4,5},{5,4},{6,7},{7,6},{8,9},{9,8},{10,11... | collective-permute-start | bytes 245768 | tf_op jit(solution)/shard_map/ppermute | solution.py:467
  17.4 2.7 %inner_kernel.1 = (f32[3,2,8,1024]{3,2,1,0:T(8,128)S(1)}, f32[3,2,8,1024]{3,2,1,0:T(8,128)S(1)}, f32[2,3,8,1024]{3,2,1,0:T(8,128)S(1)}, f32[4,256,256]{2,1,0:T(8...) custom-call(f32[1,3]{1,0:T(1,128)} %bitcast.3, ...), custom_call_target="tpu_custom_call" | custom-call | flops 805306368 | bytes 3150168 | tf_op jit(solution)/shard_map/inner_kernel/pallas_call | solution.py:453
  20.0 0.0 collective-permute-done.3.far_ref
  20.0 0.0 collective-permute-done.2.far_next_ref
  20.1 0.1 halo_kernel.1.halo_ref
  20.2 0.0 collective-permute-done.4.other_ref
  20.2 0.0 collective-permute-done.5.pair_ref
  20.2 0.9 %image_kernel.1 = (f32[3,2,8,1024]{3,2,1,0:T(8,128)S(1)}, f32[3,2,8,1024]{3,2,1,0:T(8,128)S(1)}, f32[32,1,128]{2,1,0:T(1,128)S(1)}) custom-call(f32[3,2,8,1024]{3,2,1,0:T(8,128)S(1)} %get-tuple-element.23.b_ref, f32[3,2,8,1024]{3,2,1,0:T(8,128)S(1)} %get-tuple-element.30.v_ref, f32[3,2,8,1024]{3,2,1,0:T(8,128)S(1)} %get-tuple-element.31.data_ref, ...), custom_call_target="tpu_custom_call" | custom-call | flops 134217728 | bytes 3612748 | tf_op jit(solution)/shard_map/image_kernel/pallas_call | solution.py:453
  21.1 10.2 %all_to_all.5.gram_ref = f32[32,1,128]{2,1,0:T(1,128)S(1)} all-to-all(f32[32,1,128]{2,1,0:T(1,128)S(1)} %get-tuple-element.41), channel_id=1, replica_groups=mesh['inline'=8,'col'=4] {'inline','col'}, dimensions={0} | all-to-all | bytes 32768 | tf_op jit(solution)/shard_map/all_to_all | solution.py:542
  31.3 0.9 %finish_kernel.1 = (f32[3,2,8,1024]{3,2,1,0:T(8,128)}, f32[3,2,8,1024]{3,2,1,0:T(8,128)}) custom-call(f32[32,1,128]{2,1,0:T(1,128)S(1)} %all_to_all.5.gram_ref, f32[3,2,8,1024]{3,2,1,0:T(8,128)S(1)} %get-tuple-element.23.b_ref, f32[3,2,8,1024]{3,2,1,0:T(8,128)S(1)} %get-tuple-element.42.one_ref, f32[3,2,8,1024]{3,2,1,0:T(8,128)S(1)} %get-tuple-element.43.two_ref), custom_call_target="tpu_custom_call" | custom-call | flops 393216 | bytes 999424 | tf_op jit(solution)/shard_map/finish_kernel/pallas_call | solution.py:453
Async XLA Ops:
  2.1 8.0 %collective-permute-start = (f32[25,8,128]{2,1,0:T(8,128)S(1)}, f32[25,8,128]{2,1,0:T(8,128)S(1)}, u32[]{:S(2)}, u32[]{:S(2)}) collective-permute-start(f32[25,8,128]{2,1,0:T(8,128)S(1)} %get-tuple-element.24), channel_id=1, source_target_pairs={{0,4},{4,0},{8,12},{12,8},{16,20},{20,16},{24,28},{28,24},{1,5},{5... | collective-permute-start | bytes 307208 | tf_op jit(solution)/shard_map/ppermute | solution.py:467
  5.1 8.5 %collective-permute-start.1 = (f32[25,8,128]{2,1,0:T(8,128)S(1)}, f32[25,8,128]{2,1,0:T(8,128)S(1)}, u32[]{:S(2)}, u32[]{:S(2)}) collective-permute-start(f32[25,8,128]{2,1,0:T(8,128)S(1)} %get-tuple-element.25), channel_id=1, source_target_pairs={{4,8},{8,4},{12,16},{16,12},{20,24},{24,20},{5,9},{9,5},{13,17},{1... | collective-permute-start | bytes 307208 | tf_op jit(solution)/shard_map/ppermute | solution.py:467
  5.8 14.3 %collective-permute-start.3 = (f32[25,8,128]{2,1,0:T(8,128)S(1)}, f32[25,8,128]{2,1,0:T(8,128)S(1)}, u32[]{:S(2)}, u32[]{:S(2)}) collective-permute-start(f32[25,8,128]{2,1,0:T(8,128)S(1)} %get-tuple-element.25), channel_id=1, source_target_pairs={{0,4},{4,0},{8,12},{12,8},{16,20},{20,16},{24,28},{28,24},{1,5},{5... | collective-permute-start | bytes 307208 | tf_op jit(solution)/shard_map/ppermute | solution.py:467
  10.1 9.9 %collective-permute-start.2 = (f32[25,8,128]{2,1,0:T(8,128)S(1)}, f32[25,8,128]{2,1,0:T(8,128)S(1)}, u32[]{:S(2)}, u32[]{:S(2)}) collective-permute-start(f32[25,8,128]{2,1,0:T(8,128)S(1)} %collective-permute-done.near_ref), channel_id=1, source_target_pairs={{0,8},{8,16},{12,4},{16,24},{20,12},{28,20},{1,9},{9,17},{13,5},{1... | collective-permute-start | bytes 307208 | tf_op jit(solution)/shard_map/ppermute | solution.py:473
  13.7 6.4 %collective-permute-start.4 = (f32[5,4,1024]{2,1,0:T(4,128)S(1)}, f32[5,4,1024]{2,1,0:T(4,128)S(1)}, u32[]{:S(2)}, u32[]{:S(2)}) collective-permute-start(f32[5,4,1024]{2,1,0:T(4,128)S(1)} %get-tuple-element.37), channel_id=1, source_target_pairs={{1,2},{2,1},{5,6},{6,5},{9,10},{10,9},{13,14},{14,13},{17,18},{18,... | collective-permute-start | bytes 245768 | tf_op jit(solution)/shard_map/ppermute | solution.py:467
  14.4 5.8 %collective-permute-start.5 = (f32[5,4,1024]{2,1,0:T(4,128)S(1)}, f32[5,4,1024]{2,1,0:T(4,128)S(1)}, u32[]{:S(2)}, u32[]{:S(2)}) collective-permute-start(f32[5,4,1024]{2,1,0:T(4,128)S(1)} %get-tuple-element.38), channel_id=1, source_target_pairs={{0,1},{1,0},{2,3},{3,2},{4,5},{5,4},{6,7},{7,6},{8,9},{9,8},{10,11... | collective-permute-start | bytes 245768 | tf_op jit(solution)/shard_map/ppermute | solution.py:467

commit v25 on v24

--- a/solution.py
+++ b/solution.py
@@ -200,13 +200,16 @@
         for a in range(angles):
             note = jnp.where(lane == a, masks[a][r * traces : (r + 1) * traces], note)
         notes.append(note)
-    edges = [
-        [*[b_ref[c, r, :, pl.ds(k * LANES, LANES)] for c in range(contrasts) for k in range(n)], note]
-        for r, note in zip((0, rows - 1), notes)
-    ]
-    for e, (top, bottom) in enumerate(zip(*edges)):
-        near_ref[e] = jnp.where(first, bottom, top)
-        far_ref[e] = jnp.where(first, top, bottom)
+
+    @pl.loop(0, contrasts)
+    def _(c):
+        for k in range(n):
+            top, bottom = (b_ref[c, r, :, pl.ds(k * LANES, LANES)] for r in (0, rows - 1))
+            near_ref[c * n + k] = jnp.where(first, bottom, top)
+            far_ref[c * n + k] = jnp.where(first, top, bottom)
+
+    near_ref[contrasts * n] = jnp.where(first, notes[1], notes[0])
+    far_ref[contrasts * n] = jnp.where(first, notes[0], notes[1])
 
 
 def either_side(pair_ref, next_ref, *where):
@@ -421,9 +424,7 @@
     gram_ref[...] = jnp.broadcast_to(packed[None], gram_ref.shape)
 
 
-def finish_kernel(
-    gram_ref, b_ref, one_ref, two_ref, solution_hbm, residual_hbm, solution_ref, residual_ref, sems
-):
+def finish_kernel(gram_ref, b_ref, one_ref, two_ref, solution_ref, residual_ref):
     sums = jnp.sum(gram_ref[...], axis=0)
     g00, g01, g11, g12 = (sums[:, q : q + 1] for q in range(4))
     first = g00 / g01
@@ -431,30 +432,27 @@
     second = (ratio - 1.0) * g01 / (first * g12 - ratio * g11)
     near = first + second * ratio
     far = first * second
-    blocks = [(c, r) for c in range(b_ref.shape[0]) for r in range(b_ref.shape[1])]
-    for block in blocks:
-        solution_ref[block] = near * b_ref[block] - far * one_ref[block]
-    done = pltpu.make_async_copy(solution_ref, solution_hbm, sems.at[0])
-    done.start()
-    for block in blocks:
-        residual_ref[block] = b_ref[block] - near * one_ref[block] + far * two_ref[block]
-    last = pltpu.make_async_copy(residual_ref, residual_hbm, sems.at[1])
-    last.start()
-    done.wait()
-    last.wait()
+    rows = b_ref.shape[1]
+
+    @pl.loop(0, b_ref.shape[0] * rows)
+    def _(i):
+        block = (i // rows, i % rows)
+        b, one, two = b_ref[block], one_ref[block], two_ref[block]
+        solution_ref[block] = near * b - far * one
+        residual_ref[block] = b - near * one + far * two
 
 
 VMEM = pl.BlockSpec(memory_space=pltpu.VMEM)
 HBM = pl.BlockSpec(memory_space=pltpu.HBM)
 
 
-def call(kernel, outs, ins, flops, scratch=(), places=None, to=VMEM):
+def call(kernel, outs, ins, flops, scratch=(), places=None):
     moved = sum(x.size * x.dtype.itemsize for x in (*ins, *outs))
     return pl.pallas_call(
         kernel,
         out_shape=outs,
         in_specs=[VMEM] * len(ins) if places is None else places,
-        out_specs=jax.tree.map(lambda _: to, outs),
+        out_specs=jax.tree.map(lambda _: VMEM, outs),
         scratch_shapes=list(scratch),
         compiler_params=pltpu.CompilerParams(vmem_limit_bytes=24 * 1024 * 1024),
         cost_estimate=pl.CostEstimate(flops=flops, bytes_accessed=moved, transcendentals=0),
@@ -540,11 +538,7 @@
         work,
     )
     gram = lax.all_to_all(gram, axes, 0, 0)
-    work = 8 * field.size
-    room = [pltpu.VMEM(field.shape, F32)] * 2 + [pltpu.SemaphoreType.DMA((2,))]
-    return tuple(
-        call(finish_kernel, (field, field), (gram, b, one, two), work, room, to=HBM)
-    )
+    return tuple(call(finish_kernel, (field, field), (gram, b, one, two), 8 * field.size))
 
 
 def solution(mesh):

time: 32.5 us -> 32.7 us (level)
  no operation moved by 1% of the time
where the time goes in v25:
time: 32.7 us; the launch traced here: 32.5 us
  starting transfers between devices  15.1 us (46%)
  blocking collectives  10.2 us (31%)
  Pallas kernels  6.44 us (20%)
  between operations  0.72 us (2%)
    ppermute x5, starting transfers between devices, swap(): lax.ppermute(value, axis, [(i + d, i + 1 - d) for i in starts for d in (0...  11.6 us
    all_to_all x1, blocking collectives, shards(): gram = lax.all_to_all(gram, axes, 0, 0)  10.2 us
    pallas_call x6, Pallas kernels, call(): pl.pallas_call(kernel, out_shape=outs, in_specs=[VMEM] * len(ins) if plac...  6.44 us
    ppermute x1, starting transfers between devices, hand_on(): lax.ppermute(value, axis, [(i, j) for i, j in steps if 0 <= j < size])  3.48 us
  transfers between devices with their start and end apart: 6, of which 0 were waited for; matrix products, arithmetic and copies ran while one was open for 0% of the time, Pallas kernels for 9%

profile of v25, /device:TPU:0, one launch (start us, length us, event | category | flops | bytes accessed | tf_op | source)
XLA Modules:
  0.0 32.5 jit_solution(8602975281581224067)
XLA Ops:
  0.6 1.5 %start_kernel.1 = (f32[3,2,8,1024]{3,2,1,0:T(8,128)S(1)}, f32[25,8,128]{2,1,0:T(8,128)S(1)}, f32[25,8,128]{2,1,0:T(8,128)S(1)}, f32[8,256]{1,0:T(8,128)S(1)}, s3...) custom-call(bf16[4,2,8,1024]{3,2,1,0:T(8,128)(2,1)} %seis_hbm.1, s32[4,2,8]{2,1,0:T(2,128)} %valid_hbm.1, ...), custom_call_target="tpu_custom_call" | custom-call | flops 134217728 | bytes 641680 | tf_op jit(solution)/shard_map/start_kernel/pallas_call | solution.py:451
  2.1 3.0 %collective-permute-start = (f32[25,8,128]{2,1,0:T(8,128)S(1)}, f32[25,8,128]{2,1,0:T(8,128)S(1)}, u32[]{:S(2)}, u32[]{:S(2)}) collective-permute-start(f32[25,8,128]{2,1,0:T(8,128)S(1)} %get-tuple-element.24), channel_id=1, source_target_pairs={{0,4},{4,0},{8,12},{12,8},{16,20},{20,16},{24,28},{28,24},{1,5},{5... | collective-permute-start | bytes 307208 | tf_op jit(solution)/shard_map/ppermute | solution.py:465
  5.1 0.7 %collective-permute-start.1 = (f32[25,8,128]{2,1,0:T(8,128)S(1)}, f32[25,8,128]{2,1,0:T(8,128)S(1)}, u32[]{:S(2)}, u32[]{:S(2)}) collective-permute-start(f32[25,8,128]{2,1,0:T(8,128)S(1)} %get-tuple-element.25), channel_id=1, source_target_pairs={{4,8},{8,4},{12,16},{16,12},{20,24},{24,20},{5,9},{9,5},{13,17},{1... | collective-permute-start | bytes 307208 | tf_op jit(solution)/shard_map/ppermute | solution.py:465
  5.8 4.3 %collective-permute-start.3 = (f32[25,8,128]{2,1,0:T(8,128)S(1)}, f32[25,8,128]{2,1,0:T(8,128)S(1)}, u32[]{:S(2)}, u32[]{:S(2)}) collective-permute-start(f32[25,8,128]{2,1,0:T(8,128)S(1)} %get-tuple-element.25), channel_id=1, source_target_pairs={{0,4},{4,0},{8,12},{12,8},{16,20},{20,16},{24,28},{28,24},{1,5},{5... | collective-permute-start | bytes 307208 | tf_op jit(solution)/shard_map/ppermute | solution.py:465
  10.1 0.0 collective-permute-done.near_ref
  10.1 3.5 %collective-permute-start.2 = (f32[25,8,128]{2,1,0:T(8,128)S(1)}, f32[25,8,128]{2,1,0:T(8,128)S(1)}, u32[]{:S(2)}, u32[]{:S(2)}) collective-permute-start(f32[25,8,128]{2,1,0:T(8,128)S(1)} %collective-permute-done.near_ref), channel_id=1, source_target_pairs={{0,8},{8,16},{12,4},{16,24},{20,12},{28,20},{1,9},{9,17},{13,5},{1... | collective-permute-start | bytes 307208 | tf_op jit(solution)/shard_map/ppermute | solution.py:471
  13.6 0.0 collective-permute-done.1.near_next_ref
  13.6 0.1 column_kernel.1
  13.8 0.7 %collective-permute-start.4 = (f32[5,4,1024]{2,1,0:T(4,128)S(1)}, f32[5,4,1024]{2,1,0:T(4,128)S(1)}, u32[]{:S(2)}, u32[]{:S(2)}) collective-permute-start(f32[5,4,1024]{2,1,0:T(4,128)S(1)} %get-tuple-element.37), channel_id=1, source_target_pairs={{1,2},{2,1},{5,6},{6,5},{9,10},{10,9},{13,14},{14,13},{17,18},{18,... | collective-permute-start | bytes 245768 | tf_op jit(solution)/shard_map/ppermute | solution.py:465
  14.4 2.9 %collective-permute-start.5 = (f32[5,4,1024]{2,1,0:T(4,128)S(1)}, f32[5,4,1024]{2,1,0:T(4,128)S(1)}, u32[]{:S(2)}, u32[]{:S(2)}) collective-permute-start(f32[5,4,1024]{2,1,0:T(4,128)S(1)} %get-tuple-element.38), channel_id=1, source_target_pairs={{0,1},{1,0},{2,3},{3,2},{4,5},{5,4},{6,7},{7,6},{8,9},{9,8},{10,11... | collective-permute-start | bytes 245768 | tf_op jit(solution)/shard_map/ppermute | solution.py:465
  17.4 2.7 %inner_kernel.1 = (f32[3,2,8,1024]{3,2,1,0:T(8,128)S(1)}, f32[3,2,8,1024]{3,2,1,0:T(8,128)S(1)}, f32[2,3,8,1024]{3,2,1,0:T(8,128)S(1)}, f32[4,256,256]{2,1,0:T(8...) custom-call(f32[1,3]{1,0:T(1,128)} %bitcast.3, ...), custom_call_target="tpu_custom_call" | custom-call | flops 805306368 | bytes 3150168 | tf_op jit(solution)/shard_map/inner_kernel/pallas_call | solution.py:451
  20.0 0.0 collective-permute-done.3.far_ref
  20.1 0.0 collective-permute-done.2.far_next_ref
  20.1 0.1 halo_kernel.1.halo_ref
  20.2 0.0 collective-permute-done.4.other_ref
  20.2 0.0 collective-permute-done.5.pair_ref
  20.2 0.9 %image_kernel.1 = (f32[3,2,8,1024]{3,2,1,0:T(8,128)S(1)}, f32[3,2,8,1024]{3,2,1,0:T(8,128)S(1)}, f32[32,1,128]{2,1,0:T(1,128)S(1)}) custom-call(f32[3,2,8,1024]{3,2,1,0:T(8,128)S(1)} %get-tuple-element.23.b_ref, f32[3,2,8,1024]{3,2,1,0:T(8,128)S(1)} %get-tuple-element.30.v_ref, f32[3,2,8,1024]{3,2,1,0:T(8,128)S(1)} %get-tuple-element.31.data_ref, ...), custom_call_target="tpu_custom_call" | custom-call | flops 134217728 | bytes 3612748 | tf_op jit(solution)/shard_map/image_kernel/pallas_call | solution.py:451
  21.1 10.2 %all_to_all.5.gram_ref = f32[32,1,128]{2,1,0:T(1,128)S(1)} all-to-all(f32[32,1,128]{2,1,0:T(1,128)S(1)} %get-tuple-element.41), channel_id=1, replica_groups=mesh['inline'=8,'col'=4] {'inline','col'}, dimensions={0} | all-to-all | bytes 32768 | tf_op jit(solution)/shard_map/all_to_all | solution.py:540
  31.3 1.1 %finish_kernel.1 = (f32[3,2,8,1024]{3,2,1,0:T(8,128)}, f32[3,2,8,1024]{3,2,1,0:T(8,128)}) custom-call(f32[32,1,128]{2,1,0:T(1,128)S(1)} %all_to_all.5.gram_ref, f32[3,2,8,1024]{3,2,1,0:T(8,128)S(1)} %get-tuple-element.23.b_ref, f32[3,2,8,1024]{3,2,1,0:T(8,128)S(1)} %get-tuple-element.42.one_ref, f32[3,2,8,1024]{3,2,1,0:T(8,128)S(1)} %get-tuple-element.43.two_ref), custom_call_target="tpu_custom_call" | custom-call | flops 393216 | bytes 999424 | tf_op jit(solution)/shard_map/finish_kernel/pallas_call | solution.py:451
Async XLA Ops:
  2.1 8.0 %collective-permute-start = (f32[25,8,128]{2,1,0:T(8,128)S(1)}, f32[25,8,128]{2,1,0:T(8,128)S(1)}, u32[]{:S(2)}, u32[]{:S(2)}) collective-permute-start(f32[25,8,128]{2,1,0:T(8,128)S(1)} %get-tuple-element.24), channel_id=1, source_target_pairs={{0,4},{4,0},{8,12},{12,8},{16,20},{20,16},{24,28},{28,24},{1,5},{5... | collective-permute-start | bytes 307208 | tf_op jit(solution)/shard_map/ppermute | solution.py:465
  5.1 8.5 %collective-permute-start.1 = (f32[25,8,128]{2,1,0:T(8,128)S(1)}, f32[25,8,128]{2,1,0:T(8,128)S(1)}, u32[]{:S(2)}, u32[]{:S(2)}) collective-permute-start(f32[25,8,128]{2,1,0:T(8,128)S(1)} %get-tuple-element.25), channel_id=1, source_target_pairs={{4,8},{8,4},{12,16},{16,12},{20,24},{24,20},{5,9},{9,5},{13,17},{1... | collective-permute-start | bytes 307208 | tf_op jit(solution)/shard_map/ppermute | solution.py:465
  5.8 14.3 %collective-permute-start.3 = (f32[25,8,128]{2,1,0:T(8,128)S(1)}, f32[25,8,128]{2,1,0:T(8,128)S(1)}, u32[]{:S(2)}, u32[]{:S(2)}) collective-permute-start(f32[25,8,128]{2,1,0:T(8,128)S(1)} %get-tuple-element.25), channel_id=1, source_target_pairs={{0,4},{4,0},{8,12},{12,8},{16,20},{20,16},{24,28},{28,24},{1,5},{5... | collective-permute-start | bytes 307208 | tf_op jit(solution)/shard_map/ppermute | solution.py:465
  10.1 9.9 %collective-permute-start.2 = (f32[25,8,128]{2,1,0:T(8,128)S(1)}, f32[25,8,128]{2,1,0:T(8,128)S(1)}, u32[]{:S(2)}, u32[]{:S(2)}) collective-permute-start(f32[25,8,128]{2,1,0:T(8,128)S(1)} %collective-permute-done.near_ref), channel_id=1, source_target_pairs={{0,8},{8,16},{12,4},{16,24},{20,12},{28,20},{1,9},{9,17},{13,5},{1... | collective-permute-start | bytes 307208 | tf_op jit(solution)/shard_map/ppermute | solution.py:471
  13.8 6.4 %collective-permute-start.4 = (f32[5,4,1024]{2,1,0:T(4,128)S(1)}, f32[5,4,1024]{2,1,0:T(4,128)S(1)}, u32[]{:S(2)}, u32[]{:S(2)}) collective-permute-start(f32[5,4,1024]{2,1,0:T(4,128)S(1)} %get-tuple-element.37), channel_id=1, source_target_pairs={{1,2},{2,1},{5,6},{6,5},{9,10},{10,9},{13,14},{14,13},{17,18},{18,... | collective-permute-start | bytes 245768 | tf_op jit(solution)/shard_map/ppermute | solution.py:465
  14.4 5.8 %collective-permute-start.5 = (f32[5,4,1024]{2,1,0:T(4,128)S(1)}, f32[5,4,1024]{2,1,0:T(4,128)S(1)}, u32[]{:S(2)}, u32[]{:S(2)}) collective-permute-start(f32[5,4,1024]{2,1,0:T(4,128)S(1)} %get-tuple-element.38), channel_id=1, source_target_pairs={{0,1},{1,0},{2,3},{3,2},{4,5},{5,4},{6,7},{7,6},{8,9},{9,8},{10,11... | collective-permute-start | bytes 245768 | tf_op jit(solution)/shard_map/ppermute | solution.py:465

commit v26 on v23

--- a/solution.py
+++ b/solution.py
@@ -42,6 +42,7 @@
 
 
 def convolve(rows, bands):
+    rows = rows.astype(BF16)
     out = lax.dot_general(rows, bands, (((1,), (1,)), ((), ())), preferred_element_type=F32)
     return out[:, :LANES] + out[:, LANES:]
 
@@ -57,18 +58,28 @@
     return jnp.concatenate([column(rows[r : r + 1, :]) for r in range(rows.shape[0])], axis=0)
 
 
+def thirds(value):
+    kind = BF16 if value.shape[0] % 16 == 0 else F32
+    parts = []
+    for _ in range(3):
+        high = value.astype(BF16)
+        parts.append(high.astype(kind))
+        value = value - high.astype(F32)
+    return parts
+
+
 def windows(tiles):
     pairs = [jnp.concatenate(pair, axis=1) for pair in zip(tiles[:-1], tiles[1:])]
     return jnp.concatenate(pairs, axis=0)
 
 
 def forward(tiles, bands):
-    zero = jnp.zeros_like(tiles[0]).astype(BF16)
-    highs, lows = zip(*[split(t) for t in tiles])
+    parts = list(zip(*[thirds(t) for t in tiles]))
+    zero = jnp.zeros_like(parts[0][0])
     n, size = len(tiles) + 1, tiles[0].shape[0]
-    rows = [windows([zero, *part, zero]) for part in (highs, lows)]
+    rows = [windows([zero, *part, zero]) for part in parts]
     out = convolve(jnp.concatenate(rows, axis=0), bands)
-    out = out[: n * size] + out[n * size :]
+    out = out[: n * size] + (out[n * size : 2 * n * size] + out[2 * n * size :])
     return [out[k * size : (k + 1) * size] for k in range(n)]
 
 
@@ -133,7 +144,7 @@
         left_half = lax.broadcasted_iota(jnp.int32, synth[0].shape, 1) < LANES // 2
         synth[0] = jnp.where(left_half, 0.0, synth[0])
         synth[n] = jnp.where(left_half, synth[n], 0.0)
-        result = backward(list(zip(*[split(t) for t in synth])), back)
+        result = backward(list(zip(*[thirds(t) for t in synth])), back)
         add_terms(total, avo_ref, a, result)
     return total
 

time: 32.5 us -> 33.3 us (1.025)
  Pallas kernels: 6.25 us -> 7.29 us
    pallas_call x6, Pallas kernels: 6.25 us -> 7.29 us  [call(): pl.pallas_call(kernel, out_shape=outs, in_specs=[VMEM] * len(ins) if plac...]
  transfers between devices with their start and end apart: 6 -> 6, of which waited for: 0 -> 0; matrix products, arithmetic and copies ran while one was open for 0% -> 0% of each run, Pallas kernels for 9% -> 12%
where the time goes in v26:
time: 33.3 us; the launch traced here: 33 us
  starting transfers between devices  15.1 us (45%)
  blocking collectives  9.92 us (30%)
  Pallas kernels  7.29 us (22%)
  between operations  0.72 us (2%)
    ppermute x5, starting transfers between devices, swap(): lax.ppermute(value, axis, [(i + d, i + 1 - d) for i in starts for d in (0...  11.6 us
    all_to_all x1, blocking collectives, shards(): gram = lax.all_to_all(gram, axes, 0, 0)  9.92 us
    pallas_call x6, Pallas kernels, call(): pl.pallas_call(kernel, out_shape=outs, in_specs=[VMEM] * len(ins) if plac...  7.29 us
    ppermute x1, starting transfers between devices, hand_on(): lax.ppermute(value, axis, [(i, j) for i, j in steps if 0 <= j < size])  3.48 us
  transfers between devices with their start and end apart: 6, of which 0 were waited for; matrix products, arithmetic and copies ran while one was open for 0% of the time, Pallas kernels for 12%

profile of v26, /device:TPU:0, one launch (start us, length us, event | category | flops | bytes accessed | tf_op | source)
XLA Modules:
  0.0 33.0 jit_solution(7261445683948759293)
XLA Ops:
  0.6 1.5 %start_kernel.1 = (f32[3,2,8,1024]{3,2,1,0:T(8,128)S(1)}, f32[25,8,128]{2,1,0:T(8,128)S(1)}, f32[25,8,128]{2,1,0:T(8,128)S(1)}, f32[8,256]{1,0:T(8,128)S(1)}, s3...) custom-call(bf16[4,2,8,1024]{3,2,1,0:T(8,128)(2,1)} %seis_hbm.1, s32[4,2,8]{2,1,0:T(2,128)} %valid_hbm.1, ...), custom_call_target="tpu_custom_call" | custom-call | flops 134217728 | bytes 641680 | tf_op jit(solution)/shard_map/start_kernel/pallas_call | solution.py:456
  2.1 3.0 %collective-permute-start = (f32[25,8,128]{2,1,0:T(8,128)S(1)}, f32[25,8,128]{2,1,0:T(8,128)S(1)}, u32[]{:S(2)}, u32[]{:S(2)}) collective-permute-start(f32[25,8,128]{2,1,0:T(8,128)S(1)} %get-tuple-element.24), channel_id=1, source_target_pairs={{0,4},{4,0},{8,12},{12,8},{16,20},{20,16},{24,28},{28,24},{1,5},{5... | collective-permute-start | bytes 307208 | tf_op jit(solution)/shard_map/ppermute | solution.py:470
  5.1 0.7 %collective-permute-start.1 = (f32[25,8,128]{2,1,0:T(8,128)S(1)}, f32[25,8,128]{2,1,0:T(8,128)S(1)}, u32[]{:S(2)}, u32[]{:S(2)}) collective-permute-start(f32[25,8,128]{2,1,0:T(8,128)S(1)} %get-tuple-element.25), channel_id=1, source_target_pairs={{4,8},{8,4},{12,16},{16,12},{20,24},{24,20},{5,9},{9,5},{13,17},{1... | collective-permute-start | bytes 307208 | tf_op jit(solution)/shard_map/ppermute | solution.py:470
  5.8 4.3 %collective-permute-start.3 = (f32[25,8,128]{2,1,0:T(8,128)S(1)}, f32[25,8,128]{2,1,0:T(8,128)S(1)}, u32[]{:S(2)}, u32[]{:S(2)}) collective-permute-start(f32[25,8,128]{2,1,0:T(8,128)S(1)} %get-tuple-element.25), channel_id=1, source_target_pairs={{0,4},{4,0},{8,12},{12,8},{16,20},{20,16},{24,28},{28,24},{1,5},{5... | collective-permute-start | bytes 307208 | tf_op jit(solution)/shard_map/ppermute | solution.py:470
  10.1 0.0 collective-permute-done.near_ref
  10.1 3.5 %collective-permute-start.2 = (f32[25,8,128]{2,1,0:T(8,128)S(1)}, f32[25,8,128]{2,1,0:T(8,128)S(1)}, u32[]{:S(2)}, u32[]{:S(2)}) collective-permute-start(f32[25,8,128]{2,1,0:T(8,128)S(1)} %collective-permute-done.near_ref), channel_id=1, source_target_pairs={{0,8},{8,16},{12,4},{16,24},{20,12},{28,20},{1,9},{9,17},{13,5},{1... | collective-permute-start | bytes 307208 | tf_op jit(solution)/shard_map/ppermute | solution.py:476
  13.6 0.0 collective-permute-done.1.near_next_ref
  13.6 0.1 column_kernel.1
  13.7 0.7 %collective-permute-start.4 = (f32[5,4,1024]{2,1,0:T(4,128)S(1)}, f32[5,4,1024]{2,1,0:T(4,128)S(1)}, u32[]{:S(2)}, u32[]{:S(2)}) collective-permute-start(f32[5,4,1024]{2,1,0:T(4,128)S(1)} %get-tuple-element.37), channel_id=1, source_target_pairs={{1,2},{2,1},{5,6},{6,5},{9,10},{10,9},{13,14},{14,13},{17,18},{18,... | collective-permute-start | bytes 245768 | tf_op jit(solution)/shard_map/ppermute | solution.py:470
  14.4 2.9 %collective-permute-start.5 = (f32[5,4,1024]{2,1,0:T(4,128)S(1)}, f32[5,4,1024]{2,1,0:T(4,128)S(1)}, u32[]{:S(2)}, u32[]{:S(2)}) collective-permute-start(f32[5,4,1024]{2,1,0:T(4,128)S(1)} %get-tuple-element.38), channel_id=1, source_target_pairs={{0,1},{1,0},{2,3},{3,2},{4,5},{5,4},{6,7},{7,6},{8,9},{9,8},{10,11... | collective-permute-start | bytes 245768 | tf_op jit(solution)/shard_map/ppermute | solution.py:470
  17.4 3.7 %inner_kernel.1 = (f32[3,2,8,1024]{3,2,1,0:T(8,128)S(1)}, f32[3,2,8,1024]{3,2,1,0:T(8,128)S(1)}, f32[2,3,8,1024]{3,2,1,0:T(8,128)S(1)}, f32[4,256,256]{2,1,0:T(8...) custom-call(f32[1,3]{1,0:T(1,128)} %bitcast.3, ...), custom_call_target="tpu_custom_call" | custom-call | flops 805306368 | bytes 3150168 | tf_op jit(solution)/shard_map/inner_kernel/pallas_call | solution.py:456
  21.1 0.0 collective-permute-done.3.far_ref
  21.1 0.0 collective-permute-done.2.far_next_ref
  21.1 0.1 halo_kernel.1.halo_ref
  21.2 0.0 collective-permute-done.4.other_ref
  21.2 0.0 collective-permute-done.5.pair_ref
  21.2 1.0 %image_kernel.1 = (f32[3,2,8,1024]{3,2,1,0:T(8,128)S(1)}, f32[3,2,8,1024]{3,2,1,0:T(8,128)S(1)}, f32[32,1,128]{2,1,0:T(1,128)S(1)}) custom-call(f32[3,2,8,1024]{3,2,1,0:T(8,128)S(1)} %get-tuple-element.23.b_ref, f32[3,2,8,1024]{3,2,1,0:T(8,128)S(1)} %get-tuple-element.30.v_ref, f32[3,2,8,1024]{3,2,1,0:T(8,128)S(1)} %get-tuple-element.31.data_ref, ...), custom_call_target="tpu_custom_call" | custom-call | flops 134217728 | bytes 3612748 | tf_op jit(solution)/shard_map/image_kernel/pallas_call | solution.py:456
  22.2 9.9 %all_to_all.5.gram_ref = f32[32,1,128]{2,1,0:T(1,128)S(1)} all-to-all(f32[32,1,128]{2,1,0:T(1,128)S(1)} %get-tuple-element.41), channel_id=1, replica_groups=mesh['inline'=8,'col'=4] {'inline','col'}, dimensions={0} | all-to-all | bytes 32768 | tf_op jit(solution)/shard_map/all_to_all | solution.py:545
  32.1 0.9 %finish_kernel.1 = (f32[3,2,8,1024]{3,2,1,0:T(8,128)}, f32[3,2,8,1024]{3,2,1,0:T(8,128)}) custom-call(f32[32,1,128]{2,1,0:T(1,128)S(1)} %all_to_all.5.gram_ref, f32[3,2,8,1024]{3,2,1,0:T(8,128)S(1)} %get-tuple-element.23.b_ref, f32[3,2,8,1024]{3,2,1,0:T(8,128)S(1)} %get-tuple-element.42.one_ref, f32[3,2,8,1024]{3,2,1,0:T(8,128)S(1)} %get-tuple-element.43.two_ref), custom_call_target="tpu_custom_call" | custom-call | flops 393216 | bytes 999424 | tf_op jit(solution)/shard_map/finish_kernel/pallas_call | solution.py:456
Async XLA Ops:
  2.1 8.0 %collective-permute-start = (f32[25,8,128]{2,1,0:T(8,128)S(1)}, f32[25,8,128]{2,1,0:T(8,128)S(1)}, u32[]{:S(2)}, u32[]{:S(2)}) collective-permute-start(f32[25,8,128]{2,1,0:T(8,128)S(1)} %get-tuple-element.24), channel_id=1, source_target_pairs={{0,4},{4,0},{8,12},{12,8},{16,20},{20,16},{24,28},{28,24},{1,5},{5... | collective-permute-start | bytes 307208 | tf_op jit(solution)/shard_map/ppermute | solution.py:470
  5.1 8.5 %collective-permute-start.1 = (f32[25,8,128]{2,1,0:T(8,128)S(1)}, f32[25,8,128]{2,1,0:T(8,128)S(1)}, u32[]{:S(2)}, u32[]{:S(2)}) collective-permute-start(f32[25,8,128]{2,1,0:T(8,128)S(1)} %get-tuple-element.25), channel_id=1, source_target_pairs={{4,8},{8,4},{12,16},{16,12},{20,24},{24,20},{5,9},{9,5},{13,17},{1... | collective-permute-start | bytes 307208 | tf_op jit(solution)/shard_map/ppermute | solution.py:470
  5.8 15.3 %collective-permute-start.3 = (f32[25,8,128]{2,1,0:T(8,128)S(1)}, f32[25,8,128]{2,1,0:T(8,128)S(1)}, u32[]{:S(2)}, u32[]{:S(2)}) collective-permute-start(f32[25,8,128]{2,1,0:T(8,128)S(1)} %get-tuple-element.25), channel_id=1, source_target_pairs={{0,4},{4,0},{8,12},{12,8},{16,20},{20,16},{24,28},{28,24},{1,5},{5... | collective-permute-start | bytes 307208 | tf_op jit(solution)/shard_map/ppermute | solution.py:470
  10.1 11.0 %collective-permute-start.2 = (f32[25,8,128]{2,1,0:T(8,128)S(1)}, f32[25,8,128]{2,1,0:T(8,128)S(1)}, u32[]{:S(2)}, u32[]{:S(2)}) collective-permute-start(f32[25,8,128]{2,1,0:T(8,128)S(1)} %collective-permute-done.near_ref), channel_id=1, source_target_pairs={{0,8},{8,16},{12,4},{16,24},{20,12},{28,20},{1,9},{9,17},{13,5},{1... | collective-permute-start | bytes 307208 | tf_op jit(solution)/shard_map/ppermute | solution.py:476
  13.7 7.4 %collective-permute-start.4 = (f32[5,4,1024]{2,1,0:T(4,128)S(1)}, f32[5,4,1024]{2,1,0:T(4,128)S(1)}, u32[]{:S(2)}, u32[]{:S(2)}) collective-permute-start(f32[5,4,1024]{2,1,0:T(4,128)S(1)} %get-tuple-element.37), channel_id=1, source_target_pairs={{1,2},{2,1},{5,6},{6,5},{9,10},{10,9},{13,14},{14,13},{17,18},{18,... | collective-permute-start | bytes 245768 | tf_op jit(solution)/shard_map/ppermute | solution.py:470
  14.4 6.8 %collective-permute-start.5 = (f32[5,4,1024]{2,1,0:T(4,128)S(1)}, f32[5,4,1024]{2,1,0:T(4,128)S(1)}, u32[]{:S(2)}, u32[]{:S(2)}) collective-permute-start(f32[5,4,1024]{2,1,0:T(4,128)S(1)} %get-tuple-element.38), channel_id=1, source_target_pairs={{0,1},{1,0},{2,3},{3,2},{4,5},{5,4},{6,7},{7,6},{8,9},{9,8},{10,11... | collective-permute-start | bytes 245768 | tf_op jit(solution)/shard_map/ppermute | solution.py:470

commit v27 on v26

--- a/solution.py
+++ b/solution.py
@@ -245,7 +245,7 @@
 
 
 def column_kernel(
-    b_ref, near_ref, near_next_ref, valid_ref, prior_ref,
+    b_ref, near_ref, near_next_ref, valid_ref, prior_ref, _,
     pair_ref, other_ref, own_ref, note_ref, second_ref,
 ):
     contrasts, rows, traces, samples = b_ref.shape
@@ -283,12 +283,12 @@
         other_ref[contrasts + i] = jnp.where(first_col, left, right)
 
 
-def inner_kernel(
-    count, strength_hbm, b_ref, near_ref, near_next_ref, padded_ref, valid_ref, avo_ref, prior_ref,
-    v_ref, data_ref, halo_ref, ahead_ref, back_ref, norm_ref, strength_ref, sem,
+def data_kernel(
+    count, strength_hbm, b_ref, padded_ref, valid_ref, avo_ref,
+    data_ref, ahead_ref, back_ref, norm_ref, strength_ref, sem,
 ):
-    contrasts, rows, traces, samples = b_ref.shape
-    angles, n = avo_ref.shape[1], samples // LANES
+    contrasts, rows = b_ref.shape[:2]
+    angles = avo_ref.shape[1]
     (copy,) = copy_in(((strength_hbm, strength_ref),), sem)
     turned = turn(padded_ref[...], count)
     bands = []
@@ -296,43 +296,52 @@
         bands.append((band(turned[a : a + 1]), band(padded_ref[a : a + 1, :])))
         ahead_ref[a], back_ref[a] = (half.astype(F32) for half in bands[a])
     masks = [trace_columns(valid_ref, a) for a in range(angles)]
-    weights = [column(prior_ref[r : r + 1, :]) + 4.0 for r in range(rows)]
-    above, below = either_side(near_ref, near_next_ref, contrasts * n)
-    wide = [
-        jnp.concatenate([above[:, a : a + 1], mask, below[:, a : a + 1]], axis=0)
-        for a, mask in enumerate(masks)
-    ]
-    weights = [above[:, angles : angles + 1] + 4.0, *weights, below[:, angles : angles + 1] + 4.0]
-    field = []
-    for c, line in enumerate(stack_tiles(b_ref)):
-        ends = [either_side(near_ref, near_next_ref, c * n + k) for k in range(n)]
-        field.append(
-            [jnp.concatenate([up, own, low], axis=0) for (up, low), own in zip(ends, line)]
-        )
-    total = normal(field, wide, avo_ref, bands)
-    copy.wait()
-    has_above, has_below = inside("inline")
-    for c in range(contrasts):
-        strength = strength_ref[:, c : c + 1]
-        whole, data = jnp.concatenate(field[c], axis=1), jnp.concatenate(total[c], axis=1)
-        lines = [whole[r * traces : (r + 1) * traces] for r in range(rows + 2)]
-        for r, here in enumerate(lines):
-            north = lines[r - 1] if r else None
-            south = lines[r + 1] if r < rows + 1 else None
-            if r == 0:
-                south = has_above * south
-            if r == rows + 1:
-                north = has_below * north
-            around = lateral(here, north, south, None, None)
-            image = data[r * traces : (r + 1) * traces] + strength * (weights[r] * here - around)
-            if 0 < r <= rows:
-                v_ref[c, r - 1] = image
-            else:
-                halo_ref[min(r, 1), c] = image
-    store_tiles(data_ref, normal(stack_tiles(v_ref), masks, avo_ref, bands))
+    store_tiles(data_ref, normal(stack_tiles(b_ref), masks, avo_ref, bands))
     norm_ref[...] = functools.reduce(
         jnp.add, [lane_tiles(b_ref[c, r] * b_ref[c, r]) for c in range(contrasts) for r in range(rows)]
     )
+    copy.wait()
+
+
+def inner_kernel(
+    b_ref, first_ref, near_ref, near_next_ref, valid_ref, avo_ref, prior_ref, strength_ref,
+    ahead_ref, back_ref, v_ref, data_ref, halo_ref,
+):
+    contrasts, rows, traces, samples = b_ref.shape
+    angles, n = avo_ref.shape[1], samples // LANES
+    bands = [(ahead_ref[a].astype(BF16), back_ref[a].astype(BF16)) for a in range(angles)]
+    above, below = either_side(near_ref, near_next_ref, contrasts * n)
+    weights = [column(prior_ref[r : r + 1, :]) + 4.0 for r in range(rows)]
+    ends = [row_pair(near_ref, near_next_ref, c, n) for c in range(contrasts)]
+    for c in range(contrasts):
+        strength = strength_ref[:, c : c + 1]
+        lines = [ends[c][0], *[b_ref[c, r] for r in range(rows)], ends[c][1]]
+        for r in range(rows):
+            around = lateral(lines[r + 1], lines[r], lines[r + 2], None, None)
+            v_ref[c, r] = first_ref[c, r] + strength * (weights[r] * lines[r + 1] - around)
+    masks = [
+        jnp.concatenate([above[:, a : a + 1], trace_columns(valid_ref, a), below[:, a : a + 1]], axis=0)
+        for a in range(angles)
+    ]
+    field = [
+        [
+            jnp.concatenate([up[:, k : k + LANES], own, low[:, k : k + LANES]], axis=0)
+            for k, own in zip(range(0, samples, LANES), line)
+        ]
+        for (up, low), line in zip(ends, stack_tiles(v_ref))
+    ]
+    total = normal(field, masks, avo_ref, bands)
+    has = inside("inline")
+    for c in range(contrasts):
+        strength = strength_ref[:, c : c + 1]
+        data = jnp.concatenate(total[c], axis=1)
+        for r in range(rows):
+            data_ref[c, r] = data[(r + 1) * traces : (r + 2) * traces]
+        for i, (note, own, at) in enumerate(((above, 0, 0), (below, rows - 1, rows + 1))):
+            here = ends[c][i]
+            around = lateral(here, None, has[i] * b_ref[c, own], None, None)
+            prior = (note[:, angles : angles + 1] + 4.0) * here - around
+            halo_ref[i, c] = data[at * traces : (at + 1) * traces] + strength * prior
 
 
 def lane_tiles(product):
@@ -508,10 +517,20 @@
     near_next = swap("inline", far, 1)
     far_next = hand_on("inline", near)
     far = swap("inline", far, 0)
+    bands = shape(angles, 2 * LANES, 2 * LANES)
+    strength = lateral_strength.reshape(1, -1)
+    first, ahead, back, norm, strength = call(
+        functools.partial(data_kernel, wavelets.shape[1]),
+        (field, bands, bands, shape(traces, LANES), shape(*strength.shape)),
+        (pltpu.with_memory_space_constraint(strength, pltpu.HBM), b, padded, kept[0], kept[1]),
+        2 * work,
+        [pltpu.SemaphoreType.DMA((1,))],
+        [HBM] + [VMEM] * 4,
+    )
     col_pair, col_other, own, note = call(
         column_kernel,
         (side, side, shape(contrasts, 2 * rows + 4, samples), shape(traces, LANES)),
-        (b, near, near_next, kept[0], kept[2]),
+        (b, near, near_next, kept[0], kept[2], first),
         2 * field.size,
         [pltpu.VMEM((2, 2 * rows + 4, samples), F32)],
     )
@@ -519,17 +538,11 @@
     col_pair = swap("col", col_pair, 0)
     bands = shape(angles, 2 * LANES, 2 * LANES)
     halo = shape(2, contrasts, traces, samples)
-    strength = lateral_strength.reshape(1, -1)
-    image, data, part, ahead, back, norm, strength = call(
-        functools.partial(inner_kernel, wavelets.shape[1]),
-        (field, field, halo, bands, bands, shape(traces, LANES), shape(*strength.shape)),
-        (
-            pltpu.with_memory_space_constraint(strength, pltpu.HBM),
-            b, near, near_next, padded, *kept,
-        ),
-        6 * work,
-        [pltpu.SemaphoreType.DMA((1,))],
-        [HBM] + [VMEM] * 7,
+    image, data, part = call(
+        inner_kernel,
+        (field, field, halo),
+        (b, first, near, near_next, *kept, strength, ahead, back),
+        4 * work,
     )
     (halo,) = call(halo_kernel, (halo,), (part, far_next, far, strength), field.size)
     axes = ("inline", "col")

time: 33.3 us -> 33.3 us (level)
    pallas_call x6 -> x7, Pallas kernels: 7.29 us -> 7.25 us  [call(): pl.pallas_call(kernel, out_shape=outs, in_specs=[VMEM] * len(ins) if plac...]
where the time goes in v27:
time: 33.3 us; the launch traced here: 33.1 us
  starting transfers between devices  15.1 us (45%)
  blocking collectives  10 us (30%)
  Pallas kernels  7.25 us (22%)
  between operations  0.72 us (2%)
    ppermute x5, starting transfers between devices, swap(): lax.ppermute(value, axis, [(i + d, i + 1 - d) for i in starts for d in (0...  11.6 us
    all_to_all x1, blocking collectives, shards(): gram = lax.all_to_all(gram, axes, 0, 0)  10 us
    pallas_call x7, Pallas kernels, call(): pl.pallas_call(kernel, out_shape=outs, in_specs=[VMEM] * len(ins) if plac...  7.25 us
    ppermute x1, starting transfers between devices, hand_on(): lax.ppermute(value, axis, [(i, j) for i, j in steps if 0 <= j < size])  3.48 us
  transfers between devices with their start and end apart: 6, of which 0 were waited for; matrix products, arithmetic and copies ran while one was open for 0% of the time, Pallas kernels for 12%

profile of v27, /device:TPU:0, one launch (start us, length us, event | category | flops | bytes accessed | tf_op | source)
XLA Modules:
  0.0 33.1 jit_solution(16853516925301903674)
XLA Ops:
  0.6 1.5 %start_kernel.1 = (f32[3,2,8,1024]{3,2,1,0:T(8,128)S(1)}, f32[25,8,128]{2,1,0:T(8,128)S(1)}, f32[25,8,128]{2,1,0:T(8,128)S(1)}, f32[8,256]{1,0:T(8,128)S(1)}, s3...) custom-call(bf16[4,2,8,1024]{3,2,1,0:T(8,128)(2,1)} %seis_hbm.1, s32[4,2,8]{2,1,0:T(2,128)} %valid_hbm.1, ...), custom_call_target="tpu_custom_call" | custom-call | flops 134217728 | bytes 641680 | tf_op jit(solution)/shard_map/start_kernel/pallas_call | solution.py:465
  2.1 3.0 %collective-permute-start = (f32[25,8,128]{2,1,0:T(8,128)S(1)}, f32[25,8,128]{2,1,0:T(8,128)S(1)}, u32[]{:S(2)}, u32[]{:S(2)}) collective-permute-start(f32[25,8,128]{2,1,0:T(8,128)S(1)} %get-tuple-element.29), channel_id=1, source_target_pairs={{0,4},{4,0},{8,12},{12,8},{16,20},{20,16},{24,28},{28,24},{1,5},{5... | collective-permute-start | bytes 307208 | tf_op jit(solution)/shard_map/ppermute | solution.py:479
  5.1 0.7 %collective-permute-start.1 = (f32[25,8,128]{2,1,0:T(8,128)S(1)}, f32[25,8,128]{2,1,0:T(8,128)S(1)}, u32[]{:S(2)}, u32[]{:S(2)}) collective-permute-start(f32[25,8,128]{2,1,0:T(8,128)S(1)} %get-tuple-element.30), channel_id=1, source_target_pairs={{4,8},{8,4},{12,16},{16,12},{20,24},{24,20},{5,9},{9,5},{13,17},{1... | collective-permute-start | bytes 307208 | tf_op jit(solution)/shard_map/ppermute | solution.py:479
  5.8 4.3 %collective-permute-start.3 = (f32[25,8,128]{2,1,0:T(8,128)S(1)}, f32[25,8,128]{2,1,0:T(8,128)S(1)}, u32[]{:S(2)}, u32[]{:S(2)}) collective-permute-start(f32[25,8,128]{2,1,0:T(8,128)S(1)} %get-tuple-element.30), channel_id=1, source_target_pairs={{0,4},{4,0},{8,12},{12,8},{16,20},{20,16},{24,28},{28,24},{1,5},{5... | collective-permute-start | bytes 307208 | tf_op jit(solution)/shard_map/ppermute | solution.py:479
  10.1 0.0 collective-permute-done.near_ref
  10.1 3.5 %collective-permute-start.2 = (f32[25,8,128]{2,1,0:T(8,128)S(1)}, f32[25,8,128]{2,1,0:T(8,128)S(1)}, u32[]{:S(2)}, u32[]{:S(2)}) collective-permute-start(f32[25,8,128]{2,1,0:T(8,128)S(1)} %collective-permute-done.near_ref), channel_id=1, source_target_pairs={{0,8},{8,16},{12,4},{16,24},{20,12},{28,20},{1,9},{9,17},{13,5},{1... | collective-permute-start | bytes 307208 | tf_op jit(solution)/shard_map/ppermute | solution.py:485
  13.6 1.5 %data_kernel.1 = (f32[3,2,8,1024]{3,2,1,0:T(8,128)S(1)}, f32[4,256,256]{2,1,0:T(8,128)S(1)}, f32[4,256,256]{2,1,0:T(8,128)S(1)}, f32[8,128]{1,0:T(8,128)S(1)}, f32[1,3]{1,0:T(1,128)S(1)}) custom-call(f32[1,3]{1,0:T(1,128)} %bitcast.3, f32[3,2,8,1024]{3,2,1,0:T(8,128)S(1)} %get-tuple-element.24.b_ref, f32[8,256]{1,0:T(8,128)S(1)} %get-tuple-element.25.padded_ref, ...), custom_call_target="tpu_custom_call" | custom-call | flops 268435456 | bytes 2552088 | tf_op jit(solution)/shard_map/data_kernel/pallas_call | solution.py:465
  15.1 0.0 collective-permute-done.1.near_next_ref
  15.1 0.1 column_kernel.1
  15.2 0.7 %collective-permute-start.4 = (f32[5,4,1024]{2,1,0:T(4,128)S(1)}, f32[5,4,1024]{2,1,0:T(4,128)S(1)}, u32[]{:S(2)}, u32[]{:S(2)}) collective-permute-start(f32[5,4,1024]{2,1,0:T(4,128)S(1)} %get-tuple-element.41), channel_id=1, source_target_pairs={{1,2},{2,1},{5,6},{6,5},{9,10},{10,9},{13,14},{14,13},{17,18},{18,... | collective-permute-start | bytes 245768 | tf_op jit(solution)/shard_map/ppermute | solution.py:479
  15.9 2.9 %collective-permute-start.5 = (f32[5,4,1024]{2,1,0:T(4,128)S(1)}, f32[5,4,1024]{2,1,0:T(4,128)S(1)}, u32[]{:S(2)}, u32[]{:S(2)}) collective-permute-start(f32[5,4,1024]{2,1,0:T(4,128)S(1)} %get-tuple-element.42), channel_id=1, source_target_pairs={{0,1},{1,0},{2,3},{3,2},{4,5},{5,4},{6,7},{7,6},{8,9},{9,8},{10,11... | collective-permute-start | bytes 245768 | tf_op jit(solution)/shard_map/ppermute | solution.py:479
  18.8 2.2 %inner_kernel.1 = (f32[3,2,8,1024]{3,2,1,0:T(8,128)S(1)}, f32[3,2,8,1024]{3,2,1,0:T(8,128)S(1)}, f32[2,3,8,1024]{3,2,1,0:T(8,128)S(1)}) custom-call(f32[3,2,8,1024]{3,2,1,0:T(8,128)S(1)} %get-tuple-element.24.b_ref, f32[3,2,8,1024]{3,2,1,0:T(8,128)S(1)} %get-tuple-element.28.first_ref._, f32[25,8,128]{2,1,0:T(8,128)S(1)} %collective-permute-done.near_ref, ...), custom_call_target="tpu_custom_call" | custom-call | flops 536870912 | bytes 3334476 | tf_op jit(solution)/shard_map/inner_kernel/pallas_call | solution.py:465
  21.0 0.0 collective-permute-done.3.far_ref
  21.0 0.0 collective-permute-done.2.far_next_ref
  21.1 0.1 halo_kernel.1.halo_ref
  21.2 0.0 collective-permute-done.4.other_ref
  21.2 0.0 collective-permute-done.5.pair_ref
  21.2 1.0 %image_kernel.1 = (f32[3,2,8,1024]{3,2,1,0:T(8,128)S(1)}, f32[3,2,8,1024]{3,2,1,0:T(8,128)S(1)}, f32[32,1,128]{2,1,0:T(1,128)S(1)}) custom-call(f32[3,2,8,1024]{3,2,1,0:T(8,128)S(1)} %get-tuple-element.24.b_ref, f32[3,2,8,1024]{3,2,1,0:T(8,128)S(1)} %get-tuple-element.35.v_ref, f32[3,2,8,1024]{3,2,1,0:T(8,128)S(1)} %get-tuple-element.36.data_ref, ...), custom_call_target="tpu_custom_call" | custom-call | flops 134217728 | bytes 3612748 | tf_op jit(solution)/shard_map/image_kernel/pallas_call | solution.py:465
  22.1 10.0 %all_to_all.5.gram_ref = f32[32,1,128]{2,1,0:T(1,128)S(1)} all-to-all(f32[32,1,128]{2,1,0:T(1,128)S(1)} %get-tuple-element.43), channel_id=1, replica_groups=mesh['inline'=8,'col'=4] {'inline','col'}, dimensions={0} | all-to-all | bytes 32768 | tf_op jit(solution)/shard_map/all_to_all | solution.py:558
  32.1 0.9 %finish_kernel.1 = (f32[3,2,8,1024]{3,2,1,0:T(8,128)}, f32[3,2,8,1024]{3,2,1,0:T(8,128)}) custom-call(f32[32,1,128]{2,1,0:T(1,128)S(1)} %all_to_all.5.gram_ref, f32[3,2,8,1024]{3,2,1,0:T(8,128)S(1)} %get-tuple-element.24.b_ref, f32[3,2,8,1024]{3,2,1,0:T(8,128)S(1)} %get-tuple-element.44.one_ref, f32[3,2,8,1024]{3,2,1,0:T(8,128)S(1)} %get-tuple-element.45.two_ref), custom_call_target="tpu_custom_call" | custom-call | flops 393216 | bytes 999424 | tf_op jit(solution)/shard_map/finish_kernel/pallas_call | solution.py:465
Async XLA Ops:
  2.1 8.0 %collective-permute-start = (f32[25,8,128]{2,1,0:T(8,128)S(1)}, f32[25,8,128]{2,1,0:T(8,128)S(1)}, u32[]{:S(2)}, u32[]{:S(2)}) collective-permute-start(f32[25,8,128]{2,1,0:T(8,128)S(1)} %get-tuple-element.29), channel_id=1, source_target_pairs={{0,4},{4,0},{8,12},{12,8},{16,20},{20,16},{24,28},{28,24},{1,5},{5... | collective-permute-start | bytes 307208 | tf_op jit(solution)/shard_map/ppermute | solution.py:479
  5.1 10.0 %collective-permute-start.1 = (f32[25,8,128]{2,1,0:T(8,128)S(1)}, f32[25,8,128]{2,1,0:T(8,128)S(1)}, u32[]{:S(2)}, u32[]{:S(2)}) collective-permute-start(f32[25,8,128]{2,1,0:T(8,128)S(1)} %get-tuple-element.30), channel_id=1, source_target_pairs={{4,8},{8,4},{12,16},{16,12},{20,24},{24,20},{5,9},{9,5},{13,17},{1... | collective-permute-start | bytes 307208 | tf_op jit(solution)/shard_map/ppermute | solution.py:479
  5.8 15.3 %collective-permute-start.3 = (f32[25,8,128]{2,1,0:T(8,128)S(1)}, f32[25,8,128]{2,1,0:T(8,128)S(1)}, u32[]{:S(2)}, u32[]{:S(2)}) collective-permute-start(f32[25,8,128]{2,1,0:T(8,128)S(1)} %get-tuple-element.30), channel_id=1, source_target_pairs={{0,4},{4,0},{8,12},{12,8},{16,20},{20,16},{24,28},{28,24},{1,5},{5... | collective-permute-start | bytes 307208 | tf_op jit(solution)/shard_map/ppermute | solution.py:479
  10.1 10.9 %collective-permute-start.2 = (f32[25,8,128]{2,1,0:T(8,128)S(1)}, f32[25,8,128]{2,1,0:T(8,128)S(1)}, u32[]{:S(2)}, u32[]{:S(2)}) collective-permute-start(f32[25,8,128]{2,1,0:T(8,128)S(1)} %collective-permute-done.near_ref), channel_id=1, source_target_pairs={{0,8},{8,16},{12,4},{16,24},{20,12},{28,20},{1,9},{9,17},{13,5},{1... | collective-permute-start | bytes 307208 | tf_op jit(solution)/shard_map/ppermute | solution.py:485
  15.2 6.0 %collective-permute-start.4 = (f32[5,4,1024]{2,1,0:T(4,128)S(1)}, f32[5,4,1024]{2,1,0:T(4,128)S(1)}, u32[]{:S(2)}, u32[]{:S(2)}) collective-permute-start(f32[5,4,1024]{2,1,0:T(4,128)S(1)} %get-tuple-element.41), channel_id=1, source_target_pairs={{1,2},{2,1},{5,6},{6,5},{9,10},{10,9},{13,14},{14,13},{17,18},{18,... | collective-permute-start | bytes 245768 | tf_op jit(solution)/shard_map/ppermute | solution.py:479
  15.9 5.3 %collective-permute-start.5 = (f32[5,4,1024]{2,1,0:T(4,128)S(1)}, f32[5,4,1024]{2,1,0:T(4,128)S(1)}, u32[]{:S(2)}, u32[]{:S(2)}) collective-permute-start(f32[5,4,1024]{2,1,0:T(4,128)S(1)} %get-tuple-element.42), channel_id=1, source_target_pairs={{0,1},{1,0},{2,3},{3,2},{4,5},{5,4},{6,7},{7,6},{8,9},{9,8},{10,11... | collective-permute-start | bytes 245768 | tf_op jit(solution)/shard_map/ppermute | solution.py:479

commit v28 on v27

--- a/solution.py
+++ b/solution.py
@@ -179,7 +179,7 @@
         (
             (taps_hbm, taps_ref),
             (valid_hbm, valid_ref),
-            *((seis_hbm.at[a], seis_ref.at[a]) for a in range(angles)),
+            (seis_hbm, seis_ref),
             (avo_hbm, avo_ref),
             (prior_hbm, prior_ref),
         ),
@@ -509,7 +509,7 @@
         [
             pltpu.VMEM(seismic.shape, seismic.dtype),
             pltpu.VMEM(wavelets.shape, F32),
-            pltpu.SemaphoreType.DMA((angles + 4,)),
+            pltpu.SemaphoreType.DMA((5,)),
         ],
         [HBM] * 5,
     )

time: 33.3 us -> 33.3 us (level)
  no operation moved by 1% of the time
where the time goes in v28:
time: 33.3 us; the launch traced here: 33.1 us
  starting transfers between devices  15.1 us (45%)
  blocking collectives  10 us (30%)
  Pallas kernels  7.22 us (22%)
  between operations  0.72 us (2%)
    ppermute x5, starting transfers between devices, swap(): lax.ppermute(value, axis, [(i + d, i + 1 - d) for i in starts for d in (0...  11.6 us
    all_to_all x1, blocking collectives, shards(): gram = lax.all_to_all(gram, axes, 0, 0)  10 us
    pallas_call x7, Pallas kernels, call(): pl.pallas_call(kernel, out_shape=outs, in_specs=[VMEM] * len(ins) if plac...  7.22 us
    ppermute x1, starting transfers between devices, hand_on(): lax.ppermute(value, axis, [(i, j) for i, j in steps if 0 <= j < size])  3.47 us
  transfers between devices with their start and end apart: 6, of which 0 were waited for; matrix products, arithmetic and copies ran while one was open for 0% of the time, Pallas kernels for 12%

profile of v28, /device:TPU:0, one launch (start us, length us, event | category | flops | bytes accessed | tf_op | source)
XLA Modules:
  0.0 33.1 jit_solution(8264850562635925615)
XLA Ops:
  0.6 1.4 %start_kernel.1 = (f32[3,2,8,1024]{3,2,1,0:T(8,128)S(1)}, f32[25,8,128]{2,1,0:T(8,128)S(1)}, f32[25,8,128]{2,1,0:T(8,128)S(1)}, f32[8,256]{1,0:T(8,128)S(1)}, s3...) custom-call(bf16[4,2,8,1024]{3,2,1,0:T(8,128)(2,1)} %seis_hbm.1, s32[4,2,8]{2,1,0:T(2,128)} %valid_hbm.1, ...), custom_call_target="tpu_custom_call" | custom-call | flops 134217728 | bytes 641680 | tf_op jit(solution)/shard_map/start_kernel/pallas_call | solution.py:465
  2.1 3.0 %collective-permute-start = (f32[25,8,128]{2,1,0:T(8,128)S(1)}, f32[25,8,128]{2,1,0:T(8,128)S(1)}, u32[]{:S(2)}, u32[]{:S(2)}) collective-permute-start(f32[25,8,128]{2,1,0:T(8,128)S(1)} %get-tuple-element.29), channel_id=1, source_target_pairs={{0,4},{4,0},{8,12},{12,8},{16,20},{20,16},{24,28},{28,24},{1,5},{5... | collective-permute-start | bytes 307208 | tf_op jit(solution)/shard_map/ppermute | solution.py:479
  5.1 0.7 %collective-permute-start.1 = (f32[25,8,128]{2,1,0:T(8,128)S(1)}, f32[25,8,128]{2,1,0:T(8,128)S(1)}, u32[]{:S(2)}, u32[]{:S(2)}) collective-permute-start(f32[25,8,128]{2,1,0:T(8,128)S(1)} %get-tuple-element.30), channel_id=1, source_target_pairs={{4,8},{8,4},{12,16},{16,12},{20,24},{24,20},{5,9},{9,5},{13,17},{1... | collective-permute-start | bytes 307208 | tf_op jit(solution)/shard_map/ppermute | solution.py:479
  5.7 4.3 %collective-permute-start.3 = (f32[25,8,128]{2,1,0:T(8,128)S(1)}, f32[25,8,128]{2,1,0:T(8,128)S(1)}, u32[]{:S(2)}, u32[]{:S(2)}) collective-permute-start(f32[25,8,128]{2,1,0:T(8,128)S(1)} %get-tuple-element.30), channel_id=1, source_target_pairs={{0,4},{4,0},{8,12},{12,8},{16,20},{20,16},{24,28},{28,24},{1,5},{5... | collective-permute-start | bytes 307208 | tf_op jit(solution)/shard_map/ppermute | solution.py:479
  10.1 0.0 collective-permute-done.near_ref
  10.1 3.5 %collective-permute-start.2 = (f32[25,8,128]{2,1,0:T(8,128)S(1)}, f32[25,8,128]{2,1,0:T(8,128)S(1)}, u32[]{:S(2)}, u32[]{:S(2)}) collective-permute-start(f32[25,8,128]{2,1,0:T(8,128)S(1)} %collective-permute-done.near_ref), channel_id=1, source_target_pairs={{0,8},{8,16},{12,4},{16,24},{20,12},{28,20},{1,9},{9,17},{13,5},{1... | collective-permute-start | bytes 307208 | tf_op jit(solution)/shard_map/ppermute | solution.py:485
  13.6 1.5 %data_kernel.1 = (f32[3,2,8,1024]{3,2,1,0:T(8,128)S(1)}, f32[4,256,256]{2,1,0:T(8,128)S(1)}, f32[4,256,256]{2,1,0:T(8,128)S(1)}, f32[8,128]{1,0:T(8,128)S(1)}, f32[1,3]{1,0:T(1,128)S(1)}) custom-call(f32[1,3]{1,0:T(1,128)} %bitcast.3, f32[3,2,8,1024]{3,2,1,0:T(8,128)S(1)} %get-tuple-element.24.b_ref, f32[8,256]{1,0:T(8,128)S(1)} %get-tuple-element.25.padded_ref, ...), custom_call_target="tpu_custom_call" | custom-call | flops 268435456 | bytes 2552088 | tf_op jit(solution)/shard_map/data_kernel/pallas_call | solution.py:465
  15.0 0.0 collective-permute-done.1.near_next_ref
  15.0 0.1 column_kernel.1
  15.2 0.7 %collective-permute-start.4 = (f32[5,4,1024]{2,1,0:T(4,128)S(1)}, f32[5,4,1024]{2,1,0:T(4,128)S(1)}, u32[]{:S(2)}, u32[]{:S(2)}) collective-permute-start(f32[5,4,1024]{2,1,0:T(4,128)S(1)} %get-tuple-element.41), channel_id=1, source_target_pairs={{1,2},{2,1},{5,6},{6,5},{9,10},{10,9},{13,14},{14,13},{17,18},{18,... | collective-permute-start | bytes 245768 | tf_op jit(solution)/shard_map/ppermute | solution.py:479
  15.8 2.9 %collective-permute-start.5 = (f32[5,4,1024]{2,1,0:T(4,128)S(1)}, f32[5,4,1024]{2,1,0:T(4,128)S(1)}, u32[]{:S(2)}, u32[]{:S(2)}) collective-permute-start(f32[5,4,1024]{2,1,0:T(4,128)S(1)} %get-tuple-element.42), channel_id=1, source_target_pairs={{0,1},{1,0},{2,3},{3,2},{4,5},{5,4},{6,7},{7,6},{8,9},{9,8},{10,11... | collective-permute-start | bytes 245768 | tf_op jit(solution)/shard_map/ppermute | solution.py:479
  18.8 2.2 %inner_kernel.1 = (f32[3,2,8,1024]{3,2,1,0:T(8,128)S(1)}, f32[3,2,8,1024]{3,2,1,0:T(8,128)S(1)}, f32[2,3,8,1024]{3,2,1,0:T(8,128)S(1)}) custom-call(f32[3,2,8,1024]{3,2,1,0:T(8,128)S(1)} %get-tuple-element.24.b_ref, f32[3,2,8,1024]{3,2,1,0:T(8,128)S(1)} %get-tuple-element.28.first_ref._, f32[25,8,128]{2,1,0:T(8,128)S(1)} %collective-permute-done.near_ref, ...), custom_call_target="tpu_custom_call" | custom-call | flops 536870912 | bytes 3334476 | tf_op jit(solution)/shard_map/inner_kernel/pallas_call | solution.py:465
  21.0 0.0 collective-permute-done.3.far_ref
  21.0 0.0 collective-permute-done.2.far_next_ref
  21.0 0.1 halo_kernel.1.halo_ref
  21.1 0.0 collective-permute-done.4.other_ref
  21.1 0.0 collective-permute-done.5.pair_ref
  21.1 1.0 %image_kernel.1 = (f32[3,2,8,1024]{3,2,1,0:T(8,128)S(1)}, f32[3,2,8,1024]{3,2,1,0:T(8,128)S(1)}, f32[32,1,128]{2,1,0:T(1,128)S(1)}) custom-call(f32[3,2,8,1024]{3,2,1,0:T(8,128)S(1)} %get-tuple-element.24.b_ref, f32[3,2,8,1024]{3,2,1,0:T(8,128)S(1)} %get-tuple-element.35.v_ref, f32[3,2,8,1024]{3,2,1,0:T(8,128)S(1)} %get-tuple-element.36.data_ref, ...), custom_call_target="tpu_custom_call" | custom-call | flops 134217728 | bytes 3612748 | tf_op jit(solution)/shard_map/image_kernel/pallas_call | solution.py:465
  22.1 10.0 %all_to_all.5.gram_ref = f32[32,1,128]{2,1,0:T(1,128)S(1)} all-to-all(f32[32,1,128]{2,1,0:T(1,128)S(1)} %get-tuple-element.43), channel_id=1, replica_groups=mesh['inline'=8,'col'=4] {'inline','col'}, dimensions={0} | all-to-all | bytes 32768 | tf_op jit(solution)/shard_map/all_to_all | solution.py:558
  32.1 0.9 %finish_kernel.1 = (f32[3,2,8,1024]{3,2,1,0:T(8,128)}, f32[3,2,8,1024]{3,2,1,0:T(8,128)}) custom-call(f32[32,1,128]{2,1,0:T(1,128)S(1)} %all_to_all.5.gram_ref, f32[3,2,8,1024]{3,2,1,0:T(8,128)S(1)} %get-tuple-element.24.b_ref, f32[3,2,8,1024]{3,2,1,0:T(8,128)S(1)} %get-tuple-element.44.one_ref, f32[3,2,8,1024]{3,2,1,0:T(8,128)S(1)} %get-tuple-element.45.two_ref), custom_call_target="tpu_custom_call" | custom-call | flops 393216 | bytes 999424 | tf_op jit(solution)/shard_map/finish_kernel/pallas_call | solution.py:465
Async XLA Ops:
  2.1 8.0 %collective-permute-start = (f32[25,8,128]{2,1,0:T(8,128)S(1)}, f32[25,8,128]{2,1,0:T(8,128)S(1)}, u32[]{:S(2)}, u32[]{:S(2)}) collective-permute-start(f32[25,8,128]{2,1,0:T(8,128)S(1)} %get-tuple-element.29), channel_id=1, source_target_pairs={{0,4},{4,0},{8,12},{12,8},{16,20},{20,16},{24,28},{28,24},{1,5},{5... | collective-permute-start | bytes 307208 | tf_op jit(solution)/shard_map/ppermute | solution.py:479
  5.1 10.0 %collective-permute-start.1 = (f32[25,8,128]{2,1,0:T(8,128)S(1)}, f32[25,8,128]{2,1,0:T(8,128)S(1)}, u32[]{:S(2)}, u32[]{:S(2)}) collective-permute-start(f32[25,8,128]{2,1,0:T(8,128)S(1)} %get-tuple-element.30), channel_id=1, source_target_pairs={{4,8},{8,4},{12,16},{16,12},{20,24},{24,20},{5,9},{9,5},{13,17},{1... | collective-permute-start | bytes 307208 | tf_op jit(solution)/shard_map/ppermute | solution.py:479
  5.7 15.3 %collective-permute-start.3 = (f32[25,8,128]{2,1,0:T(8,128)S(1)}, f32[25,8,128]{2,1,0:T(8,128)S(1)}, u32[]{:S(2)}, u32[]{:S(2)}) collective-permute-start(f32[25,8,128]{2,1,0:T(8,128)S(1)} %get-tuple-element.30), channel_id=1, source_target_pairs={{0,4},{4,0},{8,12},{12,8},{16,20},{20,16},{24,28},{28,24},{1,5},{5... | collective-permute-start | bytes 307208 | tf_op jit(solution)/shard_map/ppermute | solution.py:479
  10.1 10.9 %collective-permute-start.2 = (f32[25,8,128]{2,1,0:T(8,128)S(1)}, f32[25,8,128]{2,1,0:T(8,128)S(1)}, u32[]{:S(2)}, u32[]{:S(2)}) collective-permute-start(f32[25,8,128]{2,1,0:T(8,128)S(1)} %collective-permute-done.near_ref), channel_id=1, source_target_pairs={{0,8},{8,16},{12,4},{16,24},{20,12},{28,20},{1,9},{9,17},{13,5},{1... | collective-permute-start | bytes 307208 | tf_op jit(solution)/shard_map/ppermute | solution.py:485
  15.2 6.0 %collective-permute-start.4 = (f32[5,4,1024]{2,1,0:T(4,128)S(1)}, f32[5,4,1024]{2,1,0:T(4,128)S(1)}, u32[]{:S(2)}, u32[]{:S(2)}) collective-permute-start(f32[5,4,1024]{2,1,0:T(4,128)S(1)} %get-tuple-element.41), channel_id=1, source_target_pairs={{1,2},{2,1},{5,6},{6,5},{9,10},{10,9},{13,14},{14,13},{17,18},{18,... | collective-permute-start | bytes 245768 | tf_op jit(solution)/shard_map/ppermute | solution.py:479
  15.8 5.3 %collective-permute-start.5 = (f32[5,4,1024]{2,1,0:T(4,128)S(1)}, f32[5,4,1024]{2,1,0:T(4,128)S(1)}, u32[]{:S(2)}, u32[]{:S(2)}) collective-permute-start(f32[5,4,1024]{2,1,0:T(4,128)S(1)} %get-tuple-element.42), channel_id=1, source_target_pairs={{0,1},{1,0},{2,3},{3,2},{4,5},{5,4},{6,7},{7,6},{8,9},{9,8},{10,11... | collective-permute-start | bytes 245768 | tf_op jit(solution)/shard_map/ppermute | solution.py:479

commit v29 on v28

--- a/solution.py
+++ b/solution.py
@@ -171,7 +171,7 @@
 
 def start_kernel(
     seis_hbm, valid_hbm, avo_hbm, taps_hbm, prior_hbm,
-    b_ref, near_ref, far_ref, padded_ref, valid_ref, avo_ref, prior_ref,
+    b_ref, near_ref, far_ref, padded_ref, turned_ref, valid_ref, avo_ref, prior_ref,
     seis_ref, taps_ref, sems,
 ):
     angles = avo_ref.shape[1]
@@ -187,6 +187,7 @@
     )
     taps.wait()
     pad_taps(taps_ref, padded_ref)
+    turned_ref[...] = turn(padded_ref[...], taps_ref.shape[1])
     bands = [band(padded_ref[a : a + 1, :]) for a in range(angles)]
     valid.wait()
     masks = [trace_columns(valid_ref, a) for a in range(angles)]
@@ -284,28 +285,23 @@
 
 
 def data_kernel(
-    count, strength_hbm, b_ref, padded_ref, valid_ref, avo_ref,
-    data_ref, ahead_ref, back_ref, norm_ref, strength_ref, sem,
+    strength_hbm, b_ref, padded_ref, turned_ref, valid_ref, avo_ref,
+    data_ref, ahead_ref, back_ref, strength_ref, sem,
 ):
-    contrasts, rows = b_ref.shape[:2]
     angles = avo_ref.shape[1]
     (copy,) = copy_in(((strength_hbm, strength_ref),), sem)
-    turned = turn(padded_ref[...], count)
     bands = []
     for a in range(angles):
-        bands.append((band(turned[a : a + 1]), band(padded_ref[a : a + 1, :])))
+        bands.append((band(turned_ref[a : a + 1, :]), band(padded_ref[a : a + 1, :])))
         ahead_ref[a], back_ref[a] = (half.astype(F32) for half in bands[a])
     masks = [trace_columns(valid_ref, a) for a in range(angles)]
     store_tiles(data_ref, normal(stack_tiles(b_ref), masks, avo_ref, bands))
-    norm_ref[...] = functools.reduce(
-        jnp.add, [lane_tiles(b_ref[c, r] * b_ref[c, r]) for c in range(contrasts) for r in range(rows)]
-    )
     copy.wait()
 
 
 def inner_kernel(
     b_ref, first_ref, near_ref, near_next_ref, valid_ref, avo_ref, prior_ref, strength_ref,
-    ahead_ref, back_ref, v_ref, data_ref, halo_ref,
+    ahead_ref, back_ref, v_ref, data_ref, halo_ref, norm_ref,
 ):
     contrasts, rows, traces, samples = b_ref.shape
     angles, n = avo_ref.shape[1], samples // LANES
@@ -331,6 +327,9 @@
         for (up, low), line in zip(ends, stack_tiles(v_ref))
     ]
     total = normal(field, masks, avo_ref, bands)
+    norm_ref[...] = functools.reduce(
+        jnp.add, [lane_tiles(b_ref[c, r] * b_ref[c, r]) for c in range(contrasts) for r in range(rows)]
+    )
     has = inside("inline")
     for c in range(contrasts):
         strength = strength_ref[:, c : c + 1]
@@ -498,10 +497,10 @@
     given = (seismic, validity, avo_coeffs, wavelets, prior_weight)
     kept = [given[i] for i in (1, 2, 4)]
     edge = shape(contrasts * samples // LANES + 1, traces, LANES)
-    b, near, far, padded, *kept = call(
+    b, near, far, padded, turned, *kept = call(
         start_kernel,
         (
-            field, edge, edge, lines,
+            field, edge, edge, lines, lines,
             *[jax.ShapeDtypeStruct(x.shape, x.dtype) for x in kept],
         ),
         [pltpu.with_memory_space_constraint(x, pltpu.HBM) for x in given],
@@ -519,13 +518,13 @@
     far = swap("inline", far, 0)
     bands = shape(angles, 2 * LANES, 2 * LANES)
     strength = lateral_strength.reshape(1, -1)
-    first, ahead, back, norm, strength = call(
-        functools.partial(data_kernel, wavelets.shape[1]),
-        (field, bands, bands, shape(traces, LANES), shape(*strength.shape)),
-        (pltpu.with_memory_space_constraint(strength, pltpu.HBM), b, padded, kept[0], kept[1]),
+    first, ahead, back, strength = call(
+        data_kernel,
+        (field, bands, bands, shape(*strength.shape)),
+        (pltpu.with_memory_space_constraint(strength, pltpu.HBM), b, padded, turned, *kept[:2]),
         2 * work,
         [pltpu.SemaphoreType.DMA((1,))],
-        [HBM] + [VMEM] * 4,
+        [HBM] + [VMEM] * 5,
     )
     col_pair, col_other, own, note = call(
         column_kernel,
@@ -538,9 +537,9 @@
     col_pair = swap("col", col_pair, 0)
     bands = shape(angles, 2 * LANES, 2 * LANES)
     halo = shape(2, contrasts, traces, samples)
-    image, data, part = call(
+    image, data, part, norm = call(
         inner_kernel,
-        (field, field, halo),
+        (field, field, halo, shape(traces, LANES)),
         (b, first, near, near_next, *kept, strength, ahead, back),
         4 * work,
     )

time: 33.3 us -> 33.4 us (level)
  no operation moved by 1% of the time
where the time goes in v29:
time: 33.4 us; the launch traced here: 33.1 us
  starting transfers between devices  15.1 us (45%)
  blocking collectives  9.99 us (30%)
  Pallas kernels  7.28 us (22%)
  between operations  0.73 us (2%)
    ppermute x5, starting transfers between devices, swap(): lax.ppermute(value, axis, [(i + d, i + 1 - d) for i in starts for d in (0...  11.6 us
    all_to_all x1, blocking collectives, shards(): gram = lax.all_to_all(gram, axes, 0, 0)  9.99 us
    pallas_call x7, Pallas kernels, call(): pl.pallas_call(kernel, out_shape=outs, in_specs=[VMEM] * len(ins) if plac...  7.28 us
    ppermute x1, starting transfers between devices, hand_on(): lax.ppermute(value, axis, [(i, j) for i, j in steps if 0 <= j < size])  3.48 us
  transfers between devices with their start and end apart: 6, of which 0 were waited for; matrix products, arithmetic and copies ran while one was open for 0% of the time, Pallas kernels for 12%

profile of v29, /device:TPU:0, one launch (start us, length us, event | category | flops | bytes accessed | tf_op | source)
XLA Modules:
  0.0 33.1 jit_solution(2627629221148859880)
XLA Ops:
  0.6 1.4 %start_kernel.1 = (f32[3,2,8,1024]{3,2,1,0:T(8,128)S(1)}, f32[25,8,128]{2,1,0:T(8,128)S(1)}, f32[25,8,128]{2,1,0:T(8,128)S(1)}, f32[8,256]{1,0:T(8,128)S(1)}, f3...) custom-call(bf16[4,2,8,1024]{3,2,1,0:T(8,128)(2,1)} %seis_hbm.1, ...), custom_call_target="tpu_custom_call" | custom-call | flops 134217728 | bytes 649872 | tf_op jit(solution)/shard_map/start_kernel/pallas_call | solution.py:464
  2.1 3.0 %collective-permute-start = (f32[25,8,128]{2,1,0:T(8,128)S(1)}, f32[25,8,128]{2,1,0:T(8,128)S(1)}, u32[]{:S(2)}, u32[]{:S(2)}) collective-permute-start(f32[25,8,128]{2,1,0:T(8,128)S(1)} %get-tuple-element.31), channel_id=1, source_target_pairs={{0,4},{4,0},{8,12},{12,8},{16,20},{20,16},{24,28},{28,24},{1,5},{5... | collective-permute-start | bytes 307208 | tf_op jit(solution)/shard_map/ppermute | solution.py:478
  5.1 0.7 %collective-permute-start.1 = (f32[25,8,128]{2,1,0:T(8,128)S(1)}, f32[25,8,128]{2,1,0:T(8,128)S(1)}, u32[]{:S(2)}, u32[]{:S(2)}) collective-permute-start(f32[25,8,128]{2,1,0:T(8,128)S(1)} %get-tuple-element.32), channel_id=1, source_target_pairs={{4,8},{8,4},{12,16},{16,12},{20,24},{24,20},{5,9},{9,5},{13,17},{1... | collective-permute-start | bytes 307208 | tf_op jit(solution)/shard_map/ppermute | solution.py:478
  5.7 4.3 %collective-permute-start.3 = (f32[25,8,128]{2,1,0:T(8,128)S(1)}, f32[25,8,128]{2,1,0:T(8,128)S(1)}, u32[]{:S(2)}, u32[]{:S(2)}) collective-permute-start(f32[25,8,128]{2,1,0:T(8,128)S(1)} %get-tuple-element.32), channel_id=1, source_target_pairs={{0,4},{4,0},{8,12},{12,8},{16,20},{20,16},{24,28},{28,24},{1,5},{5... | collective-permute-start | bytes 307208 | tf_op jit(solution)/shard_map/ppermute | solution.py:478
  10.1 0.0 collective-permute-done.near_ref
  10.1 3.5 %collective-permute-start.2 = (f32[25,8,128]{2,1,0:T(8,128)S(1)}, f32[25,8,128]{2,1,0:T(8,128)S(1)}, u32[]{:S(2)}, u32[]{:S(2)}) collective-permute-start(f32[25,8,128]{2,1,0:T(8,128)S(1)} %collective-permute-done.near_ref), channel_id=1, source_target_pairs={{0,8},{8,16},{12,4},{16,24},{20,12},{28,20},{1,9},{9,17},{13,5},{1... | collective-permute-start | bytes 307208 | tf_op jit(solution)/shard_map/ppermute | solution.py:484
  13.6 1.5 %data_kernel.1 = (f32[3,2,8,1024]{3,2,1,0:T(8,128)S(1)}, f32[4,256,256]{2,1,0:T(8,128)S(1)}, f32[4,256,256]{2,1,0:T(8,128)S(1)}, f32[1,3]{1,0:T(1,128)S(1)}) custom-call(f32[1,3]{1,0:T(1,128)} %bitcast.3, f32[3,2,8,1024]{3,2,1,0:T(8,128)S(1)} %get-tuple-element.25.b_ref, f32[8,256]{1,0:T(8,128)S(1)} %get-tuple-element.26.padded_ref, ...), custom_call_target="tpu_custom_call" | custom-call | flops 268435456 | bytes 2556184 | tf_op jit(solution)/shard_map/data_kernel/pallas_call | solution.py:464
  15.1 0.0 collective-permute-done.1.near_next_ref
  15.1 0.1 column_kernel.1
  15.2 0.7 %collective-permute-start.4 = (f32[5,4,1024]{2,1,0:T(4,128)S(1)}, f32[5,4,1024]{2,1,0:T(4,128)S(1)}, u32[]{:S(2)}, u32[]{:S(2)}) collective-permute-start(f32[5,4,1024]{2,1,0:T(4,128)S(1)} %get-tuple-element.43), channel_id=1, source_target_pairs={{1,2},{2,1},{5,6},{6,5},{9,10},{10,9},{13,14},{14,13},{17,18},{18,... | collective-permute-start | bytes 245768 | tf_op jit(solution)/shard_map/ppermute | solution.py:478
  15.9 2.9 %collective-permute-start.5 = (f32[5,4,1024]{2,1,0:T(4,128)S(1)}, f32[5,4,1024]{2,1,0:T(4,128)S(1)}, u32[]{:S(2)}, u32[]{:S(2)}) collective-permute-start(f32[5,4,1024]{2,1,0:T(4,128)S(1)} %get-tuple-element.44), channel_id=1, source_target_pairs={{0,1},{1,0},{2,3},{3,2},{4,5},{5,4},{6,7},{7,6},{8,9},{9,8},{10,11... | collective-permute-start | bytes 245768 | tf_op jit(solution)/shard_map/ppermute | solution.py:478
  18.8 2.2 %inner_kernel.1 = (f32[3,2,8,1024]{3,2,1,0:T(8,128)S(1)}, f32[3,2,8,1024]{3,2,1,0:T(8,128)S(1)}, f32[2,3,8,1024]{3,2,1,0:T(8,128)S(1)}, f32[8,128]{1,0:T(8,128)S(1)}) custom-call(f32[3,2,8,1024]{3,2,1,0:T(8,128)S(1)} %get-tuple-element.25.b_ref, f32[3,2,8,1024]{3,2,1,0:T(8,128)S(1)} %get-tuple-element.30.first_ref._, ...), custom_call_target="tpu_custom_call" | custom-call | flops 536870912 | bytes 3338572 | tf_op jit(solution)/shard_map/inner_kernel/pallas_call | solution.py:464
  21.1 0.0 collective-permute-done.3.far_ref
  21.1 0.0 collective-permute-done.2.far_next_ref
  21.1 0.1 halo_kernel.1.halo_ref
  21.2 0.0 collective-permute-done.4.other_ref
  21.2 0.0 collective-permute-done.5.pair_ref
  21.2 1.0 %image_kernel.1 = (f32[3,2,8,1024]{3,2,1,0:T(8,128)S(1)}, f32[3,2,8,1024]{3,2,1,0:T(8,128)S(1)}, f32[32,1,128]{2,1,0:T(1,128)S(1)}) custom-call(f32[3,2,8,1024]{3,2,1,0:T(8,128)S(1)} %get-tuple-element.25.b_ref, f32[3,2,8,1024]{3,2,1,0:T(8,128)S(1)} %get-tuple-element.37.v_ref, f32[3,2,8,1024]{3,2,1,0:T(8,128)S(1)} %get-tuple-element.38.data_ref, ...), custom_call_target="tpu_custom_call" | custom-call | flops 134217728 | bytes 3612748 | tf_op jit(solution)/shard_map/image_kernel/pallas_call | solution.py:464
  22.2 10.0 %all_to_all.5.gram_ref = f32[32,1,128]{2,1,0:T(1,128)S(1)} all-to-all(f32[32,1,128]{2,1,0:T(1,128)S(1)} %get-tuple-element.45), channel_id=1, replica_groups=mesh['inline'=8,'col'=4] {'inline','col'}, dimensions={0} | all-to-all | bytes 32768 | tf_op jit(solution)/shard_map/all_to_all | solution.py:557
  32.2 0.9 %finish_kernel.1 = (f32[3,2,8,1024]{3,2,1,0:T(8,128)}, f32[3,2,8,1024]{3,2,1,0:T(8,128)}) custom-call(f32[32,1,128]{2,1,0:T(1,128)S(1)} %all_to_all.5.gram_ref, f32[3,2,8,1024]{3,2,1,0:T(8,128)S(1)} %get-tuple-element.25.b_ref, f32[3,2,8,1024]{3,2,1,0:T(8,128)S(1)} %get-tuple-element.46.one_ref, f32[3,2,8,1024]{3,2,1,0:T(8,128)S(1)} %get-tuple-element.47.two_ref), custom_call_target="tpu_custom_call" | custom-call | flops 393216 | bytes 999424 | tf_op jit(solution)/shard_map/finish_kernel/pallas_call | solution.py:464
Async XLA Ops:
  2.1 8.0 %collective-permute-start = (f32[25,8,128]{2,1,0:T(8,128)S(1)}, f32[25,8,128]{2,1,0:T(8,128)S(1)}, u32[]{:S(2)}, u32[]{:S(2)}) collective-permute-start(f32[25,8,128]{2,1,0:T(8,128)S(1)} %get-tuple-element.31), channel_id=1, source_target_pairs={{0,4},{4,0},{8,12},{12,8},{16,20},{20,16},{24,28},{28,24},{1,5},{5... | collective-permute-start | bytes 307208 | tf_op jit(solution)/shard_map/ppermute | solution.py:478
  5.1 10.0 %collective-permute-start.1 = (f32[25,8,128]{2,1,0:T(8,128)S(1)}, f32[25,8,128]{2,1,0:T(8,128)S(1)}, u32[]{:S(2)}, u32[]{:S(2)}) collective-permute-start(f32[25,8,128]{2,1,0:T(8,128)S(1)} %get-tuple-element.32), channel_id=1, source_target_pairs={{4,8},{8,4},{12,16},{16,12},{20,24},{24,20},{5,9},{9,5},{13,17},{1... | collective-permute-start | bytes 307208 | tf_op jit(solution)/shard_map/ppermute | solution.py:478
  5.7 15.3 %collective-permute-start.3 = (f32[25,8,128]{2,1,0:T(8,128)S(1)}, f32[25,8,128]{2,1,0:T(8,128)S(1)}, u32[]{:S(2)}, u32[]{:S(2)}) collective-permute-start(f32[25,8,128]{2,1,0:T(8,128)S(1)} %get-tuple-element.32), channel_id=1, source_target_pairs={{0,4},{4,0},{8,12},{12,8},{16,20},{20,16},{24,28},{28,24},{1,5},{5... | collective-permute-start | bytes 307208 | tf_op jit(solution)/shard_map/ppermute | solution.py:478
  10.1 11.0 %collective-permute-start.2 = (f32[25,8,128]{2,1,0:T(8,128)S(1)}, f32[25,8,128]{2,1,0:T(8,128)S(1)}, u32[]{:S(2)}, u32[]{:S(2)}) collective-permute-start(f32[25,8,128]{2,1,0:T(8,128)S(1)} %collective-permute-done.near_ref), channel_id=1, source_target_pairs={{0,8},{8,16},{12,4},{16,24},{20,12},{28,20},{1,9},{9,17},{13,5},{1... | collective-permute-start | bytes 307208 | tf_op jit(solution)/shard_map/ppermute | solution.py:484
  15.2 6.0 %collective-permute-start.4 = (f32[5,4,1024]{2,1,0:T(4,128)S(1)}, f32[5,4,1024]{2,1,0:T(4,128)S(1)}, u32[]{:S(2)}, u32[]{:S(2)}) collective-permute-start(f32[5,4,1024]{2,1,0:T(4,128)S(1)} %get-tuple-element.43), channel_id=1, source_target_pairs={{1,2},{2,1},{5,6},{6,5},{9,10},{10,9},{13,14},{14,13},{17,18},{18,... | collective-permute-start | bytes 245768 | tf_op jit(solution)/shard_map/ppermute | solution.py:478
  15.9 5.3 %collective-permute-start.5 = (f32[5,4,1024]{2,1,0:T(4,128)S(1)}, f32[5,4,1024]{2,1,0:T(4,128)S(1)}, u32[]{:S(2)}, u32[]{:S(2)}) collective-permute-start(f32[5,4,1024]{2,1,0:T(4,128)S(1)} %get-tuple-element.44), channel_id=1, source_target_pairs={{0,1},{1,0},{2,3},{3,2},{4,5},{5,4},{6,7},{7,6},{8,9},{9,8},{10,11... | collective-permute-start | bytes 245768 | tf_op jit(solution)/shard_map/ppermute | solution.py:478

commit v30 on v28

--- a/solution.py
+++ b/solution.py
@@ -59,7 +59,7 @@
 
 
 def thirds(value):
-    kind = BF16 if value.shape[0] % 16 == 0 else F32
+    kind = BF16
     parts = []
     for _ in range(3):
         high = value.astype(BF16)

time: 33.3 us -> 33.3 us (level)
  no operation moved by 1% of the time
where the time goes in v30:
time: 33.3 us; the launch traced here: 33 us
  starting transfers between devices  15.1 us (45%)
  blocking collectives  10 us (30%)
  Pallas kernels  7.22 us (22%)
  between operations  0.72 us (2%)
    ppermute x5, starting transfers between devices, swap(): lax.ppermute(value, axis, [(i + d, i + 1 - d) for i in starts for d in (0...  11.6 us
    all_to_all x1, blocking collectives, shards(): gram = lax.all_to_all(gram, axes, 0, 0)  10 us
    pallas_call x7, Pallas kernels, call(): pl.pallas_call(kernel, out_shape=outs, in_specs=[VMEM] * len(ins) if plac...  7.22 us
    ppermute x1, starting transfers between devices, hand_on(): lax.ppermute(value, axis, [(i, j) for i, j in steps if 0 <= j < size])  3.47 us
  transfers between devices with their start and end apart: 6, of which 0 were waited for; matrix products, arithmetic and copies ran while one was open for 0% of the time, Pallas kernels for 12%

profile of v30, /device:TPU:0, one launch (start us, length us, event | category | flops | bytes accessed | tf_op | source)
XLA Modules:
  0.0 33.0 jit_solution(4471918471503761989)
XLA Ops:
  0.6 1.4 %start_kernel.1 = (f32[3,2,8,1024]{3,2,1,0:T(8,128)S(1)}, f32[25,8,128]{2,1,0:T(8,128)S(1)}, f32[25,8,128]{2,1,0:T(8,128)S(1)}, f32[8,256]{1,0:T(8,128)S(1)}, s3...) custom-call(bf16[4,2,8,1024]{3,2,1,0:T(8,128)(2,1)} %seis_hbm.1, s32[4,2,8]{2,1,0:T(2,128)} %valid_hbm.1, ...), custom_call_target="tpu_custom_call" | custom-call | flops 134217728 | bytes 641680 | tf_op jit(solution)/shard_map/start_kernel/pallas_call | solution.py:465
  2.1 3.0 %collective-permute-start = (f32[25,8,128]{2,1,0:T(8,128)S(1)}, f32[25,8,128]{2,1,0:T(8,128)S(1)}, u32[]{:S(2)}, u32[]{:S(2)}) collective-permute-start(f32[25,8,128]{2,1,0:T(8,128)S(1)} %get-tuple-element.29), channel_id=1, source_target_pairs={{0,4},{4,0},{8,12},{12,8},{16,20},{20,16},{24,28},{28,24},{1,5},{5... | collective-permute-start | bytes 307208 | tf_op jit(solution)/shard_map/ppermute | solution.py:479
  5.1 0.7 %collective-permute-start.1 = (f32[25,8,128]{2,1,0:T(8,128)S(1)}, f32[25,8,128]{2,1,0:T(8,128)S(1)}, u32[]{:S(2)}, u32[]{:S(2)}) collective-permute-start(f32[25,8,128]{2,1,0:T(8,128)S(1)} %get-tuple-element.30), channel_id=1, source_target_pairs={{4,8},{8,4},{12,16},{16,12},{20,24},{24,20},{5,9},{9,5},{13,17},{1... | collective-permute-start | bytes 307208 | tf_op jit(solution)/shard_map/ppermute | solution.py:479
  5.7 4.3 %collective-permute-start.3 = (f32[25,8,128]{2,1,0:T(8,128)S(1)}, f32[25,8,128]{2,1,0:T(8,128)S(1)}, u32[]{:S(2)}, u32[]{:S(2)}) collective-permute-start(f32[25,8,128]{2,1,0:T(8,128)S(1)} %get-tuple-element.30), channel_id=1, source_target_pairs={{0,4},{4,0},{8,12},{12,8},{16,20},{20,16},{24,28},{28,24},{1,5},{5... | collective-permute-start | bytes 307208 | tf_op jit(solution)/shard_map/ppermute | solution.py:479
  10.1 0.0 collective-permute-done.near_ref
  10.1 3.5 %collective-permute-start.2 = (f32[25,8,128]{2,1,0:T(8,128)S(1)}, f32[25,8,128]{2,1,0:T(8,128)S(1)}, u32[]{:S(2)}, u32[]{:S(2)}) collective-permute-start(f32[25,8,128]{2,1,0:T(8,128)S(1)} %collective-permute-done.near_ref), channel_id=1, source_target_pairs={{0,8},{8,16},{12,4},{16,24},{20,12},{28,20},{1,9},{9,17},{13,5},{1... | collective-permute-start | bytes 307208 | tf_op jit(solution)/shard_map/ppermute | solution.py:485
  13.6 1.5 %data_kernel.1 = (f32[3,2,8,1024]{3,2,1,0:T(8,128)S(1)}, f32[4,256,256]{2,1,0:T(8,128)S(1)}, f32[4,256,256]{2,1,0:T(8,128)S(1)}, f32[8,128]{1,0:T(8,128)S(1)}, f32[1,3]{1,0:T(1,128)S(1)}) custom-call(f32[1,3]{1,0:T(1,128)} %bitcast.3, f32[3,2,8,1024]{3,2,1,0:T(8,128)S(1)} %get-tuple-element.24.b_ref, f32[8,256]{1,0:T(8,128)S(1)} %get-tuple-element.25.padded_ref, ...), custom_call_target="tpu_custom_call" | custom-call | flops 268435456 | bytes 2552088 | tf_op jit(solution)/shard_map/data_kernel/pallas_call | solution.py:465
  15.0 0.0 collective-permute-done.1.near_next_ref
  15.0 0.1 column_kernel.1
  15.2 0.7 %collective-permute-start.4 = (f32[5,4,1024]{2,1,0:T(4,128)S(1)}, f32[5,4,1024]{2,1,0:T(4,128)S(1)}, u32[]{:S(2)}, u32[]{:S(2)}) collective-permute-start(f32[5,4,1024]{2,1,0:T(4,128)S(1)} %get-tuple-element.41), channel_id=1, source_target_pairs={{1,2},{2,1},{5,6},{6,5},{9,10},{10,9},{13,14},{14,13},{17,18},{18,... | collective-permute-start | bytes 245768 | tf_op jit(solution)/shard_map/ppermute | solution.py:479
  15.8 2.9 %collective-permute-start.5 = (f32[5,4,1024]{2,1,0:T(4,128)S(1)}, f32[5,4,1024]{2,1,0:T(4,128)S(1)}, u32[]{:S(2)}, u32[]{:S(2)}) collective-permute-start(f32[5,4,1024]{2,1,0:T(4,128)S(1)} %get-tuple-element.42), channel_id=1, source_target_pairs={{0,1},{1,0},{2,3},{3,2},{4,5},{5,4},{6,7},{7,6},{8,9},{9,8},{10,11... | collective-permute-start | bytes 245768 | tf_op jit(solution)/shard_map/ppermute | solution.py:479
  18.8 2.2 %inner_kernel.1 = (f32[3,2,8,1024]{3,2,1,0:T(8,128)S(1)}, f32[3,2,8,1024]{3,2,1,0:T(8,128)S(1)}, f32[2,3,8,1024]{3,2,1,0:T(8,128)S(1)}) custom-call(f32[3,2,8,1024]{3,2,1,0:T(8,128)S(1)} %get-tuple-element.24.b_ref, f32[3,2,8,1024]{3,2,1,0:T(8,128)S(1)} %get-tuple-element.28.first_ref._, f32[25,8,128]{2,1,0:T(8,128)S(1)} %collective-permute-done.near_ref, ...), custom_call_target="tpu_custom_call" | custom-call | flops 536870912 | bytes 3334476 | tf_op jit(solution)/shard_map/inner_kernel/pallas_call | solution.py:465
  21.0 0.0 collective-permute-done.3.far_ref
  21.0 0.0 collective-permute-done.2.far_next_ref
  21.0 0.1 halo_kernel.1.halo_ref
  21.1 0.0 collective-permute-done.4.other_ref
  21.1 0.0 collective-permute-done.5.pair_ref
  21.1 0.9 %image_kernel.1 = (f32[3,2,8,1024]{3,2,1,0:T(8,128)S(1)}, f32[3,2,8,1024]{3,2,1,0:T(8,128)S(1)}, f32[32,1,128]{2,1,0:T(1,128)S(1)}) custom-call(f32[3,2,8,1024]{3,2,1,0:T(8,128)S(1)} %get-tuple-element.24.b_ref, f32[3,2,8,1024]{3,2,1,0:T(8,128)S(1)} %get-tuple-element.35.v_ref, f32[3,2,8,1024]{3,2,1,0:T(8,128)S(1)} %get-tuple-element.36.data_ref, ...), custom_call_target="tpu_custom_call" | custom-call | flops 134217728 | bytes 3612748 | tf_op jit(solution)/shard_map/image_kernel/pallas_call | solution.py:465
  22.1 10.0 %all_to_all.5.gram_ref = f32[32,1,128]{2,1,0:T(1,128)S(1)} all-to-all(f32[32,1,128]{2,1,0:T(1,128)S(1)} %get-tuple-element.43), channel_id=1, replica_groups=mesh['inline'=8,'col'=4] {'inline','col'}, dimensions={0} | all-to-all | bytes 32768 | tf_op jit(solution)/shard_map/all_to_all | solution.py:558
  32.1 0.9 %finish_kernel.1 = (f32[3,2,8,1024]{3,2,1,0:T(8,128)}, f32[3,2,8,1024]{3,2,1,0:T(8,128)}) custom-call(f32[32,1,128]{2,1,0:T(1,128)S(1)} %all_to_all.5.gram_ref, f32[3,2,8,1024]{3,2,1,0:T(8,128)S(1)} %get-tuple-element.24.b_ref, f32[3,2,8,1024]{3,2,1,0:T(8,128)S(1)} %get-tuple-element.44.one_ref, f32[3,2,8,1024]{3,2,1,0:T(8,128)S(1)} %get-tuple-element.45.two_ref), custom_call_target="tpu_custom_call" | custom-call | flops 393216 | bytes 999424 | tf_op jit(solution)/shard_map/finish_kernel/pallas_call | solution.py:465
Async XLA Ops:
  2.1 8.0 %collective-permute-start = (f32[25,8,128]{2,1,0:T(8,128)S(1)}, f32[25,8,128]{2,1,0:T(8,128)S(1)}, u32[]{:S(2)}, u32[]{:S(2)}) collective-permute-start(f32[25,8,128]{2,1,0:T(8,128)S(1)} %get-tuple-element.29), channel_id=1, source_target_pairs={{0,4},{4,0},{8,12},{12,8},{16,20},{20,16},{24,28},{28,24},{1,5},{5... | collective-permute-start | bytes 307208 | tf_op jit(solution)/shard_map/ppermute | solution.py:479
  5.1 10.0 %collective-permute-start.1 = (f32[25,8,128]{2,1,0:T(8,128)S(1)}, f32[25,8,128]{2,1,0:T(8,128)S(1)}, u32[]{:S(2)}, u32[]{:S(2)}) collective-permute-start(f32[25,8,128]{2,1,0:T(8,128)S(1)} %get-tuple-element.30), channel_id=1, source_target_pairs={{4,8},{8,4},{12,16},{16,12},{20,24},{24,20},{5,9},{9,5},{13,17},{1... | collective-permute-start | bytes 307208 | tf_op jit(solution)/shard_map/ppermute | solution.py:479
  5.7 15.3 %collective-permute-start.3 = (f32[25,8,128]{2,1,0:T(8,128)S(1)}, f32[25,8,128]{2,1,0:T(8,128)S(1)}, u32[]{:S(2)}, u32[]{:S(2)}) collective-permute-start(f32[25,8,128]{2,1,0:T(8,128)S(1)} %get-tuple-element.30), channel_id=1, source_target_pairs={{0,4},{4,0},{8,12},{12,8},{16,20},{20,16},{24,28},{28,24},{1,5},{5... | collective-permute-start | bytes 307208 | tf_op jit(solution)/shard_map/ppermute | solution.py:479
  10.1 10.9 %collective-permute-start.2 = (f32[25,8,128]{2,1,0:T(8,128)S(1)}, f32[25,8,128]{2,1,0:T(8,128)S(1)}, u32[]{:S(2)}, u32[]{:S(2)}) collective-permute-start(f32[25,8,128]{2,1,0:T(8,128)S(1)} %collective-permute-done.near_ref), channel_id=1, source_target_pairs={{0,8},{8,16},{12,4},{16,24},{20,12},{28,20},{1,9},{9,17},{13,5},{1... | collective-permute-start | bytes 307208 | tf_op jit(solution)/shard_map/ppermute | solution.py:485
  15.2 6.0 %collective-permute-start.4 = (f32[5,4,1024]{2,1,0:T(4,128)S(1)}, f32[5,4,1024]{2,1,0:T(4,128)S(1)}, u32[]{:S(2)}, u32[]{:S(2)}) collective-permute-start(f32[5,4,1024]{2,1,0:T(4,128)S(1)} %get-tuple-element.41), channel_id=1, source_target_pairs={{1,2},{2,1},{5,6},{6,5},{9,10},{10,9},{13,14},{14,13},{17,18},{18,... | collective-permute-start | bytes 245768 | tf_op jit(solution)/shard_map/ppermute | solution.py:479
  15.8 5.3 %collective-permute-start.5 = (f32[5,4,1024]{2,1,0:T(4,128)S(1)}, f32[5,4,1024]{2,1,0:T(4,128)S(1)}, u32[]{:S(2)}, u32[]{:S(2)}) collective-permute-start(f32[5,4,1024]{2,1,0:T(4,128)S(1)} %get-tuple-element.42), channel_id=1, source_target_pairs={{0,1},{1,0},{2,3},{3,2},{4,5},{5,4},{6,7},{7,6},{8,9},{9,8},{10,11... | collective-permute-start | bytes 245768 | tf_op jit(solution)/shard_map/ppermute | solution.py:479
